TPU v7x, 32 devices: a whole 2x2x4 slice. The times are simulated.
32 devices in a mesh: grp: 4 (over y, x), tile: 8 (over z, core).
Axes of the slice: x: 2, y: 2, z: 4, core: 2. Of those that a mesh axis runs over, the one named last changes fastest.
Arguments:
- tangents: float32 [2, 192, 64, 512], P(None, None, 'tile', 'grp'), may hold values from -60000 to 60000
- reaction_self: float32 [64, 512], P('tile', 'grp'), may hold values from -0.45 to -0.2
- reaction_cross: float32 [64, 512], P('tile', 'grp'), may hold values from -0.3 to -0.02
Outputs:
- corrections: float32 [6144, 192], P(('grp', 'tile'))
- growth: float32 [192], replicated
All inputs are finite; a program needn't handle non-finite values.
Results may differ from a plain program's by a relative error of at most 0.0003.
Values sent between devices are 32-bit elements; how exact they have to be, the bound alone decides.
No kernel may reach another device: no remote copies, remote signals or barrier semaphores. Data moves between devices by JAX's collectives and lax.ppermute only.
A program may use at most 64 MiB of HBM per device.

v0:
```python
import functools
import math

import jax
import jax.numpy as jnp
from jax import lax
from jax.experimental import pallas as pl
from jax.experimental.pallas import tpu as pltpu
from jax.sharding import PartitionSpec as P


STEPS = 4
diffusion = 0.2
slow_rate = 0.05
SIDE = 64
LANES = 128
SUB = 8
HI = lax.Precision.HIGHEST

def dot_nn(a, b):
    return lax.dot_general(a, b, (((1,), (0,)), ((), ())), precision=HI, preferred_element_type=jnp.float32)
def dot_tn(a, b):
    return lax.dot_general(a, b, (((0,), (0,)), ((), ())), precision=HI, preferred_element_type=jnp.float32)
def dot_nt(a, b):
    return lax.dot_general(a, b, (((1,), (1,)), ((), ())), precision=HI, preferred_element_type=jnp.float32)

def block_pairs(n):
    return [(i, j) for i in range(n) for j in range(i, n)]

def unpack_blocks(ref, n):
    out = {}
    for index, key in enumerate(block_pairs(n)):
        row, half = divmod(index, 2)
        out[key] = ref[row*SIDE:(row+1)*SIDE, half*SIDE:(half+1)*SIDE]
    return out

def spread_lane(x, lane):
    return jnp.broadcast_to(x[:, lane:lane+1], (x.shape[0], LANES))
def spread_row(x, row):
    return jnp.broadcast_to(x[row:row+1, :], (SUB, x.shape[1]))

def factor_blocks(blocks):
    groups = SIDE // SUB
    eye = (lax.broadcasted_iota(jnp.int32, (SIDE, SIDE), 0) == lax.broadcasted_iota(jnp.int32, (SIDE, SIDE), 1)).astype(jnp.float32)
    sub = lax.broadcasted_iota(jnp.int32, (SUB, LANES), 0)
    states = []
    for d in blocks:
        whole = jnp.concatenate([d, eye], axis=1)
        states.append([whole[g*SUB:(g+1)*SUB] for g in range(groups)])
    done = [[] for _ in blocks]
    for p in range(groups):
        for s, v in enumerate(states):
            cols = {}
            for g in range(p, groups):
                for c in range(SUB):
                    cols[g, c] = spread_lane(v[g], p*SUB + c)
            rows = [spread_row(v[p], c) for c in range(SUB)]
            pivots = {(a, c): spread_row(cols[p, c], a) for c in range(SUB) for a in range(c, SUB)}
            mult = {}
            scale = []
            for c in range(SUB):
                inv = 1.0 / pivots[c, c]
                scale.append(lax.rsqrt(pivots[c, c]))
                for a in range(c + 1, SUB):
                    mult[a, c] = pivots[a, c] * inv
                    rows[a] = rows[a] - mult[a, c] * rows[c]
                    for b in range(c + 1, a + 1):
                        pivots[a, b] = pivots[a, b] - mult[a, c] * pivots[b, c]
            scaled = [rows[c] * scale[c] for c in range(SUB)]
            panel = scaled[0]
            for c in range(1, SUB):
                panel = jnp.where(sub == c, scaled[c], panel)
            done[s].append(panel)
            for g in range(p + 1, groups):
                for c in range(SUB):
                    for a in range(c + 1, SUB):
                        cols[g, a] = cols[g, a] - mult[a, c] * cols[g, c]
                    v[g] = v[g] - (cols[g, c] * scale[c]) * scaled[c]
    out = []
    for panels in done:
        whole = jnp.concatenate(panels, axis=0)
        out.append((whole[:, :SIDE], whole[:, SIDE:]))
    return out

def factor_kernel(n, weight, tot_ref, loc_ref, out_ref, growth_ref):
    total = unpack_blocks(tot_ref, n)
    local = unpack_blocks(loc_ref, n)
    keep = (lax.broadcasted_iota(jnp.int32, (SIDE, SIDE), 0) <= lax.broadcasted_iota(jnp.int32, (SIDE, SIDE), 1))
    diag = (lax.broadcasted_iota(jnp.int32, (SIDE, SIDE), 0) == lax.broadcasted_iota(jnp.int32, (SIDE, SIDE), 1))
    inverse = {}
    answer = {}
    for k in range(n):
        (r_t, i_t), (r_l, i_l) = factor_blocks([total[k, k], local[k, k]])
        inverse[k] = i_t
        local[k, k] = jnp.where(keep, r_l, 0.0)
        growth_ref[0, k*SIDE:(k+1)*SIDE] = jnp.log(jnp.sum(jnp.where(diag, r_t, 0.0), axis=0))
        for grams, inv in ((total, i_t), (local, i_l)):
            if k + 1 < n:
                row = dot_nn(inv, jnp.concatenate([grams[k, j] for j in range(k + 1, n)], axis=1))
                for j in range(k + 1, n):
                    grams[k, j] = row[:, (j-k-1)*SIDE:(j-k)*SIDE]
                for i in range(k + 1, n):
                    rest = dot_tn(grams[k, i], row[:, (i-k-1)*SIDE:])
                    for j in range(i, n):
                        grams[i, j] = grams[i, j] - rest[:, (j-i)*SIDE:(j-i+1)*SIDE]
    for j in range(n):
        for i in range(j + 1):
            rest = local[i, j]
            for m in range(i, j):
                rest = rest - dot_nn(answer[i, m], total[m, j])
            answer[i, j] = dot_nt(rest, inverse[j])
            out_ref[i*SIDE:(i+1)*SIDE, j*SIDE:(j+1)*SIDE] = weight * answer[i, j]
        for i in range(j + 1, n):
            out_ref[i*SIDE:(i+1)*SIDE, j*SIDE:(j+1)*SIDE] = jnp.zeros((SIDE, SIDE), jnp.float32)

def factor_call(total, local, k, weight):
    vm = pl.BlockSpec(memory_space=pltpu.VMEM)
    out, growth = pl.pallas_call(
        functools.partial(factor_kernel, k // SIDE, weight),
        out_shape=(jax.ShapeDtypeStruct((k, k), jnp.float32), jax.ShapeDtypeStruct((1, k), jnp.float32)),
        in_specs=[vm, vm], out_specs=(vm, vm), name="factor",
    )(total, local)
    return out, growth[0]


def pick(flag, first, second):
    return jnp.where(flag, first, second)


def roll(x, shift):
    return pltpu.roll(x, shift % LANES, 1)


def lane_index():
    return lax.broadcasted_iota(jnp.int32, (SUB, LANES), 1)


def group(g):
    return pl.ds(pl.multiple_of(g * SUB, SUB), SUB)


def own_rows(tangents, g):
    return [[tangents[f, pl.ds(g * SUB * SUB + r, SUB, stride=SUB), :] for r in range(SUB)] for f in range(2)]


def own_coeffs(coeff_self, coeff_cross):
    return [[spread_row(ref[...], r) for r in range(SUB)] for ref in (coeff_self, coeff_cross)]


def edge_columns(slots):
    cell = lane_index() // SUB
    cells = LANES // SUB
    last, first = None, None
    for s, row in slots.items():
        turned = roll(row, (s + 1) * SUB)
        last = turned if last is None else jnp.where(cell == s, turned, last)
        first = turned if first is None else jnp.where(cell == (s + 1) % cells, turned, first)
    return last, roll(first, -SUB)


def pack_kernel(fields, tangents, coeff_self, coeff_cross, near, far, edges):
    odd = lax.axis_index("tile") % 2 == 1
    inner = lane_index() % SUB < STEPS

    def send(g, rows):
        for f in range(2):
            count = STEPS - f
            for j in range(count):
                top, bottom = rows[f][j], rows[f][SUB - count + j]
                near[f * STEPS + j, group(g), :] = pick(odd, top, bottom)
                far[f * STEPS + j, group(g), :] = pick(odd, bottom, top)
        last, first = edge_columns({f * SUB + r: rows[f][r] for f in range(2) for r in range(SUB)})
        edges[group(g), :] = jnp.where(inner, first, last)

    @pl.loop(0, fields // SUB)
    def _(g):
        send(g, own_rows(tangents, g))

    send(fields // SUB, own_coeffs(coeff_self, coeff_cross))


def column_kernel(edges, near, far, fast_edges, slow_edges, near_out, far_out):
    tile, tiles = lax.axis_index("tile"), lax.axis_size("tile")
    odd = tile % 2 == 1
    grp_odd = lax.axis_index("grp") % 2 == 1
    lane = lane_index()
    cell, low = lane // SUB, lane < LANES // 2
    inner = lane % SUB < STEPS

    @pl.loop(0, edges.shape[0] // SUB)
    def _(g):
        own, one, two = edges[group(g), :], near[group(g), :], far[group(g), :]
        flipped = roll(own, -7 * SUB)
        for s in range(1, SUB):
            flipped = jnp.where(cell % SUB == s, roll(own, (2 * s - 7) * SUB), flipped)
        above = pick(tile == 0, flipped, pick(odd, one, two))
        below = pick(tile == tiles - 1, flipped, pick(odd, two, one))
        outer = jnp.where(cell % SUB < STEPS, below, above)
        fast = jnp.where(low, own, roll(outer, LANES // 2))
        slow = jnp.where(low, roll(own, LANES // 2), outer)
        fast_edges[group(g), :] = fast
        slow_edges[group(g), :] = slow
        to_left = jnp.where(inner, fast, roll(slow, STEPS))
        to_right = jnp.where(inner, roll(fast, -STEPS), slow)
        near_out[group(g), :] = pick(grp_odd, to_left, to_right)
        far_out[group(g), :] = pick(grp_odd, to_right, to_left)


def extended_rows(own, near, far, g):
    tile, tiles = lax.axis_index("tile"), lax.axis_size("tile")
    odd, at_top, at_bottom = tile % 2 == 1, tile == 0, tile == tiles - 1
    out = []
    for f in range(2):
        count = STEPS - f
        rows = dict(enumerate(own[f]))
        for j in range(count):
            one, two = near[f * STEPS + j, group(g), :], far[f * STEPS + j, group(g), :]
            rows[j - count] = pick(at_top, own[f][count - 1 - j], pick(odd, one, two))
            rows[SUB + j] = pick(at_bottom, own[f][SUB - 1 - j], pick(odd, two, one))
        out.append(rows)
    return out


def strip_neighbours(last, first, halo):
    c = lane_index() % SUB
    end, begin = c == SUB - 1, c == 0
    out = []
    for x, after, before in (
        (last, roll(halo, 7), None),
        (first, None, roll(halo, -7)),
        (halo, roll(first, 7), roll(last, -7)),
    ):
        right, left = roll(x, -1), roll(x, 1)
        if after is not None:
            right = jnp.where(end, after, right)
        if before is not None:
            left = jnp.where(begin, before, left)
        out.append(roll(x, SUB) + roll(x, -SUB) + right + left)
    return out


def advance(fast, slow, around, gain, cross):
    return gain * fast + diffusion * around + cross * slow


def relax(fast, slow):
    return (1.0 - slow_rate) * slow + slow_rate * fast


def evolve_kernel(
    fields, tangents, coeff_self, coeff_cross, near, far, fast_edges, slow_edges, near_cols, far_cols,
    gram, halo, row_coeffs, strip_coeffs, cells,
):
    grp, grps = lax.axis_index("grp"), lax.axis_size("grp")
    grp_odd = grp % 2 == 1
    lane = lane_index()
    c = lane % SUB
    inner = c < STEPS
    groups = fields // SUB

    @pl.loop(0, groups + 1)
    def _(g):
        one, two = near_cols[group(g), :], far_cols[group(g), :]
        left, right = pick(grp_odd, one, two), pick(grp_odd, two, one)
        halo[0, group(g), :] = jnp.where(inner, right, roll(left, STEPS))
        halo[1, group(g), :] = jnp.where(inner, roll(right, -STEPS), left)

    @pl.when((grp == 0) | (grp == grps - 1))
    def _():
        outside = (inner & (grp == grps - 1)) | (~inner & (grp == 0))

        @pl.loop(0, groups + 1)
        def _(g):
            for f, ref in enumerate((fast_edges, slow_edges)):
                own = ref[group(g), :]
                mirrored = roll(own, -7)
                for s in range(1, SUB):
                    mirrored = jnp.where(c == s, roll(own, 2 * s - 7), mirrored)
                halo[f, group(g), :] = jnp.where(outside, mirrored, halo[f, group(g), :])

    def strips(rows, f, g):
        slots = {r % (2 * SUB): row for r, row in rows.items()}
        last, first = edge_columns(slots)
        return [last, first, halo[f, group(g), :]]

    coeff_rows = extended_rows(own_coeffs(coeff_self, coeff_cross), near, far, groups)
    for f in range(2):
        base = (1.0 - 4.0 * diffusion) * (1 - f)
        for r in range(1 - STEPS, SUB + STEPS - 1):
            row_coeffs[f, r + STEPS - 1, :, :] = coeff_rows[f][r] + base
        for part, strip in enumerate(strips(coeff_rows[f], f, groups)):
            strip_coeffs[f, part, :, :] = strip + base

    @pl.loop(0, groups)
    def _(g):
        fast, slow = extended_rows(own_rows(tangents, g), near, far, g)
        strip_fast, strip_slow = strips(fast, 0, g), strips(slow, 1, g)
        for step in range(1, STEPS + 1):
            margin = STEPS - step
            new_fast = {}
            for r in range(-margin, SUB + margin):
                around = fast[r - 1] + fast[r + 1] + roll(fast[r], 1) + roll(fast[r], -1)
                new_fast[r] = advance(fast[r], slow[r], around, row_coeffs[0, r + STEPS - 1], row_coeffs[1, r + STEPS - 1])
            keep = max(margin - 1, 0)
            slow = {r: relax(fast[r], slow[r]) for r in range(-keep, SUB + keep)}
            fast = new_fast
            around = strip_neighbours(*strip_fast)
            moved = [
                advance(strip_fast[p], strip_slow[p], around[p], strip_coeffs[0, p], strip_coeffs[1, p]) for p in range(3)
            ]
            strip_slow = [relax(a, b) for a, b in zip(strip_fast, strip_slow)]
            strip_fast = moved
        middle = (lane >= STEPS) & (lane < LANES - STEPS)
        for f, rows in enumerate((fast, slow)):
            for r in range(SUB):
                cells[group(g), (f * SUB + r) * LANES:(f * SUB + r + 1) * LANES] = jnp.where(middle, rows[r], 0.0)
        ends = [jnp.where(inner, s[1], s[0]) for s in (strip_fast, strip_slow)]
        cells[group(g), 2 * SUB * LANES:] = jnp.where(lane < LANES // 2, ends[0], roll(ends[1], LANES // 2))

    for index, (i, j) in enumerate(block_pairs(fields // SIDE)):
        row, half = divmod(index, 2)
        gram[row * SIDE:(row + 1) * SIDE, half * SIDE:(half + 1) * SIDE] = dot_nt(
            cells[i * SIDE:(i + 1) * SIDE, :], cells[j * SIDE:(j + 1) * SIDE, :]
        )


def local_call(body, name, out_shapes, scratch, *args):
    spec = pl.BlockSpec(memory_space=pltpu.VMEM)
    return pl.pallas_call(
        body,
        out_shape=[jax.ShapeDtypeStruct(s, jnp.float32) for s in out_shapes],
        in_specs=[spec] * len(args),
        out_specs=[spec] * len(out_shapes),
        scratch_shapes=[pltpu.VMEM(s, jnp.float32) for s in scratch],
        compiler_params=pltpu.CompilerParams(vmem_limit_bytes=40 * 1024 * 1024),
        name=name,
    )(*args)


def swap(cells, axis, first):
    count = lax.axis_size(axis)
    pairs = [(i, i + 1) for i in range(first, count - 1, 2)]
    return lax.ppermute(cells, axis, pairs + [(b, a) for a, b in pairs])


def exchange(cells, axis, bit):
    count = lax.axis_size(axis)
    return lax.ppermute(cells, axis, [(i, i ^ bit) for i in range(count)])


def sum_blocks(packed):
    half = packed.shape[0] // 2
    odd = lax.axis_index("tile") % 2 == 1
    low, high = packed[:half], packed[half:]
    part = jnp.where(odd, high, low) + exchange(jnp.where(odd, low, high), "tile", 1)
    for axis, first in (("grp", 1), ("tile", 2)):
        bit = first
        while bit < lax.axis_size(axis):
            part = part + exchange(part, axis, bit)
            bit *= 2
    other = exchange(part, "tile", 1)
    return jnp.concatenate([jnp.where(odd, other, part), jnp.where(odd, part, other)], axis=0)


def per_device(tangents, reaction_self, reaction_cross):
    fields = tangents.shape[1]
    padded = fields + SUB
    rows = tangents.reshape(2, fields * tangents.shape[2], tangents.shape[3])
    message, strip = (2 * STEPS - 1, padded, LANES), (padded, LANES)
    near, far, edges = local_call(
        functools.partial(pack_kernel, fields), "pack", [message, message, strip], [], rows, reaction_self, reaction_cross
    )
    near_edges, far_edges = swap(edges, "tile", 0), swap(edges, "tile", 1)
    near_rows, far_rows = swap(near, "tile", 0), swap(far, "tile", 1)
    fast_edges, slow_edges, near_cols, far_cols = local_call(
        column_kernel, "columns", [strip] * 4, [], edges, near_edges, far_edges
    )
    near_cols, far_cols = swap(near_cols, "grp", 0), swap(far_cols, "grp", 1)
    side_blocks = fields // SIDE
    blocks = side_blocks * (side_blocks + 1) // 2
    (packed,) = local_call(
        functools.partial(evolve_kernel, fields), "evolve", [((blocks + 1) // 2 * SIDE, 2 * SIDE)],
        [(2, padded, LANES), (2, SUB + 2 * STEPS - 2, SUB, LANES), (2, 3, SUB, LANES), (fields, (2 * SUB + 1) * LANES)],
        rows, reaction_self, reaction_cross, near_rows, far_rows, fast_edges, slow_edges, near_cols, far_cols,
    )
    block_total = lax.axis_size("grp") * lax.axis_size("tile")
    corrections, growth = factor_call(sum_blocks(packed), packed, fields, math.sqrt(block_total))
    return (corrections, growth)


def solution(mesh):
    in_specs = (P(None, None, "tile", "grp"), P("tile", "grp"), P("tile", "grp"))
    out_specs = (P(("grp", "tile"), None), P())
    return jax.shard_map(
        per_device, mesh=mesh, in_specs=in_specs, out_specs=out_specs, check_vma=False
    )
```

profile of v0, /device:TPU:0, one launch (start us, length us, event | category | flops | bytes accessed | tf_op | source)
XLA Modules:
  0.0 88.1 jit_solution(4912396487650040592)
XLA Ops:
  0.6 0.0 copy-start
  0.6 1.4 %copy-done = f32[2,192,8,128]{3,2,1,0:T(8,128)S(1)} copy-done((f32[2,192,8,128]{3,2,1,0:T(8,128)S(1)}, f32[2,192,8,128]{3,2,1,0:T(8,128)}, u32[]{:S(2)}) %copy-start) | copy-done | bytes 1572888
  2.0 0.0 copy-start.3
  2.0 0.7 copy-done.3
  2.7 0.0 copy-start.5
  2.7 0.7 copy-done.5
  3.4 0.0 copy-start.1
  3.4 0.0 copy-start.4
  3.4 0.0 copy-start.6
  3.4 4.8 %pack.1 = (f32[7,200,128]{2,1,0:T(8,128)}, f32[7,200,128]{2,1,0:T(8,128)}, f32[200,128]{1,0:T(8,128)S(1)}) custom-call(f32[2,1536,128]{2,1,0:T(8,128)S(1)} %bitcast.2, f32[8,128]{1,0:T(8,128)S(1)} %copy-done.3, f32[8,128]{1,0:T(8,128)S(1)} %copy-done.5), custom_call_target="tpu_custom_call" | custom-call | tf_op jit(solution)/shard_map/pack/pallas_call | solution.py:329
  8.2 0.5 collective-permute-start
  8.6 0.7 collective-permute-start.1
  9.3 4.0 %collective-permute-start.2 = (f32[200,128]{1,0:T(8,128)S(1)}, f32[200,128]{1,0:T(8,128)S(1)}, u32[]{:S(2)}, u32[]{:S(2)}) collective-permute-start(f32[200,128]{1,0:T(8,128)S(1)} %get-tuple-element.13.edges), channel_id=1, source_target_pairs={{0,1},{2,3},{4,5},{6,7},{1,0},{3,2},{5,4},{7,6},{8,9},{10,11},{12,... | collective-permute-start | bytes 307208 | tf_op jit(solution)/shard_map/ppermute | solution.py:343
  13.3 0.7 collective-permute-start.3
  14.0 0.3 collective-permute-done.2.near
  14.3 0.0 collective-permute-done.3.far
  14.3 6.0 %columns.1 = (f32[200,128]{1,0:T(8,128)S(1)}, f32[200,128]{1,0:T(8,128)S(1)}, f32[200,128]{1,0:T(8,128)}, f32[200,128]{1,0:T(8,128)}) custom-call(f32[200,128]{1,0:T(8,128)S(1)} %get-tuple-element.13.edges, f32[200,128]{1,0:T(8,128)S(1)} %collective-permute-done.2.near, f32[200,128]{1,0:T(8,128)S(1)} %collective-permute-done.3.far), custom_call_target="tpu_custom_call" | custom-call | tf_op jit(solution)/shard_map/columns/pallas_call | solution.py:329
  20.3 1.5 %collective-permute-start.4 = (f32[200,128]{1,0:T(8,128)}, f32[200,128]{1,0:T(8,128)S(1)}, u32[]{:S(2)}, u32[]{:S(2)}) collective-permute-start(f32[200,128]{1,0:T(8,128)} %get-tuple-element.16), channel_id=1, source_target_pairs={{0,8},{16,24},{8,0},{24,16},{1,9},{17,25},{9,1},{25,17},{2,10},{18... | collective-permute-start | bytes 307208 | tf_op jit(solution)/shard_map/ppermute | solution.py:343
  21.8 0.7 collective-permute-start.5
  22.5 2.7 %collective-permute-done.4.near_cols = f32[200,128]{1,0:T(8,128)S(1)} collective-permute-done((f32[200,128]{1,0:T(8,128)}, f32[200,128]{1,0:T(8,128)S(1)}, u32[]{:S(2)}, u32[]{:S(2)}) %collective-permute-start.4) | collective-permute-done | bytes 102432 | tf_op jit(solution)/shard_map/ppermute | solution.py:343
  25.2 0.0 collective-permute-done.5.far_cols
  25.2 0.0 collective-permute-done.near
  25.2 0.0 collective-permute-done.1.far
  25.2 0.0 copy-done.1
  25.2 0.0 copy-done.4
  25.2 0.0 copy-done.6
  25.2 20.2 %evolve.1.loc_ref = f32[192,128]{1,0:T(8,128)S(1)} custom-call(f32[2,1536,128]{2,1,0:T(8,128)S(1)} %bitcast.3, f32[8,128]{1,0:T(8,128)S(1)} %copy-done.4, f32[8,128]{1,0:T(8,128)S(1)} %copy-done.6, f32[7,200,128]{2,1,0:T(8,128)S(1)} %collective-permute-done.near, f32[7,200,128]{2,1,0:T(8,128)S(1)} %collective-permute-done.1.far, ...), custom_call_target="tpu_custom_call" | custom-call | tf_op jit(solution)/shard_map/evolve/pallas_call | solution.py:329
  45.4 0.0 copy-start.2
  45.4 8.7 %collective-permute-start.6 = (f32[96,128]{1,0:T(8,128)S(1)}, f32[96,128]{1,0:T(8,128)S(1)}, u32[]{:S(2)}, u32[]{:S(2)}) collective-permute-start(f32[96,128]{1,0:T(8,128)S(1)} %slice_select_fusion), channel_id=1, source_target_pairs={{0,1},{1,0},{2,3},{3,2},{4,5},{5,4},{6,7},{7,6},{8,9},{9,8},{10,11... | collective-permute-start | bytes 147464 | tf_op jit(solution)/shard_map/ppermute | solution.py:348
  54.1 0.9 collective-permute-done.6
  55.0 2.5 %collective-permute-start.7 = (f32[96,128]{1,0:T(8,128)S(1)}, f32[96,128]{1,0:T(8,128)S(1)}, u32[]{:S(2)}, u32[]{:S(2)}) collective-permute-start(f32[96,128]{1,0:T(8,128)S(1)} %select_add_fusion), channel_id=1, source_target_pairs={{0,8},{8,0},{16,24},{24,16},{1,9},{9,1},{17,25},{25,17},{2,10},{10... | collective-permute-start | bytes 147464 | tf_op jit(solution)/shard_map/ppermute | solution.py:348
  57.5 2.3 %collective-permute-done.7 = f32[96,128]{1,0:T(8,128)S(1)} collective-permute-done((f32[96,128]{1,0:T(8,128)S(1)}, f32[96,128]{1,0:T(8,128)S(1)}, u32[]{:S(2)}, u32[]{:S(2)}) %collective-permute-start.7) | collective-permute-done | bytes 49184 | tf_op jit(solution)/shard_map/ppermute | solution.py:348
  59.8 3.1 %collective-permute-start.8 = (f32[96,128]{1,0:T(8,128)S(1)}, f32[96,128]{1,0:T(8,128)S(1)}, u32[]{:S(2)}, u32[]{:S(2)}) collective-permute-start(f32[96,128]{1,0:T(8,128)S(1)} %add.21), channel_id=1, source_target_pairs={{0,16},{8,24},{16,0},{24,8},{1,17},{9,25},{17,1},{25,9},{2,18},{10... | collective-permute-start | bytes 147464 | tf_op jit(solution)/shard_map/ppermute | solution.py:348
  62.8 2.1 %collective-permute-done.8 = f32[96,128]{1,0:T(8,128)S(1)} collective-permute-done((f32[96,128]{1,0:T(8,128)S(1)}, f32[96,128]{1,0:T(8,128)S(1)}, u32[]{:S(2)}, u32[]{:S(2)}) %collective-permute-start.8) | collective-permute-done | bytes 49184 | tf_op jit(solution)/shard_map/ppermute | solution.py:348
  64.9 3.0 %collective-permute-start.9 = (f32[96,128]{1,0:T(8,128)S(1)}, f32[96,128]{1,0:T(8,128)S(1)}, u32[]{:S(2)}, u32[]{:S(2)}) collective-permute-start(f32[96,128]{1,0:T(8,128)S(1)} %add.22), channel_id=1, source_target_pairs={{0,2},{1,3},{2,0},{3,1},{4,6},{5,7},{6,4},{7,5},{8,10},{9,11},{10,... | collective-permute-start | bytes 147464 | tf_op jit(solution)/shard_map/ppermute | solution.py:348
  67.9 2.1 %collective-permute-done.9 = f32[96,128]{1,0:T(8,128)S(1)} collective-permute-done((f32[96,128]{1,0:T(8,128)S(1)}, f32[96,128]{1,0:T(8,128)S(1)}, u32[]{:S(2)}, u32[]{:S(2)}) %collective-permute-start.9) | collective-permute-done | bytes 49184 | tf_op jit(solution)/shard_map/ppermute | solution.py:348
  70.0 3.5 %collective-permute-start.10 = (f32[96,128]{1,0:T(8,128)S(1)}, f32[96,128]{1,0:T(8,128)S(1)}, u32[]{:S(2)}, u32[]{:S(2)}) collective-permute-start(f32[96,128]{1,0:T(8,128)S(1)} %add.23), channel_id=1, source_target_pairs={{0,4},{1,5},{2,6},{3,7},{4,0},{5,1},{6,2},{7,3},{8,12},{9,13},{10,... | collective-permute-start | bytes 147464 | tf_op jit(solution)/shard_map/ppermute | solution.py:348
  73.5 2.1 %collective-permute-done.10 = f32[96,128]{1,0:T(8,128)S(1)} collective-permute-done((f32[96,128]{1,0:T(8,128)S(1)}, f32[96,128]{1,0:T(8,128)S(1)}, u32[]{:S(2)}, u32[]{:S(2)}) %collective-permute-start.10) | collective-permute-done | bytes 49184 | tf_op jit(solution)/shard_map/ppermute | solution.py:348
  75.6 0.1 collective-permute-start.11
  75.7 1.2 %collective-permute-done.11 = f32[96,128]{1,0:T(8,128)S(1)} collective-permute-done((f32[96,128]{1,0:T(8,128)S(1)}, f32[96,128]{1,0:T(8,128)S(1)}, u32[]{:S(2)}, u32[]{:S(2)}) %collective-permute-start.11) | collective-permute-done | bytes 49184 | tf_op jit(solution)/shard_map/ppermute | solution.py:348
  76.9 0.6 pad_maximum_fusion.tot_ref
  77.5 0.0 copy-done.2
  77.6 10.6 %factor.1 = (f32[192,192]{1,0:T(8,128)}, f32[1,192]{1,0:T(1,128)}) custom-call(f32[192,128]{1,0:T(8,128)} %pad_maximum_fusion.tot_ref, f32[192,128]{1,0:T(8,128)} %copy-done.2), custom_call_target="tpu_custom_call" | custom-call | tf_op jit(solution)/shard_map/factor/pallas_call | solution.py:118
  (7 shorter events, 0.1 us)
Async XLA Ops:
  0.6 1.4 %copy-start = (f32[2,192,8,128]{3,2,1,0:T(8,128)S(1)}, f32[2,192,8,128]{3,2,1,0:T(8,128)}, u32[]{:S(2)}) copy-start(f32[2,192,8,128]{3,2,1,0:T(8,128)} %param.3) | copy-start | bytes 4718596
  2.0 0.7 copy-start.3
  2.7 0.7 copy-start.5
  3.4 21.8 %copy-start.1 = (f32[2,192,8,128]{3,2,1,0:T(8,128)S(1)}, f32[2,192,8,128]{3,2,1,0:T(8,128)}, u32[]{:S(2)}) copy-start(f32[2,192,8,128]{3,2,1,0:T(8,128)} %param.3) | copy-start | bytes 4718596
  3.4 21.8 %copy-start.4 = (f32[8,128]{1,0:T(8,128)S(1)}, f32[8,128]{1,0:T(8,128)}, u32[]{:S(2)}) copy-start(f32[8,128]{1,0:T(8,128)} %coeff_self.3) | copy-start | bytes 12292
  3.4 21.8 %copy-start.6 = (f32[8,128]{1,0:T(8,128)S(1)}, f32[8,128]{1,0:T(8,128)}, u32[]{:S(2)}) copy-start(f32[8,128]{1,0:T(8,128)} %coeff_cross.3) | copy-start | bytes 12292
  8.2 17.0 %collective-permute-start = (f32[7,200,128]{2,1,0:T(8,128)}, f32[7,200,128]{2,1,0:T(8,128)S(1)}, u32[]{:S(2)}, u32[]{:S(2)}) collective-permute-start(f32[7,200,128]{2,1,0:T(8,128)} %get-tuple-element.11), channel_id=1, source_target_pairs={{0,1},{2,3},{4,5},{6,7},{1,0},{3,2},{5,4},{7,6},{8,9},{10,11},{12,... | collective-permute-start | bytes 2150408 | tf_op jit(solution)/shard_map/ppermute | solution.py:343
  8.6 16.5 %collective-permute-start.1 = (f32[7,200,128]{2,1,0:T(8,128)}, f32[7,200,128]{2,1,0:T(8,128)S(1)}, u32[]{:S(2)}, u32[]{:S(2)}) collective-permute-start(f32[7,200,128]{2,1,0:T(8,128)} %get-tuple-element.12), channel_id=1, source_target_pairs={{1,2},{3,4},{5,6},{2,1},{4,3},{6,5},{9,10},{11,12},{13,14},{10,9},... | collective-permute-start | bytes 2150408 | tf_op jit(solution)/shard_map/ppermute | solution.py:343
  9.3 4.9 %collective-permute-start.2 = (f32[200,128]{1,0:T(8,128)S(1)}, f32[200,128]{1,0:T(8,128)S(1)}, u32[]{:S(2)}, u32[]{:S(2)}) collective-permute-start(f32[200,128]{1,0:T(8,128)S(1)} %get-tuple-element.13.edges), channel_id=1, source_target_pairs={{0,1},{2,3},{4,5},{6,7},{1,0},{3,2},{5,4},{7,6},{8,9},{10,11},{12,... | collective-permute-start | bytes 307208 | tf_op jit(solution)/shard_map/ppermute | solution.py:343
  13.3 1.0 %collective-permute-start.3 = (f32[200,128]{1,0:T(8,128)S(1)}, f32[200,128]{1,0:T(8,128)S(1)}, u32[]{:S(2)}, u32[]{:S(2)}) collective-permute-start(f32[200,128]{1,0:T(8,128)S(1)} %get-tuple-element.13.edges), channel_id=1, source_target_pairs={{1,2},{3,4},{5,6},{2,1},{4,3},{6,5},{9,10},{11,12},{13,14},{10,9},... | collective-permute-start | bytes 307208 | tf_op jit(solution)/shard_map/ppermute | solution.py:343
  20.3 4.9 %collective-permute-start.4 = (f32[200,128]{1,0:T(8,128)}, f32[200,128]{1,0:T(8,128)S(1)}, u32[]{:S(2)}, u32[]{:S(2)}) collective-permute-start(f32[200,128]{1,0:T(8,128)} %get-tuple-element.16), channel_id=1, source_target_pairs={{0,8},{16,24},{8,0},{24,16},{1,9},{17,25},{9,1},{25,17},{2,10},{18... | collective-permute-start | bytes 307208 | tf_op jit(solution)/shard_map/ppermute | solution.py:343
  21.8 3.4 %collective-permute-start.5 = (f32[200,128]{1,0:T(8,128)}, f32[200,128]{1,0:T(8,128)S(1)}, u32[]{:S(2)}, u32[]{:S(2)}) collective-permute-start(f32[200,128]{1,0:T(8,128)} %get-tuple-element.17), channel_id=1, source_target_pairs={{8,16},{16,8},{9,17},{17,9},{10,18},{18,10},{11,19},{19,11},{12,20... | collective-permute-start | bytes 307208 | tf_op jit(solution)/shard_map/ppermute | solution.py:343
  45.4 32.2 %copy-start.2 = (f32[192,128]{1,0:T(8,128)}, f32[192,128]{1,0:T(8,128)S(1)}, u32[]{:S(2)}) copy-start(f32[192,128]{1,0:T(8,128)S(1)} %evolve.1.loc_ref) | copy-start | bytes 294916
  45.4 9.6 %collective-permute-start.6 = (f32[96,128]{1,0:T(8,128)S(1)}, f32[96,128]{1,0:T(8,128)S(1)}, u32[]{:S(2)}, u32[]{:S(2)}) collective-permute-start(f32[96,128]{1,0:T(8,128)S(1)} %slice_select_fusion), channel_id=1, source_target_pairs={{0,1},{1,0},{2,3},{3,2},{4,5},{5,4},{6,7},{7,6},{8,9},{9,8},{10,11... | collective-permute-start | bytes 147464 | tf_op jit(solution)/shard_map/ppermute | solution.py:348
  55.0 4.8 %collective-permute-start.7 = (f32[96,128]{1,0:T(8,128)S(1)}, f32[96,128]{1,0:T(8,128)S(1)}, u32[]{:S(2)}, u32[]{:S(2)}) collective-permute-start(f32[96,128]{1,0:T(8,128)S(1)} %select_add_fusion), channel_id=1, source_target_pairs={{0,8},{8,0},{16,24},{24,16},{1,9},{9,1},{17,25},{25,17},{2,10},{10... | collective-permute-start | bytes 147464 | tf_op jit(solution)/shard_map/ppermute | solution.py:348
  59.8 5.1 %collective-permute-start.8 = (f32[96,128]{1,0:T(8,128)S(1)}, f32[96,128]{1,0:T(8,128)S(1)}, u32[]{:S(2)}, u32[]{:S(2)}) collective-permute-start(f32[96,128]{1,0:T(8,128)S(1)} %add.21), channel_id=1, source_target_pairs={{0,16},{8,24},{16,0},{24,8},{1,17},{9,25},{17,1},{25,9},{2,18},{10... | collective-permute-start | bytes 147464 | tf_op jit(solution)/shard_map/ppermute | solution.py:348
  64.9 5.0 %collective-permute-start.9 = (f32[96,128]{1,0:T(8,128)S(1)}, f32[96,128]{1,0:T(8,128)S(1)}, u32[]{:S(2)}, u32[]{:S(2)}) collective-permute-start(f32[96,128]{1,0:T(8,128)S(1)} %add.22), channel_id=1, source_target_pairs={{0,2},{1,3},{2,0},{3,1},{4,6},{5,7},{6,4},{7,5},{8,10},{9,11},{10,... | collective-permute-start | bytes 147464 | tf_op jit(solution)/shard_map/ppermute | solution.py:348
  70.0 5.6 %collective-permute-start.10 = (f32[96,128]{1,0:T(8,128)S(1)}, f32[96,128]{1,0:T(8,128)S(1)}, u32[]{:S(2)}, u32[]{:S(2)}) collective-permute-start(f32[96,128]{1,0:T(8,128)S(1)} %add.23), channel_id=1, source_target_pairs={{0,4},{1,5},{2,6},{3,7},{4,0},{5,1},{6,2},{7,3},{8,12},{9,13},{10,... | collective-permute-start | bytes 147464 | tf_op jit(solution)/shard_map/ppermute | solution.py:348
  75.6 1.3 %collective-permute-start.11 = (f32[96,128]{1,0:T(8,128)S(1)}, f32[96,128]{1,0:T(8,128)S(1)}, u32[]{:S(2)}, u32[]{:S(2)}) collective-permute-start(f32[96,128]{1,0:T(8,128)S(1)} %add.24), channel_id=1, source_target_pairs={{0,1},{1,0},{2,3},{3,2},{4,5},{5,4},{6,7},{7,6},{8,9},{9,8},{10,11... | collective-permute-start | bytes 147464 | tf_op jit(solution)/shard_map/ppermute | solution.py:348
where the time goes:
time: 88.4 us; the launch traced here: 88.1 us
  Pallas kernels  41.6 us (47%)
  starting transfers between devices  28.8 us (33%)
  waiting for transfers between devices  13.6 us (15%)
  local copies, waits for them, and re-layouts  2.79 us (3%)
    pallas_call x3, Pallas kernels, local_call(): pl.pallas_call(body, out_shape=[jax.ShapeDtypeStruct(s, jnp.float32) for...  31 us
    ppermute x6, starting transfers between devices, exchange(): return lax.ppermute(cells, axis, [(i, i ^ bit) for i in range(count)])  20.9 us
    pallas_call x1, Pallas kernels, factor_call(): pl.pallas_call(functools.partial(factor_kernel, k // SIDE, weight), out_s...  10.6 us
    ppermute x6, waiting for transfers between devices, exchange(): return lax.ppermute(cells, axis, [(i, i ^ bit) for i in range(count)])  10.6 us
    ppermute x6, starting transfers between devices, swap(): return lax.ppermute(cells, axis, pairs + [(b, a) for a, b in pairs])  7.9 us
    ppermute x6, waiting for transfers between devices, swap(): return lax.ppermute(cells, axis, pairs + [(b, a) for a, b in pairs])  3 us
    unnamed x14, local copies, waits for them, and re-layouts  2.79 us
  transfers between devices with their start and end apart: 12, of which 8 were waited for; matrix products, arithmetic and copies ran while one was open for 0% of the time, Pallas kernels for 7%

commit v1 on v0

v1 whole, which is shorter than its diff:
```python
import functools
import math

import jax
import jax.numpy as jnp
from jax import lax
from jax.experimental import pallas as pl
from jax.experimental.pallas import tpu as pltpu
from jax.sharding import PartitionSpec as P


STEPS = 4
diffusion = 0.2
slow_rate = 0.05
HEIGHT_EDGE = 24
HEIGHT_ROW = 24
HEIGHT_STRIP = 24
HEIGHT_EVOLVE = 16
SIDE = 64
LANES = 128
SUB = 8
HI = lax.Precision.HIGHEST

def dot_nn(a, b):
    return lax.dot_general(a, b, (((1,), (0,)), ((), ())), precision=HI, preferred_element_type=jnp.float32)
def dot_tn(a, b):
    return lax.dot_general(a, b, (((0,), (0,)), ((), ())), precision=HI, preferred_element_type=jnp.float32)
def dot_nt(a, b):
    return lax.dot_general(a, b, (((1,), (1,)), ((), ())), precision=HI, preferred_element_type=jnp.float32)

def block_pairs(n):
    return [(i, j) for i in range(n) for j in range(i, n)]

def unpack_blocks(ref, n):
    out = {}
    for index, key in enumerate(block_pairs(n)):
        row, half = divmod(index, 2)
        out[key] = ref[row*SIDE:(row+1)*SIDE, half*SIDE:(half+1)*SIDE]
    return out

def spread_lane(x, lane):
    return jnp.broadcast_to(x[:, lane:lane+1], (x.shape[0], LANES))
def spread_row(x, row):
    return jnp.broadcast_to(x[row:row+1, :], (SUB, x.shape[1]))

def factor_blocks(blocks):
    groups = SIDE // SUB
    eye = (lax.broadcasted_iota(jnp.int32, (SIDE, SIDE), 0) == lax.broadcasted_iota(jnp.int32, (SIDE, SIDE), 1)).astype(jnp.float32)
    sub = lax.broadcasted_iota(jnp.int32, (SUB, LANES), 0)
    states = []
    for d in blocks:
        whole = jnp.concatenate([d, eye], axis=1)
        states.append([whole[g*SUB:(g+1)*SUB] for g in range(groups)])
    done = [[] for _ in blocks]
    for p in range(groups):
        for s, v in enumerate(states):
            cols = {}
            for g in range(p, groups):
                for c in range(SUB):
                    cols[g, c] = spread_lane(v[g], p*SUB + c)
            rows = [spread_row(v[p], c) for c in range(SUB)]
            pivots = {(a, c): spread_row(cols[p, c], a) for c in range(SUB) for a in range(c, SUB)}
            mult = {}
            scale = []
            for c in range(SUB):
                inv = 1.0 / pivots[c, c]
                scale.append(lax.rsqrt(pivots[c, c]))
                for a in range(c + 1, SUB):
                    mult[a, c] = pivots[a, c] * inv
                    rows[a] = rows[a] - mult[a, c] * rows[c]
                    for b in range(c + 1, a + 1):
                        pivots[a, b] = pivots[a, b] - mult[a, c] * pivots[b, c]
            scaled = [rows[c] * scale[c] for c in range(SUB)]
            panel = scaled[0]
            for c in range(1, SUB):
                panel = jnp.where(sub == c, scaled[c], panel)
            done[s].append(panel)
            for g in range(p + 1, groups):
                for c in range(SUB):
                    for a in range(c + 1, SUB):
                        cols[g, a] = cols[g, a] - mult[a, c] * cols[g, c]
                    v[g] = v[g] - (cols[g, c] * scale[c]) * scaled[c]
    out = []
    for panels in done:
        whole = jnp.concatenate(panels, axis=0)
        out.append((whole[:, :SIDE], whole[:, SIDE:]))
    return out

def factor_kernel(n, weight, tot_ref, loc_ref, out_ref, growth_ref):
    total = unpack_blocks(tot_ref, n)
    local = unpack_blocks(loc_ref, n)
    keep = (lax.broadcasted_iota(jnp.int32, (SIDE, SIDE), 0) <= lax.broadcasted_iota(jnp.int32, (SIDE, SIDE), 1))
    diag = (lax.broadcasted_iota(jnp.int32, (SIDE, SIDE), 0) == lax.broadcasted_iota(jnp.int32, (SIDE, SIDE), 1))
    inverse = {}
    answer = {}
    for k in range(n):
        (r_t, i_t), (r_l, i_l) = factor_blocks([total[k, k], local[k, k]])
        inverse[k] = i_t
        local[k, k] = jnp.where(keep, r_l, 0.0)
        growth_ref[0, k*SIDE:(k+1)*SIDE] = jnp.log(jnp.sum(jnp.where(diag, r_t, 0.0), axis=0))
        for grams, inv in ((total, i_t), (local, i_l)):
            if k + 1 < n:
                row = dot_nn(inv, jnp.concatenate([grams[k, j] for j in range(k + 1, n)], axis=1))
                for j in range(k + 1, n):
                    grams[k, j] = row[:, (j-k-1)*SIDE:(j-k)*SIDE]
                for i in range(k + 1, n):
                    rest = dot_tn(grams[k, i], row[:, (i-k-1)*SIDE:])
                    for j in range(i, n):
                        grams[i, j] = grams[i, j] - rest[:, (j-i)*SIDE:(j-i+1)*SIDE]
    for j in range(n):
        for i in range(j + 1):
            rest = local[i, j]
            for m in range(i, j):
                rest = rest - dot_nn(answer[i, m], total[m, j])
            answer[i, j] = dot_nt(rest, inverse[j])
            out_ref[i*SIDE:(i+1)*SIDE, j*SIDE:(j+1)*SIDE] = weight * answer[i, j]
        for i in range(j + 1, n):
            out_ref[i*SIDE:(i+1)*SIDE, j*SIDE:(j+1)*SIDE] = jnp.zeros((SIDE, SIDE), jnp.float32)

def factor_call(total, local, k, weight):
    vm = pl.BlockSpec(memory_space=pltpu.VMEM)
    out, growth = pl.pallas_call(
        functools.partial(factor_kernel, k // SIDE, weight),
        out_shape=(jax.ShapeDtypeStruct((k, k), jnp.float32), jax.ShapeDtypeStruct((1, k), jnp.float32)),
        in_specs=[vm, vm], out_specs=(vm, vm), name="factor",
    )(total, local)
    return out, growth[0]


def pick(flag, first, second):
    return jnp.where(flag, first, second)


def roll(x, shift):
    return pltpu.roll(x, shift % LANES, 1)


def lane_index(like):
    return lax.broadcasted_iota(jnp.int32, like.shape, like.ndim - 1)


def chunk(g, height):
    return pl.ds(pl.multiple_of(g * height, height), height)


def own_rows(tangents, g, height):
    return [[tangents[f, pl.ds(g * height * SUB + r, height, stride=SUB), :] for r in range(SUB)] for f in range(2)]


def own_coeffs(coeff_self, coeff_cross):
    return [[spread_row(ref[...], r) for r in range(SUB)] for ref in (coeff_self, coeff_cross)]


def tall(x, height):
    return jnp.concatenate([x] * (height // SUB), axis=0)


def edge_kernel(fields, height, tangents_hbm, self_hbm, cross_hbm, last_out, first_out, near, far, tangents, coeff_self, coeff_cross, sems):
    loads = [
        pltpu.make_async_copy(src, dst, sems.at[i])
        for i, (src, dst) in enumerate(((tangents_hbm, tangents), (self_hbm, coeff_self), (cross_hbm, coeff_cross)))
    ]
    for load in loads:
        load.start()
    for load in loads:
        load.wait()
    odd = lax.axis_index("tile") % 2 == 1

    def send(at, rows):
        cell = lane_index(rows[0][0]) // SUB
        cells = LANES // SUB
        last, first = None, None
        for f in range(2):
            for r in range(SUB):
                s = f * SUB + r
                turned = roll(rows[f][r], (s + 1) * SUB)
                last = turned if last is None else jnp.where(cell == s, turned, last)
                first = turned if first is None else jnp.where(cell == (s + 1) % cells, turned, first)
        first = roll(first, -SUB)
        last_out[at, :] = last
        first_out[at, :] = first
        half = cell % SUB < STEPS
        to_above = jnp.where(half, last, roll(first, STEPS * SUB))
        to_below = jnp.where(half, roll(last, -STEPS * SUB), first)
        near[at, :] = pick(odd, to_above, to_below)
        far[at, :] = pick(odd, to_below, to_above)

    @pl.loop(0, fields // height)
    def _(g):
        send(chunk(g, height), own_rows(tangents, g, height))

    send(pl.ds(fields, SUB), own_coeffs(coeff_self, coeff_cross))


def row_kernel(fields, height, after, tangents, coeff_self, coeff_cross, near, far):
    odd = lax.axis_index("tile") % 2 == 1

    def send(at, rows):
        for f in range(2):
            count = STEPS - f
            for j in range(count):
                top, bottom = rows[f][j], rows[f][SUB - count + j]
                near[f * STEPS + j, at, :] = pick(odd, top, bottom)
                far[f * STEPS + j, at, :] = pick(odd, bottom, top)

    @pl.loop(0, fields // height)
    def _(g):
        send(chunk(g, height), own_rows(tangents, g, height))

    send(pl.ds(fields, SUB), own_coeffs(coeff_self, coeff_cross))


def column_kernel(last, first, near, far, strips, near_out, far_out, outer):
    tile, tiles = lax.axis_index("tile"), lax.axis_size("tile")
    odd, at_top, at_bottom = tile % 2 == 1, tile == 0, tile == tiles - 1
    grp_odd = lax.axis_index("grp") % 2 == 1
    one, two = near[...], far[...]
    lane = lane_index(one)
    cell, low, inner = lane // SUB % SUB, lane < LANES // 2, lane % SUB < STEPS
    half = cell < STEPS
    above, below = pick(odd, one, two), pick(odd, two, one)
    outer[0] = jnp.where(half, below, roll(above, STEPS * SUB))
    outer[1] = jnp.where(half, roll(below, -STEPS * SUB), above)

    @pl.when(at_top | at_bottom)
    def _():
        outside = (half & at_bottom) | (~half & at_top)
        for i, ref in enumerate((last, first)):
            own = ref[...]
            mirrored = roll(own, -7 * SUB)
            for s in range(1, SUB):
                mirrored = jnp.where(cell == s, roll(own, (2 * s - 7) * SUB), mirrored)
            outer[i] = jnp.where(outside, mirrored, outer[i])

    sides = []
    for i, ref in enumerate((last, first)):
        own, more = ref[...], outer[i]
        fast = jnp.where(low, own, roll(more, LANES // 2))
        slow = jnp.where(low, roll(own, LANES // 2), more)
        strips[2 * i] = fast
        strips[2 * i + 1] = slow
        sides.append((fast, slow))
    to_left = jnp.where(inner, sides[1][0], roll(sides[1][1], STEPS))
    to_right = jnp.where(inner, roll(sides[0][0], -STEPS), sides[0][1])
    near_out[...] = pick(grp_odd, to_left, to_right)
    far_out[...] = pick(grp_odd, to_right, to_left)


def strip_neighbours(last, first, halo):
    c = lane_index(last) % SUB
    end, begin = c == SUB - 1, c == 0
    out = []
    for x, after, before in (
        (last, roll(halo, 7), None),
        (first, None, roll(halo, -7)),
        (halo, roll(first, 7), roll(last, -7)),
    ):
        right, left = roll(x, -1), roll(x, 1)
        if after is not None:
            right = jnp.where(end, after, right)
        if before is not None:
            left = jnp.where(begin, before, left)
        out.append(roll(x, SUB) + roll(x, -SUB) + right + left)
    return out


def advance(fast, slow, around, gain, cross):
    return gain * fast + diffusion * around + cross * slow


def relax(fast, slow):
    return (1.0 - slow_rate) * slow + slow_rate * fast


def strip_kernel(fields, height, strips, near, far, ends, halo):
    grp, grps = lax.axis_index("grp"), lax.axis_size("grp")
    grp_odd = grp % 2 == 1
    one, two = near[...], far[...]
    lane = lane_index(one)
    c = lane % SUB
    inner = c < STEPS
    left, right = pick(grp_odd, one, two), pick(grp_odd, two, one)
    halo[0] = jnp.where(inner, right, roll(left, STEPS))
    halo[1] = jnp.where(inner, roll(right, -STEPS), left)

    @pl.when((grp == 0) | (grp == grps - 1))
    def _():
        after, before = inner & (grp == grps - 1), ~inner & (grp == 0)
        for f in range(2):
            tail, start = strips[f], strips[2 + f]
            mirrored = halo[f]
            for s in range(STEPS):
                mirrored = jnp.where(after & (c == s), roll(tail, 2 * s - 7), mirrored)
                mirrored = jnp.where(before & (c == 7 - s), roll(start, 7 - 2 * s), mirrored)
            halo[f] = mirrored

    def parts(f, at):
        return [strips[f, at, :], strips[2 + f, at, :], halo[f, at, :]]

    gains = [tall(x + (1.0 - 4.0 * diffusion), height) for x in parts(0, pl.ds(fields, SUB))]
    crosses = [tall(x, height) for x in parts(1, pl.ds(fields, SUB))]

    @pl.loop(0, fields // height)
    def _(g):
        fast, slow = parts(0, chunk(g, height)), parts(1, chunk(g, height))
        for step in range(STEPS):
            around = strip_neighbours(*fast)
            moved = [advance(fast[p], slow[p], around[p], gains[p], crosses[p]) for p in range(3)]
            slow = [relax(a, b) for a, b in zip(fast, slow)]
            fast = moved
        l = lane_index(fast[0])
        joined = [jnp.where(l % SUB < STEPS, s[1], s[0]) for s in (fast, slow)]
        ends[chunk(g, height), :] = jnp.where(l < LANES // 2, joined[0], roll(joined[1], LANES // 2))


def extended_rows(own, near, far, at):
    tile, tiles = lax.axis_index("tile"), lax.axis_size("tile")
    odd, at_top, at_bottom = tile % 2 == 1, tile == 0, tile == tiles - 1
    out = []
    for f in range(2):
        count = STEPS - f
        rows = dict(enumerate(own[f]))
        for j in range(count):
            one, two = near[f * STEPS + j, at, :], far[f * STEPS + j, at, :]
            rows[j - count] = pick(at_top, own[f][count - 1 - j], pick(odd, one, two))
            rows[SUB + j] = pick(at_bottom, own[f][SUB - 1 - j], pick(odd, two, one))
        out.append(rows)
    return out


def evolve_kernel(fields, height, tangents, coeff_self, coeff_cross, near, far, ends, gram, row_coeffs, cells):
    coeff_rows = extended_rows(own_coeffs(coeff_self, coeff_cross), near, far, pl.ds(fields, SUB))
    for f in range(2):
        for r in range(1 - STEPS, SUB + STEPS - 1):
            row_coeffs[f, r + STEPS - 1, :, :] = coeff_rows[f][r] + (1.0 - 4.0 * diffusion) * (1 - f)

    @pl.loop(0, fields // height)
    def _(g):
        at = chunk(g, height)
        fast, slow = extended_rows(own_rows(tangents, g, height), near, far, at)
        for step in range(1, STEPS + 1):
            margin = STEPS - step
            new_fast = {}
            for r in range(-margin, SUB + margin):
                around = fast[r - 1] + fast[r + 1] + roll(fast[r], 1) + roll(fast[r], -1)
                gain, cross = (tall(row_coeffs[f, r + STEPS - 1], height) for f in range(2))
                new_fast[r] = advance(fast[r], slow[r], around, gain, cross)
            keep = max(margin - 1, 0)
            slow = {r: relax(fast[r], slow[r]) for r in range(-keep, SUB + keep)}
            fast = new_fast
        lane = lane_index(fast[0])
        middle = (lane >= STEPS) & (lane < LANES - STEPS)
        for f, rows in enumerate((fast, slow)):
            for r in range(SUB):
                cells[at, (f * SUB + r) * LANES:(f * SUB + r + 1) * LANES] = jnp.where(middle, rows[r], 0.0)

    cells[:, 2 * SUB * LANES:] = ends[...]
    whole = dot_nt(cells[...], cells[...])
    for index, (i, j) in enumerate(block_pairs(fields // SIDE)):
        row, half = divmod(index, 2)
        gram[row * SIDE:(row + 1) * SIDE, half * SIDE:(half + 1) * SIDE] = whole[
            i * SIDE:(i + 1) * SIDE, j * SIDE:(j + 1) * SIDE
        ]


def local_call(body, name, out_shapes, scratch, *args, outside=0):
    spec = pl.BlockSpec(memory_space=pltpu.VMEM)
    own = [pltpu.VMEM(a.shape, a.dtype) for a in args[:outside]]
    if outside:
        own.append(pltpu.SemaphoreType.DMA((outside,)))
    return pl.pallas_call(
        body,
        out_shape=[jax.ShapeDtypeStruct(s, jnp.float32) for s in out_shapes],
        in_specs=[pl.BlockSpec(memory_space=pl.ANY)] * outside + [spec] * (len(args) - outside),
        out_specs=[spec] * len(out_shapes),
        scratch_shapes=[pltpu.VMEM(s, jnp.float32) for s in scratch] + own,
        compiler_params=pltpu.CompilerParams(vmem_limit_bytes=40 * 1024 * 1024),
        name=name,
    )(*args)


def swap(cells, axis, first):
    count = lax.axis_size(axis)
    pairs = [(i, i + 1) for i in range(first, count - 1, 2)]
    return lax.ppermute(cells, axis, pairs + [(b, a) for a, b in pairs])


def exchange(cells, axis, bit):
    count = lax.axis_size(axis)
    return lax.ppermute(cells, axis, [(i, i ^ bit) for i in range(count)])


def sum_blocks(packed):
    half = packed.shape[0] // 2
    odd = lax.axis_index("tile") % 2 == 1
    low, high = packed[:half], packed[half:]
    part = jnp.where(odd, high, low) + exchange(jnp.where(odd, low, high), "tile", 1)
    for axis, first in (("grp", 1), ("tile", 2)):
        bit = first
        while bit < lax.axis_size(axis):
            part = part + exchange(part, axis, bit)
            bit *= 2
    other = exchange(part, "tile", 1)
    return jnp.concatenate([jnp.where(odd, other, part), jnp.where(odd, part, other)], axis=0)


def per_device(tangents, reaction_self, reaction_cross):
    fields = tangents.shape[1]
    padded = fields + SUB
    rows = tangents.reshape(2, fields * tangents.shape[2], tangents.shape[3])
    message, strip = (2 * STEPS - 1, padded, LANES), (padded, LANES)
    inputs = (rows, reaction_self, reaction_cross)
    last, first, near_edges, far_edges = local_call(
        functools.partial(edge_kernel, fields, HEIGHT_EDGE), "edges", [strip] * 4, [], *inputs, outside=3
    )
    near_edges, far_edges = swap(near_edges, "tile", 0), swap(far_edges, "tile", 1)
    near_rows, far_rows = local_call(
        functools.partial(row_kernel, fields, HEIGHT_ROW), "rows", [message] * 2, [], last, *inputs
    )
    near_rows, far_rows = swap(near_rows, "tile", 0), swap(far_rows, "tile", 1)
    strips, near_cols, far_cols = local_call(
        column_kernel, "columns", [(4,) + strip, strip, strip], [(2,) + strip], last, first, near_edges, far_edges
    )
    near_cols, far_cols = swap(near_cols, "grp", 0), swap(far_cols, "grp", 1)
    (ends,) = local_call(
        functools.partial(strip_kernel, fields, HEIGHT_STRIP), "strips", [(fields, LANES)], [(2,) + strip], strips, near_cols, far_cols
    )
    side_blocks = fields // SIDE
    blocks = side_blocks * (side_blocks + 1) // 2
    (packed,) = local_call(
        functools.partial(evolve_kernel, fields, HEIGHT_EVOLVE), "evolve", [((blocks + 1) // 2 * SIDE, 2 * SIDE)],
        [(2, SUB + 2 * STEPS - 2, SUB, LANES), (fields, (2 * SUB + 1) * LANES)],
        *inputs, near_rows, far_rows, ends,
    )
    block_total = lax.axis_size("grp") * lax.axis_size("tile")
    corrections, growth = factor_call(sum_blocks(packed), packed, fields, math.sqrt(block_total))
    return (corrections, growth)


def solution(mesh):
    in_specs = (P(None, None, "tile", "grp"), P("tile", "grp"), P("tile", "grp"))
    out_specs = (P(("grp", "tile"), None), P())
    return jax.shard_map(
        per_device, mesh=mesh, in_specs=in_specs, out_specs=out_specs, check_vma=False
    )
```

time: 88.4 us -> 75.7 us (0.86)
  Pallas kernels: 41.6 us -> 27.6 us
  starting transfers between devices: 28.8 us -> 30.6 us
    pallas_call x3 -> x5, Pallas kernels: 31 us -> 17 us  [local_call(): pl.pallas_call(body, out_shape=[jax.ShapeDtypeStruct(s, jnp.float32) for...]
    ppermute x6, starting transfers between devices: 20.9 us -> 22 us  [exchange(): return lax.ppermute(cells, axis, [(i, i ^ bit) for i in range(count)])]
  transfers between devices with their start and end apart: 12 -> 12, of which waited for: 8 -> 8; matrix products, arithmetic and copies ran while one was open for 0% -> 0% of each run, Pallas kernels for 7% -> 9%
where the time goes in v1:
time: 75.7 us; the launch traced here: 75.4 us
  starting transfers between devices  30.6 us (40%)
  Pallas kernels  27.6 us (36%)
  waiting for transfers between devices  13 us (17%)
  local copies, waits for them, and re-layouts  2.8 us (4%)
  between operations  0.77 us (1%)
    ppermute x6, starting transfers between devices, exchange(): return lax.ppermute(cells, axis, [(i, i ^ bit) for i in range(count)])  22 us
    pallas_call x5, Pallas kernels, local_call(): pl.pallas_call(body, out_shape=[jax.ShapeDtypeStruct(s, jnp.float32) for...  17 us
    pallas_call x1, Pallas kernels, factor_call(): pl.pallas_call(functools.partial(factor_kernel, k // SIDE, weight), out_s...  10.6 us
    ppermute x6, waiting for transfers between devices, exchange(): return lax.ppermute(cells, axis, [(i, i ^ bit) for i in range(count)])  10.6 us
    ppermute x6, starting transfers between devices, swap(): return lax.ppermute(cells, axis, pairs + [(b, a) for a, b in pairs])  8.56 us
    unnamed x14, local copies, waits for them, and re-layouts  2.8 us
    ppermute x6, waiting for transfers between devices, swap(): return lax.ppermute(cells, axis, pairs + [(b, a) for a, b in pairs])  2.47 us
  transfers between devices with their start and end apart: 12, of which 8 were waited for; matrix products, arithmetic and copies ran while one was open for 0% of the time, Pallas kernels for 9%

profile of v1, /device:TPU:0, one launch (start us, length us, event | category | flops | bytes accessed | tf_op | source)
XLA Modules:
  0.0 75.4 jit_solution(15571546313825446955)
XLA Ops:
  0.6 0.0 copy-start
  0.6 1.4 %copy-done = f32[2,192,8,128]{3,2,1,0:T(8,128)S(1)} copy-done((f32[2,192,8,128]{3,2,1,0:T(8,128)S(1)}, f32[2,192,8,128]{3,2,1,0:T(8,128)}, u32[]{:S(2)}) %copy-start) | copy-done | bytes 1572888
  2.0 0.0 copy-start.3
  2.0 0.7 copy-done.3
  2.7 0.0 copy-start.5
  2.7 0.7 copy-done.5
  3.4 2.4 %edges.1 = (f32[200,128]{1,0:T(8,128)S(1)}, f32[200,128]{1,0:T(8,128)S(1)}, f32[200,128]{1,0:T(8,128)S(1)}, f32[200,128]{1,0:T(8,128)S(1)}) custom-call(f32[2,1536,128]{2,1,0:T(8,128)S(1)} %bitcast.2, f32[8,128]{1,0:T(8,128)S(1)} %copy-done.3, f32[8,128]{1,0:T(8,128)S(1)} %copy-done.5), custom_call_target="tpu_custom_call" | custom-call | tf_op jit(solution)/shard_map/edges/pallas_call | solution.py:371
  5.8 0.0 copy-start.1
  5.8 0.0 copy-start.4
  5.8 0.0 copy-start.6
  5.8 1.4 %rows.1 = (f32[7,200,128]{2,1,0:T(8,128)}, f32[7,200,128]{2,1,0:T(8,128)}) custom-call(f32[200,128]{1,0:T(8,128)S(1)} %get-tuple-element.13.after.last, f32[2,1536,128]{2,1,0:T(8,128)S(1)} %bitcast.3, f32[8,128]{1,0:T(8,128)S(1)} %copy-done.3, f32[8,128]{1,0:T(8,128)S(1)} %copy-done.5), custom_call_target="tpu_custom_call" | custom-call | tf_op jit(solution)/shard_map/rows/pallas_call | solution.py:371
  7.2 0.5 collective-permute-start
  7.7 0.7 collective-permute-start.1
  8.4 4.0 %collective-permute-start.2 = (f32[200,128]{1,0:T(8,128)S(1)}, f32[200,128]{1,0:T(8,128)S(1)}, u32[]{:S(2)}, u32[]{:S(2)}) collective-permute-start(f32[200,128]{1,0:T(8,128)S(1)} %get-tuple-element.17), channel_id=1, source_target_pairs={{0,1},{2,3},{4,5},{6,7},{1,0},{3,2},{5,4},{7,6},{8,9},{10,11},{12,... | collective-permute-start | bytes 307208 | tf_op jit(solution)/shard_map/ppermute | solution.py:385
  12.3 0.7 collective-permute-start.3
  13.0 0.3 collective-permute-done.2.near
  13.3 0.0 collective-permute-done.3.far
  13.3 1.6 %columns.1 = (f32[4,200,128]{2,1,0:T(8,128)S(1)}, f32[200,128]{1,0:T(8,128)}, f32[200,128]{1,0:T(8,128)}) custom-call(f32[200,128]{1,0:T(8,128)S(1)} %get-tuple-element.13.after.last, f32[200,128]{1,0:T(8,128)S(1)} %get-tuple-element.16.first, f32[200,128]{1,0:T(8,128)S(1)} %collective-permute-done.2.near, f32[200,128]{1,0:T(8,128)S(1)} %collective-permute-done.3.far), custom_call_target="tpu_custom_call" | custom-call | tf_op jit(solution)/shard_map/columns/pallas_call | solution.py:371
  14.8 1.5 %collective-permute-start.4 = (f32[200,128]{1,0:T(8,128)}, f32[200,128]{1,0:T(8,128)}, u32[]{:S(2)}, u32[]{:S(2)}) collective-permute-start(f32[200,128]{1,0:T(8,128)} %get-tuple-element.20), channel_id=1, source_target_pairs={{0,8},{16,24},{8,0},{24,16},{1,9},{17,25},{9,1},{25,17},{2,10},{18... | collective-permute-start | bytes 307208 | tf_op jit(solution)/shard_map/ppermute | solution.py:385
  16.3 1.3 %collective-permute-start.5 = (f32[200,128]{1,0:T(8,128)}, f32[200,128]{1,0:T(8,128)}, u32[]{:S(2)}, u32[]{:S(2)}) collective-permute-start(f32[200,128]{1,0:T(8,128)} %get-tuple-element.21), channel_id=1, source_target_pairs={{8,16},{16,8},{9,17},{17,9},{10,18},{18,10},{11,19},{19,11},{12,20... | collective-permute-start | bytes 307208 | tf_op jit(solution)/shard_map/ppermute | solution.py:385
  17.6 2.2 %collective-permute-done.4.near = f32[200,128]{1,0:T(8,128)} collective-permute-done((f32[200,128]{1,0:T(8,128)}, f32[200,128]{1,0:T(8,128)}, u32[]{:S(2)}, u32[]{:S(2)}) %collective-permute-start.4) | collective-permute-done | bytes 102432 | tf_op jit(solution)/shard_map/ppermute | solution.py:385
  19.8 0.0 collective-permute-done.5.far
  19.8 5.3 %strips.1.ends = f32[192,128]{1,0:T(8,128)S(1)} custom-call(f32[4,200,128]{2,1,0:T(8,128)S(1)} %get-tuple-element.19.strips, f32[200,128]{1,0:T(8,128)} %collective-permute-done.4.near, f32[200,128]{1,0:T(8,128)} %collective-permute-done.5.far), custom_call_target="tpu_custom_call" | custom-call | tf_op jit(solution)/shard_map/strips/pallas_call | solution.py:371
  25.1 0.0 collective-permute-done.near
  25.1 0.0 collective-permute-done.1.far
  25.1 0.0 copy-done.1
  25.1 0.0 copy-done.4
  25.1 0.0 copy-done.6
  25.1 6.4 %evolve.1.loc_ref = f32[192,128]{1,0:T(8,128)S(1)} custom-call(f32[2,1536,128]{2,1,0:T(8,128)S(1)} %bitcast.4, f32[8,128]{1,0:T(8,128)S(1)} %copy-done.4, f32[8,128]{1,0:T(8,128)S(1)} %copy-done.6, f32[7,200,128]{2,1,0:T(8,128)S(1)} %collective-permute-done.near, f32[7,200,128]{2,1,0:T(8,128)S(1)} %collective-permute-done.1.far, f32[192,128]{1,0:T(8,128)S(1)} %strips.1.ends), custom_call_target="tpu_custom_call" | custom-call | tf_op jit(solution)/shard_map/evolve/pallas_call | solution.py:371
  31.5 0.0 copy-start.2
  31.6 8.1 %collective-permute-start.6 = (f32[96,128]{1,0:T(8,128)S(1)}, f32[96,128]{1,0:T(8,128)S(1)}, u32[]{:S(2)}, u32[]{:S(2)}) collective-permute-start(f32[96,128]{1,0:T(8,128)S(1)} %slice_select_fusion), channel_id=1, source_target_pairs={{0,1},{1,0},{2,3},{3,2},{4,5},{5,4},{6,7},{7,6},{8,9},{9,8},{10,11... | collective-permute-start | bytes 147464 | tf_op jit(solution)/shard_map/ppermute | solution.py:390
  39.7 0.9 %collective-permute-done.6 = f32[96,128]{1,0:T(8,128)S(1)} collective-permute-done((f32[96,128]{1,0:T(8,128)S(1)}, f32[96,128]{1,0:T(8,128)S(1)}, u32[]{:S(2)}, u32[]{:S(2)}) %collective-permute-start.6) | collective-permute-done | bytes 49184 | tf_op jit(solution)/shard_map/ppermute | solution.py:390
  40.6 4.1 %collective-permute-start.7 = (f32[96,128]{1,0:T(8,128)S(1)}, f32[96,128]{1,0:T(8,128)S(1)}, u32[]{:S(2)}, u32[]{:S(2)}) collective-permute-start(f32[96,128]{1,0:T(8,128)S(1)} %select_add_fusion), channel_id=1, source_target_pairs={{0,8},{8,0},{16,24},{24,16},{1,9},{9,1},{17,25},{25,17},{2,10},{10... | collective-permute-start | bytes 147464 | tf_op jit(solution)/shard_map/ppermute | solution.py:390
  44.7 2.3 %collective-permute-done.7 = f32[96,128]{1,0:T(8,128)S(1)} collective-permute-done((f32[96,128]{1,0:T(8,128)S(1)}, f32[96,128]{1,0:T(8,128)S(1)}, u32[]{:S(2)}, u32[]{:S(2)}) %collective-permute-start.7) | collective-permute-done | bytes 49184 | tf_op jit(solution)/shard_map/ppermute | solution.py:390
  46.9 2.9 %collective-permute-start.8 = (f32[96,128]{1,0:T(8,128)S(1)}, f32[96,128]{1,0:T(8,128)S(1)}, u32[]{:S(2)}, u32[]{:S(2)}) collective-permute-start(f32[96,128]{1,0:T(8,128)S(1)} %add.21), channel_id=1, source_target_pairs={{0,16},{8,24},{16,0},{24,8},{1,17},{9,25},{17,1},{25,9},{2,18},{10... | collective-permute-start | bytes 147464 | tf_op jit(solution)/shard_map/ppermute | solution.py:390
  49.9 2.1 %collective-permute-done.8 = f32[96,128]{1,0:T(8,128)S(1)} collective-permute-done((f32[96,128]{1,0:T(8,128)S(1)}, f32[96,128]{1,0:T(8,128)S(1)}, u32[]{:S(2)}, u32[]{:S(2)}) %collective-permute-start.8) | collective-permute-done | bytes 49184 | tf_op jit(solution)/shard_map/ppermute | solution.py:390
  51.9 3.3 %collective-permute-start.9 = (f32[96,128]{1,0:T(8,128)S(1)}, f32[96,128]{1,0:T(8,128)S(1)}, u32[]{:S(2)}, u32[]{:S(2)}) collective-permute-start(f32[96,128]{1,0:T(8,128)S(1)} %add.22), channel_id=1, source_target_pairs={{0,2},{1,3},{2,0},{3,1},{4,6},{5,7},{6,4},{7,5},{8,10},{9,11},{10,... | collective-permute-start | bytes 147464 | tf_op jit(solution)/shard_map/ppermute | solution.py:390
  55.2 2.1 %collective-permute-done.9 = f32[96,128]{1,0:T(8,128)S(1)} collective-permute-done((f32[96,128]{1,0:T(8,128)S(1)}, f32[96,128]{1,0:T(8,128)S(1)}, u32[]{:S(2)}, u32[]{:S(2)}) %collective-permute-start.9) | collective-permute-done | bytes 49184 | tf_op jit(solution)/shard_map/ppermute | solution.py:390
  57.3 3.5 %collective-permute-start.10 = (f32[96,128]{1,0:T(8,128)S(1)}, f32[96,128]{1,0:T(8,128)S(1)}, u32[]{:S(2)}, u32[]{:S(2)}) collective-permute-start(f32[96,128]{1,0:T(8,128)S(1)} %add.23), channel_id=1, source_target_pairs={{0,4},{1,5},{2,6},{3,7},{4,0},{5,1},{6,2},{7,3},{8,12},{9,13},{10,... | collective-permute-start | bytes 147464 | tf_op jit(solution)/shard_map/ppermute | solution.py:390
  60.8 2.1 %collective-permute-done.10 = f32[96,128]{1,0:T(8,128)S(1)} collective-permute-done((f32[96,128]{1,0:T(8,128)S(1)}, f32[96,128]{1,0:T(8,128)S(1)}, u32[]{:S(2)}, u32[]{:S(2)}) %collective-permute-start.10) | collective-permute-done | bytes 49184 | tf_op jit(solution)/shard_map/ppermute | solution.py:390
  62.9 0.1 collective-permute-start.11
  63.0 1.2 %collective-permute-done.11 = f32[96,128]{1,0:T(8,128)S(1)} collective-permute-done((f32[96,128]{1,0:T(8,128)S(1)}, f32[96,128]{1,0:T(8,128)S(1)}, u32[]{:S(2)}, u32[]{:S(2)}) %collective-permute-start.11) | collective-permute-done | bytes 49184 | tf_op jit(solution)/shard_map/ppermute | solution.py:390
  64.2 0.6 pad_maximum_fusion.tot_ref
  64.8 0.0 copy-done.2
  64.8 10.6 %factor.1 = (f32[192,192]{1,0:T(8,128)}, f32[1,192]{1,0:T(1,128)}) custom-call(f32[192,128]{1,0:T(8,128)} %pad_maximum_fusion.tot_ref, f32[192,128]{1,0:T(8,128)} %copy-done.2), custom_call_target="tpu_custom_call" | custom-call | tf_op jit(solution)/shard_map/factor/pallas_call | solution.py:122
  (7 shorter events, 0.1 us)
Async XLA Ops:
  0.6 1.4 %copy-start = (f32[2,192,8,128]{3,2,1,0:T(8,128)S(1)}, f32[2,192,8,128]{3,2,1,0:T(8,128)}, u32[]{:S(2)}) copy-start(f32[2,192,8,128]{3,2,1,0:T(8,128)} %param.3) | copy-start | bytes 4718596
  2.0 0.7 copy-start.3
  2.7 0.7 copy-start.5
  5.8 19.3 %copy-start.1 = (f32[2,192,8,128]{3,2,1,0:T(8,128)S(1)}, f32[2,192,8,128]{3,2,1,0:T(8,128)}, u32[]{:S(2)}) copy-start(f32[2,192,8,128]{3,2,1,0:T(8,128)} %param.3) | copy-start | bytes 4718596
  5.8 19.3 %copy-start.4 = (f32[8,128]{1,0:T(8,128)S(1)}, f32[8,128]{1,0:T(8,128)}, u32[]{:S(2)}) copy-start(f32[8,128]{1,0:T(8,128)} %coeff_self.3) | copy-start | bytes 12292
  5.8 19.3 %copy-start.6 = (f32[8,128]{1,0:T(8,128)S(1)}, f32[8,128]{1,0:T(8,128)}, u32[]{:S(2)}) copy-start(f32[8,128]{1,0:T(8,128)} %coeff_cross.3) | copy-start | bytes 12292
  7.2 17.9 %collective-permute-start = (f32[7,200,128]{2,1,0:T(8,128)}, f32[7,200,128]{2,1,0:T(8,128)S(1)}, u32[]{:S(2)}, u32[]{:S(2)}) collective-permute-start(f32[7,200,128]{2,1,0:T(8,128)} %get-tuple-element.14), channel_id=1, source_target_pairs={{0,1},{2,3},{4,5},{6,7},{1,0},{3,2},{5,4},{7,6},{8,9},{10,11},{12,... | collective-permute-start | bytes 2150408 | tf_op jit(solution)/shard_map/ppermute | solution.py:385
  7.7 17.4 %collective-permute-start.1 = (f32[7,200,128]{2,1,0:T(8,128)}, f32[7,200,128]{2,1,0:T(8,128)S(1)}, u32[]{:S(2)}, u32[]{:S(2)}) collective-permute-start(f32[7,200,128]{2,1,0:T(8,128)} %get-tuple-element.15), channel_id=1, source_target_pairs={{1,2},{3,4},{5,6},{2,1},{4,3},{6,5},{9,10},{11,12},{13,14},{10,9},... | collective-permute-start | bytes 2150408 | tf_op jit(solution)/shard_map/ppermute | solution.py:385
  8.4 4.9 %collective-permute-start.2 = (f32[200,128]{1,0:T(8,128)S(1)}, f32[200,128]{1,0:T(8,128)S(1)}, u32[]{:S(2)}, u32[]{:S(2)}) collective-permute-start(f32[200,128]{1,0:T(8,128)S(1)} %get-tuple-element.17), channel_id=1, source_target_pairs={{0,1},{2,3},{4,5},{6,7},{1,0},{3,2},{5,4},{7,6},{8,9},{10,11},{12,... | collective-permute-start | bytes 307208 | tf_op jit(solution)/shard_map/ppermute | solution.py:385
  12.3 1.0 %collective-permute-start.3 = (f32[200,128]{1,0:T(8,128)S(1)}, f32[200,128]{1,0:T(8,128)S(1)}, u32[]{:S(2)}, u32[]{:S(2)}) collective-permute-start(f32[200,128]{1,0:T(8,128)S(1)} %get-tuple-element.18), channel_id=1, source_target_pairs={{1,2},{3,4},{5,6},{2,1},{4,3},{6,5},{9,10},{11,12},{13,14},{10,9},... | collective-permute-start | bytes 307208 | tf_op jit(solution)/shard_map/ppermute | solution.py:385
  14.8 5.0 %collective-permute-start.4 = (f32[200,128]{1,0:T(8,128)}, f32[200,128]{1,0:T(8,128)}, u32[]{:S(2)}, u32[]{:S(2)}) collective-permute-start(f32[200,128]{1,0:T(8,128)} %get-tuple-element.20), channel_id=1, source_target_pairs={{0,8},{16,24},{8,0},{24,16},{1,9},{17,25},{9,1},{25,17},{2,10},{18... | collective-permute-start | bytes 307208 | tf_op jit(solution)/shard_map/ppermute | solution.py:385
  16.3 3.5 %collective-permute-start.5 = (f32[200,128]{1,0:T(8,128)}, f32[200,128]{1,0:T(8,128)}, u32[]{:S(2)}, u32[]{:S(2)}) collective-permute-start(f32[200,128]{1,0:T(8,128)} %get-tuple-element.21), channel_id=1, source_target_pairs={{8,16},{16,8},{9,17},{17,9},{10,18},{18,10},{11,19},{19,11},{12,20... | collective-permute-start | bytes 307208 | tf_op jit(solution)/shard_map/ppermute | solution.py:385
  31.5 33.3 %copy-start.2 = (f32[192,128]{1,0:T(8,128)}, f32[192,128]{1,0:T(8,128)S(1)}, u32[]{:S(2)}) copy-start(f32[192,128]{1,0:T(8,128)S(1)} %evolve.1.loc_ref) | copy-start | bytes 294916
  31.6 9.0 %collective-permute-start.6 = (f32[96,128]{1,0:T(8,128)S(1)}, f32[96,128]{1,0:T(8,128)S(1)}, u32[]{:S(2)}, u32[]{:S(2)}) collective-permute-start(f32[96,128]{1,0:T(8,128)S(1)} %slice_select_fusion), channel_id=1, source_target_pairs={{0,1},{1,0},{2,3},{3,2},{4,5},{5,4},{6,7},{7,6},{8,9},{9,8},{10,11... | collective-permute-start | bytes 147464 | tf_op jit(solution)/shard_map/ppermute | solution.py:390
  40.6 6.4 %collective-permute-start.7 = (f32[96,128]{1,0:T(8,128)S(1)}, f32[96,128]{1,0:T(8,128)S(1)}, u32[]{:S(2)}, u32[]{:S(2)}) collective-permute-start(f32[96,128]{1,0:T(8,128)S(1)} %select_add_fusion), channel_id=1, source_target_pairs={{0,8},{8,0},{16,24},{24,16},{1,9},{9,1},{17,25},{25,17},{2,10},{10... | collective-permute-start | bytes 147464 | tf_op jit(solution)/shard_map/ppermute | solution.py:390
  46.9 5.0 %collective-permute-start.8 = (f32[96,128]{1,0:T(8,128)S(1)}, f32[96,128]{1,0:T(8,128)S(1)}, u32[]{:S(2)}, u32[]{:S(2)}) collective-permute-start(f32[96,128]{1,0:T(8,128)S(1)} %add.21), channel_id=1, source_target_pairs={{0,16},{8,24},{16,0},{24,8},{1,17},{9,25},{17,1},{25,9},{2,18},{10... | collective-permute-start | bytes 147464 | tf_op jit(solution)/shard_map/ppermute | solution.py:390
  51.9 5.3 %collective-permute-start.9 = (f32[96,128]{1,0:T(8,128)S(1)}, f32[96,128]{1,0:T(8,128)S(1)}, u32[]{:S(2)}, u32[]{:S(2)}) collective-permute-start(f32[96,128]{1,0:T(8,128)S(1)} %add.22), channel_id=1, source_target_pairs={{0,2},{1,3},{2,0},{3,1},{4,6},{5,7},{6,4},{7,5},{8,10},{9,11},{10,... | collective-permute-start | bytes 147464 | tf_op jit(solution)/shard_map/ppermute | solution.py:390
  57.3 5.6 %collective-permute-start.10 = (f32[96,128]{1,0:T(8,128)S(1)}, f32[96,128]{1,0:T(8,128)S(1)}, u32[]{:S(2)}, u32[]{:S(2)}) collective-permute-start(f32[96,128]{1,0:T(8,128)S(1)} %add.23), channel_id=1, source_target_pairs={{0,4},{1,5},{2,6},{3,7},{4,0},{5,1},{6,2},{7,3},{8,12},{9,13},{10,... | collective-permute-start | bytes 147464 | tf_op jit(solution)/shard_map/ppermute | solution.py:390
  62.9 1.3 %collective-permute-start.11 = (f32[96,128]{1,0:T(8,128)S(1)}, f32[96,128]{1,0:T(8,128)S(1)}, u32[]{:S(2)}, u32[]{:S(2)}) collective-permute-start(f32[96,128]{1,0:T(8,128)S(1)} %add.24), channel_id=1, source_target_pairs={{0,1},{1,0},{2,3},{3,2},{4,5},{5,4},{6,7},{7,6},{8,9},{9,8},{10,11... | collective-permute-start | bytes 147464 | tf_op jit(solution)/shard_map/ppermute | solution.py:390

commit v2 on v1

--- a/solution.py
+++ b/solution.py
@@ -12,11 +12,12 @@
 STEPS = 4
 diffusion = 0.2
 slow_rate = 0.05
-HEIGHT_EDGE = 24
-HEIGHT_ROW = 24
-HEIGHT_STRIP = 24
-HEIGHT_EVOLVE = 16
+HEIGHT_EDGE = 48
+HEIGHT_ROW = 48
+HEIGHT_STRIP = 96
+HEIGHT_EVOLVE = 48
 SIDE = 64
+VMEM_BYTES = 24 * 1024 * 1024
 LANES = 128
 SUB = 8
 HI = lax.Precision.HIGHEST
@@ -31,11 +32,11 @@
 def block_pairs(n):
     return [(i, j) for i in range(n) for j in range(i, n)]
 
-def unpack_blocks(ref, n):
+def unpack_blocks(packed, n):
     out = {}
     for index, key in enumerate(block_pairs(n)):
         row, half = divmod(index, 2)
-        out[key] = ref[row*SIDE:(row+1)*SIDE, half*SIDE:(half+1)*SIDE]
+        out[key] = packed[row*SIDE:(row+1)*SIDE, half*SIDE:(half+1)*SIDE]
     return out
 
 def spread_lane(x, lane):
@@ -86,9 +87,11 @@
         out.append((whole[:, :SIDE], whole[:, SIDE:]))
     return out
 
-def factor_kernel(n, weight, tot_ref, loc_ref, out_ref, growth_ref):
-    total = unpack_blocks(tot_ref, n)
-    local = unpack_blocks(loc_ref, n)
+def factor_kernel(n, weight, own_ref, other_ref, loc_ref, out_ref, growth_ref):
+    odd = lax.axis_index("tile") % 2 == 1
+    own, other = own_ref[...], other_ref[...]
+    total = unpack_blocks(jnp.concatenate([jnp.where(odd, other, own), jnp.where(odd, own, other)], axis=0), n)
+    local = unpack_blocks(loc_ref[...], n)
     keep = (lax.broadcasted_iota(jnp.int32, (SIDE, SIDE), 0) <= lax.broadcasted_iota(jnp.int32, (SIDE, SIDE), 1))
     diag = (lax.broadcasted_iota(jnp.int32, (SIDE, SIDE), 0) == lax.broadcasted_iota(jnp.int32, (SIDE, SIDE), 1))
     inverse = {}
@@ -117,13 +120,10 @@
         for i in range(j + 1, n):
             out_ref[i*SIDE:(i+1)*SIDE, j*SIDE:(j+1)*SIDE] = jnp.zeros((SIDE, SIDE), jnp.float32)
 
-def factor_call(total, local, k, weight):
-    vm = pl.BlockSpec(memory_space=pltpu.VMEM)
-    out, growth = pl.pallas_call(
-        functools.partial(factor_kernel, k // SIDE, weight),
-        out_shape=(jax.ShapeDtypeStruct((k, k), jnp.float32), jax.ShapeDtypeStruct((1, k), jnp.float32)),
-        in_specs=[vm, vm], out_specs=(vm, vm), name="factor",
-    )(total, local)
+def factor_call(own, other, local, k, weight):
+    out, growth = local_call(
+        functools.partial(factor_kernel, k // SIDE, weight), "factor", [(k, k), (1, k)], [], own, other, local
+    )
     return out, growth[0]
 
 
@@ -156,14 +156,18 @@
 
 
 def edge_kernel(fields, height, tangents_hbm, self_hbm, cross_hbm, last_out, first_out, near, far, tangents, coeff_self, coeff_cross, sems):
+    chunks = fields // height
+    span = height * SUB
     loads = [
-        pltpu.make_async_copy(src, dst, sems.at[i])
-        for i, (src, dst) in enumerate(((tangents_hbm, tangents), (self_hbm, coeff_self), (cross_hbm, coeff_cross)))
+        pltpu.make_async_copy(tangents_hbm.at[:, pl.ds(g * span, span), :], tangents.at[:, pl.ds(g * span, span), :], sems.at[g])
+        for g in range(chunks)
     ]
-    for load in loads:
+    small = [
+        pltpu.make_async_copy(src, dst, sems.at[chunks + i])
+        for i, (src, dst) in enumerate(((self_hbm, coeff_self), (cross_hbm, coeff_cross)))
+    ]
+    for load in loads + small:
         load.start()
-    for load in loads:
-        load.wait()
     odd = lax.axis_index("tile") % 2 == 1
 
     def send(at, rows):
@@ -185,10 +189,11 @@
         near[at, :] = pick(odd, to_above, to_below)
         far[at, :] = pick(odd, to_below, to_above)
 
-    @pl.loop(0, fields // height)
-    def _(g):
-        send(chunk(g, height), own_rows(tangents, g, height))
-
+    for g, load in enumerate(loads):
+        load.wait()
+        send(pl.ds(g * height, height), own_rows(tangents, g, height))
+    for load in small:
+        load.wait()
     send(pl.ds(fields, SUB), own_coeffs(coeff_self, coeff_cross))
 
 
@@ -354,8 +359,7 @@
             for r in range(SUB):
                 cells[at, (f * SUB + r) * LANES:(f * SUB + r + 1) * LANES] = jnp.where(middle, rows[r], 0.0)
 
-    cells[:, 2 * SUB * LANES:] = ends[...]
-    whole = dot_nt(cells[...], cells[...])
+    whole = dot_nt(cells[...], cells[...]) + dot_nt(ends[...], ends[...])
     for index, (i, j) in enumerate(block_pairs(fields // SIDE)):
         row, half = divmod(index, 2)
         gram[row * SIDE:(row + 1) * SIDE, half * SIDE:(half + 1) * SIDE] = whole[
@@ -363,25 +367,24 @@
         ]
 
 
-def local_call(body, name, out_shapes, scratch, *args, outside=0):
+def local_call(body, name, out_shapes, scratch, *args, hbm=False):
     spec = pl.BlockSpec(memory_space=pltpu.VMEM)
-    own = [pltpu.VMEM(a.shape, a.dtype) for a in args[:outside]]
-    if outside:
-        own.append(pltpu.SemaphoreType.DMA((outside,)))
     return pl.pallas_call(
         body,
         out_shape=[jax.ShapeDtypeStruct(s, jnp.float32) for s in out_shapes],
-        in_specs=[pl.BlockSpec(memory_space=pl.ANY)] * outside + [spec] * (len(args) - outside),
+        in_specs=[pl.BlockSpec(memory_space=pltpu.HBM) if hbm else spec] * len(args),
         out_specs=[spec] * len(out_shapes),
-        scratch_shapes=[pltpu.VMEM(s, jnp.float32) for s in scratch] + own,
-        compiler_params=pltpu.CompilerParams(vmem_limit_bytes=40 * 1024 * 1024),
+        scratch_shapes=[pltpu.VMEM(s, jnp.float32) if isinstance(s, tuple) else s for s in scratch],
+        compiler_params=pltpu.CompilerParams(vmem_limit_bytes=VMEM_BYTES),
         name=name,
     )(*args)
 
 
-def swap(cells, axis, first):
+def swap(cells, axis, first, close=False):
     count = lax.axis_size(axis)
     pairs = [(i, i + 1) for i in range(first, count - 1, 2)]
+    if close and first:
+        pairs.append((0, count - 1))
     return lax.ppermute(cells, axis, pairs + [(b, a) for a, b in pairs])
 
 
@@ -400,8 +403,7 @@
         while bit < lax.axis_size(axis):
             part = part + exchange(part, axis, bit)
             bit *= 2
-    other = exchange(part, "tile", 1)
-    return jnp.concatenate([jnp.where(odd, other, part), jnp.where(odd, part, other)], axis=0)
+    return part, exchange(part, "tile", 1)
 
 
 def per_device(tangents, reaction_self, reaction_cross):
@@ -410,18 +412,20 @@
     rows = tangents.reshape(2, fields * tangents.shape[2], tangents.shape[3])
     message, strip = (2 * STEPS - 1, padded, LANES), (padded, LANES)
     inputs = (rows, reaction_self, reaction_cross)
-    last, first, near_edges, far_edges = local_call(
-        functools.partial(edge_kernel, fields, HEIGHT_EDGE), "edges", [strip] * 4, [], *inputs, outside=3
+    last, first, near_edges, far_edges, *inputs = local_call(
+        functools.partial(edge_kernel, fields, HEIGHT_EDGE), "edges", [strip] * 4 + [a.shape for a in inputs],
+        [pltpu.SemaphoreType.DMA((fields // HEIGHT_EDGE + 2,))], *inputs, hbm=True,
     )
     near_edges, far_edges = swap(near_edges, "tile", 0), swap(far_edges, "tile", 1)
     near_rows, far_rows = local_call(
-        functools.partial(row_kernel, fields, HEIGHT_ROW), "rows", [message] * 2, [], last, *inputs
-    )
+        functools.partial(row_kernel, fields, HEIGHT_ROW), "rows", [message] * 2, [], near_edges, *inputs
+    )
+    far_edges, near_rows, far_rows = lax.optimization_barrier((far_edges, near_rows, far_rows))
     near_rows, far_rows = swap(near_rows, "tile", 0), swap(far_rows, "tile", 1)
     strips, near_cols, far_cols = local_call(
         column_kernel, "columns", [(4,) + strip, strip, strip], [(2,) + strip], last, first, near_edges, far_edges
     )
-    near_cols, far_cols = swap(near_cols, "grp", 0), swap(far_cols, "grp", 1)
+    near_cols, far_cols = swap(near_cols, "grp", 0), swap(far_cols, "grp", 1, close=True)
     (ends,) = local_call(
         functools.partial(strip_kernel, fields, HEIGHT_STRIP), "strips", [(fields, LANES)], [(2,) + strip], strips, near_cols, far_cols
     )
@@ -429,11 +433,10 @@
     blocks = side_blocks * (side_blocks + 1) // 2
     (packed,) = local_call(
         functools.partial(evolve_kernel, fields, HEIGHT_EVOLVE), "evolve", [((blocks + 1) // 2 * SIDE, 2 * SIDE)],
-        [(2, SUB + 2 * STEPS - 2, SUB, LANES), (fields, (2 * SUB + 1) * LANES)],
-        *inputs, near_rows, far_rows, ends,
+        [(2, SUB + 2 * STEPS - 2, SUB, LANES), (fields, 2 * SUB * LANES)], *inputs, near_rows, far_rows, ends,
     )
     block_total = lax.axis_size("grp") * lax.axis_size("tile")
-    corrections, growth = factor_call(sum_blocks(packed), packed, fields, math.sqrt(block_total))
+    corrections, growth = factor_call(*sum_blocks(packed), packed, fields, math.sqrt(block_total))
     return (corrections, growth)
 
 

time: 75.7 us -> 63.5 us (0.84)
  starting transfers between devices: 30.6 us -> 17.7 us
  waiting for transfers between devices: 13 us -> 19.4 us
  Pallas kernels: 27.6 us -> 22.7 us
    ppermute x6, starting transfers between devices: 22 us -> 7.66 us  [exchange(): return lax.ppermute(cells, axis, [(i, i ^ bit) for i in range(count)])]
    pallas_call x1 -> x0, Pallas kernels: 10.6 us -> none  [factor_call(): pl.pallas_call(functools.partial(factor_kernel, k // SIDE, weight), out_s...]
    pallas_call x5 -> x6, Pallas kernels: 17 us -> 22.7 us  [local_call(): pl.pallas_call(body, out_shape=[jax.ShapeDtypeStruct(s, jnp.float32) for...]
    ppermute x6, waiting for transfers between devices: 2.47 us -> 5.77 us  [swap(): return lax.ppermute(cells, axis, pairs + [(b, a) for a, b in pairs])]
    ppermute x6, waiting for transfers between devices: 10.6 us -> 13.6 us  [exchange(): return lax.ppermute(cells, axis, [(i, i ^ bit) for i in range(count)])]
    ppermute x6, starting transfers between devices: 8.56 us -> 10 us  [swap(): return lax.ppermute(cells, axis, pairs + [(b, a) for a, b in pairs])]
    unnamed x14 -> x6, local copies, waits for them, and re-layouts: 2.8 us -> 2.77 us
  transfers between devices with their start and end apart: 12 -> 12, of which waited for: 8 -> 9; matrix products, arithmetic and copies ran while one was open for 0% -> 0% of each run, Pallas kernels for 9% -> 11%
where the time goes in v2:
time: 63.5 us; the launch traced here: 63.3 us
  Pallas kernels  22.7 us (36%)
  waiting for transfers between devices  19.4 us (31%)
  starting transfers between devices  17.7 us (28%)
  local copies, waits for them, and re-layouts  2.77 us (4%)
  between operations  0.72 us (1%)
    pallas_call x6, Pallas kernels, local_call(): pl.pallas_call(body, out_shape=[jax.ShapeDtypeStruct(s, jnp.float32) for...  22.7 us
    ppermute x6, waiting for transfers between devices, exchange(): return lax.ppermute(cells, axis, [(i, i ^ bit) for i in range(count)])  13.6 us
    ppermute x6, starting transfers between devices, swap(): return lax.ppermute(cells, axis, pairs + [(b, a) for a, b in pairs])  10 us
    ppermute x6, starting transfers between devices, exchange(): return lax.ppermute(cells, axis, [(i, i ^ bit) for i in range(count)])  7.66 us
    ppermute x6, waiting for transfers between devices, swap(): return lax.ppermute(cells, axis, pairs + [(b, a) for a, b in pairs])  5.77 us
    unnamed x6, local copies, waits for them, and re-layouts  2.77 us
  transfers between devices with their start and end apart: 12, of which 9 were waited for; matrix products, arithmetic and copies ran while one was open for 0% of the time, Pallas kernels for 11%

profile of v2, /device:TPU:0, one launch (start us, length us, event | category | flops | bytes accessed | tf_op | source)
XLA Modules:
  0.0 63.3 jit_solution(16329057701046499965)
XLA Ops:
  0.6 0.0 copy-start
  0.6 1.4 %copy-done = f32[2,192,8,128]{3,2,1,0:T(8,128)S(1)} copy-done((f32[2,192,8,128]{3,2,1,0:T(8,128)S(1)}, f32[2,192,8,128]{3,2,1,0:T(8,128)}, u32[]{:S(2)}) %copy-start) | copy-done | bytes 1572888
  2.0 0.0 copy-start.1
  2.0 0.7 %copy-done.1 = f32[8,128]{1,0:T(8,128)S(1)} copy-done((f32[8,128]{1,0:T(8,128)S(1)}, f32[8,128]{1,0:T(8,128)}, u32[]{:S(2)}) %copy-start.1) | copy-done | bytes 4120
  2.7 0.0 copy-start.2
  2.7 0.7 %copy-done.2 = f32[8,128]{1,0:T(8,128)S(1)} copy-done((f32[8,128]{1,0:T(8,128)S(1)}, f32[8,128]{1,0:T(8,128)}, u32[]{:S(2)}) %copy-start.2) | copy-done | bytes 4120
  3.4 1.9 %edges.1 = (f32[200,128]{1,0:T(8,128)S(1)}, f32[200,128]{1,0:T(8,128)S(1)}, f32[200,128]{1,0:T(8,128)S(1)}, f32[200,128]{1,0:T(8,128)S(1)}, f32[2,1536,128]{2,1,...) custom-call(f32[2,1536,128]{2,1,0:T(8,128)S(1)} %bitcast.2, f32[8,128]{1,0:T(8,128)S(1)} %copy-done.1, ...), custom_call_target="tpu_custom_call" | custom-call | tf_op jit(solution)/shard_map/edges/pallas_call | solution.py:372
  5.4 0.5 collective-permute-start.1
  5.9 0.7 %collective-permute-start = (f32[200,128]{1,0:T(8,128)S(1)}, f32[200,128]{1,0:T(8,128)S(1)}, u32[]{:S(2)}, u32[]{:S(2)}) collective-permute-start(f32[200,128]{1,0:T(8,128)S(1)} %get-tuple-element.22), channel_id=1, source_target_pairs={{1,2},{3,4},{5,6},{2,1},{4,3},{6,5},{9,10},{11,12},{13,14},{10,9},... | collective-permute-start | bytes 307208 | tf_op jit(solution)/shard_map/ppermute | solution.py:388
  6.5 0.3 collective-permute-done.1.after.near
  6.8 1.3 %rows.1 = (f32[7,200,128]{2,1,0:T(8,128)}, f32[7,200,128]{2,1,0:T(8,128)}) custom-call(f32[200,128]{1,0:T(8,128)S(1)} %collective-permute-done.1.after.near, f32[2,1536,128]{2,1,0:T(8,128)S(1)} %get-tuple-element.19.tangents, f32[8,128]{1,0:T(8,128)S(1)} %get-tuple-element.20.coeff_self, f32[8,128]{1,0:T(8,128)S(1)} %get-tuple-element.21.coeff_cross), custom_call_target="tpu_custom_call" | custom-call | tf_op jit(solution)/shard_map/rows/pallas_call | solution.py:372
  8.2 0.0 collective-permute-done.far
  8.2 4.7 %collective-permute-start.2 = (f32[7,200,128]{2,1,0:T(8,128)}, f32[7,200,128]{2,1,0:T(8,128)S(1)}, u32[]{:S(2)}, u32[]{:S(2)}) collective-permute-start(f32[7,200,128]{2,1,0:T(8,128)} %get-tuple-element.26), channel_id=1, source_target_pairs={{0,1},{2,3},{4,5},{6,7},{1,0},{3,2},{5,4},{7,6},{8,9},{10,11},{12,... | collective-permute-start | bytes 2150408 | tf_op jit(solution)/shard_map/ppermute | solution.py:388
  12.8 0.7 %collective-permute-start.3 = (f32[7,200,128]{2,1,0:T(8,128)}, f32[7,200,128]{2,1,0:T(8,128)S(1)}, u32[]{:S(2)}, u32[]{:S(2)}) collective-permute-start(f32[7,200,128]{2,1,0:T(8,128)} %get-tuple-element.27), channel_id=1, source_target_pairs={{1,2},{3,4},{5,6},{2,1},{4,3},{6,5},{9,10},{11,12},{13,14},{10,9},... | collective-permute-start | bytes 2150408 | tf_op jit(solution)/shard_map/ppermute | solution.py:388
  13.5 1.6 %columns.1 = (f32[4,200,128]{2,1,0:T(8,128)S(1)}, f32[200,128]{1,0:T(8,128)}, f32[200,128]{1,0:T(8,128)}) custom-call(f32[200,128]{1,0:T(8,128)S(1)} %get-tuple-element.28.last, f32[200,128]{1,0:T(8,128)S(1)} %get-tuple-element.29.first, f32[200,128]{1,0:T(8,128)S(1)} %collective-permute-done.1.after.near, f32[200,128]{1,0:T(8,128)S(1)} %collective-permute-done.far), custom_call_target="tpu_custom_call" | custom-call | tf_op jit(solution)/shard_map/columns/pallas_call | solution.py:372
  15.1 2.0 %collective-permute-start.4 = (f32[200,128]{1,0:T(8,128)}, f32[200,128]{1,0:T(8,128)S(1)}, u32[]{:S(2)}, u32[]{:S(2)}) collective-permute-start(f32[200,128]{1,0:T(8,128)} %get-tuple-element.32), channel_id=1, source_target_pairs={{0,8},{16,24},{8,0},{24,16},{1,9},{17,25},{9,1},{25,17},{2,10},{18... | collective-permute-start | bytes 307208 | tf_op jit(solution)/shard_map/ppermute | solution.py:388
  17.1 1.5 %collective-permute-start.5 = (f32[200,128]{1,0:T(8,128)}, f32[200,128]{1,0:T(8,128)}, u32[]{:S(2)}, u32[]{:S(2)}) collective-permute-start(f32[200,128]{1,0:T(8,128)} %get-tuple-element.33), channel_id=1, source_target_pairs={{8,16},{0,24},{16,8},{24,0},{9,17},{1,25},{17,9},{25,1},{10,18},{2... | collective-permute-start | bytes 307208 | tf_op jit(solution)/shard_map/ppermute | solution.py:388
  18.6 1.4 %collective-permute-done.4.near = f32[200,128]{1,0:T(8,128)S(1)} collective-permute-done((f32[200,128]{1,0:T(8,128)}, f32[200,128]{1,0:T(8,128)S(1)}, u32[]{:S(2)}, u32[]{:S(2)}) %collective-permute-start.4) | collective-permute-done | bytes 102432 | tf_op jit(solution)/shard_map/ppermute | solution.py:388
  20.0 4.1 %collective-permute-done.5.far = f32[200,128]{1,0:T(8,128)} collective-permute-done((f32[200,128]{1,0:T(8,128)}, f32[200,128]{1,0:T(8,128)}, u32[]{:S(2)}, u32[]{:S(2)}) %collective-permute-start.5) | collective-permute-done | bytes 102432 | tf_op jit(solution)/shard_map/ppermute | solution.py:388
  24.1 3.8 %strips.1.ends = f32[192,128]{1,0:T(8,128)S(1)} custom-call(f32[4,200,128]{2,1,0:T(8,128)S(1)} %get-tuple-element.31.strips, f32[200,128]{1,0:T(8,128)S(1)} %collective-permute-done.4.near, f32[200,128]{1,0:T(8,128)} %collective-permute-done.5.far), custom_call_target="tpu_custom_call" | custom-call | tf_op jit(solution)/shard_map/strips/pallas_call | solution.py:372
  27.9 0.0 collective-permute-done.2.near
  27.9 0.0 collective-permute-done.3.far
  27.9 4.4 %evolve.1.loc_ref = f32[192,128]{1,0:T(8,128)S(1)} custom-call(f32[2,1536,128]{2,1,0:T(8,128)S(1)} %get-tuple-element.19.tangents, f32[8,128]{1,0:T(8,128)S(1)} %get-tuple-element.20.coeff_self, f32[8,128]{1,0:T(8,128)S(1)} %get-tuple-element.21.coeff_cross, f32[7,200,128]{2,1,0:T(8,128)S(1)} %collective-permute-done.2.near, ...), custom_call_target="tpu_custom_call" | custom-call | tf_op jit(solution)/shard_map/evolve/pallas_call | solution.py:372
  32.3 1.0 %collective-permute-start.6 = (f32[96,128]{1,0:T(8,128)S(1)}, f32[96,128]{1,0:T(8,128)S(1)}, u32[]{:S(2)}, u32[]{:S(2)}) collective-permute-start(f32[96,128]{1,0:T(8,128)S(1)} %slice_select_fusion), channel_id=1, source_target_pairs={{0,1},{1,0},{2,3},{3,2},{4,5},{5,4},{6,7},{7,6},{8,9},{9,8},{10,11... | collective-permute-start | bytes 147464 | tf_op jit(solution)/shard_map/ppermute | solution.py:393
  33.3 0.9 %collective-permute-done.6 = f32[96,128]{1,0:T(8,128)S(1)} collective-permute-done((f32[96,128]{1,0:T(8,128)S(1)}, f32[96,128]{1,0:T(8,128)S(1)}, u32[]{:S(2)}, u32[]{:S(2)}) %collective-permute-start.6) | collective-permute-done | bytes 49184 | tf_op jit(solution)/shard_map/ppermute | solution.py:393
  34.2 0.7 %collective-permute-start.7 = (f32[96,128]{1,0:T(8,128)S(1)}, f32[96,128]{1,0:T(8,128)S(1)}, u32[]{:S(2)}, u32[]{:S(2)}) collective-permute-start(f32[96,128]{1,0:T(8,128)S(1)} %select_add_fusion), channel_id=1, source_target_pairs={{0,8},{8,0},{16,24},{24,16},{1,9},{9,1},{17,25},{25,17},{2,10},{10... | collective-permute-start | bytes 147464 | tf_op jit(solution)/shard_map/ppermute | solution.py:393
  34.9 3.4 %collective-permute-done.7 = f32[96,128]{1,0:T(8,128)S(1)} collective-permute-done((f32[96,128]{1,0:T(8,128)S(1)}, f32[96,128]{1,0:T(8,128)S(1)}, u32[]{:S(2)}, u32[]{:S(2)}) %collective-permute-start.7) | collective-permute-done | bytes 49184 | tf_op jit(solution)/shard_map/ppermute | solution.py:393
  38.4 0.2 collective-permute-start.8
  38.6 3.9 %collective-permute-done.8 = f32[96,128]{1,0:T(8,128)S(1)} collective-permute-done((f32[96,128]{1,0:T(8,128)S(1)}, f32[96,128]{1,0:T(8,128)S(1)}, u32[]{:S(2)}, u32[]{:S(2)}) %collective-permute-start.8) | collective-permute-done | bytes 49184 | tf_op jit(solution)/shard_map/ppermute | solution.py:393
  42.5 2.1 %collective-permute-start.9 = (f32[96,128]{1,0:T(8,128)S(1)}, f32[96,128]{1,0:T(8,128)S(1)}, u32[]{:S(2)}, u32[]{:S(2)}) collective-permute-start(f32[96,128]{1,0:T(8,128)S(1)} %add.22), channel_id=1, source_target_pairs={{0,2},{1,3},{2,0},{3,1},{4,6},{5,7},{6,4},{7,5},{8,10},{9,11},{10,... | collective-permute-start | bytes 147464 | tf_op jit(solution)/shard_map/ppermute | solution.py:393
  44.6 2.1 %collective-permute-done.9 = f32[96,128]{1,0:T(8,128)S(1)} collective-permute-done((f32[96,128]{1,0:T(8,128)S(1)}, f32[96,128]{1,0:T(8,128)S(1)}, u32[]{:S(2)}, u32[]{:S(2)}) %collective-permute-start.9) | collective-permute-done | bytes 49184 | tf_op jit(solution)/shard_map/ppermute | solution.py:393
  46.7 3.6 %collective-permute-start.10 = (f32[96,128]{1,0:T(8,128)S(1)}, f32[96,128]{1,0:T(8,128)S(1)}, u32[]{:S(2)}, u32[]{:S(2)}) collective-permute-start(f32[96,128]{1,0:T(8,128)S(1)} %add.23), channel_id=1, source_target_pairs={{0,4},{1,5},{2,6},{3,7},{4,0},{5,1},{6,2},{7,3},{8,12},{9,13},{10,... | collective-permute-start | bytes 147464 | tf_op jit(solution)/shard_map/ppermute | solution.py:393
  50.3 2.1 %collective-permute-done.10 = f32[96,128]{1,0:T(8,128)S(1)} collective-permute-done((f32[96,128]{1,0:T(8,128)S(1)}, f32[96,128]{1,0:T(8,128)S(1)}, u32[]{:S(2)}, u32[]{:S(2)}) %collective-permute-start.10) | collective-permute-done | bytes 49184 | tf_op jit(solution)/shard_map/ppermute | solution.py:393
  52.4 0.1 collective-permute-start.11
  52.4 1.2 %collective-permute-done.11.other_ref = f32[96,128]{1,0:T(8,128)S(1)} collective-permute-done((f32[96,128]{1,0:T(8,128)S(1)}, f32[96,128]{1,0:T(8,128)S(1)}, u32[]{:S(2)}, u32[]{:S(2)}) %collective-permute-start.11) | collective-permute-done | bytes 49184 | tf_op jit(solution)/shard_map/ppermute | solution.py:393
  53.6 9.6 %factor.1 = (f32[192,192]{1,0:T(8,128)}, f32[1,192]{1,0:T(1,128)}) custom-call(f32[96,128]{1,0:T(8,128)S(1)} %add.24.own_ref, f32[96,128]{1,0:T(8,128)S(1)} %collective-permute-done.11.other_ref, f32[192,128]{1,0:T(8,128)S(1)} %evolve.1.loc_ref), custom_call_target="tpu_custom_call" | custom-call | tf_op jit(solution)/shard_map/factor/pallas_call | solution.py:372
  (6 shorter events, 0.0 us)
Async XLA Ops:
  0.6 1.4 %copy-start = (f32[2,192,8,128]{3,2,1,0:T(8,128)S(1)}, f32[2,192,8,128]{3,2,1,0:T(8,128)}, u32[]{:S(2)}) copy-start(f32[2,192,8,128]{3,2,1,0:T(8,128)} %param.3) | copy-start | bytes 4718596
  2.0 0.7 %copy-start.1 = (f32[8,128]{1,0:T(8,128)S(1)}, f32[8,128]{1,0:T(8,128)}, u32[]{:S(2)}) copy-start(f32[8,128]{1,0:T(8,128)} %self_hbm.1) | copy-start | bytes 12292
  2.7 0.7 %copy-start.2 = (f32[8,128]{1,0:T(8,128)S(1)}, f32[8,128]{1,0:T(8,128)}, u32[]{:S(2)}) copy-start(f32[8,128]{1,0:T(8,128)} %cross_hbm.1) | copy-start | bytes 12292
  5.4 1.5 %collective-permute-start.1 = (f32[200,128]{1,0:T(8,128)S(1)}, f32[200,128]{1,0:T(8,128)S(1)}, u32[]{:S(2)}, u32[]{:S(2)}) collective-permute-start(f32[200,128]{1,0:T(8,128)S(1)} %get-tuple-element.23), channel_id=1, source_target_pairs={{0,1},{2,3},{4,5},{6,7},{1,0},{3,2},{5,4},{7,6},{8,9},{10,11},{12,... | collective-permute-start | bytes 307208 | tf_op jit(solution)/shard_map/ppermute | solution.py:388
  5.9 2.3 %collective-permute-start = (f32[200,128]{1,0:T(8,128)S(1)}, f32[200,128]{1,0:T(8,128)S(1)}, u32[]{:S(2)}, u32[]{:S(2)}) collective-permute-start(f32[200,128]{1,0:T(8,128)S(1)} %get-tuple-element.22), channel_id=1, source_target_pairs={{1,2},{3,4},{5,6},{2,1},{4,3},{6,5},{9,10},{11,12},{13,14},{10,9},... | collective-permute-start | bytes 307208 | tf_op jit(solution)/shard_map/ppermute | solution.py:388
  8.2 19.7 %collective-permute-start.2 = (f32[7,200,128]{2,1,0:T(8,128)}, f32[7,200,128]{2,1,0:T(8,128)S(1)}, u32[]{:S(2)}, u32[]{:S(2)}) collective-permute-start(f32[7,200,128]{2,1,0:T(8,128)} %get-tuple-element.26), channel_id=1, source_target_pairs={{0,1},{2,3},{4,5},{6,7},{1,0},{3,2},{5,4},{7,6},{8,9},{10,11},{12,... | collective-permute-start | bytes 2150408 | tf_op jit(solution)/shard_map/ppermute | solution.py:388
  12.8 15.1 %collective-permute-start.3 = (f32[7,200,128]{2,1,0:T(8,128)}, f32[7,200,128]{2,1,0:T(8,128)S(1)}, u32[]{:S(2)}, u32[]{:S(2)}) collective-permute-start(f32[7,200,128]{2,1,0:T(8,128)} %get-tuple-element.27), channel_id=1, source_target_pairs={{1,2},{3,4},{5,6},{2,1},{4,3},{6,5},{9,10},{11,12},{13,14},{10,9},... | collective-permute-start | bytes 2150408 | tf_op jit(solution)/shard_map/ppermute | solution.py:388
  15.1 4.9 %collective-permute-start.4 = (f32[200,128]{1,0:T(8,128)}, f32[200,128]{1,0:T(8,128)S(1)}, u32[]{:S(2)}, u32[]{:S(2)}) collective-permute-start(f32[200,128]{1,0:T(8,128)} %get-tuple-element.32), channel_id=1, source_target_pairs={{0,8},{16,24},{8,0},{24,16},{1,9},{17,25},{9,1},{25,17},{2,10},{18... | collective-permute-start | bytes 307208 | tf_op jit(solution)/shard_map/ppermute | solution.py:388
  17.1 7.0 %collective-permute-start.5 = (f32[200,128]{1,0:T(8,128)}, f32[200,128]{1,0:T(8,128)}, u32[]{:S(2)}, u32[]{:S(2)}) collective-permute-start(f32[200,128]{1,0:T(8,128)} %get-tuple-element.33), channel_id=1, source_target_pairs={{8,16},{0,24},{16,8},{24,0},{9,17},{1,25},{17,9},{25,1},{10,18},{2... | collective-permute-start | bytes 307208 | tf_op jit(solution)/shard_map/ppermute | solution.py:388
  32.3 1.9 %collective-permute-start.6 = (f32[96,128]{1,0:T(8,128)S(1)}, f32[96,128]{1,0:T(8,128)S(1)}, u32[]{:S(2)}, u32[]{:S(2)}) collective-permute-start(f32[96,128]{1,0:T(8,128)S(1)} %slice_select_fusion), channel_id=1, source_target_pairs={{0,1},{1,0},{2,3},{3,2},{4,5},{5,4},{6,7},{7,6},{8,9},{9,8},{10,11... | collective-permute-start | bytes 147464 | tf_op jit(solution)/shard_map/ppermute | solution.py:393
  34.2 4.2 %collective-permute-start.7 = (f32[96,128]{1,0:T(8,128)S(1)}, f32[96,128]{1,0:T(8,128)S(1)}, u32[]{:S(2)}, u32[]{:S(2)}) collective-permute-start(f32[96,128]{1,0:T(8,128)S(1)} %select_add_fusion), channel_id=1, source_target_pairs={{0,8},{8,0},{16,24},{24,16},{1,9},{9,1},{17,25},{25,17},{2,10},{10... | collective-permute-start | bytes 147464 | tf_op jit(solution)/shard_map/ppermute | solution.py:393
  38.4 4.2 %collective-permute-start.8 = (f32[96,128]{1,0:T(8,128)S(1)}, f32[96,128]{1,0:T(8,128)S(1)}, u32[]{:S(2)}, u32[]{:S(2)}) collective-permute-start(f32[96,128]{1,0:T(8,128)S(1)} %add.21), channel_id=1, source_target_pairs={{0,16},{8,24},{16,0},{24,8},{1,17},{9,25},{17,1},{25,9},{2,18},{10... | collective-permute-start | bytes 147464 | tf_op jit(solution)/shard_map/ppermute | solution.py:393
  42.5 4.2 %collective-permute-start.9 = (f32[96,128]{1,0:T(8,128)S(1)}, f32[96,128]{1,0:T(8,128)S(1)}, u32[]{:S(2)}, u32[]{:S(2)}) collective-permute-start(f32[96,128]{1,0:T(8,128)S(1)} %add.22), channel_id=1, source_target_pairs={{0,2},{1,3},{2,0},{3,1},{4,6},{5,7},{6,4},{7,5},{8,10},{9,11},{10,... | collective-permute-start | bytes 147464 | tf_op jit(solution)/shard_map/ppermute | solution.py:393
  46.7 5.7 %collective-permute-start.10 = (f32[96,128]{1,0:T(8,128)S(1)}, f32[96,128]{1,0:T(8,128)S(1)}, u32[]{:S(2)}, u32[]{:S(2)}) collective-permute-start(f32[96,128]{1,0:T(8,128)S(1)} %add.23), channel_id=1, source_target_pairs={{0,4},{1,5},{2,6},{3,7},{4,0},{5,1},{6,2},{7,3},{8,12},{9,13},{10,... | collective-permute-start | bytes 147464 | tf_op jit(solution)/shard_map/ppermute | solution.py:393
  52.4 1.3 %collective-permute-start.11 = (f32[96,128]{1,0:T(8,128)S(1)}, f32[96,128]{1,0:T(8,128)S(1)}, u32[]{:S(2)}, u32[]{:S(2)}) collective-permute-start(f32[96,128]{1,0:T(8,128)S(1)} %add.24.own_ref), channel_id=1, source_target_pairs={{0,1},{1,0},{2,3},{3,2},{4,5},{5,4},{6,7},{7,6},{8,9},{9,8},{10,11... | collective-permute-start | bytes 147464 | tf_op jit(solution)/shard_map/ppermute | solution.py:393

commit v3 on v2

--- a/solution.py
+++ b/solution.py
@@ -13,11 +13,11 @@
 diffusion = 0.2
 slow_rate = 0.05
 HEIGHT_EDGE = 48
-HEIGHT_ROW = 48
 HEIGHT_STRIP = 96
 HEIGHT_EVOLVE = 48
 SIDE = 64
 VMEM_BYTES = 24 * 1024 * 1024
+EDGE_VMEM_BYTES = 52 * 1024 * 1024
 LANES = 128
 SUB = 8
 HI = lax.Precision.HIGHEST
@@ -88,9 +88,9 @@
     return out
 
 def factor_kernel(n, weight, own_ref, other_ref, loc_ref, out_ref, growth_ref):
-    odd = lax.axis_index("tile") % 2 == 1
+    high_half = parity()
     own, other = own_ref[...], other_ref[...]
-    total = unpack_blocks(jnp.concatenate([jnp.where(odd, other, own), jnp.where(odd, own, other)], axis=0), n)
+    total = unpack_blocks(jnp.concatenate([jnp.where(high_half, other, own), jnp.where(high_half, own, other)], axis=0), n)
     local = unpack_blocks(loc_ref[...], n)
     keep = (lax.broadcasted_iota(jnp.int32, (SIDE, SIDE), 0) <= lax.broadcasted_iota(jnp.int32, (SIDE, SIDE), 1))
     diag = (lax.broadcasted_iota(jnp.int32, (SIDE, SIDE), 0) == lax.broadcasted_iota(jnp.int32, (SIDE, SIDE), 1))
@@ -155,7 +155,7 @@
     return jnp.concatenate([x] * (height // SUB), axis=0)
 
 
-def edge_kernel(fields, height, tangents_hbm, self_hbm, cross_hbm, last_out, first_out, near, far, tangents, coeff_self, coeff_cross, sems):
+def edge_kernel(fields, height, tangents_hbm, self_hbm, cross_hbm, last_out, first_out, near, far, near_fast, far_fast, tangents, coeff_self, coeff_cross, sems):
     chunks = fields // height
     span = height * SUB
     loads = [
@@ -186,8 +186,14 @@
         half = cell % SUB < STEPS
         to_above = jnp.where(half, last, roll(first, STEPS * SUB))
         to_below = jnp.where(half, roll(last, -STEPS * SUB), first)
-        near[at, :] = pick(odd, to_above, to_below)
-        far[at, :] = pick(odd, to_below, to_above)
+        near[0, at, :] = pick(odd, to_above, to_below)
+        far[0, at, :] = pick(odd, to_below, to_above)
+        for f in range(2):
+            count = STEPS - f
+            for j in range(count):
+                top, bottom = rows[f][j], rows[f][SUB - count + j]
+                (near if f else near_fast)[j + f, at, :] = pick(odd, top, bottom)
+                (far if f else far_fast)[j + f, at, :] = pick(odd, bottom, top)
 
     for g, load in enumerate(loads):
         load.wait()
@@ -197,29 +203,11 @@
     send(pl.ds(fields, SUB), own_coeffs(coeff_self, coeff_cross))
 
 
-def row_kernel(fields, height, after, tangents, coeff_self, coeff_cross, near, far):
-    odd = lax.axis_index("tile") % 2 == 1
-
-    def send(at, rows):
-        for f in range(2):
-            count = STEPS - f
-            for j in range(count):
-                top, bottom = rows[f][j], rows[f][SUB - count + j]
-                near[f * STEPS + j, at, :] = pick(odd, top, bottom)
-                far[f * STEPS + j, at, :] = pick(odd, bottom, top)
-
-    @pl.loop(0, fields // height)
-    def _(g):
-        send(chunk(g, height), own_rows(tangents, g, height))
-
-    send(pl.ds(fields, SUB), own_coeffs(coeff_self, coeff_cross))
-
-
 def column_kernel(last, first, near, far, strips, near_out, far_out, outer):
     tile, tiles = lax.axis_index("tile"), lax.axis_size("tile")
     odd, at_top, at_bottom = tile % 2 == 1, tile == 0, tile == tiles - 1
     grp_odd = lax.axis_index("grp") % 2 == 1
-    one, two = near[...], far[...]
+    one, two = near[0], far[0]
     lane = lane_index(one)
     cell, low, inner = lane // SUB % SUB, lane < LANES // 2, lane % SUB < STEPS
     half = cell < STEPS
@@ -277,7 +265,7 @@
     return (1.0 - slow_rate) * slow + slow_rate * fast
 
 
-def strip_kernel(fields, height, strips, near, far, ends, halo):
+def gram_kernel(fields, height, cells, strips, near, far, gram, halo, ends):
     grp, grps = lax.axis_index("grp"), lax.axis_size("grp")
     grp_odd = grp % 2 == 1
     one, two = near[...], far[...]
@@ -317,8 +305,15 @@
         joined = [jnp.where(l % SUB < STEPS, s[1], s[0]) for s in (fast, slow)]
         ends[chunk(g, height), :] = jnp.where(l < LANES // 2, joined[0], roll(joined[1], LANES // 2))
 
-
-def extended_rows(own, near, far, at):
+    whole = dot_nt(cells[...], cells[...]) + dot_nt(ends[...], ends[...])
+    for index, (i, j) in enumerate(block_pairs(fields // SIDE)):
+        row, half = divmod(index, 2)
+        gram[row * SIDE:(row + 1) * SIDE, half * SIDE:(half + 1) * SIDE] = whole[
+            i * SIDE:(i + 1) * SIDE, j * SIDE:(j + 1) * SIDE
+        ]
+
+
+def extended_rows(own, near, far, near_fast, far_fast, at):
     tile, tiles = lax.axis_index("tile"), lax.axis_size("tile")
     odd, at_top, at_bottom = tile % 2 == 1, tile == 0, tile == tiles - 1
     out = []
@@ -326,15 +321,15 @@
         count = STEPS - f
         rows = dict(enumerate(own[f]))
         for j in range(count):
-            one, two = near[f * STEPS + j, at, :], far[f * STEPS + j, at, :]
+            one, two = ((near if f else near_fast)[j + f, at, :], (far if f else far_fast)[j + f, at, :])
             rows[j - count] = pick(at_top, own[f][count - 1 - j], pick(odd, one, two))
             rows[SUB + j] = pick(at_bottom, own[f][SUB - 1 - j], pick(odd, two, one))
         out.append(rows)
     return out
 
 
-def evolve_kernel(fields, height, tangents, coeff_self, coeff_cross, near, far, ends, gram, row_coeffs, cells):
-    coeff_rows = extended_rows(own_coeffs(coeff_self, coeff_cross), near, far, pl.ds(fields, SUB))
+def evolve_kernel(fields, height, tangents, coeff_self, coeff_cross, near, far, near_fast, far_fast, cells, row_coeffs):
+    coeff_rows = extended_rows(own_coeffs(coeff_self, coeff_cross), near, far, near_fast, far_fast, pl.ds(fields, SUB))
     for f in range(2):
         for r in range(1 - STEPS, SUB + STEPS - 1):
             row_coeffs[f, r + STEPS - 1, :, :] = coeff_rows[f][r] + (1.0 - 4.0 * diffusion) * (1 - f)
@@ -342,7 +337,7 @@
     @pl.loop(0, fields // height)
     def _(g):
         at = chunk(g, height)
-        fast, slow = extended_rows(own_rows(tangents, g, height), near, far, at)
+        fast, slow = extended_rows(own_rows(tangents, g, height), near, far, near_fast, far_fast, at)
         for step in range(1, STEPS + 1):
             margin = STEPS - step
             new_fast = {}
@@ -359,15 +354,8 @@
             for r in range(SUB):
                 cells[at, (f * SUB + r) * LANES:(f * SUB + r + 1) * LANES] = jnp.where(middle, rows[r], 0.0)
 
-    whole = dot_nt(cells[...], cells[...]) + dot_nt(ends[...], ends[...])
-    for index, (i, j) in enumerate(block_pairs(fields // SIDE)):
-        row, half = divmod(index, 2)
-        gram[row * SIDE:(row + 1) * SIDE, half * SIDE:(half + 1) * SIDE] = whole[
-            i * SIDE:(i + 1) * SIDE, j * SIDE:(j + 1) * SIDE
-        ]
-
-
-def local_call(body, name, out_shapes, scratch, *args, hbm=False):
+
+def local_call(body, name, out_shapes, scratch, *args, hbm=False, vmem=VMEM_BYTES):
     spec = pl.BlockSpec(memory_space=pltpu.VMEM)
     return pl.pallas_call(
         body,
@@ -375,7 +363,7 @@
         in_specs=[pl.BlockSpec(memory_space=pltpu.HBM) if hbm else spec] * len(args),
         out_specs=[spec] * len(out_shapes),
         scratch_shapes=[pltpu.VMEM(s, jnp.float32) if isinstance(s, tuple) else s for s in scratch],
-        compiler_params=pltpu.CompilerParams(vmem_limit_bytes=VMEM_BYTES),
+        compiler_params=pltpu.CompilerParams(vmem_limit_bytes=vmem),
         name=name,
     )(*args)
 
@@ -388,52 +376,60 @@
     return lax.ppermute(cells, axis, pairs + [(b, a) for a, b in pairs])
 
 
-def exchange(cells, axis, bit):
-    count = lax.axis_size(axis)
-    return lax.ppermute(cells, axis, [(i, i ^ bit) for i in range(count)])
+def exchange(cells, grp_bit, tile_bit):
+    grps, tiles = lax.axis_size("grp"), lax.axis_size("tile")
+    moves = [(g * tiles + t, (g ^ grp_bit) * tiles + (t ^ tile_bit)) for g in range(grps) for t in range(tiles)]
+    return lax.ppermute(cells, ("grp", "tile"), moves)
+
+
+def parity():
+    bits = lax.axis_index("grp") ^ lax.axis_index("tile")
+    shift = 1
+    while shift < max(lax.axis_size("grp"), lax.axis_size("tile")):
+        bits = bits ^ (bits >> shift)
+        shift *= 2
+    return (bits & 1) == 1
 
 
 def sum_blocks(packed):
     half = packed.shape[0] // 2
-    odd = lax.axis_index("tile") % 2 == 1
+    high_half = parity()
     low, high = packed[:half], packed[half:]
-    part = jnp.where(odd, high, low) + exchange(jnp.where(odd, low, high), "tile", 1)
-    for axis, first in (("grp", 1), ("tile", 2)):
-        bit = first
+    part = jnp.where(high_half, high, low) + exchange(jnp.where(high_half, low, high), 0, 1)
+    for axis in ("grp", "tile"):
+        bit = 1 if axis == "grp" else 2
         while bit < lax.axis_size(axis):
-            part = part + exchange(part, axis, bit)
+            part = part + (exchange(part, bit, 1) if axis == "grp" else exchange(part, 0, bit + 1))
             bit *= 2
-    return part, exchange(part, "tile", 1)
+    return part, exchange(part, 0, 1)
 
 
 def per_device(tangents, reaction_self, reaction_cross):
     fields = tangents.shape[1]
     padded = fields + SUB
     rows = tangents.reshape(2, fields * tangents.shape[2], tangents.shape[3])
-    message, strip = (2 * STEPS - 1, padded, LANES), (padded, LANES)
+    message, strip = (STEPS, padded, LANES), (padded, LANES)
     inputs = (rows, reaction_self, reaction_cross)
-    last, first, near_edges, far_edges, *inputs = local_call(
-        functools.partial(edge_kernel, fields, HEIGHT_EDGE), "edges", [strip] * 4 + [a.shape for a in inputs],
-        [pltpu.SemaphoreType.DMA((fields // HEIGHT_EDGE + 2,))], *inputs, hbm=True,
-    )
-    near_edges, far_edges = swap(near_edges, "tile", 0), swap(far_edges, "tile", 1)
-    near_rows, far_rows = local_call(
-        functools.partial(row_kernel, fields, HEIGHT_ROW), "rows", [message] * 2, [], near_edges, *inputs
-    )
-    far_edges, near_rows, far_rows = lax.optimization_barrier((far_edges, near_rows, far_rows))
-    near_rows, far_rows = swap(near_rows, "tile", 0), swap(far_rows, "tile", 1)
+    last, first, near, far, near_fast, far_fast = local_call(
+        functools.partial(edge_kernel, fields, HEIGHT_EDGE), "edges", [strip] * 2 + [message] * 4,
+        [a.shape for a in inputs] + [pltpu.SemaphoreType.DMA((fields // HEIGHT_EDGE + 2,))], *inputs,
+        hbm=True, vmem=EDGE_VMEM_BYTES,
+    )
+    near, far = swap(near, "tile", 0), swap(far, "tile", 1)
+    near_fast, far_fast = swap(near_fast, "tile", 0), swap(far_fast, "tile", 1)
     strips, near_cols, far_cols = local_call(
-        column_kernel, "columns", [(4,) + strip, strip, strip], [(2,) + strip], last, first, near_edges, far_edges
+        column_kernel, "columns", [(4,) + strip, strip, strip], [(2,) + strip], last, first, near, far
     )
     near_cols, far_cols = swap(near_cols, "grp", 0), swap(far_cols, "grp", 1, close=True)
-    (ends,) = local_call(
-        functools.partial(strip_kernel, fields, HEIGHT_STRIP), "strips", [(fields, LANES)], [(2,) + strip], strips, near_cols, far_cols
+    (cells,) = local_call(
+        functools.partial(evolve_kernel, fields, HEIGHT_EVOLVE), "evolve", [(fields, 2 * SUB * LANES)],
+        [(2, SUB + 2 * STEPS - 2, SUB, LANES)], *inputs, near, far, near_fast, far_fast,
     )
     side_blocks = fields // SIDE
     blocks = side_blocks * (side_blocks + 1) // 2
     (packed,) = local_call(
-        functools.partial(evolve_kernel, fields, HEIGHT_EVOLVE), "evolve", [((blocks + 1) // 2 * SIDE, 2 * SIDE)],
-        [(2, SUB + 2 * STEPS - 2, SUB, LANES), (fields, 2 * SUB * LANES)], *inputs, near_rows, far_rows, ends,
+        functools.partial(gram_kernel, fields, HEIGHT_STRIP), "gram", [((blocks + 1) // 2 * SIDE, 2 * SIDE)],
+        [(2,) + strip, (fields, LANES)], cells, strips, near_cols, far_cols,
     )
     block_total = lax.axis_size("grp") * lax.axis_size("tile")
     corrections, growth = factor_call(*sum_blocks(packed), packed, fields, math.sqrt(block_total))

time: 63.5 us -> 59.4 us (0.935)
  waiting for transfers between devices: 19.4 us -> 11.9 us
  starting transfers between devices: 17.7 us -> 22.6 us
  Pallas kernels: 22.7 us -> 21.7 us
    ppermute x6, starting transfers between devices: 7.66 us -> 13.7 us  [exchange(): return lax.ppermute(cells, ('grp', 'tile'), moves)]
    ppermute x6, waiting for transfers between devices: 5.77 us -> 1.24 us  [swap(): return lax.ppermute(cells, axis, pairs + [(b, a) for a, b in pairs])]
    ppermute x6, waiting for transfers between devices: 13.6 us -> 10.6 us  [exchange(): return lax.ppermute(cells, ('grp', 'tile'), moves)]
    ppermute x6, starting transfers between devices: 10 us -> 8.85 us  [swap(): return lax.ppermute(cells, axis, pairs + [(b, a) for a, b in pairs])]
    pallas_call x6 -> x5, Pallas kernels: 22.7 us -> 21.7 us  [local_call(): pl.pallas_call(body, out_shape=[jax.ShapeDtypeStruct(s, jnp.float32) for...]
    unnamed x6 -> x14, local copies, waits for them, and re-layouts: 2.77 us -> 2.27 us
  transfers between devices with their start and end apart: 12 -> 12, of which waited for: 9 -> 7; matrix products, arithmetic and copies ran while one was open for 0% -> 0% of each run, Pallas kernels for 11% -> 7%
where the time goes in v3:
time: 59.4 us; the launch traced here: 59.2 us
  starting transfers between devices  22.6 us (38%)
  Pallas kernels  21.7 us (37%)
  waiting for transfers between devices  11.9 us (20%)
  local copies, waits for them, and re-layouts  2.27 us (4%)
  between operations  0.75 us (1%)
    pallas_call x5, Pallas kernels, local_call(): pl.pallas_call(body, out_shape=[jax.ShapeDtypeStruct(s, jnp.float32) for...  21.7 us
    ppermute x6, starting transfers between devices, exchange(): return lax.ppermute(cells, ('grp', 'tile'), moves)  13.7 us
    ppermute x6, waiting for transfers between devices, exchange(): return lax.ppermute(cells, ('grp', 'tile'), moves)  10.6 us
    ppermute x6, starting transfers between devices, swap(): return lax.ppermute(cells, axis, pairs + [(b, a) for a, b in pairs])  8.85 us
    unnamed x14, local copies, waits for them, and re-layouts  2.27 us
    ppermute x6, waiting for transfers between devices, swap(): return lax.ppermute(cells, axis, pairs + [(b, a) for a, b in pairs])  1.24 us
  transfers between devices with their start and end apart: 12, of which 7 were waited for; matrix products, arithmetic and copies ran while one was open for 0% of the time, Pallas kernels for 7%

profile of v3, /device:TPU:0, one launch (start us, length us, event | category | flops | bytes accessed | tf_op | source)
XLA Modules:
  0.0 59.2 jit_solution(17042482889216948549)
XLA Ops:
  0.6 0.0 copy-start
  0.6 0.0 copy-start.3
  0.6 0.8 %copy-done.3 = f32[8,128]{1,0:T(8,128)S(1)} copy-done((f32[8,128]{1,0:T(8,128)S(1)}, f32[8,128]{1,0:T(8,128)}, u32[]{:S(2)}) %copy-start.3) | copy-done | bytes 4120
  1.4 0.0 copy-start.5
  1.4 0.7 %copy-done.5 = f32[8,128]{1,0:T(8,128)S(1)} copy-done((f32[8,128]{1,0:T(8,128)S(1)}, f32[8,128]{1,0:T(8,128)}, u32[]{:S(2)}) %copy-start.5) | copy-done | bytes 4120
  2.1 0.0 copy-start.4
  2.1 0.0 copy-start.6
  2.1 3.2 %edges.1 = (f32[200,128]{1,0:T(8,128)S(1)}, f32[200,128]{1,0:T(8,128)S(1)}, f32[4,200,128]{2,1,0:T(8,128)S(1)}, f32[4,200,128]{2,1,0:T(8,128)S(1)}, f32[4,200,128]{2,1,0:T(8,128)}, /*index=5*/f32[4,200,128]{2,1,0:T(8,128)}) custom-call(f32[2,1536,128]{2,1,0:T(8,128)} %bitcast.2, f32[8,128]{1,0:T(8,128)S(1)} %copy-done.3, f32[8,128]{1,0:T(8,128)S(1)} %copy-done.5), custom_call_target="tpu_custom_call" | custom-call | tf_op jit(solution)/shard_map/edges/pallas_call | solution.py:360
  5.4 0.5 collective-permute-start
  5.9 0.7 %collective-permute-start.1 = (f32[4,200,128]{2,1,0:T(8,128)S(1)}, f32[4,200,128]{2,1,0:T(8,128)S(1)}, u32[]{:S(2)}, u32[]{:S(2)}) collective-permute-start(f32[4,200,128]{2,1,0:T(8,128)S(1)} %get-tuple-element.14), channel_id=1, source_target_pairs={{1,2},{3,4},{5,6},{2,1},{4,3},{6,5},{9,10},{11,12},{13,14},{10,9},... | collective-permute-start | bytes 1228808 | tf_op jit(solution)/shard_map/ppermute | solution.py:376
  6.6 4.0 %collective-permute-start.2 = (f32[4,200,128]{2,1,0:T(8,128)}, f32[4,200,128]{2,1,0:T(8,128)S(1)}, u32[]{:S(2)}, u32[]{:S(2)}) collective-permute-start(f32[4,200,128]{2,1,0:T(8,128)} %get-tuple-element.15), channel_id=1, source_target_pairs={{0,1},{2,3},{4,5},{6,7},{1,0},{3,2},{5,4},{7,6},{8,9},{10,11},{12,... | collective-permute-start | bytes 1228808 | tf_op jit(solution)/shard_map/ppermute | solution.py:376
  10.6 0.7 %collective-permute-start.3 = (f32[4,200,128]{2,1,0:T(8,128)}, f32[4,200,128]{2,1,0:T(8,128)S(1)}, u32[]{:S(2)}, u32[]{:S(2)}) collective-permute-start(f32[4,200,128]{2,1,0:T(8,128)} %get-tuple-element.16), channel_id=1, source_target_pairs={{1,2},{3,4},{5,6},{2,1},{4,3},{6,5},{9,10},{11,12},{13,14},{10,9},... | collective-permute-start | bytes 1228808 | tf_op jit(solution)/shard_map/ppermute | solution.py:376
  11.2 0.0 collective-permute-done.near
  11.3 0.0 collective-permute-done.1.far
  11.3 1.5 %columns.1 = (f32[4,200,128]{2,1,0:T(8,128)S(1)}, f32[200,128]{1,0:T(8,128)}, f32[200,128]{1,0:T(8,128)S(1)}) custom-call(f32[200,128]{1,0:T(8,128)S(1)} %get-tuple-element.17.last, f32[200,128]{1,0:T(8,128)S(1)} %get-tuple-element.18.first, f32[4,200,128]{2,1,0:T(8,128)S(1)} %collective-permute-done.near, f32[4,200,128]{2,1,0:T(8,128)S(1)} %collective-permute-done.1.far), custom_call_target="tpu_custom_call" | custom-call | tf_op jit(solution)/shard_map/columns/pallas_call | solution.py:360
  12.8 0.0 copy-start.1
  12.8 0.8 %copy-done.1 = f32[4,200,128]{2,1,0:T(8,128)} copy-done((f32[4,200,128]{2,1,0:T(8,128)}, f32[4,200,128]{2,1,0:T(8,128)S(1)}, u32[]{:S(2)}) %copy-start.1) | copy-done | bytes 409624
  13.6 1.5 %collective-permute-start.4 = (f32[200,128]{1,0:T(8,128)}, f32[200,128]{1,0:T(8,128)S(1)}, u32[]{:S(2)}, u32[]{:S(2)}) collective-permute-start(f32[200,128]{1,0:T(8,128)} %get-tuple-element.20), channel_id=1, source_target_pairs={{0,8},{16,24},{8,0},{24,16},{1,9},{17,25},{9,1},{25,17},{2,10},{18... | collective-permute-start | bytes 307208 | tf_op jit(solution)/shard_map/ppermute | solution.py:376
  15.1 1.5 %collective-permute-start.5 = (f32[200,128]{1,0:T(8,128)S(1)}, f32[200,128]{1,0:T(8,128)S(1)}, u32[]{:S(2)}, u32[]{:S(2)}) collective-permute-start(f32[200,128]{1,0:T(8,128)S(1)} %get-tuple-element.21), channel_id=1, source_target_pairs={{8,16},{0,24},{16,8},{24,0},{9,17},{1,25},{17,9},{25,1},{10,18},{2... | collective-permute-start | bytes 307208 | tf_op jit(solution)/shard_map/ppermute | solution.py:376
  16.6 0.0 copy-start.2
  16.6 0.0 collective-permute-done.2.near_fast
  16.6 0.0 collective-permute-done.3.far_fast
  16.6 0.0 copy-done
  16.6 0.0 copy-done.4
  16.6 0.0 copy-done.6
  16.6 2.8 %evolve.1.cells = f32[192,2048]{1,0:T(8,128)S(1)} custom-call(f32[2,1536,128]{2,1,0:T(8,128)S(1)} %bitcast.3, f32[8,128]{1,0:T(8,128)S(1)} %copy-done.4, f32[8,128]{1,0:T(8,128)S(1)} %copy-done.6, f32[4,200,128]{2,1,0:T(8,128)S(1)} %collective-permute-done.near, f32[4,200,128]{2,1,0:T(8,128)S(1)} %collective-permute-done.1.far, ...), custom_call_target="tpu_custom_call" | custom-call | tf_op jit(solution)/shard_map/evolve/pallas_call | solution.py:360
  19.4 0.0 collective-permute-done.4.near
  19.4 1.2 %collective-permute-done.5.far = f32[200,128]{1,0:T(8,128)S(1)} collective-permute-done((f32[200,128]{1,0:T(8,128)S(1)}, f32[200,128]{1,0:T(8,128)S(1)}, u32[]{:S(2)}, u32[]{:S(2)}) %collective-permute-start.5) | collective-permute-done | bytes 102432 | tf_op jit(solution)/shard_map/ppermute | solution.py:376
  20.6 0.0 copy-done.2
  20.6 4.5 %gram.1.loc_ref = f32[192,128]{1,0:T(8,128)S(1)} custom-call(f32[192,2048]{1,0:T(8,128)S(1)} %evolve.1.cells, f32[4,200,128]{2,1,0:T(8,128)S(1)} %copy-done.2, f32[200,128]{1,0:T(8,128)S(1)} %collective-permute-done.4.near, f32[200,128]{1,0:T(8,128)S(1)} %collective-permute-done.5.far), custom_call_target="tpu_custom_call" | custom-call | tf_op jit(solution)/shard_map/gram/pallas_call | solution.py:360
  25.1 3.7 %collective-permute-start.6 = (f32[96,128]{1,0:T(8,128)S(1)}, f32[96,128]{1,0:T(8,128)S(1)}, u32[]{:S(2)}, u32[]{:S(2)}) collective-permute-start(f32[96,128]{1,0:T(8,128)S(1)} %slice_select_fusion), channel_id=1, source_target_pairs={{0,1},{1,0},{2,3},{3,2},{4,5},{5,4},{6,7},{7,6},{8,9},{9,8},{10,11... | collective-permute-start | bytes 147464 | tf_op jit(solution)/shard_map/ppermute | solution.py:382
  28.8 0.9 %collective-permute-done.6 = f32[96,128]{1,0:T(8,128)S(1)} collective-permute-done((f32[96,128]{1,0:T(8,128)S(1)}, f32[96,128]{1,0:T(8,128)S(1)}, u32[]{:S(2)}, u32[]{:S(2)}) %collective-permute-start.6) | collective-permute-done | bytes 49184 | tf_op jit(solution)/shard_map/ppermute | solution.py:382
  29.7 1.0 %collective-permute-start.7 = (f32[96,128]{1,0:T(8,128)S(1)}, f32[96,128]{1,0:T(8,128)S(1)}, u32[]{:S(2)}, u32[]{:S(2)}) collective-permute-start(f32[96,128]{1,0:T(8,128)S(1)} %select_add_fusion), channel_id=1, source_target_pairs={{0,9},{1,8},{2,11},{3,10},{4,13},{5,12},{6,15},{7,14},{8,1},{9,0},... | collective-permute-start | bytes 147464 | tf_op jit(solution)/shard_map/ppermute | solution.py:382
  30.7 2.6 %collective-permute-done.7 = f32[96,128]{1,0:T(8,128)S(1)} collective-permute-done((f32[96,128]{1,0:T(8,128)S(1)}, f32[96,128]{1,0:T(8,128)S(1)}, u32[]{:S(2)}, u32[]{:S(2)}) %collective-permute-start.7) | collective-permute-done | bytes 49184 | tf_op jit(solution)/shard_map/ppermute | solution.py:382
  33.3 0.9 %collective-permute-start.8 = (f32[96,128]{1,0:T(8,128)S(1)}, f32[96,128]{1,0:T(8,128)S(1)}, u32[]{:S(2)}, u32[]{:S(2)}) collective-permute-start(f32[96,128]{1,0:T(8,128)S(1)} %add.16), channel_id=1, source_target_pairs={{0,17},{1,16},{2,19},{3,18},{4,21},{5,20},{6,23},{7,22},{8,25},{9,... | collective-permute-start | bytes 147464 | tf_op jit(solution)/shard_map/ppermute | solution.py:382
  34.2 2.7 %collective-permute-done.8 = f32[96,128]{1,0:T(8,128)S(1)} collective-permute-done((f32[96,128]{1,0:T(8,128)S(1)}, f32[96,128]{1,0:T(8,128)S(1)}, u32[]{:S(2)}, u32[]{:S(2)}) %collective-permute-start.8) | collective-permute-done | bytes 49184 | tf_op jit(solution)/shard_map/ppermute | solution.py:382
  36.9 4.8 %collective-permute-start.9 = (f32[96,128]{1,0:T(8,128)S(1)}, f32[96,128]{1,0:T(8,128)S(1)}, u32[]{:S(2)}, u32[]{:S(2)}) collective-permute-start(f32[96,128]{1,0:T(8,128)S(1)} %add.17), channel_id=1, source_target_pairs={{0,3},{1,2},{2,1},{3,0},{4,7},{5,6},{6,5},{7,4},{8,11},{9,10},{10,... | collective-permute-start | bytes 147464 | tf_op jit(solution)/shard_map/ppermute | solution.py:382
  41.7 1.8 %collective-permute-done.9 = f32[96,128]{1,0:T(8,128)S(1)} collective-permute-done((f32[96,128]{1,0:T(8,128)S(1)}, f32[96,128]{1,0:T(8,128)S(1)}, u32[]{:S(2)}, u32[]{:S(2)}) %collective-permute-start.9) | collective-permute-done | bytes 49184 | tf_op jit(solution)/shard_map/ppermute | solution.py:382
  43.5 3.0 %collective-permute-start.10 = (f32[96,128]{1,0:T(8,128)S(1)}, f32[96,128]{1,0:T(8,128)S(1)}, u32[]{:S(2)}, u32[]{:S(2)}) collective-permute-start(f32[96,128]{1,0:T(8,128)S(1)} %add.18), channel_id=1, source_target_pairs={{0,5},{1,4},{2,7},{3,6},{4,1},{5,0},{6,3},{7,2},{8,13},{9,12},{10,... | collective-permute-start | bytes 147464 | tf_op jit(solution)/shard_map/ppermute | solution.py:382
  46.4 1.8 %collective-permute-done.10 = f32[96,128]{1,0:T(8,128)S(1)} collective-permute-done((f32[96,128]{1,0:T(8,128)S(1)}, f32[96,128]{1,0:T(8,128)S(1)}, u32[]{:S(2)}, u32[]{:S(2)}) %collective-permute-start.10) | collective-permute-done | bytes 49184 | tf_op jit(solution)/shard_map/ppermute | solution.py:382
  48.2 0.4 collective-permute-start.11
  48.6 0.9 %collective-permute-done.11.other_ref = f32[96,128]{1,0:T(8,128)S(1)} collective-permute-done((f32[96,128]{1,0:T(8,128)S(1)}, f32[96,128]{1,0:T(8,128)S(1)}, u32[]{:S(2)}, u32[]{:S(2)}) %collective-permute-start.11) | collective-permute-done | bytes 49184 | tf_op jit(solution)/shard_map/ppermute | solution.py:382
  49.5 9.6 %factor.1 = (f32[192,192]{1,0:T(8,128)}, f32[1,192]{1,0:T(1,128)}) custom-call(f32[96,128]{1,0:T(8,128)S(1)} %add.19.own_ref, f32[96,128]{1,0:T(8,128)S(1)} %collective-permute-done.11.other_ref, f32[192,128]{1,0:T(8,128)S(1)} %gram.1.loc_ref), custom_call_target="tpu_custom_call" | custom-call | tf_op jit(solution)/shard_map/factor/pallas_call | solution.py:360
  (6 shorter events, 0.0 us)
Async XLA Ops:
  0.6 15.9 %copy-start = (f32[2,192,8,128]{3,2,1,0:T(8,128)S(1)}, f32[2,192,8,128]{3,2,1,0:T(8,128)}, u32[]{:S(2)}) copy-start(f32[2,192,8,128]{3,2,1,0:T(8,128)} %param.3) | copy-start | bytes 4718596
  0.6 0.8 %copy-start.3 = (f32[8,128]{1,0:T(8,128)S(1)}, f32[8,128]{1,0:T(8,128)}, u32[]{:S(2)}) copy-start(f32[8,128]{1,0:T(8,128)} %coeff_self.1) | copy-start | bytes 12292
  1.4 0.7 %copy-start.5 = (f32[8,128]{1,0:T(8,128)S(1)}, f32[8,128]{1,0:T(8,128)}, u32[]{:S(2)}) copy-start(f32[8,128]{1,0:T(8,128)} %coeff_cross.1) | copy-start | bytes 12292
  2.1 14.5 %copy-start.4 = (f32[8,128]{1,0:T(8,128)S(1)}, f32[8,128]{1,0:T(8,128)}, u32[]{:S(2)}) copy-start(f32[8,128]{1,0:T(8,128)} %coeff_self.1) | copy-start | bytes 12292
  2.1 14.5 %copy-start.6 = (f32[8,128]{1,0:T(8,128)S(1)}, f32[8,128]{1,0:T(8,128)}, u32[]{:S(2)}) copy-start(f32[8,128]{1,0:T(8,128)} %coeff_cross.1) | copy-start | bytes 12292
  5.4 5.9 %collective-permute-start = (f32[4,200,128]{2,1,0:T(8,128)S(1)}, f32[4,200,128]{2,1,0:T(8,128)S(1)}, u32[]{:S(2)}, u32[]{:S(2)}) collective-permute-start(f32[4,200,128]{2,1,0:T(8,128)S(1)} %get-tuple-element.13), channel_id=1, source_target_pairs={{0,1},{2,3},{4,5},{6,7},{1,0},{3,2},{5,4},{7,6},{8,9},{10,11},{12,... | collective-permute-start | bytes 1228808 | tf_op jit(solution)/shard_map/ppermute | solution.py:376
  5.9 5.4 %collective-permute-start.1 = (f32[4,200,128]{2,1,0:T(8,128)S(1)}, f32[4,200,128]{2,1,0:T(8,128)S(1)}, u32[]{:S(2)}, u32[]{:S(2)}) collective-permute-start(f32[4,200,128]{2,1,0:T(8,128)S(1)} %get-tuple-element.14), channel_id=1, source_target_pairs={{1,2},{3,4},{5,6},{2,1},{4,3},{6,5},{9,10},{11,12},{13,14},{10,9},... | collective-permute-start | bytes 1228808 | tf_op jit(solution)/shard_map/ppermute | solution.py:376
  6.6 10.0 %collective-permute-start.2 = (f32[4,200,128]{2,1,0:T(8,128)}, f32[4,200,128]{2,1,0:T(8,128)S(1)}, u32[]{:S(2)}, u32[]{:S(2)}) collective-permute-start(f32[4,200,128]{2,1,0:T(8,128)} %get-tuple-element.15), channel_id=1, source_target_pairs={{0,1},{2,3},{4,5},{6,7},{1,0},{3,2},{5,4},{7,6},{8,9},{10,11},{12,... | collective-permute-start | bytes 1228808 | tf_op jit(solution)/shard_map/ppermute | solution.py:376
  10.6 6.0 %collective-permute-start.3 = (f32[4,200,128]{2,1,0:T(8,128)}, f32[4,200,128]{2,1,0:T(8,128)S(1)}, u32[]{:S(2)}, u32[]{:S(2)}) collective-permute-start(f32[4,200,128]{2,1,0:T(8,128)} %get-tuple-element.16), channel_id=1, source_target_pairs={{1,2},{3,4},{5,6},{2,1},{4,3},{6,5},{9,10},{11,12},{13,14},{10,9},... | collective-permute-start | bytes 1228808 | tf_op jit(solution)/shard_map/ppermute | solution.py:376
  12.8 0.8 %copy-start.1 = (f32[4,200,128]{2,1,0:T(8,128)}, f32[4,200,128]{2,1,0:T(8,128)S(1)}, u32[]{:S(2)}) copy-start(f32[4,200,128]{2,1,0:T(8,128)S(1)} %get-tuple-element.19.strips) | copy-start | bytes 1228804
  13.6 5.8 %collective-permute-start.4 = (f32[200,128]{1,0:T(8,128)}, f32[200,128]{1,0:T(8,128)S(1)}, u32[]{:S(2)}, u32[]{:S(2)}) collective-permute-start(f32[200,128]{1,0:T(8,128)} %get-tuple-element.20), channel_id=1, source_target_pairs={{0,8},{16,24},{8,0},{24,16},{1,9},{17,25},{9,1},{25,17},{2,10},{18... | collective-permute-start | bytes 307208 | tf_op jit(solution)/shard_map/ppermute | solution.py:376
  15.1 5.6 %collective-permute-start.5 = (f32[200,128]{1,0:T(8,128)S(1)}, f32[200,128]{1,0:T(8,128)S(1)}, u32[]{:S(2)}, u32[]{:S(2)}) collective-permute-start(f32[200,128]{1,0:T(8,128)S(1)} %get-tuple-element.21), channel_id=1, source_target_pairs={{8,16},{0,24},{16,8},{24,0},{9,17},{1,25},{17,9},{25,1},{10,18},{2... | collective-permute-start | bytes 307208 | tf_op jit(solution)/shard_map/ppermute | solution.py:376
  16.6 4.1 %copy-start.2 = (f32[4,200,128]{2,1,0:T(8,128)S(1)}, f32[4,200,128]{2,1,0:T(8,128)}, u32[]{:S(2)}) copy-start(f32[4,200,128]{2,1,0:T(8,128)} %copy-done.1) | copy-start | bytes 1228804
  25.1 4.5 %collective-permute-start.6 = (f32[96,128]{1,0:T(8,128)S(1)}, f32[96,128]{1,0:T(8,128)S(1)}, u32[]{:S(2)}, u32[]{:S(2)}) collective-permute-start(f32[96,128]{1,0:T(8,128)S(1)} %slice_select_fusion), channel_id=1, source_target_pairs={{0,1},{1,0},{2,3},{3,2},{4,5},{5,4},{6,7},{7,6},{8,9},{9,8},{10,11... | collective-permute-start | bytes 147464 | tf_op jit(solution)/shard_map/ppermute | solution.py:382
  29.7 3.6 %collective-permute-start.7 = (f32[96,128]{1,0:T(8,128)S(1)}, f32[96,128]{1,0:T(8,128)S(1)}, u32[]{:S(2)}, u32[]{:S(2)}) collective-permute-start(f32[96,128]{1,0:T(8,128)S(1)} %select_add_fusion), channel_id=1, source_target_pairs={{0,9},{1,8},{2,11},{3,10},{4,13},{5,12},{6,15},{7,14},{8,1},{9,0},... | collective-permute-start | bytes 147464 | tf_op jit(solution)/shard_map/ppermute | solution.py:382
  33.3 3.6 %collective-permute-start.8 = (f32[96,128]{1,0:T(8,128)S(1)}, f32[96,128]{1,0:T(8,128)S(1)}, u32[]{:S(2)}, u32[]{:S(2)}) collective-permute-start(f32[96,128]{1,0:T(8,128)S(1)} %add.16), channel_id=1, source_target_pairs={{0,17},{1,16},{2,19},{3,18},{4,21},{5,20},{6,23},{7,22},{8,25},{9,... | collective-permute-start | bytes 147464 | tf_op jit(solution)/shard_map/ppermute | solution.py:382
  36.9 6.6 %collective-permute-start.9 = (f32[96,128]{1,0:T(8,128)S(1)}, f32[96,128]{1,0:T(8,128)S(1)}, u32[]{:S(2)}, u32[]{:S(2)}) collective-permute-start(f32[96,128]{1,0:T(8,128)S(1)} %add.17), channel_id=1, source_target_pairs={{0,3},{1,2},{2,1},{3,0},{4,7},{5,6},{6,5},{7,4},{8,11},{9,10},{10,... | collective-permute-start | bytes 147464 | tf_op jit(solution)/shard_map/ppermute | solution.py:382
  43.5 4.8 %collective-permute-start.10 = (f32[96,128]{1,0:T(8,128)S(1)}, f32[96,128]{1,0:T(8,128)S(1)}, u32[]{:S(2)}, u32[]{:S(2)}) collective-permute-start(f32[96,128]{1,0:T(8,128)S(1)} %add.18), channel_id=1, source_target_pairs={{0,5},{1,4},{2,7},{3,6},{4,1},{5,0},{6,3},{7,2},{8,13},{9,12},{10,... | collective-permute-start | bytes 147464 | tf_op jit(solution)/shard_map/ppermute | solution.py:382
  48.2 1.3 %collective-permute-start.11 = (f32[96,128]{1,0:T(8,128)S(1)}, f32[96,128]{1,0:T(8,128)S(1)}, u32[]{:S(2)}, u32[]{:S(2)}) collective-permute-start(f32[96,128]{1,0:T(8,128)S(1)} %add.19.own_ref), channel_id=1, source_target_pairs={{0,1},{1,0},{2,3},{3,2},{4,5},{5,4},{6,7},{7,6},{8,9},{9,8},{10,11... | collective-permute-start | bytes 147464 | tf_op jit(solution)/shard_map/ppermute | solution.py:382

commit v4 on v3

--- a/solution.py
+++ b/solution.py
@@ -12,8 +12,8 @@
 STEPS = 4
 diffusion = 0.2
 slow_rate = 0.05
-HEIGHT_EDGE = 48
-HEIGHT_STRIP = 96
+HEIGHT_EDGE = 96
+HEIGHT_STRIP = 192
 HEIGHT_EVOLVE = 48
 SIDE = 64
 VMEM_BYTES = 24 * 1024 * 1024
@@ -76,11 +76,20 @@
             for c in range(1, SUB):
                 panel = jnp.where(sub == c, scaled[c], panel)
             done[s].append(panel)
-            for g in range(p + 1, groups):
+            if p + 1 == groups:
+                continue
+            near = [cols[p + 1, c] for c in range(SUB)]
+            for c in range(SUB):
+                for a in range(c + 1, SUB):
+                    near[a] = near[a] - mult[a, c] * near[c]
+                v[p + 1] = v[p + 1] - (near[c] * scale[c]) * scaled[c]
+            whole = [scaled[c] * scale[c] for c in range(SUB)]
+            for c in reversed(range(SUB)):
+                for a in range(c):
+                    whole[a] = whole[a] - mult[c, a] * whole[c]
+            for g in range(p + 2, groups):
                 for c in range(SUB):
-                    for a in range(c + 1, SUB):
-                        cols[g, a] = cols[g, a] - mult[a, c] * cols[g, c]
-                    v[g] = v[g] - (cols[g, c] * scale[c]) * scaled[c]
+                    v[g] = v[g] - cols[g, c] * whole[c]
     out = []
     for panels in done:
         whole = jnp.concatenate(panels, axis=0)
@@ -94,31 +103,30 @@
     local = unpack_blocks(loc_ref[...], n)
     keep = (lax.broadcasted_iota(jnp.int32, (SIDE, SIDE), 0) <= lax.broadcasted_iota(jnp.int32, (SIDE, SIDE), 1))
     diag = (lax.broadcasted_iota(jnp.int32, (SIDE, SIDE), 0) == lax.broadcasted_iota(jnp.int32, (SIDE, SIDE), 1))
-    inverse = {}
-    answer = {}
+    rest = {j: [] for j in range(n)}
     for k in range(n):
         (r_t, i_t), (r_l, i_l) = factor_blocks([total[k, k], local[k, k]])
-        inverse[k] = i_t
-        local[k, k] = jnp.where(keep, r_l, 0.0)
         growth_ref[0, k*SIDE:(k+1)*SIDE] = jnp.log(jnp.sum(jnp.where(diag, r_t, 0.0), axis=0))
+        panels = []
         for grams, inv in ((total, i_t), (local, i_l)):
             if k + 1 < n:
                 row = dot_nn(inv, jnp.concatenate([grams[k, j] for j in range(k + 1, n)], axis=1))
-                for j in range(k + 1, n):
-                    grams[k, j] = row[:, (j-k-1)*SIDE:(j-k)*SIDE]
                 for i in range(k + 1, n):
-                    rest = dot_tn(grams[k, i], row[:, (i-k-1)*SIDE:])
+                    less = dot_tn(row[:, (i-k-1)*SIDE:(i-k)*SIDE], row[:, (i-k-1)*SIDE:])
                     for j in range(i, n):
-                        grams[i, j] = grams[i, j] - rest[:, (j-i)*SIDE:(j-i+1)*SIDE]
-    for j in range(n):
-        for i in range(j + 1):
-            rest = local[i, j]
-            for m in range(i, j):
-                rest = rest - dot_nn(answer[i, m], total[m, j])
-            answer[i, j] = dot_nt(rest, inverse[j])
-            out_ref[i*SIDE:(i+1)*SIDE, j*SIDE:(j+1)*SIDE] = weight * answer[i, j]
-        for i in range(j + 1, n):
-            out_ref[i*SIDE:(i+1)*SIDE, j*SIDE:(j+1)*SIDE] = jnp.zeros((SIDE, SIDE), jnp.float32)
+                        grams[i, j] = grams[i, j] - less[:, (j-i)*SIDE:(j-i+1)*SIDE]
+                panels.append(row)
+        rest[k].append(jnp.where(keep, r_l, 0.0))
+        answer = dot_nt(jnp.concatenate(rest[k], axis=0), i_t)
+        out_ref[:(k+1)*SIDE, k*SIDE:(k+1)*SIDE] = weight * answer
+        if k + 1 < n:
+            out_ref[(k+1)*SIDE:, k*SIDE:(k+1)*SIDE] = jnp.zeros(((n-k-1)*SIDE, SIDE), jnp.float32)
+            less = dot_nn(answer, panels[0])
+            for j in range(k + 1, n):
+                at = (j-k-1)*SIDE
+                rest[j].append(panels[1][:, at:at+SIDE])
+                rest[j] = [part - less[i*SIDE:(i+1)*SIDE, at:at+SIDE] for i, part in enumerate(rest[j])]
+
 
 def factor_call(own, other, local, k, weight):
     out, growth = local_call(
@@ -239,15 +247,13 @@
     far_out[...] = pick(grp_odd, to_right, to_left)
 
 
-def strip_neighbours(last, first, halo):
+def strip_neighbours(last, first, halo, wanted):
     c = lane_index(last) % SUB
     end, begin = c == SUB - 1, c == 0
     out = []
-    for x, after, before in (
-        (last, roll(halo, 7), None),
-        (first, None, roll(halo, -7)),
-        (halo, roll(first, 7), roll(last, -7)),
-    ):
+    sides = (lambda: (last, roll(halo, 7), None), lambda: (first, None, roll(halo, -7)), lambda: (halo, roll(first, 7), roll(last, -7)))
+    for side in sides[:wanted]:
+        x, after, before = side()
         right, left = roll(x, -1), roll(x, 1)
         if after is not None:
             right = jnp.where(end, after, right)
@@ -265,7 +271,7 @@
     return (1.0 - slow_rate) * slow + slow_rate * fast
 
 
-def gram_kernel(fields, height, cells, strips, near, far, gram, halo, ends):
+def gram_kernel(fields, height, middle_gram, strips, near, far, gram, halo, ends):
     grp, grps = lax.axis_index("grp"), lax.axis_size("grp")
     grp_odd = grp % 2 == 1
     one, two = near[...], far[...]
@@ -297,15 +303,16 @@
     def _(g):
         fast, slow = parts(0, chunk(g, height)), parts(1, chunk(g, height))
         for step in range(STEPS):
-            around = strip_neighbours(*fast)
-            moved = [advance(fast[p], slow[p], around[p], gains[p], crosses[p]) for p in range(3)]
-            slow = [relax(a, b) for a, b in zip(fast, slow)]
+            wanted = 3 if step + 1 < STEPS else 2
+            around = strip_neighbours(*fast, wanted)
+            moved = [advance(fast[p], slow[p], around[p], gains[p], crosses[p]) for p in range(wanted)]
+            slow = [relax(fast[p], slow[p]) for p in range(wanted)]
             fast = moved
         l = lane_index(fast[0])
         joined = [jnp.where(l % SUB < STEPS, s[1], s[0]) for s in (fast, slow)]
         ends[chunk(g, height), :] = jnp.where(l < LANES // 2, joined[0], roll(joined[1], LANES // 2))
 
-    whole = dot_nt(cells[...], cells[...]) + dot_nt(ends[...], ends[...])
+    whole = middle_gram[...] + dot_nt(ends[...], ends[...])
     for index, (i, j) in enumerate(block_pairs(fields // SIDE)):
         row, half = divmod(index, 2)
         gram[row * SIDE:(row + 1) * SIDE, half * SIDE:(half + 1) * SIDE] = whole[
@@ -328,7 +335,7 @@
     return out
 
 
-def evolve_kernel(fields, height, tangents, coeff_self, coeff_cross, near, far, near_fast, far_fast, cells, row_coeffs):
+def evolve_kernel(fields, height, tangents, coeff_self, coeff_cross, near, far, near_fast, far_fast, middle_gram, row_coeffs, cells):
     coeff_rows = extended_rows(own_coeffs(coeff_self, coeff_cross), near, far, near_fast, far_fast, pl.ds(fields, SUB))
     for f in range(2):
         for r in range(1 - STEPS, SUB + STEPS - 1):
@@ -354,6 +361,8 @@
             for r in range(SUB):
                 cells[at, (f * SUB + r) * LANES:(f * SUB + r + 1) * LANES] = jnp.where(middle, rows[r], 0.0)
 
+    middle_gram[...] = dot_nt(cells[...], cells[...])
+
 
 def local_call(body, name, out_shapes, scratch, *args, hbm=False, vmem=VMEM_BYTES):
     spec = pl.BlockSpec(memory_space=pltpu.VMEM)
@@ -420,16 +429,17 @@
     strips, near_cols, far_cols = local_call(
         column_kernel, "columns", [(4,) + strip, strip, strip], [(2,) + strip], last, first, near, far
     )
-    near_cols, far_cols = swap(near_cols, "grp", 0), swap(far_cols, "grp", 1, close=True)
-    (cells,) = local_call(
-        functools.partial(evolve_kernel, fields, HEIGHT_EVOLVE), "evolve", [(fields, 2 * SUB * LANES)],
-        [(2, SUB + 2 * STEPS - 2, SUB, LANES)], *inputs, near, far, near_fast, far_fast,
+    far_cols = swap(far_cols, "grp", 1, close=True)
+    near_cols = swap(near_cols, "grp", 0)
+    (middle_gram,) = local_call(
+        functools.partial(evolve_kernel, fields, HEIGHT_EVOLVE), "evolve", [(fields, fields)],
+        [(2, SUB + 2 * STEPS - 2, SUB, LANES), (fields, 2 * SUB * LANES)], *inputs, near, far, near_fast, far_fast,
     )
     side_blocks = fields // SIDE
     blocks = side_blocks * (side_blocks + 1) // 2
     (packed,) = local_call(
         functools.partial(gram_kernel, fields, HEIGHT_STRIP), "gram", [((blocks + 1) // 2 * SIDE, 2 * SIDE)],
-        [(2,) + strip, (fields, LANES)], cells, strips, near_cols, far_cols,
+        [(2,) + strip, (fields, LANES)], middle_gram, strips, near_cols, far_cols,
     )
     block_total = lax.axis_size("grp") * lax.axis_size("tile")
     corrections, growth = factor_call(*sum_blocks(packed), packed, fields, math.sqrt(block_total))

time: 59.4 us -> 56.3 us (0.948)
  waiting for transfers between devices: 11.9 us -> 9.86 us
  local copies, waits for them, and re-layouts: 2.27 us -> 1.5 us
    ppermute x6, waiting for transfers between devices: 1.24 us -> 0.02 us  [swap(): return lax.ppermute(cells, axis, pairs + [(b, a) for a, b in pairs])]
    ppermute x6, starting transfers between devices: 13.7 us -> 12.6 us  [exchange(): return lax.ppermute(cells, ('grp', 'tile'), moves)]
    ppermute x6, waiting for transfers between devices: 10.6 us -> 9.84 us  [exchange(): return lax.ppermute(cells, ('grp', 'tile'), moves)]
    unnamed x14 -> x10, local copies, waits for them, and re-layouts: 2.27 us -> 1.5 us
    ppermute x6, starting transfers between devices: 8.85 us -> 9.6 us  [swap(): return lax.ppermute(cells, axis, pairs + [(b, a) for a, b in pairs])]
  transfers between devices with their start and end apart: 12 -> 12, of which waited for: 7 -> 6; matrix products, arithmetic and copies ran while one was open for 0% -> 0% of each run, Pallas kernels for 7% -> 12%
where the time goes in v4:
time: 56.3 us; the launch traced here: 55.9 us
  starting transfers between devices  22.2 us (39%)
  Pallas kernels  21.7 us (39%)
  waiting for transfers between devices  9.86 us (18%)
  local copies, waits for them, and re-layouts  1.5 us (3%)
  between operations  0.73 us (1%)
    pallas_call x5, Pallas kernels, local_call(): pl.pallas_call(body, out_shape=[jax.ShapeDtypeStruct(s, jnp.float32) for...  21.7 us
    ppermute x6, starting transfers between devices, exchange(): return lax.ppermute(cells, ('grp', 'tile'), moves)  12.6 us
    ppermute x6, waiting for transfers between devices, exchange(): return lax.ppermute(cells, ('grp', 'tile'), moves)  9.84 us
    ppermute x6, starting transfers between devices, swap(): return lax.ppermute(cells, axis, pairs + [(b, a) for a, b in pairs])  9.6 us
    unnamed x10, local copies, waits for them, and re-layouts  1.5 us
  transfers between devices with their start and end apart: 12, of which 6 were waited for; matrix products, arithmetic and copies ran while one was open for 0% of the time, Pallas kernels for 12%

profile of v4, /device:TPU:0, one launch (start us, length us, event | category | flops | bytes accessed | tf_op | source)
XLA Modules:
  0.0 55.9 jit_solution(17753455385084512253)
XLA Ops:
  0.6 0.0 copy-start
  0.6 0.0 copy-start.1
  0.6 0.8 %copy-done.1 = f32[8,128]{1,0:T(8,128)S(1)} copy-done((f32[8,128]{1,0:T(8,128)S(1)}, f32[8,128]{1,0:T(8,128)}, u32[]{:S(2)}) %copy-start.1) | copy-done | bytes 4120
  1.4 0.0 copy-start.3
  1.4 0.7 %copy-done.3 = f32[8,128]{1,0:T(8,128)S(1)} copy-done((f32[8,128]{1,0:T(8,128)S(1)}, f32[8,128]{1,0:T(8,128)}, u32[]{:S(2)}) %copy-start.3) | copy-done | bytes 4120
  2.1 0.0 copy-start.2
  2.1 0.0 copy-start.4
  2.1 2.9 %edges.1 = (f32[200,128]{1,0:T(8,128)S(1)}, f32[200,128]{1,0:T(8,128)S(1)}, f32[4,200,128]{2,1,0:T(8,128)S(1)}, f32[4,200,128]{2,1,0:T(8,128)S(1)}, f32[4,200,128]{2,1,0:T(8,128)}, /*index=5*/f32[4,200,128]{2,1,0:T(8,128)}) custom-call(f32[2,1536,128]{2,1,0:T(8,128)} %bitcast.2, f32[8,128]{1,0:T(8,128)S(1)} %copy-done.1, f32[8,128]{1,0:T(8,128)S(1)} %copy-done.3), custom_call_target="tpu_custom_call" | custom-call | tf_op jit(solution)/shard_map/edges/pallas_call | solution.py:369
  5.1 0.5 collective-permute-start
  5.6 0.7 %collective-permute-start.1 = (f32[4,200,128]{2,1,0:T(8,128)S(1)}, f32[4,200,128]{2,1,0:T(8,128)S(1)}, u32[]{:S(2)}, u32[]{:S(2)}) collective-permute-start(f32[4,200,128]{2,1,0:T(8,128)S(1)} %get-tuple-element.14), channel_id=1, source_target_pairs={{1,2},{3,4},{5,6},{2,1},{4,3},{6,5},{9,10},{11,12},{13,14},{10,9},... | collective-permute-start | bytes 1228808 | tf_op jit(solution)/shard_map/ppermute | solution.py:385
  6.3 4.0 %collective-permute-start.2 = (f32[4,200,128]{2,1,0:T(8,128)}, f32[4,200,128]{2,1,0:T(8,128)S(1)}, u32[]{:S(2)}, u32[]{:S(2)}) collective-permute-start(f32[4,200,128]{2,1,0:T(8,128)} %get-tuple-element.15), channel_id=1, source_target_pairs={{0,1},{2,3},{4,5},{6,7},{1,0},{3,2},{5,4},{7,6},{8,9},{10,11},{12,... | collective-permute-start | bytes 1228808 | tf_op jit(solution)/shard_map/ppermute | solution.py:385
  10.3 1.4 %collective-permute-start.3 = (f32[4,200,128]{2,1,0:T(8,128)}, f32[4,200,128]{2,1,0:T(8,128)}, u32[]{:S(2)}, u32[]{:S(2)}) collective-permute-start(f32[4,200,128]{2,1,0:T(8,128)} %get-tuple-element.16), channel_id=1, source_target_pairs={{1,2},{3,4},{5,6},{2,1},{4,3},{6,5},{9,10},{11,12},{13,14},{10,9},... | collective-permute-start | bytes 1228808 | tf_op jit(solution)/shard_map/ppermute | solution.py:385
  11.7 0.0 collective-permute-done.near
  11.7 0.0 collective-permute-done.1.far
  11.7 1.5 %columns.1 = (f32[4,200,128]{2,1,0:T(8,128)S(1)}, f32[200,128]{1,0:T(8,128)}, f32[200,128]{1,0:T(8,128)S(1)}) custom-call(f32[200,128]{1,0:T(8,128)S(1)} %get-tuple-element.17.last, f32[200,128]{1,0:T(8,128)S(1)} %get-tuple-element.18.first, f32[4,200,128]{2,1,0:T(8,128)S(1)} %collective-permute-done.near, f32[4,200,128]{2,1,0:T(8,128)S(1)} %collective-permute-done.1.far), custom_call_target="tpu_custom_call" | custom-call | tf_op jit(solution)/shard_map/columns/pallas_call | solution.py:369
  13.3 1.5 %collective-permute-start.4 = (f32[200,128]{1,0:T(8,128)}, f32[200,128]{1,0:T(8,128)S(1)}, u32[]{:S(2)}, u32[]{:S(2)}) collective-permute-start(f32[200,128]{1,0:T(8,128)} %get-tuple-element.20), channel_id=1, source_target_pairs={{0,8},{16,24},{8,0},{24,16},{1,9},{17,25},{9,1},{25,17},{2,10},{18... | collective-permute-start | bytes 307208 | tf_op jit(solution)/shard_map/ppermute | solution.py:385
  14.7 1.5 %collective-permute-start.5 = (f32[200,128]{1,0:T(8,128)S(1)}, f32[200,128]{1,0:T(8,128)S(1)}, u32[]{:S(2)}, u32[]{:S(2)}) collective-permute-start(f32[200,128]{1,0:T(8,128)S(1)} %get-tuple-element.21), channel_id=1, source_target_pairs={{8,16},{0,24},{16,8},{24,0},{9,17},{1,25},{17,9},{25,1},{10,18},{2... | collective-permute-start | bytes 307208 | tf_op jit(solution)/shard_map/ppermute | solution.py:385
  16.2 0.0 collective-permute-done.2.near_fast
  16.2 0.0 collective-permute-done.3.far_fast
  16.2 0.0 copy-done
  16.2 0.0 copy-done.2
  16.3 0.0 copy-done.4
  16.3 5.2 %evolve.1.middle_gram = f32[192,192]{1,0:T(8,128)S(1)} custom-call(f32[2,1536,128]{2,1,0:T(8,128)S(1)} %bitcast.3, f32[8,128]{1,0:T(8,128)S(1)} %copy-done.2, f32[8,128]{1,0:T(8,128)S(1)} %copy-done.4, f32[4,200,128]{2,1,0:T(8,128)S(1)} %collective-permute-done.near, f32[4,200,128]{2,1,0:T(8,128)S(1)} %collective-permute-done.1.far, ...), custom_call_target="tpu_custom_call" | custom-call | tf_op jit(solution)/shard_map/evolve/pallas_call | solution.py:369
  21.5 0.0 collective-permute-done.4.near
  21.5 0.0 collective-permute-done.5.far
  21.5 2.9 %gram.1.loc_ref = f32[192,128]{1,0:T(8,128)S(1)} custom-call(f32[192,192]{1,0:T(8,128)S(1)} %evolve.1.middle_gram, f32[4,200,128]{2,1,0:T(8,128)S(1)} %get-tuple-element.19.strips, f32[200,128]{1,0:T(8,128)S(1)} %collective-permute-done.4.near, f32[200,128]{1,0:T(8,128)S(1)} %collective-permute-done.5.far), custom_call_target="tpu_custom_call" | custom-call | tf_op jit(solution)/shard_map/gram/pallas_call | solution.py:369
  24.4 4.2 %collective-permute-start.6 = (f32[96,128]{1,0:T(8,128)S(1)}, f32[96,128]{1,0:T(8,128)S(1)}, u32[]{:S(2)}, u32[]{:S(2)}) collective-permute-start(f32[96,128]{1,0:T(8,128)S(1)} %slice_select_fusion), channel_id=1, source_target_pairs={{0,1},{1,0},{2,3},{3,2},{4,5},{5,4},{6,7},{7,6},{8,9},{9,8},{10,11... | collective-permute-start | bytes 147464 | tf_op jit(solution)/shard_map/ppermute | solution.py:391
  28.6 0.9 %collective-permute-done.6 = f32[96,128]{1,0:T(8,128)S(1)} collective-permute-done((f32[96,128]{1,0:T(8,128)S(1)}, f32[96,128]{1,0:T(8,128)S(1)}, u32[]{:S(2)}, u32[]{:S(2)}) %collective-permute-start.6) | collective-permute-done | bytes 49184 | tf_op jit(solution)/shard_map/ppermute | solution.py:391
  29.5 1.5 %collective-permute-start.7 = (f32[96,128]{1,0:T(8,128)S(1)}, f32[96,128]{1,0:T(8,128)S(1)}, u32[]{:S(2)}, u32[]{:S(2)}) collective-permute-start(f32[96,128]{1,0:T(8,128)S(1)} %select_add_fusion), channel_id=1, source_target_pairs={{0,9},{1,8},{2,11},{3,10},{4,13},{5,12},{6,15},{7,14},{8,1},{9,0},... | collective-permute-start | bytes 147464 | tf_op jit(solution)/shard_map/ppermute | solution.py:391
  31.0 2.1 %collective-permute-done.7 = f32[96,128]{1,0:T(8,128)S(1)} collective-permute-done((f32[96,128]{1,0:T(8,128)S(1)}, f32[96,128]{1,0:T(8,128)S(1)}, u32[]{:S(2)}, u32[]{:S(2)}) %collective-permute-start.7) | collective-permute-done | bytes 49184 | tf_op jit(solution)/shard_map/ppermute | solution.py:391
  33.1 1.7 %collective-permute-start.8 = (f32[96,128]{1,0:T(8,128)S(1)}, f32[96,128]{1,0:T(8,128)S(1)}, u32[]{:S(2)}, u32[]{:S(2)}) collective-permute-start(f32[96,128]{1,0:T(8,128)S(1)} %add.16), channel_id=1, source_target_pairs={{0,17},{1,16},{2,19},{3,18},{4,21},{5,20},{6,23},{7,22},{8,25},{9,... | collective-permute-start | bytes 147464 | tf_op jit(solution)/shard_map/ppermute | solution.py:391
  34.8 1.9 %collective-permute-done.8 = f32[96,128]{1,0:T(8,128)S(1)} collective-permute-done((f32[96,128]{1,0:T(8,128)S(1)}, f32[96,128]{1,0:T(8,128)S(1)}, u32[]{:S(2)}, u32[]{:S(2)}) %collective-permute-start.8) | collective-permute-done | bytes 49184 | tf_op jit(solution)/shard_map/ppermute | solution.py:391
  36.7 2.3 %collective-permute-start.9 = (f32[96,128]{1,0:T(8,128)S(1)}, f32[96,128]{1,0:T(8,128)S(1)}, u32[]{:S(2)}, u32[]{:S(2)}) collective-permute-start(f32[96,128]{1,0:T(8,128)S(1)} %add.17), channel_id=1, source_target_pairs={{0,3},{1,2},{2,1},{3,0},{4,7},{5,6},{6,5},{7,4},{8,11},{9,10},{10,... | collective-permute-start | bytes 147464 | tf_op jit(solution)/shard_map/ppermute | solution.py:391
  39.0 1.9 %collective-permute-done.9 = f32[96,128]{1,0:T(8,128)S(1)} collective-permute-done((f32[96,128]{1,0:T(8,128)S(1)}, f32[96,128]{1,0:T(8,128)S(1)}, u32[]{:S(2)}, u32[]{:S(2)}) %collective-permute-start.9) | collective-permute-done | bytes 49184 | tf_op jit(solution)/shard_map/ppermute | solution.py:391
  40.9 2.6 %collective-permute-start.10 = (f32[96,128]{1,0:T(8,128)S(1)}, f32[96,128]{1,0:T(8,128)S(1)}, u32[]{:S(2)}, u32[]{:S(2)}) collective-permute-start(f32[96,128]{1,0:T(8,128)S(1)} %add.18), channel_id=1, source_target_pairs={{0,5},{1,4},{2,7},{3,6},{4,1},{5,0},{6,3},{7,2},{8,13},{9,12},{10,... | collective-permute-start | bytes 147464 | tf_op jit(solution)/shard_map/ppermute | solution.py:391
  43.5 2.0 %collective-permute-done.10 = f32[96,128]{1,0:T(8,128)S(1)} collective-permute-done((f32[96,128]{1,0:T(8,128)S(1)}, f32[96,128]{1,0:T(8,128)S(1)}, u32[]{:S(2)}, u32[]{:S(2)}) %collective-permute-start.10) | collective-permute-done | bytes 49184 | tf_op jit(solution)/shard_map/ppermute | solution.py:391
  45.6 0.2 collective-permute-start.11
  45.8 1.1 %collective-permute-done.11.other_ref = f32[96,128]{1,0:T(8,128)S(1)} collective-permute-done((f32[96,128]{1,0:T(8,128)S(1)}, f32[96,128]{1,0:T(8,128)S(1)}, u32[]{:S(2)}, u32[]{:S(2)}) %collective-permute-start.11) | collective-permute-done | bytes 49184 | tf_op jit(solution)/shard_map/ppermute | solution.py:391
  46.9 9.1 %factor.1 = (f32[192,192]{1,0:T(8,128)}, f32[1,192]{1,0:T(1,128)}) custom-call(f32[96,128]{1,0:T(8,128)S(1)} %add.19.own_ref, f32[96,128]{1,0:T(8,128)S(1)} %collective-permute-done.11.other_ref, f32[192,128]{1,0:T(8,128)S(1)} %gram.1.loc_ref), custom_call_target="tpu_custom_call" | custom-call | tf_op jit(solution)/shard_map/factor/pallas_call | solution.py:369
  (6 shorter events, 0.0 us)
Async XLA Ops:
  0.6 15.6 %copy-start = (f32[2,192,8,128]{3,2,1,0:T(8,128)S(1)}, f32[2,192,8,128]{3,2,1,0:T(8,128)}, u32[]{:S(2)}) copy-start(f32[2,192,8,128]{3,2,1,0:T(8,128)} %param.3) | copy-start | bytes 4718596
  0.6 0.8 %copy-start.1 = (f32[8,128]{1,0:T(8,128)S(1)}, f32[8,128]{1,0:T(8,128)}, u32[]{:S(2)}) copy-start(f32[8,128]{1,0:T(8,128)} %coeff_self.1) | copy-start | bytes 12292
  1.4 0.7 %copy-start.3 = (f32[8,128]{1,0:T(8,128)S(1)}, f32[8,128]{1,0:T(8,128)}, u32[]{:S(2)}) copy-start(f32[8,128]{1,0:T(8,128)} %coeff_cross.1) | copy-start | bytes 12292
  2.1 14.1 %copy-start.2 = (f32[8,128]{1,0:T(8,128)S(1)}, f32[8,128]{1,0:T(8,128)}, u32[]{:S(2)}) copy-start(f32[8,128]{1,0:T(8,128)} %coeff_self.1) | copy-start | bytes 12292
  2.1 14.1 %copy-start.4 = (f32[8,128]{1,0:T(8,128)S(1)}, f32[8,128]{1,0:T(8,128)}, u32[]{:S(2)}) copy-start(f32[8,128]{1,0:T(8,128)} %coeff_cross.1) | copy-start | bytes 12292
  5.1 6.6 %collective-permute-start = (f32[4,200,128]{2,1,0:T(8,128)S(1)}, f32[4,200,128]{2,1,0:T(8,128)S(1)}, u32[]{:S(2)}, u32[]{:S(2)}) collective-permute-start(f32[4,200,128]{2,1,0:T(8,128)S(1)} %get-tuple-element.13), channel_id=1, source_target_pairs={{0,1},{2,3},{4,5},{6,7},{1,0},{3,2},{5,4},{7,6},{8,9},{10,11},{12,... | collective-permute-start | bytes 1228808 | tf_op jit(solution)/shard_map/ppermute | solution.py:385
  5.6 6.1 %collective-permute-start.1 = (f32[4,200,128]{2,1,0:T(8,128)S(1)}, f32[4,200,128]{2,1,0:T(8,128)S(1)}, u32[]{:S(2)}, u32[]{:S(2)}) collective-permute-start(f32[4,200,128]{2,1,0:T(8,128)S(1)} %get-tuple-element.14), channel_id=1, source_target_pairs={{1,2},{3,4},{5,6},{2,1},{4,3},{6,5},{9,10},{11,12},{13,14},{10,9},... | collective-permute-start | bytes 1228808 | tf_op jit(solution)/shard_map/ppermute | solution.py:385
  6.3 9.9 %collective-permute-start.2 = (f32[4,200,128]{2,1,0:T(8,128)}, f32[4,200,128]{2,1,0:T(8,128)S(1)}, u32[]{:S(2)}, u32[]{:S(2)}) collective-permute-start(f32[4,200,128]{2,1,0:T(8,128)} %get-tuple-element.15), channel_id=1, source_target_pairs={{0,1},{2,3},{4,5},{6,7},{1,0},{3,2},{5,4},{7,6},{8,9},{10,11},{12,... | collective-permute-start | bytes 1228808 | tf_op jit(solution)/shard_map/ppermute | solution.py:385
  10.3 5.9 %collective-permute-start.3 = (f32[4,200,128]{2,1,0:T(8,128)}, f32[4,200,128]{2,1,0:T(8,128)}, u32[]{:S(2)}, u32[]{:S(2)}) collective-permute-start(f32[4,200,128]{2,1,0:T(8,128)} %get-tuple-element.16), channel_id=1, source_target_pairs={{1,2},{3,4},{5,6},{2,1},{4,3},{6,5},{9,10},{11,12},{13,14},{10,9},... | collective-permute-start | bytes 1228808 | tf_op jit(solution)/shard_map/ppermute | solution.py:385
  13.3 8.2 %collective-permute-start.4 = (f32[200,128]{1,0:T(8,128)}, f32[200,128]{1,0:T(8,128)S(1)}, u32[]{:S(2)}, u32[]{:S(2)}) collective-permute-start(f32[200,128]{1,0:T(8,128)} %get-tuple-element.20), channel_id=1, source_target_pairs={{0,8},{16,24},{8,0},{24,16},{1,9},{17,25},{9,1},{25,17},{2,10},{18... | collective-permute-start | bytes 307208 | tf_op jit(solution)/shard_map/ppermute | solution.py:385
  14.7 6.7 %collective-permute-start.5 = (f32[200,128]{1,0:T(8,128)S(1)}, f32[200,128]{1,0:T(8,128)S(1)}, u32[]{:S(2)}, u32[]{:S(2)}) collective-permute-start(f32[200,128]{1,0:T(8,128)S(1)} %get-tuple-element.21), channel_id=1, source_target_pairs={{8,16},{0,24},{16,8},{24,0},{9,17},{1,25},{17,9},{25,1},{10,18},{2... | collective-permute-start | bytes 307208 | tf_op jit(solution)/shard_map/ppermute | solution.py:385
  24.4 5.1 %collective-permute-start.6 = (f32[96,128]{1,0:T(8,128)S(1)}, f32[96,128]{1,0:T(8,128)S(1)}, u32[]{:S(2)}, u32[]{:S(2)}) collective-permute-start(f32[96,128]{1,0:T(8,128)S(1)} %slice_select_fusion), channel_id=1, source_target_pairs={{0,1},{1,0},{2,3},{3,2},{4,5},{5,4},{6,7},{7,6},{8,9},{9,8},{10,11... | collective-permute-start | bytes 147464 | tf_op jit(solution)/shard_map/ppermute | solution.py:391
  29.5 3.6 %collective-permute-start.7 = (f32[96,128]{1,0:T(8,128)S(1)}, f32[96,128]{1,0:T(8,128)S(1)}, u32[]{:S(2)}, u32[]{:S(2)}) collective-permute-start(f32[96,128]{1,0:T(8,128)S(1)} %select_add_fusion), channel_id=1, source_target_pairs={{0,9},{1,8},{2,11},{3,10},{4,13},{5,12},{6,15},{7,14},{8,1},{9,0},... | collective-permute-start | bytes 147464 | tf_op jit(solution)/shard_map/ppermute | solution.py:391
  33.1 3.6 %collective-permute-start.8 = (f32[96,128]{1,0:T(8,128)S(1)}, f32[96,128]{1,0:T(8,128)S(1)}, u32[]{:S(2)}, u32[]{:S(2)}) collective-permute-start(f32[96,128]{1,0:T(8,128)S(1)} %add.16), channel_id=1, source_target_pairs={{0,17},{1,16},{2,19},{3,18},{4,21},{5,20},{6,23},{7,22},{8,25},{9,... | collective-permute-start | bytes 147464 | tf_op jit(solution)/shard_map/ppermute | solution.py:391
  36.7 4.2 %collective-permute-start.9 = (f32[96,128]{1,0:T(8,128)S(1)}, f32[96,128]{1,0:T(8,128)S(1)}, u32[]{:S(2)}, u32[]{:S(2)}) collective-permute-start(f32[96,128]{1,0:T(8,128)S(1)} %add.17), channel_id=1, source_target_pairs={{0,3},{1,2},{2,1},{3,0},{4,7},{5,6},{6,5},{7,4},{8,11},{9,10},{10,... | collective-permute-start | bytes 147464 | tf_op jit(solution)/shard_map/ppermute | solution.py:391
  40.9 4.7 %collective-permute-start.10 = (f32[96,128]{1,0:T(8,128)S(1)}, f32[96,128]{1,0:T(8,128)S(1)}, u32[]{:S(2)}, u32[]{:S(2)}) collective-permute-start(f32[96,128]{1,0:T(8,128)S(1)} %add.18), channel_id=1, source_target_pairs={{0,5},{1,4},{2,7},{3,6},{4,1},{5,0},{6,3},{7,2},{8,13},{9,12},{10,... | collective-permute-start | bytes 147464 | tf_op jit(solution)/shard_map/ppermute | solution.py:391
  45.6 1.3 %collective-permute-start.11 = (f32[96,128]{1,0:T(8,128)S(1)}, f32[96,128]{1,0:T(8,128)S(1)}, u32[]{:S(2)}, u32[]{:S(2)}) collective-permute-start(f32[96,128]{1,0:T(8,128)S(1)} %add.19.own_ref), channel_id=1, source_target_pairs={{0,1},{1,0},{2,3},{3,2},{4,5},{5,4},{6,7},{7,6},{8,9},{9,8},{10,11... | collective-permute-start | bytes 147464 | tf_op jit(solution)/shard_map/ppermute | solution.py:391

commit v5 on v4

--- a/solution.py
+++ b/solution.py
@@ -17,6 +17,7 @@
 HEIGHT_EVOLVE = 48
 SIDE = 64
 VMEM_BYTES = 24 * 1024 * 1024
+LOCAL_COST = pl.CostEstimate(flops=10**9, bytes_accessed=10**6, transcendentals=0)
 EDGE_VMEM_BYTES = 52 * 1024 * 1024
 LANES = 128
 SUB = 8
@@ -53,21 +54,21 @@
         whole = jnp.concatenate([d, eye], axis=1)
         states.append([whole[g*SUB:(g+1)*SUB] for g in range(groups)])
     done = [[] for _ in blocks]
+    ready = [None for _ in blocks]
     for p in range(groups):
         for s, v in enumerate(states):
-            cols = {}
-            for g in range(p, groups):
-                for c in range(SUB):
-                    cols[g, c] = spread_lane(v[g], p*SUB + c)
+            spread = {(g, c): spread_lane(v[g], p*SUB + c) for g in range(p + 1, groups) for c in range(SUB)}
+            if p + 1 < groups:
+                coming = [spread_lane(v[p + 1], (p + 1)*SUB + c) for c in range(SUB)]
+            columns = ready[s] or [spread_lane(v[p], p*SUB + c) for c in range(SUB)]
             rows = [spread_row(v[p], c) for c in range(SUB)]
-            pivots = {(a, c): spread_row(cols[p, c], a) for c in range(SUB) for a in range(c, SUB)}
-            mult = {}
-            scale = []
+            pivots = {(a, c): spread_row(columns[c], a) for c in range(SUB) for a in range(c, SUB)}
+            mult, inverses, scale = {}, [], []
             for c in range(SUB):
-                inv = 1.0 / pivots[c, c]
+                inverses.append(1.0 / pivots[c, c])
                 scale.append(lax.rsqrt(pivots[c, c]))
                 for a in range(c + 1, SUB):
-                    mult[a, c] = pivots[a, c] * inv
+                    mult[a, c] = pivots[a, c] * inverses[c]
                     rows[a] = rows[a] - mult[a, c] * rows[c]
                     for b in range(c + 1, a + 1):
                         pivots[a, b] = pivots[a, b] - mult[a, c] * pivots[b, c]
@@ -76,61 +77,94 @@
             for c in range(1, SUB):
                 panel = jnp.where(sub == c, scaled[c], panel)
             done[s].append(panel)
-            if p + 1 == groups:
-                continue
-            near = [cols[p + 1, c] for c in range(SUB)]
-            for c in range(SUB):
-                for a in range(c + 1, SUB):
-                    near[a] = near[a] - mult[a, c] * near[c]
-                v[p + 1] = v[p + 1] - (near[c] * scale[c]) * scaled[c]
-            whole = [scaled[c] * scale[c] for c in range(SUB)]
-            for c in reversed(range(SUB)):
-                for a in range(c):
-                    whole[a] = whole[a] - mult[c, a] * whole[c]
-            for g in range(p + 2, groups):
+            for g in range(p + 1, min(p + 3, groups)):
+                cols = [spread[g, c] for c in range(SUB)]
                 for c in range(SUB):
-                    v[g] = v[g] - cols[g, c] * whole[c]
+                    for a in range(c + 1, SUB):
+                        cols[a] = cols[a] - mult[a, c] * cols[c]
+                    if g == p + 1:
+                        part = cols[c] * inverses[c]
+                        coming = [x - part * spread_row(cols[c], b) for b, x in enumerate(coming)]
+                    v[g] = v[g] - (cols[c] * scale[c]) * scaled[c]
+                if g == p + 1:
+                    ready[s] = coming
+            if p + 3 < groups:
+                solved = [scaled[c] * scale[c] for c in range(SUB)]
+                for c in reversed(range(SUB)):
+                    for a in range(c):
+                        solved[a] = solved[a] - mult[c, a] * solved[c]
+                for g in range(p + 3, groups):
+                    for c in range(SUB):
+                        v[g] = v[g] - spread[g, c] * solved[c]
     out = []
     for panels in done:
         whole = jnp.concatenate(panels, axis=0)
         out.append((whole[:, :SIDE], whole[:, SIDE:]))
     return out
 
-def factor_kernel(n, weight, own_ref, other_ref, loc_ref, out_ref, growth_ref):
+def square_masks():
+    row = lax.broadcasted_iota(jnp.int32, (SIDE, SIDE), 0)
+    col = lax.broadcasted_iota(jnp.int32, (SIDE, SIDE), 1)
+    return row <= col, row == col
+
+
+def local_kernel(n, packed, gram, panel, *after):
+    blocks = unpack_blocks(gram[...], n) if packed else {
+        (i, j): gram[i*SIDE:(i+1)*SIDE, j*SIDE:(j+1)*SIDE] for i, j in block_pairs(n)
+    }
+    ((factor, inverse),) = factor_blocks([blocks[0, 0]])
+    panel[:, :SIDE] = jnp.where(square_masks()[0], factor, 0.0)
+    if n > 1:
+        row = dot_nn(inverse, jnp.concatenate([blocks[0, j] for j in range(1, n)], axis=1))
+        panel[:, SIDE:] = row
+        less = dot_tn(row, row)
+        for i, j in block_pairs(n - 1):
+            at = (slice(i*SIDE, (i+1)*SIDE), slice(j*SIDE, (j+1)*SIDE))
+            after[0][at] = blocks[i + 1, j + 1] - less[at]
+
+
+def local_factor(packed, n):
+    panels, left = [], packed
+    for k in range(n):
+        m = n - k
+        shapes = [(SIDE, m*SIDE)] + ([((m-1)*SIDE, (m-1)*SIDE)] if m > 1 else [])
+        panel, *left = local_call(functools.partial(local_kernel, m, k == 0), "local_factor", shapes, [], left, cost=LOCAL_COST)
+        left = left[0] if left else None
+        panels.append(panel)
+    return panels
+
+
+def factor_kernel(n, weight, own_ref, other_ref, *refs):
+    local, (out_ref, growth_ref) = refs[:n], refs[n:]
     high_half = parity()
     own, other = own_ref[...], other_ref[...]
     total = unpack_blocks(jnp.concatenate([jnp.where(high_half, other, own), jnp.where(high_half, own, other)], axis=0), n)
-    local = unpack_blocks(loc_ref[...], n)
-    keep = (lax.broadcasted_iota(jnp.int32, (SIDE, SIDE), 0) <= lax.broadcasted_iota(jnp.int32, (SIDE, SIDE), 1))
-    diag = (lax.broadcasted_iota(jnp.int32, (SIDE, SIDE), 0) == lax.broadcasted_iota(jnp.int32, (SIDE, SIDE), 1))
-    rest = {j: [] for j in range(n)}
+    diag = square_masks()[1]
+    rest = {j: [local[i][:, (j-i)*SIDE:(j-i+1)*SIDE] for i in range(j + 1)] for j in range(n)}
     for k in range(n):
-        (r_t, i_t), (r_l, i_l) = factor_blocks([total[k, k], local[k, k]])
-        growth_ref[0, k*SIDE:(k+1)*SIDE] = jnp.log(jnp.sum(jnp.where(diag, r_t, 0.0), axis=0))
-        panels = []
-        for grams, inv in ((total, i_t), (local, i_l)):
-            if k + 1 < n:
-                row = dot_nn(inv, jnp.concatenate([grams[k, j] for j in range(k + 1, n)], axis=1))
-                for i in range(k + 1, n):
-                    less = dot_tn(row[:, (i-k-1)*SIDE:(i-k)*SIDE], row[:, (i-k-1)*SIDE:])
-                    for j in range(i, n):
-                        grams[i, j] = grams[i, j] - less[:, (j-i)*SIDE:(j-i+1)*SIDE]
-                panels.append(row)
-        rest[k].append(jnp.where(keep, r_l, 0.0))
-        answer = dot_nt(jnp.concatenate(rest[k], axis=0), i_t)
+        ((factor, inverse),) = factor_blocks([total[k, k]])
+        growth_ref[0, k*SIDE:(k+1)*SIDE] = jnp.log(jnp.sum(jnp.where(diag, factor, 0.0), axis=0))
+        if k + 1 < n:
+            row = dot_nn(inverse, jnp.concatenate([total[k, j] for j in range(k + 1, n)], axis=1))
+            for i in range(k + 1, n):
+                less = dot_tn(row[:, (i-k-1)*SIDE:(i-k)*SIDE], row[:, (i-k-1)*SIDE:])
+                for j in range(i, n):
+                    total[i, j] = total[i, j] - less[:, (j-i)*SIDE:(j-i+1)*SIDE]
+        answer = dot_nt(jnp.concatenate(rest[k], axis=0), inverse)
         out_ref[:(k+1)*SIDE, k*SIDE:(k+1)*SIDE] = weight * answer
         if k + 1 < n:
             out_ref[(k+1)*SIDE:, k*SIDE:(k+1)*SIDE] = jnp.zeros(((n-k-1)*SIDE, SIDE), jnp.float32)
-            less = dot_nn(answer, panels[0])
+            less = dot_nn(answer, row)
             for j in range(k + 1, n):
                 at = (j-k-1)*SIDE
-                rest[j].append(panels[1][:, at:at+SIDE])
-                rest[j] = [part - less[i*SIDE:(i+1)*SIDE, at:at+SIDE] for i, part in enumerate(rest[j])]
+                rest[j] = [
+                    part - less[i*SIDE:(i+1)*SIDE, at:at+SIDE] if i <= k else part for i, part in enumerate(rest[j])
+                ]
 
 
 def factor_call(own, other, local, k, weight):
     out, growth = local_call(
-        functools.partial(factor_kernel, k // SIDE, weight), "factor", [(k, k), (1, k)], [], own, other, local
+        functools.partial(factor_kernel, k // SIDE, weight), "factor", [(k, k), (1, k)], [], own, other, *local
     )
     return out, growth[0]
 
@@ -364,7 +398,7 @@
     middle_gram[...] = dot_nt(cells[...], cells[...])
 
 
-def local_call(body, name, out_shapes, scratch, *args, hbm=False, vmem=VMEM_BYTES):
+def local_call(body, name, out_shapes, scratch, *args, hbm=False, vmem=VMEM_BYTES, cost=None):
     spec = pl.BlockSpec(memory_space=pltpu.VMEM)
     return pl.pallas_call(
         body,
@@ -374,6 +408,7 @@
         scratch_shapes=[pltpu.VMEM(s, jnp.float32) if isinstance(s, tuple) else s for s in scratch],
         compiler_params=pltpu.CompilerParams(vmem_limit_bytes=vmem),
         name=name,
+        cost_estimate=cost,
     )(*args)
 
 
@@ -442,7 +477,7 @@
         [(2,) + strip, (fields, LANES)], middle_gram, strips, near_cols, far_cols,
     )
     block_total = lax.axis_size("grp") * lax.axis_size("tile")
-    corrections, growth = factor_call(*sum_blocks(packed), packed, fields, math.sqrt(block_total))
+    corrections, growth = factor_call(*sum_blocks(packed), local_factor(packed, side_blocks), fields, math.sqrt(block_total))
     return (corrections, growth)
 
 

time: 56.3 us -> 53.9 us (0.957)
  waiting for transfers between devices: 9.86 us -> 5.07 us
  Pallas kernels: 21.7 us -> 23.9 us
    ppermute x6, waiting for transfers between devices: 9.84 us -> 5.05 us  [exchange(): return lax.ppermute(cells, ('grp', 'tile'), moves)]
    pallas_call x5 -> x8, Pallas kernels: 21.7 us -> 23.9 us  [local_call(): pl.pallas_call(body, out_shape=[jax.ShapeDtypeStruct(s, jnp.float32) for...]
  transfers between devices with their start and end apart: 12 -> 12, of which waited for: 6 -> 4; matrix products, arithmetic and copies ran while one was open for 0% -> 0% of each run, Pallas kernels for 12% -> 22%
where the time goes in v5:
time: 53.9 us; the launch traced here: 53.4 us
  Pallas kernels  23.9 us (44%)
  starting transfers between devices  22.1 us (41%)
  waiting for transfers between devices  5.07 us (9%)
  local copies, waits for them, and re-layouts  1.5 us (3%)
  between operations  0.76 us (1%)
    pallas_call x8, Pallas kernels, local_call(): pl.pallas_call(body, out_shape=[jax.ShapeDtypeStruct(s, jnp.float32) for...  23.9 us
    ppermute x6, starting transfers between devices, exchange(): return lax.ppermute(cells, ('grp', 'tile'), moves)  12.5 us
    ppermute x6, starting transfers between devices, swap(): return lax.ppermute(cells, axis, pairs + [(b, a) for a, b in pairs])  9.6 us
    ppermute x6, waiting for transfers between devices, exchange(): return lax.ppermute(cells, ('grp', 'tile'), moves)  5.05 us
    unnamed x10, local copies, waits for them, and re-layouts  1.5 us
  transfers between devices with their start and end apart: 12, of which 4 were waited for; matrix products, arithmetic and copies ran while one was open for 0% of the time, Pallas kernels for 22%

profile of v5, /device:TPU:0, one launch (start us, length us, event | category | flops | bytes accessed | tf_op | source)
XLA Modules:
  0.0 53.4 jit_solution(14061639135427743724)
XLA Ops:
  0.6 0.0 copy-start
  0.6 0.0 copy-start.1
  0.6 0.8 %copy-done.1 = f32[8,128]{1,0:T(8,128)S(1)} copy-done((f32[8,128]{1,0:T(8,128)S(1)}, f32[8,128]{1,0:T(8,128)}, u32[]{:S(2)}) %copy-start.1) | copy-done | bytes 4120
  1.4 0.0 copy-start.3
  1.4 0.7 %copy-done.3 = f32[8,128]{1,0:T(8,128)S(1)} copy-done((f32[8,128]{1,0:T(8,128)S(1)}, f32[8,128]{1,0:T(8,128)}, u32[]{:S(2)}) %copy-start.3) | copy-done | bytes 4120
  2.1 0.0 copy-start.2
  2.1 0.0 copy-start.4
  2.1 3.0 %edges.1 = (f32[200,128]{1,0:T(8,128)S(1)}, f32[200,128]{1,0:T(8,128)S(1)}, f32[4,200,128]{2,1,0:T(8,128)S(1)}, f32[4,200,128]{2,1,0:T(8,128)S(1)}, f32[4,200,128]{2,1,0:T(8,128)}, /*index=5*/f32[4,200,128]{2,1,0:T(8,128)}) custom-call(f32[2,1536,128]{2,1,0:T(8,128)} %bitcast.2, f32[8,128]{1,0:T(8,128)S(1)} %copy-done.1, f32[8,128]{1,0:T(8,128)S(1)} %copy-done.3), custom_call_target="tpu_custom_call" | custom-call | tf_op jit(solution)/shard_map/edges/pallas_call | solution.py:403
  5.1 0.5 collective-permute-start
  5.6 0.7 %collective-permute-start.1 = (f32[4,200,128]{2,1,0:T(8,128)S(1)}, f32[4,200,128]{2,1,0:T(8,128)S(1)}, u32[]{:S(2)}, u32[]{:S(2)}) collective-permute-start(f32[4,200,128]{2,1,0:T(8,128)S(1)} %get-tuple-element.18), channel_id=1, source_target_pairs={{1,2},{3,4},{5,6},{2,1},{4,3},{6,5},{9,10},{11,12},{13,14},{10,9},... | collective-permute-start | bytes 1228808 | tf_op jit(solution)/shard_map/ppermute | solution.py:420
  6.3 4.0 %collective-permute-start.2 = (f32[4,200,128]{2,1,0:T(8,128)}, f32[4,200,128]{2,1,0:T(8,128)S(1)}, u32[]{:S(2)}, u32[]{:S(2)}) collective-permute-start(f32[4,200,128]{2,1,0:T(8,128)} %get-tuple-element.19), channel_id=1, source_target_pairs={{0,1},{2,3},{4,5},{6,7},{1,0},{3,2},{5,4},{7,6},{8,9},{10,11},{12,... | collective-permute-start | bytes 1228808 | tf_op jit(solution)/shard_map/ppermute | solution.py:420
  10.3 1.4 %collective-permute-start.3 = (f32[4,200,128]{2,1,0:T(8,128)}, f32[4,200,128]{2,1,0:T(8,128)}, u32[]{:S(2)}, u32[]{:S(2)}) collective-permute-start(f32[4,200,128]{2,1,0:T(8,128)} %get-tuple-element.20), channel_id=1, source_target_pairs={{1,2},{3,4},{5,6},{2,1},{4,3},{6,5},{9,10},{11,12},{13,14},{10,9},... | collective-permute-start | bytes 1228808 | tf_op jit(solution)/shard_map/ppermute | solution.py:420
  11.7 0.0 collective-permute-done.near
  11.7 0.0 collective-permute-done.1.far
  11.7 1.5 %columns.1 = (f32[4,200,128]{2,1,0:T(8,128)S(1)}, f32[200,128]{1,0:T(8,128)}, f32[200,128]{1,0:T(8,128)S(1)}) custom-call(f32[200,128]{1,0:T(8,128)S(1)} %get-tuple-element.21.last, f32[200,128]{1,0:T(8,128)S(1)} %get-tuple-element.22.first, f32[4,200,128]{2,1,0:T(8,128)S(1)} %collective-permute-done.near, f32[4,200,128]{2,1,0:T(8,128)S(1)} %collective-permute-done.1.far), custom_call_target="tpu_custom_call" | custom-call | tf_op jit(solution)/shard_map/columns/pallas_call | solution.py:403
  13.3 1.5 %collective-permute-start.4 = (f32[200,128]{1,0:T(8,128)}, f32[200,128]{1,0:T(8,128)S(1)}, u32[]{:S(2)}, u32[]{:S(2)}) collective-permute-start(f32[200,128]{1,0:T(8,128)} %get-tuple-element.24), channel_id=1, source_target_pairs={{0,8},{16,24},{8,0},{24,16},{1,9},{17,25},{9,1},{25,17},{2,10},{18... | collective-permute-start | bytes 307208 | tf_op jit(solution)/shard_map/ppermute | solution.py:420
  14.8 1.5 %collective-permute-start.5 = (f32[200,128]{1,0:T(8,128)S(1)}, f32[200,128]{1,0:T(8,128)S(1)}, u32[]{:S(2)}, u32[]{:S(2)}) collective-permute-start(f32[200,128]{1,0:T(8,128)S(1)} %get-tuple-element.25), channel_id=1, source_target_pairs={{8,16},{0,24},{16,8},{24,0},{9,17},{1,25},{17,9},{25,1},{10,18},{2... | collective-permute-start | bytes 307208 | tf_op jit(solution)/shard_map/ppermute | solution.py:420
  16.3 0.0 collective-permute-done.2.near_fast
  16.3 0.0 collective-permute-done.3.far_fast
  16.3 0.0 copy-done
  16.3 0.0 copy-done.2
  16.3 0.0 copy-done.4
  16.3 5.2 %evolve.1.middle_gram = f32[192,192]{1,0:T(8,128)S(1)} custom-call(f32[2,1536,128]{2,1,0:T(8,128)S(1)} %bitcast.3, f32[8,128]{1,0:T(8,128)S(1)} %copy-done.2, f32[8,128]{1,0:T(8,128)S(1)} %copy-done.4, f32[4,200,128]{2,1,0:T(8,128)S(1)} %collective-permute-done.near, f32[4,200,128]{2,1,0:T(8,128)S(1)} %collective-permute-done.1.far, ...), custom_call_target="tpu_custom_call" | custom-call | tf_op jit(solution)/shard_map/evolve/pallas_call | solution.py:403
  21.5 0.0 collective-permute-done.4.near
  21.5 0.0 collective-permute-done.5.far
  21.5 2.9 %gram.1 = f32[192,128]{1,0:T(8,128)S(1)} custom-call(f32[192,192]{1,0:T(8,128)S(1)} %evolve.1.middle_gram, f32[4,200,128]{2,1,0:T(8,128)S(1)} %get-tuple-element.23.strips, f32[200,128]{1,0:T(8,128)S(1)} %collective-permute-done.4.near, f32[200,128]{1,0:T(8,128)S(1)} %collective-permute-done.5.far), custom_call_target="tpu_custom_call" | custom-call | tf_op jit(solution)/shard_map/gram/pallas_call | solution.py:403
  24.4 4.2 %collective-permute-start.6 = (f32[96,128]{1,0:T(8,128)S(1)}, f32[96,128]{1,0:T(8,128)S(1)}, u32[]{:S(2)}, u32[]{:S(2)}) collective-permute-start(f32[96,128]{1,0:T(8,128)S(1)} %slice_select_fusion), channel_id=1, source_target_pairs={{0,1},{1,0},{2,3},{3,2},{4,5},{5,4},{6,7},{7,6},{8,9},{9,8},{10,11... | collective-permute-start | bytes 147464 | tf_op jit(solution)/shard_map/ppermute | solution.py:426
  28.7 0.9 %collective-permute-done.6 = f32[96,128]{1,0:T(8,128)S(1)} collective-permute-done((f32[96,128]{1,0:T(8,128)S(1)}, f32[96,128]{1,0:T(8,128)S(1)}, u32[]{:S(2)}, u32[]{:S(2)}) %collective-permute-start.6) | collective-permute-done | bytes 49184 | tf_op jit(solution)/shard_map/ppermute | solution.py:426
  29.5 1.5 %collective-permute-start.7 = (f32[96,128]{1,0:T(8,128)S(1)}, f32[96,128]{1,0:T(8,128)S(1)}, u32[]{:S(2)}, u32[]{:S(2)}) collective-permute-start(f32[96,128]{1,0:T(8,128)S(1)} %select_add_fusion), channel_id=1, source_target_pairs={{0,9},{1,8},{2,11},{3,10},{4,13},{5,12},{6,15},{7,14},{8,1},{9,0},... | collective-permute-start | bytes 147464 | tf_op jit(solution)/shard_map/ppermute | solution.py:426
  31.0 2.1 %collective-permute-done.7 = f32[96,128]{1,0:T(8,128)S(1)} collective-permute-done((f32[96,128]{1,0:T(8,128)S(1)}, f32[96,128]{1,0:T(8,128)S(1)}, u32[]{:S(2)}, u32[]{:S(2)}) %collective-permute-start.7) | collective-permute-done | bytes 49184 | tf_op jit(solution)/shard_map/ppermute | solution.py:426
  33.1 1.7 %collective-permute-start.8 = (f32[96,128]{1,0:T(8,128)S(1)}, f32[96,128]{1,0:T(8,128)S(1)}, u32[]{:S(2)}, u32[]{:S(2)}) collective-permute-start(f32[96,128]{1,0:T(8,128)S(1)} %add.16), channel_id=1, source_target_pairs={{0,17},{1,16},{2,19},{3,18},{4,21},{5,20},{6,23},{7,22},{8,25},{9,... | collective-permute-start | bytes 147464 | tf_op jit(solution)/shard_map/ppermute | solution.py:426
  34.8 1.9 %collective-permute-done.8 = f32[96,128]{1,0:T(8,128)S(1)} collective-permute-done((f32[96,128]{1,0:T(8,128)S(1)}, f32[96,128]{1,0:T(8,128)S(1)}, u32[]{:S(2)}, u32[]{:S(2)}) %collective-permute-start.8) | collective-permute-done | bytes 49184 | tf_op jit(solution)/shard_map/ppermute | solution.py:426
  36.7 2.3 %collective-permute-start.9 = (f32[96,128]{1,0:T(8,128)S(1)}, f32[96,128]{1,0:T(8,128)S(1)}, u32[]{:S(2)}, u32[]{:S(2)}) collective-permute-start(f32[96,128]{1,0:T(8,128)S(1)} %add.17), channel_id=1, source_target_pairs={{0,3},{1,2},{2,1},{3,0},{4,7},{5,6},{6,5},{7,4},{8,11},{9,10},{10,... | collective-permute-start | bytes 147464 | tf_op jit(solution)/shard_map/ppermute | solution.py:426
  39.0 2.0 %local_factor.3 = (f32[64,192]{1,0:T(8,128)S(1)}, f32[128,128]{1,0:T(8,128)S(1)}) custom-call(f32[192,128]{1,0:T(8,128)S(1)} %gram.1), custom_call_target="tpu_custom_call" | custom-call | flops 1000000000 | bytes 1000000 | tf_op jit(solution)/shard_map/local_factor/pallas_call | solution.py:403
  41.0 0.0 collective-permute-done.9
  41.0 2.5 %collective-permute-start.10 = (f32[96,128]{1,0:T(8,128)S(1)}, f32[96,128]{1,0:T(8,128)S(1)}, u32[]{:S(2)}, u32[]{:S(2)}) collective-permute-start(f32[96,128]{1,0:T(8,128)S(1)} %add.18), channel_id=1, source_target_pairs={{0,5},{1,4},{2,7},{3,6},{4,1},{5,0},{6,3},{7,2},{8,13},{9,12},{10,... | collective-permute-start | bytes 147464 | tf_op jit(solution)/shard_map/ppermute | solution.py:426
  43.5 1.9 %local_factor.4 = (f32[64,128]{1,0:T(8,128)S(1)}, f32[64,64]{1,0:T(8,128)S(1)}) custom-call(f32[128,128]{1,0:T(8,128)S(1)} %get-tuple-element.27.gram), custom_call_target="tpu_custom_call" | custom-call | flops 1000000000 | bytes 1000000 | tf_op jit(solution)/shard_map/local_factor/pallas_call | solution.py:403
  45.5 0.2 collective-permute-done.10
  45.6 0.3 collective-permute-start.11
  45.9 1.3 %local_factor.5.refs_2_ = f32[64,64]{1,0:T(8,128)S(1)} custom-call(f32[64,64]{1,0:T(8,128)S(1)} %get-tuple-element.29.gram), custom_call_target="tpu_custom_call" | custom-call | flops 1000000000 | bytes 1000000 | tf_op jit(solution)/shard_map/local_factor/pallas_call | solution.py:403
  47.2 0.0 collective-permute-done.11.other_ref
  47.2 6.2 %factor.1 = (f32[192,192]{1,0:T(8,128)}, f32[1,192]{1,0:T(1,128)}) custom-call(f32[96,128]{1,0:T(8,128)S(1)} %add.19.own_ref, f32[96,128]{1,0:T(8,128)S(1)} %collective-permute-done.11.other_ref, f32[64,192]{1,0:T(8,128)S(1)} %get-tuple-element.26.refs_0_, f32[64,128]{1,0:T(8,128)S(1)} %get-tuple-element.28.refs_1_, f32[64,64]{1,0:T(8,128)S(1)} %local_factor.5.refs_2_), custom_call_target="tpu_custom_call" | custom-call | tf_op jit(solution)/shard_map/factor/pallas_call | solution.py:403
  (6 shorter events, 0.0 us)
Async XLA Ops:
  0.6 15.6 %copy-start = (f32[2,192,8,128]{3,2,1,0:T(8,128)S(1)}, f32[2,192,8,128]{3,2,1,0:T(8,128)}, u32[]{:S(2)}) copy-start(f32[2,192,8,128]{3,2,1,0:T(8,128)} %param.3) | copy-start | bytes 4718596
  0.6 0.8 %copy-start.1 = (f32[8,128]{1,0:T(8,128)S(1)}, f32[8,128]{1,0:T(8,128)}, u32[]{:S(2)}) copy-start(f32[8,128]{1,0:T(8,128)} %coeff_self.1) | copy-start | bytes 12292
  1.4 0.7 %copy-start.3 = (f32[8,128]{1,0:T(8,128)S(1)}, f32[8,128]{1,0:T(8,128)}, u32[]{:S(2)}) copy-start(f32[8,128]{1,0:T(8,128)} %coeff_cross.1) | copy-start | bytes 12292
  2.1 14.1 %copy-start.2 = (f32[8,128]{1,0:T(8,128)S(1)}, f32[8,128]{1,0:T(8,128)}, u32[]{:S(2)}) copy-start(f32[8,128]{1,0:T(8,128)} %coeff_self.1) | copy-start | bytes 12292
  2.1 14.1 %copy-start.4 = (f32[8,128]{1,0:T(8,128)S(1)}, f32[8,128]{1,0:T(8,128)}, u32[]{:S(2)}) copy-start(f32[8,128]{1,0:T(8,128)} %coeff_cross.1) | copy-start | bytes 12292
  5.1 6.6 %collective-permute-start = (f32[4,200,128]{2,1,0:T(8,128)S(1)}, f32[4,200,128]{2,1,0:T(8,128)S(1)}, u32[]{:S(2)}, u32[]{:S(2)}) collective-permute-start(f32[4,200,128]{2,1,0:T(8,128)S(1)} %get-tuple-element.17), channel_id=1, source_target_pairs={{0,1},{2,3},{4,5},{6,7},{1,0},{3,2},{5,4},{7,6},{8,9},{10,11},{12,... | collective-permute-start | bytes 1228808 | tf_op jit(solution)/shard_map/ppermute | solution.py:420
  5.6 6.1 %collective-permute-start.1 = (f32[4,200,128]{2,1,0:T(8,128)S(1)}, f32[4,200,128]{2,1,0:T(8,128)S(1)}, u32[]{:S(2)}, u32[]{:S(2)}) collective-permute-start(f32[4,200,128]{2,1,0:T(8,128)S(1)} %get-tuple-element.18), channel_id=1, source_target_pairs={{1,2},{3,4},{5,6},{2,1},{4,3},{6,5},{9,10},{11,12},{13,14},{10,9},... | collective-permute-start | bytes 1228808 | tf_op jit(solution)/shard_map/ppermute | solution.py:420
  6.3 10.0 %collective-permute-start.2 = (f32[4,200,128]{2,1,0:T(8,128)}, f32[4,200,128]{2,1,0:T(8,128)S(1)}, u32[]{:S(2)}, u32[]{:S(2)}) collective-permute-start(f32[4,200,128]{2,1,0:T(8,128)} %get-tuple-element.19), channel_id=1, source_target_pairs={{0,1},{2,3},{4,5},{6,7},{1,0},{3,2},{5,4},{7,6},{8,9},{10,11},{12,... | collective-permute-start | bytes 1228808 | tf_op jit(solution)/shard_map/ppermute | solution.py:420
  10.3 6.0 %collective-permute-start.3 = (f32[4,200,128]{2,1,0:T(8,128)}, f32[4,200,128]{2,1,0:T(8,128)}, u32[]{:S(2)}, u32[]{:S(2)}) collective-permute-start(f32[4,200,128]{2,1,0:T(8,128)} %get-tuple-element.20), channel_id=1, source_target_pairs={{1,2},{3,4},{5,6},{2,1},{4,3},{6,5},{9,10},{11,12},{13,14},{10,9},... | collective-permute-start | bytes 1228808 | tf_op jit(solution)/shard_map/ppermute | solution.py:420
  13.3 8.2 %collective-permute-start.4 = (f32[200,128]{1,0:T(8,128)}, f32[200,128]{1,0:T(8,128)S(1)}, u32[]{:S(2)}, u32[]{:S(2)}) collective-permute-start(f32[200,128]{1,0:T(8,128)} %get-tuple-element.24), channel_id=1, source_target_pairs={{0,8},{16,24},{8,0},{24,16},{1,9},{17,25},{9,1},{25,17},{2,10},{18... | collective-permute-start | bytes 307208 | tf_op jit(solution)/shard_map/ppermute | solution.py:420
  14.8 6.7 %collective-permute-start.5 = (f32[200,128]{1,0:T(8,128)S(1)}, f32[200,128]{1,0:T(8,128)S(1)}, u32[]{:S(2)}, u32[]{:S(2)}) collective-permute-start(f32[200,128]{1,0:T(8,128)S(1)} %get-tuple-element.25), channel_id=1, source_target_pairs={{8,16},{0,24},{16,8},{24,0},{9,17},{1,25},{17,9},{25,1},{10,18},{2... | collective-permute-start | bytes 307208 | tf_op jit(solution)/shard_map/ppermute | solution.py:420
  24.4 5.1 %collective-permute-start.6 = (f32[96,128]{1,0:T(8,128)S(1)}, f32[96,128]{1,0:T(8,128)S(1)}, u32[]{:S(2)}, u32[]{:S(2)}) collective-permute-start(f32[96,128]{1,0:T(8,128)S(1)} %slice_select_fusion), channel_id=1, source_target_pairs={{0,1},{1,0},{2,3},{3,2},{4,5},{5,4},{6,7},{7,6},{8,9},{9,8},{10,11... | collective-permute-start | bytes 147464 | tf_op jit(solution)/shard_map/ppermute | solution.py:426
  29.5 3.6 %collective-permute-start.7 = (f32[96,128]{1,0:T(8,128)S(1)}, f32[96,128]{1,0:T(8,128)S(1)}, u32[]{:S(2)}, u32[]{:S(2)}) collective-permute-start(f32[96,128]{1,0:T(8,128)S(1)} %select_add_fusion), channel_id=1, source_target_pairs={{0,9},{1,8},{2,11},{3,10},{4,13},{5,12},{6,15},{7,14},{8,1},{9,0},... | collective-permute-start | bytes 147464 | tf_op jit(solution)/shard_map/ppermute | solution.py:426
  33.1 3.6 %collective-permute-start.8 = (f32[96,128]{1,0:T(8,128)S(1)}, f32[96,128]{1,0:T(8,128)S(1)}, u32[]{:S(2)}, u32[]{:S(2)}) collective-permute-start(f32[96,128]{1,0:T(8,128)S(1)} %add.16), channel_id=1, source_target_pairs={{0,17},{1,16},{2,19},{3,18},{4,21},{5,20},{6,23},{7,22},{8,25},{9,... | collective-permute-start | bytes 147464 | tf_op jit(solution)/shard_map/ppermute | solution.py:426
  36.7 4.3 %collective-permute-start.9 = (f32[96,128]{1,0:T(8,128)S(1)}, f32[96,128]{1,0:T(8,128)S(1)}, u32[]{:S(2)}, u32[]{:S(2)}) collective-permute-start(f32[96,128]{1,0:T(8,128)S(1)} %add.17), channel_id=1, source_target_pairs={{0,3},{1,2},{2,1},{3,0},{4,7},{5,6},{6,5},{7,4},{8,11},{9,10},{10,... | collective-permute-start | bytes 147464 | tf_op jit(solution)/shard_map/ppermute | solution.py:426
  41.0 4.6 %collective-permute-start.10 = (f32[96,128]{1,0:T(8,128)S(1)}, f32[96,128]{1,0:T(8,128)S(1)}, u32[]{:S(2)}, u32[]{:S(2)}) collective-permute-start(f32[96,128]{1,0:T(8,128)S(1)} %add.18), channel_id=1, source_target_pairs={{0,5},{1,4},{2,7},{3,6},{4,1},{5,0},{6,3},{7,2},{8,13},{9,12},{10,... | collective-permute-start | bytes 147464 | tf_op jit(solution)/shard_map/ppermute | solution.py:426
  45.6 1.6 %collective-permute-start.11 = (f32[96,128]{1,0:T(8,128)S(1)}, f32[96,128]{1,0:T(8,128)S(1)}, u32[]{:S(2)}, u32[]{:S(2)}) collective-permute-start(f32[96,128]{1,0:T(8,128)S(1)} %add.19.own_ref), channel_id=1, source_target_pairs={{0,1},{1,0},{2,3},{3,2},{4,5},{5,4},{6,7},{7,6},{8,9},{9,8},{10,11... | collective-permute-start | bytes 147464 | tf_op jit(solution)/shard_map/ppermute | solution.py:426

commit v6 on v5

--- a/solution.py
+++ b/solution.py
@@ -29,6 +29,19 @@
     return lax.dot_general(a, b, (((0,), (0,)), ((), ())), precision=HI, preferred_element_type=jnp.float32)
 def dot_nt(a, b):
     return lax.dot_general(a, b, (((1,), (1,)), ((), ())), precision=HI, preferred_element_type=jnp.float32)
+
+def gram_of(cells):
+    high = cells.astype(jnp.bfloat16)
+    left = cells - high.astype(jnp.float32)
+    middle = left.astype(jnp.bfloat16)
+    low = (left - middle.astype(jnp.float32)).astype(jnp.bfloat16)
+
+    def product(a, b):
+        return lax.dot_general(a, b, (((1,), (1,)), ((), ())), preferred_element_type=jnp.float32)
+
+    mixed = product(middle, high) + product(low, high)
+    return product(high, high) + product(middle, middle) + (mixed + mixed.T)
+
 
 def block_pairs(n):
     return [(i, j) for i in range(n) for j in range(i, n)]
@@ -189,26 +202,23 @@
     return [[tangents[f, pl.ds(g * height * SUB + r, height, stride=SUB), :] for r in range(SUB)] for f in range(2)]
 
 
-def own_coeffs(coeff_self, coeff_cross):
-    return [[spread_row(ref[...], r) for r in range(SUB)] for ref in (coeff_self, coeff_cross)]
+def own_coeffs(coeffs):
+    return [[spread_row(coeffs[f], r) for r in range(SUB)] for f in range(2)]
 
 
 def tall(x, height):
     return jnp.concatenate([x] * (height // SUB), axis=0)
 
 
-def edge_kernel(fields, height, tangents_hbm, self_hbm, cross_hbm, last_out, first_out, near, far, near_fast, far_fast, tangents, coeff_self, coeff_cross, sems):
+def edge_kernel(fields, height, tangents_hbm, coeffs_hbm, last_out, first_out, near, far, near_fast, far_fast, tangents, coeffs, sems):
     chunks = fields // height
     span = height * SUB
     loads = [
         pltpu.make_async_copy(tangents_hbm.at[:, pl.ds(g * span, span), :], tangents.at[:, pl.ds(g * span, span), :], sems.at[g])
         for g in range(chunks)
     ]
-    small = [
-        pltpu.make_async_copy(src, dst, sems.at[chunks + i])
-        for i, (src, dst) in enumerate(((self_hbm, coeff_self), (cross_hbm, coeff_cross)))
-    ]
-    for load in loads + small:
+    small = pltpu.make_async_copy(coeffs_hbm, coeffs, sems.at[chunks])
+    for load in loads + [small]:
         load.start()
     odd = lax.axis_index("tile") % 2 == 1
 
@@ -240,9 +250,8 @@
     for g, load in enumerate(loads):
         load.wait()
         send(pl.ds(g * height, height), own_rows(tangents, g, height))
-    for load in small:
-        load.wait()
-    send(pl.ds(fields, SUB), own_coeffs(coeff_self, coeff_cross))
+    small.wait()
+    send(pl.ds(fields, SUB), own_coeffs(coeffs))
 
 
 def column_kernel(last, first, near, far, strips, near_out, far_out, outer):
@@ -346,7 +355,7 @@
         joined = [jnp.where(l % SUB < STEPS, s[1], s[0]) for s in (fast, slow)]
         ends[chunk(g, height), :] = jnp.where(l < LANES // 2, joined[0], roll(joined[1], LANES // 2))
 
-    whole = middle_gram[...] + dot_nt(ends[...], ends[...])
+    whole = middle_gram[...] + gram_of(ends[...])
     for index, (i, j) in enumerate(block_pairs(fields // SIDE)):
         row, half = divmod(index, 2)
         gram[row * SIDE:(row + 1) * SIDE, half * SIDE:(half + 1) * SIDE] = whole[
@@ -369,8 +378,8 @@
     return out
 
 
-def evolve_kernel(fields, height, tangents, coeff_self, coeff_cross, near, far, near_fast, far_fast, middle_gram, row_coeffs, cells):
-    coeff_rows = extended_rows(own_coeffs(coeff_self, coeff_cross), near, far, near_fast, far_fast, pl.ds(fields, SUB))
+def evolve_kernel(fields, height, tangents, coeffs, near, far, near_fast, far_fast, middle_gram, row_coeffs, cells):
+    coeff_rows = extended_rows(own_coeffs(coeffs), near, far, near_fast, far_fast, pl.ds(fields, SUB))
     for f in range(2):
         for r in range(1 - STEPS, SUB + STEPS - 1):
             row_coeffs[f, r + STEPS - 1, :, :] = coeff_rows[f][r] + (1.0 - 4.0 * diffusion) * (1 - f)
@@ -395,7 +404,7 @@
             for r in range(SUB):
                 cells[at, (f * SUB + r) * LANES:(f * SUB + r + 1) * LANES] = jnp.where(middle, rows[r], 0.0)
 
-    middle_gram[...] = dot_nt(cells[...], cells[...])
+    middle_gram[...] = gram_of(cells[...])
 
 
 def local_call(body, name, out_shapes, scratch, *args, hbm=False, vmem=VMEM_BYTES, cost=None):
@@ -453,10 +462,10 @@
     padded = fields + SUB
     rows = tangents.reshape(2, fields * tangents.shape[2], tangents.shape[3])
     message, strip = (STEPS, padded, LANES), (padded, LANES)
-    inputs = (rows, reaction_self, reaction_cross)
+    inputs = (rows, jnp.stack([reaction_self, reaction_cross]))
     last, first, near, far, near_fast, far_fast = local_call(
         functools.partial(edge_kernel, fields, HEIGHT_EDGE), "edges", [strip] * 2 + [message] * 4,
-        [a.shape for a in inputs] + [pltpu.SemaphoreType.DMA((fields // HEIGHT_EDGE + 2,))], *inputs,
+        [a.shape for a in inputs] + [pltpu.SemaphoreType.DMA((fields // HEIGHT_EDGE + 1,))], *inputs,
         hbm=True, vmem=EDGE_VMEM_BYTES,
     )
     near, far = swap(near, "tile", 0), swap(far, "tile", 1)

time: 53.9 us -> 53.3 us (0.989)
  local copies, waits for them, and re-layouts: 1.5 us -> 0.01 us
  other arithmetic: 0.05 us -> 0.87 us
  starting transfers between devices: 22.1 us -> 22.9 us
    unnamed x10 -> x2, local copies, waits for them, and re-layouts: 1.5 us -> 0.01 us
    ppermute x6, starting transfers between devices: 12.5 us -> 13.3 us  [exchange(): return lax.ppermute(cells, ('grp', 'tile'), moves)]
    another operation x0 -> x1, other arithmetic: none -> 0.82 us  [per_device(): inputs = (rows, jnp.stack([reaction_self, reaction_cross]))]
  transfers between devices with their start and end apart: 12 -> 12, of which waited for: 4 -> 3; matrix products, arithmetic and copies ran while one was open for 0% -> 0% of each run, Pallas kernels for 22% -> 22%
where the time goes in v6:
time: 53.3 us; the launch traced here: 53.1 us
  Pallas kernels  23.6 us (44%)
  starting transfers between devices  22.9 us (43%)
  waiting for transfers between devices  4.93 us (9%)
  other arithmetic  0.87 us (2%)
  between operations  0.74 us (1%)
    pallas_call x8, Pallas kernels, local_call(): pl.pallas_call(body, out_shape=[jax.ShapeDtypeStruct(s, jnp.float32) for...  23.6 us
    ppermute x6, starting transfers between devices, exchange(): return lax.ppermute(cells, ('grp', 'tile'), moves)  13.3 us
    ppermute x6, starting transfers between devices, swap(): return lax.ppermute(cells, axis, pairs + [(b, a) for a, b in pairs])  9.6 us
    ppermute x6, waiting for transfers between devices, exchange(): return lax.ppermute(cells, ('grp', 'tile'), moves)  4.92 us
  transfers between devices with their start and end apart: 12, of which 3 were waited for; matrix products, arithmetic and copies ran while one was open for 0% of the time, Pallas kernels for 22%

profile of v6, /device:TPU:0, one launch (start us, length us, event | category | flops | bytes accessed | tf_op | source)
XLA Modules:
  0.0 53.1 jit_solution(81454301793034794)
XLA Ops:
  0.6 0.0 copy-start
  0.6 0.8 %pad_maximum_fusion.coeffs_hbm.coeffs = f32[2,8,128]{2,1,0:T(8,128)S(1)} fusion(f32[1,8,128]{2,1,0:T(8,128)} %bitcast.6, f32[1,8,128]{2,1,0:T(8,128)} %bitcast.7), kind=kLoop, calls=%fused_computation.2 | loop fusion | flops 2048 | bytes 16384 | tf_op jit(solution)/shard_map/stack | solution.py:465
  1.5 2.9 %edges.1 = (f32[200,128]{1,0:T(8,128)S(1)}, f32[200,128]{1,0:T(8,128)S(1)}, f32[4,200,128]{2,1,0:T(8,128)S(1)}, f32[4,200,128]{2,1,0:T(8,128)S(1)}, f32[4,200,128]{2,1,0:T(8,128)}, /*index=5*/f32[4,200,128]{2,1,0:T(8,128)}) custom-call(f32[2,1536,128]{2,1,0:T(8,128)} %bitcast.4, f32[2,8,128]{2,1,0:T(8,128)S(1)} %pad_maximum_fusion.coeffs_hbm.coeffs), custom_call_target="tpu_custom_call" | custom-call | tf_op jit(solution)/shard_map/edges/pallas_call | solution.py:412
  4.4 0.5 collective-permute-start
  4.9 0.7 %collective-permute-start.1 = (f32[4,200,128]{2,1,0:T(8,128)S(1)}, f32[4,200,128]{2,1,0:T(8,128)S(1)}, u32[]{:S(2)}, u32[]{:S(2)}) collective-permute-start(f32[4,200,128]{2,1,0:T(8,128)S(1)} %get-tuple-element.18), channel_id=1, source_target_pairs={{1,2},{3,4},{5,6},{2,1},{4,3},{6,5},{9,10},{11,12},{13,14},{10,9},... | collective-permute-start | bytes 1228808 | tf_op jit(solution)/shard_map/ppermute | solution.py:429
  5.6 4.0 %collective-permute-start.2 = (f32[4,200,128]{2,1,0:T(8,128)}, f32[4,200,128]{2,1,0:T(8,128)S(1)}, u32[]{:S(2)}, u32[]{:S(2)}) collective-permute-start(f32[4,200,128]{2,1,0:T(8,128)} %get-tuple-element.19), channel_id=1, source_target_pairs={{0,1},{2,3},{4,5},{6,7},{1,0},{3,2},{5,4},{7,6},{8,9},{10,11},{12,... | collective-permute-start | bytes 1228808 | tf_op jit(solution)/shard_map/ppermute | solution.py:429
  9.6 1.4 %collective-permute-start.3 = (f32[4,200,128]{2,1,0:T(8,128)}, f32[4,200,128]{2,1,0:T(8,128)}, u32[]{:S(2)}, u32[]{:S(2)}) collective-permute-start(f32[4,200,128]{2,1,0:T(8,128)} %get-tuple-element.20), channel_id=1, source_target_pairs={{1,2},{3,4},{5,6},{2,1},{4,3},{6,5},{9,10},{11,12},{13,14},{10,9},... | collective-permute-start | bytes 1228808 | tf_op jit(solution)/shard_map/ppermute | solution.py:429
  11.0 0.0 collective-permute-done.near
  11.0 0.0 collective-permute-done.1.far
  11.0 1.5 %columns.1 = (f32[4,200,128]{2,1,0:T(8,128)S(1)}, f32[200,128]{1,0:T(8,128)}, f32[200,128]{1,0:T(8,128)S(1)}) custom-call(f32[200,128]{1,0:T(8,128)S(1)} %get-tuple-element.21.last, f32[200,128]{1,0:T(8,128)S(1)} %get-tuple-element.22.first, f32[4,200,128]{2,1,0:T(8,128)S(1)} %collective-permute-done.near, f32[4,200,128]{2,1,0:T(8,128)S(1)} %collective-permute-done.1.far), custom_call_target="tpu_custom_call" | custom-call | tf_op jit(solution)/shard_map/columns/pallas_call | solution.py:412
  12.6 1.5 %collective-permute-start.4 = (f32[200,128]{1,0:T(8,128)}, f32[200,128]{1,0:T(8,128)S(1)}, u32[]{:S(2)}, u32[]{:S(2)}) collective-permute-start(f32[200,128]{1,0:T(8,128)} %get-tuple-element.24), channel_id=1, source_target_pairs={{0,8},{16,24},{8,0},{24,16},{1,9},{17,25},{9,1},{25,17},{2,10},{18... | collective-permute-start | bytes 307208 | tf_op jit(solution)/shard_map/ppermute | solution.py:429
  14.1 1.5 %collective-permute-start.5 = (f32[200,128]{1,0:T(8,128)S(1)}, f32[200,128]{1,0:T(8,128)S(1)}, u32[]{:S(2)}, u32[]{:S(2)}) collective-permute-start(f32[200,128]{1,0:T(8,128)S(1)} %get-tuple-element.25), channel_id=1, source_target_pairs={{8,16},{0,24},{16,8},{24,0},{9,17},{1,25},{17,9},{25,1},{10,18},{2... | collective-permute-start | bytes 307208 | tf_op jit(solution)/shard_map/ppermute | solution.py:429
  15.5 0.0 collective-permute-done.2.near_fast
  15.5 0.0 collective-permute-done.3.far_fast
  15.6 0.0 copy-done
  15.6 4.9 %evolve.1.middle_gram = f32[192,192]{1,0:T(8,128)S(1)} custom-call(f32[2,1536,128]{2,1,0:T(8,128)S(1)} %bitcast.5, f32[2,8,128]{2,1,0:T(8,128)S(1)} %pad_maximum_fusion.coeffs_hbm.coeffs, f32[4,200,128]{2,1,0:T(8,128)S(1)} %collective-permute-done.near, f32[4,200,128]{2,1,0:T(8,128)S(1)} %collective-permute-done.1.far, ...), custom_call_target="tpu_custom_call" | custom-call | tf_op jit(solution)/shard_map/evolve/pallas_call | solution.py:412
  20.4 0.0 collective-permute-done.4.near
  20.4 0.0 collective-permute-done.5.far
  20.4 2.9 %gram.1 = f32[192,128]{1,0:T(8,128)S(1)} custom-call(f32[192,192]{1,0:T(8,128)S(1)} %evolve.1.middle_gram, f32[4,200,128]{2,1,0:T(8,128)S(1)} %get-tuple-element.23.strips, f32[200,128]{1,0:T(8,128)S(1)} %collective-permute-done.4.near, f32[200,128]{1,0:T(8,128)S(1)} %collective-permute-done.5.far), custom_call_target="tpu_custom_call" | custom-call | tf_op jit(solution)/shard_map/gram/pallas_call | solution.py:412
  23.4 4.2 %collective-permute-start.6 = (f32[96,128]{1,0:T(8,128)S(1)}, f32[96,128]{1,0:T(8,128)S(1)}, u32[]{:S(2)}, u32[]{:S(2)}) collective-permute-start(f32[96,128]{1,0:T(8,128)S(1)} %slice_select_fusion), channel_id=1, source_target_pairs={{0,1},{1,0},{2,3},{3,2},{4,5},{5,4},{6,7},{7,6},{8,9},{9,8},{10,11... | collective-permute-start | bytes 147464 | tf_op jit(solution)/shard_map/ppermute | solution.py:435
  27.6 0.9 %collective-permute-done.6 = f32[96,128]{1,0:T(8,128)S(1)} collective-permute-done((f32[96,128]{1,0:T(8,128)S(1)}, f32[96,128]{1,0:T(8,128)S(1)}, u32[]{:S(2)}, u32[]{:S(2)}) %collective-permute-start.6) | collective-permute-done | bytes 49184 | tf_op jit(solution)/shard_map/ppermute | solution.py:435
  28.5 1.5 %collective-permute-start.7 = (f32[96,128]{1,0:T(8,128)S(1)}, f32[96,128]{1,0:T(8,128)S(1)}, u32[]{:S(2)}, u32[]{:S(2)}) collective-permute-start(f32[96,128]{1,0:T(8,128)S(1)} %select_add_fusion), channel_id=1, source_target_pairs={{0,9},{1,8},{2,11},{3,10},{4,13},{5,12},{6,15},{7,14},{8,1},{9,0},... | collective-permute-start | bytes 147464 | tf_op jit(solution)/shard_map/ppermute | solution.py:435
  30.0 2.1 %collective-permute-done.7 = f32[96,128]{1,0:T(8,128)S(1)} collective-permute-done((f32[96,128]{1,0:T(8,128)S(1)}, f32[96,128]{1,0:T(8,128)S(1)}, u32[]{:S(2)}, u32[]{:S(2)}) %collective-permute-start.7) | collective-permute-done | bytes 49184 | tf_op jit(solution)/shard_map/ppermute | solution.py:435
  32.1 1.7 %collective-permute-start.8 = (f32[96,128]{1,0:T(8,128)S(1)}, f32[96,128]{1,0:T(8,128)S(1)}, u32[]{:S(2)}, u32[]{:S(2)}) collective-permute-start(f32[96,128]{1,0:T(8,128)S(1)} %add.16), channel_id=1, source_target_pairs={{0,17},{1,16},{2,19},{3,18},{4,21},{5,20},{6,23},{7,22},{8,25},{9,... | collective-permute-start | bytes 147464 | tf_op jit(solution)/shard_map/ppermute | solution.py:435
  33.8 1.9 %collective-permute-done.8 = f32[96,128]{1,0:T(8,128)S(1)} collective-permute-done((f32[96,128]{1,0:T(8,128)S(1)}, f32[96,128]{1,0:T(8,128)S(1)}, u32[]{:S(2)}, u32[]{:S(2)}) %collective-permute-start.8) | collective-permute-done | bytes 49184 | tf_op jit(solution)/shard_map/ppermute | solution.py:435
  35.7 2.8 %collective-permute-start.9 = (f32[96,128]{1,0:T(8,128)S(1)}, f32[96,128]{1,0:T(8,128)S(1)}, u32[]{:S(2)}, u32[]{:S(2)}) collective-permute-start(f32[96,128]{1,0:T(8,128)S(1)} %add.17), channel_id=1, source_target_pairs={{0,3},{1,2},{2,1},{3,0},{4,7},{5,6},{6,5},{7,4},{8,11},{9,10},{10,... | collective-permute-start | bytes 147464 | tf_op jit(solution)/shard_map/ppermute | solution.py:435
  38.5 2.0 %local_factor.3 = (f32[64,192]{1,0:T(8,128)S(1)}, f32[128,128]{1,0:T(8,128)S(1)}) custom-call(f32[192,128]{1,0:T(8,128)S(1)} %gram.1), custom_call_target="tpu_custom_call" | custom-call | flops 1000000000 | bytes 1000000 | tf_op jit(solution)/shard_map/local_factor/pallas_call | solution.py:412
  40.4 0.0 collective-permute-done.9
  40.5 2.8 %collective-permute-start.10 = (f32[96,128]{1,0:T(8,128)S(1)}, f32[96,128]{1,0:T(8,128)S(1)}, u32[]{:S(2)}, u32[]{:S(2)}) collective-permute-start(f32[96,128]{1,0:T(8,128)S(1)} %add.18), channel_id=1, source_target_pairs={{0,5},{1,4},{2,7},{3,6},{4,1},{5,0},{6,3},{7,2},{8,13},{9,12},{10,... | collective-permute-start | bytes 147464 | tf_op jit(solution)/shard_map/ppermute | solution.py:435
  43.2 1.9 %local_factor.4 = (f32[64,128]{1,0:T(8,128)S(1)}, f32[64,64]{1,0:T(8,128)S(1)}) custom-call(f32[128,128]{1,0:T(8,128)S(1)} %get-tuple-element.27.gram), custom_call_target="tpu_custom_call" | custom-call | flops 1000000000 | bytes 1000000 | tf_op jit(solution)/shard_map/local_factor/pallas_call | solution.py:412
  45.2 0.0 collective-permute-done.10
  45.2 0.4 collective-permute-start.11
  45.6 1.3 %local_factor.5.refs_2_ = f32[64,64]{1,0:T(8,128)S(1)} custom-call(f32[64,64]{1,0:T(8,128)S(1)} %get-tuple-element.29.gram), custom_call_target="tpu_custom_call" | custom-call | flops 1000000000 | bytes 1000000 | tf_op jit(solution)/shard_map/local_factor/pallas_call | solution.py:412
  46.9 0.0 collective-permute-done.11.other_ref
  46.9 6.2 %factor.1 = (f32[192,192]{1,0:T(8,128)}, f32[1,192]{1,0:T(1,128)}) custom-call(f32[96,128]{1,0:T(8,128)S(1)} %add.19.own_ref, f32[96,128]{1,0:T(8,128)S(1)} %collective-permute-done.11.other_ref, f32[64,192]{1,0:T(8,128)S(1)} %get-tuple-element.26.refs_0_, f32[64,128]{1,0:T(8,128)S(1)} %get-tuple-element.28.refs_1_, f32[64,64]{1,0:T(8,128)S(1)} %local_factor.5.refs_2_), custom_call_target="tpu_custom_call" | custom-call | tf_op jit(solution)/shard_map/factor/pallas_call | solution.py:412
  (6 shorter events, 0.0 us)
Async XLA Ops:
  0.6 14.9 %copy-start = (f32[2,192,8,128]{3,2,1,0:T(8,128)S(1)}, f32[2,192,8,128]{3,2,1,0:T(8,128)}, u32[]{:S(2)}) copy-start(f32[2,192,8,128]{3,2,1,0:T(8,128)} %param.3) | copy-start | bytes 4718596
  4.4 6.6 %collective-permute-start = (f32[4,200,128]{2,1,0:T(8,128)S(1)}, f32[4,200,128]{2,1,0:T(8,128)S(1)}, u32[]{:S(2)}, u32[]{:S(2)}) collective-permute-start(f32[4,200,128]{2,1,0:T(8,128)S(1)} %get-tuple-element.17), channel_id=1, source_target_pairs={{0,1},{2,3},{4,5},{6,7},{1,0},{3,2},{5,4},{7,6},{8,9},{10,11},{12,... | collective-permute-start | bytes 1228808 | tf_op jit(solution)/shard_map/ppermute | solution.py:429
  4.9 6.1 %collective-permute-start.1 = (f32[4,200,128]{2,1,0:T(8,128)S(1)}, f32[4,200,128]{2,1,0:T(8,128)S(1)}, u32[]{:S(2)}, u32[]{:S(2)}) collective-permute-start(f32[4,200,128]{2,1,0:T(8,128)S(1)} %get-tuple-element.18), channel_id=1, source_target_pairs={{1,2},{3,4},{5,6},{2,1},{4,3},{6,5},{9,10},{11,12},{13,14},{10,9},... | collective-permute-start | bytes 1228808 | tf_op jit(solution)/shard_map/ppermute | solution.py:429
  5.6 10.0 %collective-permute-start.2 = (f32[4,200,128]{2,1,0:T(8,128)}, f32[4,200,128]{2,1,0:T(8,128)S(1)}, u32[]{:S(2)}, u32[]{:S(2)}) collective-permute-start(f32[4,200,128]{2,1,0:T(8,128)} %get-tuple-element.19), channel_id=1, source_target_pairs={{0,1},{2,3},{4,5},{6,7},{1,0},{3,2},{5,4},{7,6},{8,9},{10,11},{12,... | collective-permute-start | bytes 1228808 | tf_op jit(solution)/shard_map/ppermute | solution.py:429
  9.6 6.0 %collective-permute-start.3 = (f32[4,200,128]{2,1,0:T(8,128)}, f32[4,200,128]{2,1,0:T(8,128)}, u32[]{:S(2)}, u32[]{:S(2)}) collective-permute-start(f32[4,200,128]{2,1,0:T(8,128)} %get-tuple-element.20), channel_id=1, source_target_pairs={{1,2},{3,4},{5,6},{2,1},{4,3},{6,5},{9,10},{11,12},{13,14},{10,9},... | collective-permute-start | bytes 1228808 | tf_op jit(solution)/shard_map/ppermute | solution.py:429
  12.6 7.9 %collective-permute-start.4 = (f32[200,128]{1,0:T(8,128)}, f32[200,128]{1,0:T(8,128)S(1)}, u32[]{:S(2)}, u32[]{:S(2)}) collective-permute-start(f32[200,128]{1,0:T(8,128)} %get-tuple-element.24), channel_id=1, source_target_pairs={{0,8},{16,24},{8,0},{24,16},{1,9},{17,25},{9,1},{25,17},{2,10},{18... | collective-permute-start | bytes 307208 | tf_op jit(solution)/shard_map/ppermute | solution.py:429
  14.1 6.4 %collective-permute-start.5 = (f32[200,128]{1,0:T(8,128)S(1)}, f32[200,128]{1,0:T(8,128)S(1)}, u32[]{:S(2)}, u32[]{:S(2)}) collective-permute-start(f32[200,128]{1,0:T(8,128)S(1)} %get-tuple-element.25), channel_id=1, source_target_pairs={{8,16},{0,24},{16,8},{24,0},{9,17},{1,25},{17,9},{25,1},{10,18},{2... | collective-permute-start | bytes 307208 | tf_op jit(solution)/shard_map/ppermute | solution.py:429
  23.4 5.1 %collective-permute-start.6 = (f32[96,128]{1,0:T(8,128)S(1)}, f32[96,128]{1,0:T(8,128)S(1)}, u32[]{:S(2)}, u32[]{:S(2)}) collective-permute-start(f32[96,128]{1,0:T(8,128)S(1)} %slice_select_fusion), channel_id=1, source_target_pairs={{0,1},{1,0},{2,3},{3,2},{4,5},{5,4},{6,7},{7,6},{8,9},{9,8},{10,11... | collective-permute-start | bytes 147464 | tf_op jit(solution)/shard_map/ppermute | solution.py:435
  28.5 3.6 %collective-permute-start.7 = (f32[96,128]{1,0:T(8,128)S(1)}, f32[96,128]{1,0:T(8,128)S(1)}, u32[]{:S(2)}, u32[]{:S(2)}) collective-permute-start(f32[96,128]{1,0:T(8,128)S(1)} %select_add_fusion), channel_id=1, source_target_pairs={{0,9},{1,8},{2,11},{3,10},{4,13},{5,12},{6,15},{7,14},{8,1},{9,0},... | collective-permute-start | bytes 147464 | tf_op jit(solution)/shard_map/ppermute | solution.py:435
  32.1 3.6 %collective-permute-start.8 = (f32[96,128]{1,0:T(8,128)S(1)}, f32[96,128]{1,0:T(8,128)S(1)}, u32[]{:S(2)}, u32[]{:S(2)}) collective-permute-start(f32[96,128]{1,0:T(8,128)S(1)} %add.16), channel_id=1, source_target_pairs={{0,17},{1,16},{2,19},{3,18},{4,21},{5,20},{6,23},{7,22},{8,25},{9,... | collective-permute-start | bytes 147464 | tf_op jit(solution)/shard_map/ppermute | solution.py:435
  35.7 4.8 %collective-permute-start.9 = (f32[96,128]{1,0:T(8,128)S(1)}, f32[96,128]{1,0:T(8,128)S(1)}, u32[]{:S(2)}, u32[]{:S(2)}) collective-permute-start(f32[96,128]{1,0:T(8,128)S(1)} %add.17), channel_id=1, source_target_pairs={{0,3},{1,2},{2,1},{3,0},{4,7},{5,6},{6,5},{7,4},{8,11},{9,10},{10,... | collective-permute-start | bytes 147464 | tf_op jit(solution)/shard_map/ppermute | solution.py:435
  40.5 4.7 %collective-permute-start.10 = (f32[96,128]{1,0:T(8,128)S(1)}, f32[96,128]{1,0:T(8,128)S(1)}, u32[]{:S(2)}, u32[]{:S(2)}) collective-permute-start(f32[96,128]{1,0:T(8,128)S(1)} %add.18), channel_id=1, source_target_pairs={{0,5},{1,4},{2,7},{3,6},{4,1},{5,0},{6,3},{7,2},{8,13},{9,12},{10,... | collective-permute-start | bytes 147464 | tf_op jit(solution)/shard_map/ppermute | solution.py:435
  45.2 1.7 %collective-permute-start.11 = (f32[96,128]{1,0:T(8,128)S(1)}, f32[96,128]{1,0:T(8,128)S(1)}, u32[]{:S(2)}, u32[]{:S(2)}) collective-permute-start(f32[96,128]{1,0:T(8,128)S(1)} %add.19.own_ref), channel_id=1, source_target_pairs={{0,1},{1,0},{2,3},{3,2},{4,5},{5,4},{6,7},{7,6},{8,9},{9,8},{10,11... | collective-permute-start | bytes 147464 | tf_op jit(solution)/shard_map/ppermute | solution.py:435

commit v7 on v6

--- a/solution.py
+++ b/solution.py
@@ -14,7 +14,7 @@
 slow_rate = 0.05
 HEIGHT_EDGE = 96
 HEIGHT_STRIP = 192
-HEIGHT_EVOLVE = 48
+HEIGHT_EVOLVE = 24
 SIDE = 64
 VMEM_BYTES = 24 * 1024 * 1024
 LOCAL_COST = pl.CostEstimate(flops=10**9, bytes_accessed=10**6, transcendentals=0)
@@ -384,8 +384,7 @@
         for r in range(1 - STEPS, SUB + STEPS - 1):
             row_coeffs[f, r + STEPS - 1, :, :] = coeff_rows[f][r] + (1.0 - 4.0 * diffusion) * (1 - f)
 
-    @pl.loop(0, fields // height)
-    def _(g):
+    for g in range(fields // height):
         at = chunk(g, height)
         fast, slow = extended_rows(own_rows(tangents, g, height), near, far, near_fast, far_fast, at)
         for step in range(1, STEPS + 1):
@@ -444,7 +443,7 @@
     return (bits & 1) == 1
 
 
-def sum_blocks(packed):
+def sum_blocks(packed, beside):
     half = packed.shape[0] // 2
     high_half = parity()
     low, high = packed[:half], packed[half:]
@@ -452,9 +451,11 @@
     for axis in ("grp", "tile"):
         bit = 1 if axis == "grp" else 2
         while bit < lax.axis_size(axis):
+            if axis == "tile" and 2 * bit >= lax.axis_size(axis):
+                part, beside = lax.optimization_barrier((part, beside))
             part = part + (exchange(part, bit, 1) if axis == "grp" else exchange(part, 0, bit + 1))
             bit *= 2
-    return part, exchange(part, 0, 1)
+    return part, exchange(part, 0, 1), beside
 
 
 def per_device(tangents, reaction_self, reaction_cross):
@@ -486,7 +487,7 @@
         [(2,) + strip, (fields, LANES)], middle_gram, strips, near_cols, far_cols,
     )
     block_total = lax.axis_size("grp") * lax.axis_size("tile")
-    corrections, growth = factor_call(*sum_blocks(packed), local_factor(packed, side_blocks), fields, math.sqrt(block_total))
+    corrections, growth = factor_call(*sum_blocks(packed, local_factor(packed, side_blocks)), fields, math.sqrt(block_total))
     return (corrections, growth)
 
 

time: 53.3 us -> 52.7 us (0.989)
  waiting for transfers between devices: 4.93 us -> 4.29 us
    ppermute x6, waiting for transfers between devices: 4.92 us -> 4.27 us  [exchange(): return lax.ppermute(cells, ('grp', 'tile'), moves)]
  transfers between devices with their start and end apart: 12 -> 12, of which waited for: 3 -> 5; matrix products, arithmetic and copies ran while one was open for 0% -> 0% of each run, Pallas kernels for 22% -> 22%
where the time goes in v7:
time: 52.7 us; the launch traced here: 52.5 us
  Pallas kernels  23.3 us (44%)
  starting transfers between devices  23.3 us (44%)
  waiting for transfers between devices  4.29 us (8%)
  other arithmetic  0.87 us (2%)
  between operations  0.72 us (1%)
    pallas_call x8, Pallas kernels, local_call(): pl.pallas_call(body, out_shape=[jax.ShapeDtypeStruct(s, jnp.float32) for...  23.3 us
    ppermute x6, starting transfers between devices, exchange(): return lax.ppermute(cells, ('grp', 'tile'), moves)  13.7 us
    ppermute x6, starting transfers between devices, swap(): return lax.ppermute(cells, axis, pairs + [(b, a) for a, b in pairs])  9.6 us
    ppermute x6, waiting for transfers between devices, exchange(): return lax.ppermute(cells, ('grp', 'tile'), moves)  4.27 us
  transfers between devices with their start and end apart: 12, of which 5 were waited for; matrix products, arithmetic and copies ran while one was open for 0% of the time, Pallas kernels for 22%

profile of v7, /device:TPU:0, one launch (start us, length us, event | category | flops | bytes accessed | tf_op | source)
XLA Modules:
  0.0 52.5 jit_solution(9382471025538821514)
XLA Ops:
  0.6 0.0 copy-start
  0.6 0.8 %pad_maximum_fusion.coeffs_hbm.coeffs = f32[2,8,128]{2,1,0:T(8,128)S(1)} fusion(f32[1,8,128]{2,1,0:T(8,128)} %bitcast.6, f32[1,8,128]{2,1,0:T(8,128)} %bitcast.7), kind=kLoop, calls=%fused_computation.2 | loop fusion | flops 2048 | bytes 16384 | tf_op jit(solution)/shard_map/stack | solution.py:466
  1.5 2.9 %edges.1 = (f32[200,128]{1,0:T(8,128)S(1)}, f32[200,128]{1,0:T(8,128)S(1)}, f32[4,200,128]{2,1,0:T(8,128)S(1)}, f32[4,200,128]{2,1,0:T(8,128)S(1)}, f32[4,200,128]{2,1,0:T(8,128)}, /*index=5*/f32[4,200,128]{2,1,0:T(8,128)}) custom-call(f32[2,1536,128]{2,1,0:T(8,128)} %bitcast.4, f32[2,8,128]{2,1,0:T(8,128)S(1)} %pad_maximum_fusion.coeffs_hbm.coeffs), custom_call_target="tpu_custom_call" | custom-call | tf_op jit(solution)/shard_map/edges/pallas_call | solution.py:411
  4.4 0.5 collective-permute-start
  4.9 0.7 %collective-permute-start.1 = (f32[4,200,128]{2,1,0:T(8,128)S(1)}, f32[4,200,128]{2,1,0:T(8,128)S(1)}, u32[]{:S(2)}, u32[]{:S(2)}) collective-permute-start(f32[4,200,128]{2,1,0:T(8,128)S(1)} %get-tuple-element.22), channel_id=1, source_target_pairs={{1,2},{3,4},{5,6},{2,1},{4,3},{6,5},{9,10},{11,12},{13,14},{10,9},... | collective-permute-start | bytes 1228808 | tf_op jit(solution)/shard_map/ppermute | solution.py:428
  5.6 4.0 %collective-permute-start.2 = (f32[4,200,128]{2,1,0:T(8,128)}, f32[4,200,128]{2,1,0:T(8,128)S(1)}, u32[]{:S(2)}, u32[]{:S(2)}) collective-permute-start(f32[4,200,128]{2,1,0:T(8,128)} %get-tuple-element.23), channel_id=1, source_target_pairs={{0,1},{2,3},{4,5},{6,7},{1,0},{3,2},{5,4},{7,6},{8,9},{10,11},{12,... | collective-permute-start | bytes 1228808 | tf_op jit(solution)/shard_map/ppermute | solution.py:428
  9.6 1.4 %collective-permute-start.3 = (f32[4,200,128]{2,1,0:T(8,128)}, f32[4,200,128]{2,1,0:T(8,128)}, u32[]{:S(2)}, u32[]{:S(2)}) collective-permute-start(f32[4,200,128]{2,1,0:T(8,128)} %get-tuple-element.24), channel_id=1, source_target_pairs={{1,2},{3,4},{5,6},{2,1},{4,3},{6,5},{9,10},{11,12},{13,14},{10,9},... | collective-permute-start | bytes 1228808 | tf_op jit(solution)/shard_map/ppermute | solution.py:428
  11.0 0.0 collective-permute-done.near
  11.0 0.0 collective-permute-done.1.far
  11.0 1.5 %columns.1 = (f32[4,200,128]{2,1,0:T(8,128)S(1)}, f32[200,128]{1,0:T(8,128)}, f32[200,128]{1,0:T(8,128)S(1)}) custom-call(f32[200,128]{1,0:T(8,128)S(1)} %get-tuple-element.25.last, f32[200,128]{1,0:T(8,128)S(1)} %get-tuple-element.26.first, f32[4,200,128]{2,1,0:T(8,128)S(1)} %collective-permute-done.near, f32[4,200,128]{2,1,0:T(8,128)S(1)} %collective-permute-done.1.far), custom_call_target="tpu_custom_call" | custom-call | tf_op jit(solution)/shard_map/columns/pallas_call | solution.py:411
  12.6 1.5 %collective-permute-start.4 = (f32[200,128]{1,0:T(8,128)}, f32[200,128]{1,0:T(8,128)S(1)}, u32[]{:S(2)}, u32[]{:S(2)}) collective-permute-start(f32[200,128]{1,0:T(8,128)} %get-tuple-element.28), channel_id=1, source_target_pairs={{0,8},{16,24},{8,0},{24,16},{1,9},{17,25},{9,1},{25,17},{2,10},{18... | collective-permute-start | bytes 307208 | tf_op jit(solution)/shard_map/ppermute | solution.py:428
  14.1 1.5 %collective-permute-start.5 = (f32[200,128]{1,0:T(8,128)S(1)}, f32[200,128]{1,0:T(8,128)S(1)}, u32[]{:S(2)}, u32[]{:S(2)}) collective-permute-start(f32[200,128]{1,0:T(8,128)S(1)} %get-tuple-element.29), channel_id=1, source_target_pairs={{8,16},{0,24},{16,8},{24,0},{9,17},{1,25},{17,9},{25,1},{10,18},{2... | collective-permute-start | bytes 307208 | tf_op jit(solution)/shard_map/ppermute | solution.py:428
  15.5 0.0 collective-permute-done.2.near_fast
  15.5 0.0 collective-permute-done.3.far_fast
  15.6 0.0 copy-done
  15.6 4.6 %evolve.1.middle_gram = f32[192,192]{1,0:T(8,128)S(1)} custom-call(f32[2,1536,128]{2,1,0:T(8,128)S(1)} %bitcast.5, f32[2,8,128]{2,1,0:T(8,128)S(1)} %pad_maximum_fusion.coeffs_hbm.coeffs, f32[4,200,128]{2,1,0:T(8,128)S(1)} %collective-permute-done.near, f32[4,200,128]{2,1,0:T(8,128)S(1)} %collective-permute-done.1.far, ...), custom_call_target="tpu_custom_call" | custom-call | tf_op jit(solution)/shard_map/evolve/pallas_call | solution.py:411
  20.2 0.0 collective-permute-done.4.near
  20.2 0.0 collective-permute-done.5.far
  20.2 2.9 %gram.1 = f32[192,128]{1,0:T(8,128)S(1)} custom-call(f32[192,192]{1,0:T(8,128)S(1)} %evolve.1.middle_gram, f32[4,200,128]{2,1,0:T(8,128)S(1)} %get-tuple-element.27.strips, f32[200,128]{1,0:T(8,128)S(1)} %collective-permute-done.4.near, f32[200,128]{1,0:T(8,128)S(1)} %collective-permute-done.5.far), custom_call_target="tpu_custom_call" | custom-call | tf_op jit(solution)/shard_map/gram/pallas_call | solution.py:411
  23.1 4.2 %collective-permute-start.6 = (f32[96,128]{1,0:T(8,128)S(1)}, f32[96,128]{1,0:T(8,128)S(1)}, u32[]{:S(2)}, u32[]{:S(2)}) collective-permute-start(f32[96,128]{1,0:T(8,128)S(1)} %slice_select_fusion), channel_id=1, source_target_pairs={{0,1},{1,0},{2,3},{3,2},{4,5},{5,4},{6,7},{7,6},{8,9},{9,8},{10,11... | collective-permute-start | bytes 147464 | tf_op jit(solution)/shard_map/ppermute | solution.py:434
  27.4 0.9 %collective-permute-done.6 = f32[96,128]{1,0:T(8,128)S(1)} collective-permute-done((f32[96,128]{1,0:T(8,128)S(1)}, f32[96,128]{1,0:T(8,128)S(1)}, u32[]{:S(2)}, u32[]{:S(2)}) %collective-permute-start.6) | collective-permute-done | bytes 49184 | tf_op jit(solution)/shard_map/ppermute | solution.py:434
  28.3 1.5 %collective-permute-start.7 = (f32[96,128]{1,0:T(8,128)S(1)}, f32[96,128]{1,0:T(8,128)S(1)}, u32[]{:S(2)}, u32[]{:S(2)}) collective-permute-start(f32[96,128]{1,0:T(8,128)S(1)} %select_add_fusion), channel_id=1, source_target_pairs={{0,9},{1,8},{2,11},{3,10},{4,13},{5,12},{6,15},{7,14},{8,1},{9,0},... | collective-permute-start | bytes 147464 | tf_op jit(solution)/shard_map/ppermute | solution.py:434
  29.7 2.0 %local_factor.3 = (f32[64,192]{1,0:T(8,128)S(1)}, f32[128,128]{1,0:T(8,128)S(1)}) custom-call(f32[192,128]{1,0:T(8,128)S(1)} %gram.1), custom_call_target="tpu_custom_call" | custom-call | flops 1000000000 | bytes 1000000 | tf_op jit(solution)/shard_map/local_factor/pallas_call | solution.py:411
  31.7 0.1 collective-permute-done.7
  31.9 1.7 %collective-permute-start.8 = (f32[96,128]{1,0:T(8,128)S(1)}, f32[96,128]{1,0:T(8,128)S(1)}, u32[]{:S(2)}, u32[]{:S(2)}) collective-permute-start(f32[96,128]{1,0:T(8,128)S(1)} %add.16), channel_id=1, source_target_pairs={{0,17},{1,16},{2,19},{3,18},{4,21},{5,20},{6,23},{7,22},{8,25},{9,... | collective-permute-start | bytes 147464 | tf_op jit(solution)/shard_map/ppermute | solution.py:434
  33.6 1.9 %local_factor.4 = (f32[64,128]{1,0:T(8,128)S(1)}, f32[64,64]{1,0:T(8,128)S(1)}) custom-call(f32[128,128]{1,0:T(8,128)S(1)} %get-tuple-element.31.gram), custom_call_target="tpu_custom_call" | custom-call | flops 1000000000 | bytes 1000000 | tf_op jit(solution)/shard_map/local_factor/pallas_call | solution.py:411
  35.5 0.0 collective-permute-done.8
  35.5 2.9 %collective-permute-start.9 = (f32[96,128]{1,0:T(8,128)S(1)}, f32[96,128]{1,0:T(8,128)S(1)}, u32[]{:S(2)}, u32[]{:S(2)}) collective-permute-start(f32[96,128]{1,0:T(8,128)S(1)} %add.17), channel_id=1, source_target_pairs={{0,3},{1,2},{2,1},{3,0},{4,7},{5,6},{6,5},{7,4},{8,11},{9,10},{10,... | collective-permute-start | bytes 147464 | tf_op jit(solution)/shard_map/ppermute | solution.py:434
  38.5 1.3 %local_factor.5.refs_2_ = f32[64,64]{1,0:T(8,128)S(1)} custom-call(f32[64,64]{1,0:T(8,128)S(1)} %get-tuple-element.33.gram), custom_call_target="tpu_custom_call" | custom-call | flops 1000000000 | bytes 1000000 | tf_op jit(solution)/shard_map/local_factor/pallas_call | solution.py:411
  39.8 0.5 collective-permute-done.9
  40.3 3.0 %collective-permute-start.10 = (f32[96,128]{1,0:T(8,128)S(1)}, f32[96,128]{1,0:T(8,128)S(1)}, u32[]{:S(2)}, u32[]{:S(2)}) collective-permute-start(f32[96,128]{1,0:T(8,128)S(1)} %add.18), channel_id=1, source_target_pairs={{0,5},{1,4},{2,7},{3,6},{4,1},{5,0},{6,3},{7,2},{8,13},{9,12},{10,... | collective-permute-start | bytes 147464 | tf_op jit(solution)/shard_map/ppermute | solution.py:434
  43.2 1.8 %collective-permute-done.10 = f32[96,128]{1,0:T(8,128)S(1)} collective-permute-done((f32[96,128]{1,0:T(8,128)S(1)}, f32[96,128]{1,0:T(8,128)S(1)}, u32[]{:S(2)}, u32[]{:S(2)}) %collective-permute-start.10) | collective-permute-done | bytes 49184 | tf_op jit(solution)/shard_map/ppermute | solution.py:434
  45.1 0.3 collective-permute-start.11
  45.4 0.9 %collective-permute-done.11.other_ref = f32[96,128]{1,0:T(8,128)S(1)} collective-permute-done((f32[96,128]{1,0:T(8,128)S(1)}, f32[96,128]{1,0:T(8,128)S(1)}, u32[]{:S(2)}, u32[]{:S(2)}) %collective-permute-start.11) | collective-permute-done | bytes 49184 | tf_op jit(solution)/shard_map/ppermute | solution.py:434
  46.3 6.2 %factor.1 = (f32[192,192]{1,0:T(8,128)}, f32[1,192]{1,0:T(1,128)}) custom-call(f32[96,128]{1,0:T(8,128)S(1)} %add.19.own_ref, f32[96,128]{1,0:T(8,128)S(1)} %collective-permute-done.11.other_ref, f32[64,192]{1,0:T(8,128)S(1)} %get-tuple-element.35.refs_0_, f32[64,128]{1,0:T(8,128)S(1)} %get-tuple-element.36.refs_1_, f32[64,64]{1,0:T(8,128)S(1)} %local_factor.5.refs_2_), custom_call_target="tpu_custom_call" | custom-call | tf_op jit(solution)/shard_map/factor/pallas_call | solution.py:411
  (6 shorter events, 0.0 us)
Async XLA Ops:
  0.6 14.9 %copy-start = (f32[2,192,8,128]{3,2,1,0:T(8,128)S(1)}, f32[2,192,8,128]{3,2,1,0:T(8,128)}, u32[]{:S(2)}) copy-start(f32[2,192,8,128]{3,2,1,0:T(8,128)} %param.3) | copy-start | bytes 4718596
  4.4 6.6 %collective-permute-start = (f32[4,200,128]{2,1,0:T(8,128)S(1)}, f32[4,200,128]{2,1,0:T(8,128)S(1)}, u32[]{:S(2)}, u32[]{:S(2)}) collective-permute-start(f32[4,200,128]{2,1,0:T(8,128)S(1)} %get-tuple-element.21), channel_id=1, source_target_pairs={{0,1},{2,3},{4,5},{6,7},{1,0},{3,2},{5,4},{7,6},{8,9},{10,11},{12,... | collective-permute-start | bytes 1228808 | tf_op jit(solution)/shard_map/ppermute | solution.py:428
  4.9 6.1 %collective-permute-start.1 = (f32[4,200,128]{2,1,0:T(8,128)S(1)}, f32[4,200,128]{2,1,0:T(8,128)S(1)}, u32[]{:S(2)}, u32[]{:S(2)}) collective-permute-start(f32[4,200,128]{2,1,0:T(8,128)S(1)} %get-tuple-element.22), channel_id=1, source_target_pairs={{1,2},{3,4},{5,6},{2,1},{4,3},{6,5},{9,10},{11,12},{13,14},{10,9},... | collective-permute-start | bytes 1228808 | tf_op jit(solution)/shard_map/ppermute | solution.py:428
  5.6 10.0 %collective-permute-start.2 = (f32[4,200,128]{2,1,0:T(8,128)}, f32[4,200,128]{2,1,0:T(8,128)S(1)}, u32[]{:S(2)}, u32[]{:S(2)}) collective-permute-start(f32[4,200,128]{2,1,0:T(8,128)} %get-tuple-element.23), channel_id=1, source_target_pairs={{0,1},{2,3},{4,5},{6,7},{1,0},{3,2},{5,4},{7,6},{8,9},{10,11},{12,... | collective-permute-start | bytes 1228808 | tf_op jit(solution)/shard_map/ppermute | solution.py:428
  9.6 6.0 %collective-permute-start.3 = (f32[4,200,128]{2,1,0:T(8,128)}, f32[4,200,128]{2,1,0:T(8,128)}, u32[]{:S(2)}, u32[]{:S(2)}) collective-permute-start(f32[4,200,128]{2,1,0:T(8,128)} %get-tuple-element.24), channel_id=1, source_target_pairs={{1,2},{3,4},{5,6},{2,1},{4,3},{6,5},{9,10},{11,12},{13,14},{10,9},... | collective-permute-start | bytes 1228808 | tf_op jit(solution)/shard_map/ppermute | solution.py:428
  12.6 7.6 %collective-permute-start.4 = (f32[200,128]{1,0:T(8,128)}, f32[200,128]{1,0:T(8,128)S(1)}, u32[]{:S(2)}, u32[]{:S(2)}) collective-permute-start(f32[200,128]{1,0:T(8,128)} %get-tuple-element.28), channel_id=1, source_target_pairs={{0,8},{16,24},{8,0},{24,16},{1,9},{17,25},{9,1},{25,17},{2,10},{18... | collective-permute-start | bytes 307208 | tf_op jit(solution)/shard_map/ppermute | solution.py:428
  14.1 6.1 %collective-permute-start.5 = (f32[200,128]{1,0:T(8,128)S(1)}, f32[200,128]{1,0:T(8,128)S(1)}, u32[]{:S(2)}, u32[]{:S(2)}) collective-permute-start(f32[200,128]{1,0:T(8,128)S(1)} %get-tuple-element.29), channel_id=1, source_target_pairs={{8,16},{0,24},{16,8},{24,0},{9,17},{1,25},{17,9},{25,1},{10,18},{2... | collective-permute-start | bytes 307208 | tf_op jit(solution)/shard_map/ppermute | solution.py:428
  23.1 5.1 %collective-permute-start.6 = (f32[96,128]{1,0:T(8,128)S(1)}, f32[96,128]{1,0:T(8,128)S(1)}, u32[]{:S(2)}, u32[]{:S(2)}) collective-permute-start(f32[96,128]{1,0:T(8,128)S(1)} %slice_select_fusion), channel_id=1, source_target_pairs={{0,1},{1,0},{2,3},{3,2},{4,5},{5,4},{6,7},{7,6},{8,9},{9,8},{10,11... | collective-permute-start | bytes 147464 | tf_op jit(solution)/shard_map/ppermute | solution.py:434
  28.3 3.6 %collective-permute-start.7 = (f32[96,128]{1,0:T(8,128)S(1)}, f32[96,128]{1,0:T(8,128)S(1)}, u32[]{:S(2)}, u32[]{:S(2)}) collective-permute-start(f32[96,128]{1,0:T(8,128)S(1)} %select_add_fusion), channel_id=1, source_target_pairs={{0,9},{1,8},{2,11},{3,10},{4,13},{5,12},{6,15},{7,14},{8,1},{9,0},... | collective-permute-start | bytes 147464 | tf_op jit(solution)/shard_map/ppermute | solution.py:434
  31.9 3.7 %collective-permute-start.8 = (f32[96,128]{1,0:T(8,128)S(1)}, f32[96,128]{1,0:T(8,128)S(1)}, u32[]{:S(2)}, u32[]{:S(2)}) collective-permute-start(f32[96,128]{1,0:T(8,128)S(1)} %add.16), channel_id=1, source_target_pairs={{0,17},{1,16},{2,19},{3,18},{4,21},{5,20},{6,23},{7,22},{8,25},{9,... | collective-permute-start | bytes 147464 | tf_op jit(solution)/shard_map/ppermute | solution.py:434
  35.5 4.7 %collective-permute-start.9 = (f32[96,128]{1,0:T(8,128)S(1)}, f32[96,128]{1,0:T(8,128)S(1)}, u32[]{:S(2)}, u32[]{:S(2)}) collective-permute-start(f32[96,128]{1,0:T(8,128)S(1)} %add.17), channel_id=1, source_target_pairs={{0,3},{1,2},{2,1},{3,0},{4,7},{5,6},{6,5},{7,4},{8,11},{9,10},{10,... | collective-permute-start | bytes 147464 | tf_op jit(solution)/shard_map/ppermute | solution.py:434
  40.3 4.8 %collective-permute-start.10 = (f32[96,128]{1,0:T(8,128)S(1)}, f32[96,128]{1,0:T(8,128)S(1)}, u32[]{:S(2)}, u32[]{:S(2)}) collective-permute-start(f32[96,128]{1,0:T(8,128)S(1)} %add.18), channel_id=1, source_target_pairs={{0,5},{1,4},{2,7},{3,6},{4,1},{5,0},{6,3},{7,2},{8,13},{9,12},{10,... | collective-permute-start | bytes 147464 | tf_op jit(solution)/shard_map/ppermute | solution.py:434
  45.1 1.3 %collective-permute-start.11 = (f32[96,128]{1,0:T(8,128)S(1)}, f32[96,128]{1,0:T(8,128)S(1)}, u32[]{:S(2)}, u32[]{:S(2)}) collective-permute-start(f32[96,128]{1,0:T(8,128)S(1)} %add.19.own_ref), channel_id=1, source_target_pairs={{0,1},{1,0},{2,3},{3,2},{4,5},{5,4},{6,7},{7,6},{8,9},{9,8},{10,11... | collective-permute-start | bytes 147464 | tf_op jit(solution)/shard_map/ppermute | solution.py:434

commit v8 on v7

--- a/solution.py
+++ b/solution.py
@@ -13,7 +13,7 @@
 diffusion = 0.2
 slow_rate = 0.05
 HEIGHT_EDGE = 96
-HEIGHT_STRIP = 192
+HEIGHT_STRIP = 8
 HEIGHT_EVOLVE = 24
 SIDE = 64
 VMEM_BYTES = 24 * 1024 * 1024
@@ -254,7 +254,25 @@
     send(pl.ds(fields, SUB), own_coeffs(coeffs))
 
 
-def column_kernel(last, first, near, far, strips, near_out, far_out, outer):
+def row_mirror_kernel(last, first, mirrored):
+    tile, tiles = lax.axis_index("tile"), lax.axis_size("tile")
+
+    @pl.when((tile == 0) | (tile == tiles - 1))
+    def _():
+        for i, ref in enumerate((last, first)):
+            own = ref[...]
+            cell = lane_index(own) // SUB % SUB
+            turned = roll(own, -7 * SUB)
+            for s in range(1, SUB):
+                turned = jnp.where(cell == s, roll(own, (2 * s - 7) * SUB), turned)
+            mirrored[i] = turned
+
+    @pl.when((tile != 0) & (tile != tiles - 1))
+    def _():
+        mirrored[...] = jnp.zeros(mirrored.shape, jnp.float32)
+
+
+def column_kernel(last, first, mirrored, near, far, strips, near_out, far_out):
     tile, tiles = lax.axis_index("tile"), lax.axis_size("tile")
     odd, at_top, at_bottom = tile % 2 == 1, tile == 0, tile == tiles - 1
     grp_odd = lax.axis_index("grp") % 2 == 1
@@ -263,22 +281,11 @@
     cell, low, inner = lane // SUB % SUB, lane < LANES // 2, lane % SUB < STEPS
     half = cell < STEPS
     above, below = pick(odd, one, two), pick(odd, two, one)
-    outer[0] = jnp.where(half, below, roll(above, STEPS * SUB))
-    outer[1] = jnp.where(half, roll(below, -STEPS * SUB), above)
-
-    @pl.when(at_top | at_bottom)
-    def _():
-        outside = (half & at_bottom) | (~half & at_top)
-        for i, ref in enumerate((last, first)):
-            own = ref[...]
-            mirrored = roll(own, -7 * SUB)
-            for s in range(1, SUB):
-                mirrored = jnp.where(cell == s, roll(own, (2 * s - 7) * SUB), mirrored)
-            outer[i] = jnp.where(outside, mirrored, outer[i])
-
+    outside = (half & at_bottom) | (~half & at_top)
+    received = (jnp.where(half, below, roll(above, STEPS * SUB)), jnp.where(half, roll(below, -STEPS * SUB), above))
     sides = []
     for i, ref in enumerate((last, first)):
-        own, more = ref[...], outer[i]
+        own, more = ref[...], jnp.where(outside, mirrored[i], received[i])
         fast = jnp.where(low, own, roll(more, LANES // 2))
         slow = jnp.where(low, roll(own, LANES // 2), more)
         strips[2 * i] = fast
@@ -314,7 +321,26 @@
     return (1.0 - slow_rate) * slow + slow_rate * fast
 
 
-def gram_kernel(fields, height, middle_gram, strips, near, far, gram, halo, ends):
+def column_mirror_kernel(strips, mirrored):
+    grp, grps = lax.axis_index("grp"), lax.axis_size("grp")
+
+    @pl.when((grp == 0) | (grp == grps - 1))
+    def _():
+        for f in range(2):
+            tail, start = strips[f], strips[2 + f]
+            c = lane_index(tail) % SUB
+            turned = roll(tail, -7)
+            for s in range(STEPS):
+                turned = jnp.where(c == s, roll(tail, 2 * s - 7), turned)
+                turned = jnp.where(c == 7 - s, roll(start, 7 - 2 * s), turned)
+            mirrored[f] = turned
+
+    @pl.when((grp != 0) & (grp != grps - 1))
+    def _():
+        mirrored[...] = jnp.zeros(mirrored.shape, jnp.float32)
+
+
+def gram_kernel(fields, height, middle_gram, strips, mirrored, near, far, gram, halo, ends):
     grp, grps = lax.axis_index("grp"), lax.axis_size("grp")
     grp_odd = grp % 2 == 1
     one, two = near[...], far[...]
@@ -322,38 +348,27 @@
     c = lane % SUB
     inner = c < STEPS
     left, right = pick(grp_odd, one, two), pick(grp_odd, two, one)
-    halo[0] = jnp.where(inner, right, roll(left, STEPS))
-    halo[1] = jnp.where(inner, roll(right, -STEPS), left)
-
-    @pl.when((grp == 0) | (grp == grps - 1))
-    def _():
-        after, before = inner & (grp == grps - 1), ~inner & (grp == 0)
-        for f in range(2):
-            tail, start = strips[f], strips[2 + f]
-            mirrored = halo[f]
-            for s in range(STEPS):
-                mirrored = jnp.where(after & (c == s), roll(tail, 2 * s - 7), mirrored)
-                mirrored = jnp.where(before & (c == 7 - s), roll(start, 7 - 2 * s), mirrored)
-            halo[f] = mirrored
+    outside = (inner & (grp == grps - 1)) | (~inner & (grp == 0))
+    halo[0] = jnp.where(outside, mirrored[0], jnp.where(inner, right, roll(left, STEPS)))
+    halo[1] = jnp.where(outside, mirrored[1], jnp.where(inner, roll(right, -STEPS), left))
 
     def parts(f, at):
         return [strips[f, at, :], strips[2 + f, at, :], halo[f, at, :]]
 
     gains = [tall(x + (1.0 - 4.0 * diffusion), height) for x in parts(0, pl.ds(fields, SUB))]
     crosses = [tall(x, height) for x in parts(1, pl.ds(fields, SUB))]
-
-    @pl.loop(0, fields // height)
-    def _(g):
-        fast, slow = parts(0, chunk(g, height)), parts(1, chunk(g, height))
-        for step in range(STEPS):
-            wanted = 3 if step + 1 < STEPS else 2
+    places = [pl.ds(at, height) for at in range(0, fields, height)]
+    held = [(parts(0, at), parts(1, at)) for at in places]
+    for step in range(STEPS):
+        wanted = 3 if step + 1 < STEPS else 2
+        for i, (fast, slow) in enumerate(held):
             around = strip_neighbours(*fast, wanted)
             moved = [advance(fast[p], slow[p], around[p], gains[p], crosses[p]) for p in range(wanted)]
-            slow = [relax(fast[p], slow[p]) for p in range(wanted)]
-            fast = moved
-        l = lane_index(fast[0])
-        joined = [jnp.where(l % SUB < STEPS, s[1], s[0]) for s in (fast, slow)]
-        ends[chunk(g, height), :] = jnp.where(l < LANES // 2, joined[0], roll(joined[1], LANES // 2))
+            held[i] = (moved, [relax(fast[p], slow[p]) for p in range(wanted)])
+    for at, pair in zip(places, held):
+        l = lane_index(pair[0][0])
+        joined = [jnp.where(l % SUB < STEPS, side[1], side[0]) for side in pair]
+        ends[at, :] = jnp.where(l < LANES // 2, joined[0], roll(joined[1], LANES // 2))
 
     whole = middle_gram[...] + gram_of(ends[...])
     for index, (i, j) in enumerate(block_pairs(fields // SIDE)):
@@ -471,9 +486,11 @@
     )
     near, far = swap(near, "tile", 0), swap(far, "tile", 1)
     near_fast, far_fast = swap(near_fast, "tile", 0), swap(far_fast, "tile", 1)
+    (row_mirror,) = local_call(row_mirror_kernel, "row_mirror", [(2,) + strip], [], last, first)
     strips, near_cols, far_cols = local_call(
-        column_kernel, "columns", [(4,) + strip, strip, strip], [(2,) + strip], last, first, near, far
+        column_kernel, "columns", [(4,) + strip, strip, strip], [], last, first, row_mirror, near, far
     )
+    (column_mirror,) = local_call(column_mirror_kernel, "column_mirror", [(2,) + strip], [], strips)
     far_cols = swap(far_cols, "grp", 1, close=True)
     near_cols = swap(near_cols, "grp", 0)
     (middle_gram,) = local_call(
@@ -484,7 +501,7 @@
     blocks = side_blocks * (side_blocks + 1) // 2
     (packed,) = local_call(
         functools.partial(gram_kernel, fields, HEIGHT_STRIP), "gram", [((blocks + 1) // 2 * SIDE, 2 * SIDE)],
-        [(2,) + strip, (fields, LANES)], middle_gram, strips, near_cols, far_cols,
+        [(2,) + strip, (fields, LANES)], middle_gram, strips, column_mirror, near_cols, far_cols,
     )
     block_total = lax.axis_size("grp") * lax.axis_size("tile")
     corrections, growth = factor_call(*sum_blocks(packed, local_factor(packed, side_blocks)), fields, math.sqrt(block_total))

time: 52.7 us -> 51.8 us (0.983)
  starting transfers between devices: 23.3 us -> 22.5 us
    ppermute x6, starting transfers between devices: 13.7 us -> 12.9 us  [exchange(): return lax.ppermute(cells, ('grp', 'tile'), moves)]
    pallas_call x8 -> x10, Pallas kernels: 23.3 us -> 23 us  [local_call(): pl.pallas_call(body, out_shape=[jax.ShapeDtypeStruct(s, jnp.float32) for...]
  transfers between devices with their start and end apart: 12 -> 12, of which waited for: 5 -> 6; matrix products, arithmetic and copies ran while one was open for 0% -> 0% of each run, Pallas kernels for 22% -> 23%
where the time goes in v8:
time: 51.8 us; the launch traced here: 51.5 us
  Pallas kernels  23 us (44%)
  starting transfers between devices  22.5 us (43%)
  waiting for transfers between devices  4.48 us (9%)
  other arithmetic  0.75 us (1%)
  between operations  0.75 us (1%)
    pallas_call x10, Pallas kernels, local_call(): pl.pallas_call(body, out_shape=[jax.ShapeDtypeStruct(s, jnp.float32) for...  23 us
    ppermute x6, starting transfers between devices, exchange(): return lax.ppermute(cells, ('grp', 'tile'), moves)  12.9 us
    ppermute x6, starting transfers between devices, swap(): return lax.ppermute(cells, axis, pairs + [(b, a) for a, b in pairs])  9.6 us
    ppermute x6, waiting for transfers between devices, exchange(): return lax.ppermute(cells, ('grp', 'tile'), moves)  4.46 us
  transfers between devices with their start and end apart: 12, of which 6 were waited for; matrix products, arithmetic and copies ran while one was open for 0% of the time, Pallas kernels for 23%

profile of v8, /device:TPU:0, one launch (start us, length us, event | category | flops | bytes accessed | tf_op | source)
XLA Modules:
  0.0 51.5 jit_solution(15115775516478396294)
XLA Ops:
  0.6 0.7 %pad_maximum_fusion.coeffs_hbm.coeffs = f32[2,8,128]{2,1,0:T(8,128)S(1)} fusion(f32[1,8,128]{2,1,0:T(8,128)} %bitcast.6, f32[1,8,128]{2,1,0:T(8,128)} %bitcast.7), kind=kLoop, calls=%fused_computation.2 | loop fusion | flops 2048 | bytes 16384 | tf_op jit(solution)/shard_map/stack | solution.py:481
  1.3 0.0 copy-start
  1.3 3.0 %edges.1 = (f32[200,128]{1,0:T(8,128)S(1)}, f32[200,128]{1,0:T(8,128)S(1)}, f32[4,200,128]{2,1,0:T(8,128)S(1)}, f32[4,200,128]{2,1,0:T(8,128)S(1)}, f32[4,200,128]{2,1,0:T(8,128)}, /*index=5*/f32[4,200,128]{2,1,0:T(8,128)}) custom-call(f32[2,1536,128]{2,1,0:T(8,128)} %bitcast.4, f32[2,8,128]{2,1,0:T(8,128)S(1)} %pad_maximum_fusion.coeffs_hbm.coeffs), custom_call_target="tpu_custom_call" | custom-call | tf_op jit(solution)/shard_map/edges/pallas_call | solution.py:426
  4.4 0.5 %collective-permute-start = (f32[4,200,128]{2,1,0:T(8,128)S(1)}, f32[4,200,128]{2,1,0:T(8,128)S(1)}, u32[]{:S(2)}, u32[]{:S(2)}) collective-permute-start(f32[4,200,128]{2,1,0:T(8,128)S(1)} %get-tuple-element.21), channel_id=1, source_target_pairs={{0,1},{2,3},{4,5},{6,7},{1,0},{3,2},{5,4},{7,6},{8,9},{10,11},{12,... | collective-permute-start | bytes 1228808 | tf_op jit(solution)/shard_map/ppermute | solution.py:443
  4.9 0.7 %collective-permute-start.1 = (f32[4,200,128]{2,1,0:T(8,128)S(1)}, f32[4,200,128]{2,1,0:T(8,128)S(1)}, u32[]{:S(2)}, u32[]{:S(2)}) collective-permute-start(f32[4,200,128]{2,1,0:T(8,128)S(1)} %get-tuple-element.22), channel_id=1, source_target_pairs={{1,2},{3,4},{5,6},{2,1},{4,3},{6,5},{9,10},{11,12},{13,14},{10,9},... | collective-permute-start | bytes 1228808 | tf_op jit(solution)/shard_map/ppermute | solution.py:443
  5.6 4.0 %collective-permute-start.2 = (f32[4,200,128]{2,1,0:T(8,128)}, f32[4,200,128]{2,1,0:T(8,128)S(1)}, u32[]{:S(2)}, u32[]{:S(2)}) collective-permute-start(f32[4,200,128]{2,1,0:T(8,128)} %get-tuple-element.23), channel_id=1, source_target_pairs={{0,1},{2,3},{4,5},{6,7},{1,0},{3,2},{5,4},{7,6},{8,9},{10,11},{12,... | collective-permute-start | bytes 1228808 | tf_op jit(solution)/shard_map/ppermute | solution.py:443
  9.6 1.4 %collective-permute-start.3 = (f32[4,200,128]{2,1,0:T(8,128)}, f32[4,200,128]{2,1,0:T(8,128)}, u32[]{:S(2)}, u32[]{:S(2)}) collective-permute-start(f32[4,200,128]{2,1,0:T(8,128)} %get-tuple-element.24), channel_id=1, source_target_pairs={{1,2},{3,4},{5,6},{2,1},{4,3},{6,5},{9,10},{11,12},{13,14},{10,9},... | collective-permute-start | bytes 1228808 | tf_op jit(solution)/shard_map/ppermute | solution.py:443
  11.0 0.5 row_mirror.1.mirrored
  11.5 0.0 collective-permute-done.near
  11.5 0.0 collective-permute-done.1.far
  11.5 1.0 %columns.1 = (f32[4,200,128]{2,1,0:T(8,128)S(1)}, f32[200,128]{1,0:T(8,128)}, f32[200,128]{1,0:T(8,128)S(1)}) custom-call(f32[200,128]{1,0:T(8,128)S(1)} %get-tuple-element.25.last, f32[200,128]{1,0:T(8,128)S(1)} %get-tuple-element.26.first, f32[2,200,128]{2,1,0:T(8,128)S(1)} %row_mirror.1.mirrored, f32[4,200,128]{2,1,0:T(8,128)S(1)} %collective-permute-done.near, ...), custom_call_target="tpu_custom_call" | custom-call | tf_op jit(solution)/shard_map/columns/pallas_call | solution.py:426
  12.5 1.5 %collective-permute-start.4 = (f32[200,128]{1,0:T(8,128)}, f32[200,128]{1,0:T(8,128)S(1)}, u32[]{:S(2)}, u32[]{:S(2)}) collective-permute-start(f32[200,128]{1,0:T(8,128)} %get-tuple-element.28), channel_id=1, source_target_pairs={{0,8},{16,24},{8,0},{24,16},{1,9},{17,25},{9,1},{25,17},{2,10},{18... | collective-permute-start | bytes 307208 | tf_op jit(solution)/shard_map/ppermute | solution.py:443
  14.0 1.5 %collective-permute-start.5 = (f32[200,128]{1,0:T(8,128)S(1)}, f32[200,128]{1,0:T(8,128)S(1)}, u32[]{:S(2)}, u32[]{:S(2)}) collective-permute-start(f32[200,128]{1,0:T(8,128)S(1)} %get-tuple-element.29), channel_id=1, source_target_pairs={{8,16},{0,24},{16,8},{24,0},{9,17},{1,25},{17,9},{25,1},{10,18},{2... | collective-permute-start | bytes 307208 | tf_op jit(solution)/shard_map/ppermute | solution.py:443
  15.5 0.5 column_mirror.1.mirrored
  16.0 0.0 collective-permute-done.2.near_fast
  16.0 0.0 collective-permute-done.3.far_fast
  16.0 0.0 copy-done
  16.0 4.6 %evolve.1.middle_gram = f32[192,192]{1,0:T(8,128)S(1)} custom-call(f32[2,1536,128]{2,1,0:T(8,128)S(1)} %bitcast.5, f32[2,8,128]{2,1,0:T(8,128)S(1)} %pad_maximum_fusion.coeffs_hbm.coeffs, f32[4,200,128]{2,1,0:T(8,128)S(1)} %collective-permute-done.near, f32[4,200,128]{2,1,0:T(8,128)S(1)} %collective-permute-done.1.far, ...), custom_call_target="tpu_custom_call" | custom-call | tf_op jit(solution)/shard_map/evolve/pallas_call | solution.py:426
  20.7 0.0 collective-permute-done.4.near
  20.7 0.0 collective-permute-done.5.far
  20.7 2.0 %gram.1 = f32[192,128]{1,0:T(8,128)S(1)} custom-call(f32[192,192]{1,0:T(8,128)S(1)} %evolve.1.middle_gram, f32[4,200,128]{2,1,0:T(8,128)S(1)} %get-tuple-element.27.strips, f32[2,200,128]{2,1,0:T(8,128)S(1)} %column_mirror.1.mirrored, f32[200,128]{1,0:T(8,128)S(1)} %collective-permute-done.4.near, f32[200,128]{1,0:T(8,128)S(1)} %collective-permute-done.5.far), custom_call_target="tpu_custom_call" | custom-call | tf_op jit(solution)/shard_map/gram/pallas_call | solution.py:426
  22.7 3.7 %collective-permute-start.6 = (f32[96,128]{1,0:T(8,128)S(1)}, f32[96,128]{1,0:T(8,128)S(1)}, u32[]{:S(2)}, u32[]{:S(2)}) collective-permute-start(f32[96,128]{1,0:T(8,128)S(1)} %slice_select_fusion), channel_id=1, source_target_pairs={{0,1},{1,0},{2,3},{3,2},{4,5},{5,4},{6,7},{7,6},{8,9},{9,8},{10,11... | collective-permute-start | bytes 147464 | tf_op jit(solution)/shard_map/ppermute | solution.py:449
  26.4 0.9 %collective-permute-done.6 = f32[96,128]{1,0:T(8,128)S(1)} collective-permute-done((f32[96,128]{1,0:T(8,128)S(1)}, f32[96,128]{1,0:T(8,128)S(1)}, u32[]{:S(2)}, u32[]{:S(2)}) %collective-permute-start.6) | collective-permute-done | bytes 49184 | tf_op jit(solution)/shard_map/ppermute | solution.py:449
  27.3 2.0 %collective-permute-start.7 = (f32[96,128]{1,0:T(8,128)S(1)}, f32[96,128]{1,0:T(8,128)S(1)}, u32[]{:S(2)}, u32[]{:S(2)}) collective-permute-start(f32[96,128]{1,0:T(8,128)S(1)} %select_add_fusion), channel_id=1, source_target_pairs={{0,9},{1,8},{2,11},{3,10},{4,13},{5,12},{6,15},{7,14},{8,1},{9,0},... | collective-permute-start | bytes 147464 | tf_op jit(solution)/shard_map/ppermute | solution.py:449
  29.3 2.0 %local_factor.3 = (f32[64,192]{1,0:T(8,128)S(1)}, f32[128,128]{1,0:T(8,128)S(1)}) custom-call(f32[192,128]{1,0:T(8,128)S(1)} %gram.1), custom_call_target="tpu_custom_call" | custom-call | flops 1000000000 | bytes 1000000 | tf_op jit(solution)/shard_map/local_factor/pallas_call | solution.py:426
  31.3 0.1 collective-permute-done.7
  31.3 1.6 %collective-permute-start.8 = (f32[96,128]{1,0:T(8,128)S(1)}, f32[96,128]{1,0:T(8,128)S(1)}, u32[]{:S(2)}, u32[]{:S(2)}) collective-permute-start(f32[96,128]{1,0:T(8,128)S(1)} %add.16), channel_id=1, source_target_pairs={{0,17},{1,16},{2,19},{3,18},{4,21},{5,20},{6,23},{7,22},{8,25},{9,... | collective-permute-start | bytes 147464 | tf_op jit(solution)/shard_map/ppermute | solution.py:449
  32.9 1.9 %local_factor.4 = (f32[64,128]{1,0:T(8,128)S(1)}, f32[64,64]{1,0:T(8,128)S(1)}) custom-call(f32[128,128]{1,0:T(8,128)S(1)} %get-tuple-element.31.gram), custom_call_target="tpu_custom_call" | custom-call | flops 1000000000 | bytes 1000000 | tf_op jit(solution)/shard_map/local_factor/pallas_call | solution.py:426
  34.8 0.3 collective-permute-done.8
  35.1 2.3 %collective-permute-start.9 = (f32[96,128]{1,0:T(8,128)S(1)}, f32[96,128]{1,0:T(8,128)S(1)}, u32[]{:S(2)}, u32[]{:S(2)}) collective-permute-start(f32[96,128]{1,0:T(8,128)S(1)} %add.17), channel_id=1, source_target_pairs={{0,3},{1,2},{2,1},{3,0},{4,7},{5,6},{6,5},{7,4},{8,11},{9,10},{10,... | collective-permute-start | bytes 147464 | tf_op jit(solution)/shard_map/ppermute | solution.py:449
  37.5 1.3 %local_factor.5.refs_2_ = f32[64,64]{1,0:T(8,128)S(1)} custom-call(f32[64,64]{1,0:T(8,128)S(1)} %get-tuple-element.33.gram), custom_call_target="tpu_custom_call" | custom-call | flops 1000000000 | bytes 1000000 | tf_op jit(solution)/shard_map/local_factor/pallas_call | solution.py:426
  38.8 0.5 collective-permute-done.9
  39.3 3.0 %collective-permute-start.10 = (f32[96,128]{1,0:T(8,128)S(1)}, f32[96,128]{1,0:T(8,128)S(1)}, u32[]{:S(2)}, u32[]{:S(2)}) collective-permute-start(f32[96,128]{1,0:T(8,128)S(1)} %add.18), channel_id=1, source_target_pairs={{0,5},{1,4},{2,7},{3,6},{4,1},{5,0},{6,3},{7,2},{8,13},{9,12},{10,... | collective-permute-start | bytes 147464 | tf_op jit(solution)/shard_map/ppermute | solution.py:449
  42.2 1.8 %collective-permute-done.10 = f32[96,128]{1,0:T(8,128)S(1)} collective-permute-done((f32[96,128]{1,0:T(8,128)S(1)}, f32[96,128]{1,0:T(8,128)S(1)}, u32[]{:S(2)}, u32[]{:S(2)}) %collective-permute-start.10) | collective-permute-done | bytes 49184 | tf_op jit(solution)/shard_map/ppermute | solution.py:449
  44.1 0.3 collective-permute-start.11
  44.4 0.9 %collective-permute-done.11.other_ref = f32[96,128]{1,0:T(8,128)S(1)} collective-permute-done((f32[96,128]{1,0:T(8,128)S(1)}, f32[96,128]{1,0:T(8,128)S(1)}, u32[]{:S(2)}, u32[]{:S(2)}) %collective-permute-start.11) | collective-permute-done | bytes 49184 | tf_op jit(solution)/shard_map/ppermute | solution.py:449
  45.4 6.2 %factor.1 = (f32[192,192]{1,0:T(8,128)}, f32[1,192]{1,0:T(1,128)}) custom-call(f32[96,128]{1,0:T(8,128)S(1)} %add.19.own_ref, f32[96,128]{1,0:T(8,128)S(1)} %collective-permute-done.11.other_ref, f32[64,192]{1,0:T(8,128)S(1)} %get-tuple-element.35.refs_0_, f32[64,128]{1,0:T(8,128)S(1)} %get-tuple-element.36.refs_1_, f32[64,64]{1,0:T(8,128)S(1)} %local_factor.5.refs_2_), custom_call_target="tpu_custom_call" | custom-call | tf_op jit(solution)/shard_map/factor/pallas_call | solution.py:426
  (6 shorter events, 0.0 us)
Async XLA Ops:
  1.3 14.7 %copy-start = (f32[2,192,8,128]{3,2,1,0:T(8,128)S(1)}, f32[2,192,8,128]{3,2,1,0:T(8,128)}, u32[]{:S(2)}) copy-start(f32[2,192,8,128]{3,2,1,0:T(8,128)} %param.3) | copy-start | bytes 4718596
  4.4 7.1 %collective-permute-start = (f32[4,200,128]{2,1,0:T(8,128)S(1)}, f32[4,200,128]{2,1,0:T(8,128)S(1)}, u32[]{:S(2)}, u32[]{:S(2)}) collective-permute-start(f32[4,200,128]{2,1,0:T(8,128)S(1)} %get-tuple-element.21), channel_id=1, source_target_pairs={{0,1},{2,3},{4,5},{6,7},{1,0},{3,2},{5,4},{7,6},{8,9},{10,11},{12,... | collective-permute-start | bytes 1228808 | tf_op jit(solution)/shard_map/ppermute | solution.py:443
  4.9 6.6 %collective-permute-start.1 = (f32[4,200,128]{2,1,0:T(8,128)S(1)}, f32[4,200,128]{2,1,0:T(8,128)S(1)}, u32[]{:S(2)}, u32[]{:S(2)}) collective-permute-start(f32[4,200,128]{2,1,0:T(8,128)S(1)} %get-tuple-element.22), channel_id=1, source_target_pairs={{1,2},{3,4},{5,6},{2,1},{4,3},{6,5},{9,10},{11,12},{13,14},{10,9},... | collective-permute-start | bytes 1228808 | tf_op jit(solution)/shard_map/ppermute | solution.py:443
  5.6 10.4 %collective-permute-start.2 = (f32[4,200,128]{2,1,0:T(8,128)}, f32[4,200,128]{2,1,0:T(8,128)S(1)}, u32[]{:S(2)}, u32[]{:S(2)}) collective-permute-start(f32[4,200,128]{2,1,0:T(8,128)} %get-tuple-element.23), channel_id=1, source_target_pairs={{0,1},{2,3},{4,5},{6,7},{1,0},{3,2},{5,4},{7,6},{8,9},{10,11},{12,... | collective-permute-start | bytes 1228808 | tf_op jit(solution)/shard_map/ppermute | solution.py:443
  9.6 6.4 %collective-permute-start.3 = (f32[4,200,128]{2,1,0:T(8,128)}, f32[4,200,128]{2,1,0:T(8,128)}, u32[]{:S(2)}, u32[]{:S(2)}) collective-permute-start(f32[4,200,128]{2,1,0:T(8,128)} %get-tuple-element.24), channel_id=1, source_target_pairs={{1,2},{3,4},{5,6},{2,1},{4,3},{6,5},{9,10},{11,12},{13,14},{10,9},... | collective-permute-start | bytes 1228808 | tf_op jit(solution)/shard_map/ppermute | solution.py:443
  12.5 8.1 %collective-permute-start.4 = (f32[200,128]{1,0:T(8,128)}, f32[200,128]{1,0:T(8,128)S(1)}, u32[]{:S(2)}, u32[]{:S(2)}) collective-permute-start(f32[200,128]{1,0:T(8,128)} %get-tuple-element.28), channel_id=1, source_target_pairs={{0,8},{16,24},{8,0},{24,16},{1,9},{17,25},{9,1},{25,17},{2,10},{18... | collective-permute-start | bytes 307208 | tf_op jit(solution)/shard_map/ppermute | solution.py:443
  14.0 6.6 %collective-permute-start.5 = (f32[200,128]{1,0:T(8,128)S(1)}, f32[200,128]{1,0:T(8,128)S(1)}, u32[]{:S(2)}, u32[]{:S(2)}) collective-permute-start(f32[200,128]{1,0:T(8,128)S(1)} %get-tuple-element.29), channel_id=1, source_target_pairs={{8,16},{0,24},{16,8},{24,0},{9,17},{1,25},{17,9},{25,1},{10,18},{2... | collective-permute-start | bytes 307208 | tf_op jit(solution)/shard_map/ppermute | solution.py:443
  22.7 4.6 %collective-permute-start.6 = (f32[96,128]{1,0:T(8,128)S(1)}, f32[96,128]{1,0:T(8,128)S(1)}, u32[]{:S(2)}, u32[]{:S(2)}) collective-permute-start(f32[96,128]{1,0:T(8,128)S(1)} %slice_select_fusion), channel_id=1, source_target_pairs={{0,1},{1,0},{2,3},{3,2},{4,5},{5,4},{6,7},{7,6},{8,9},{9,8},{10,11... | collective-permute-start | bytes 147464 | tf_op jit(solution)/shard_map/ppermute | solution.py:449
  27.3 4.0 %collective-permute-start.7 = (f32[96,128]{1,0:T(8,128)S(1)}, f32[96,128]{1,0:T(8,128)S(1)}, u32[]{:S(2)}, u32[]{:S(2)}) collective-permute-start(f32[96,128]{1,0:T(8,128)S(1)} %select_add_fusion), channel_id=1, source_target_pairs={{0,9},{1,8},{2,11},{3,10},{4,13},{5,12},{6,15},{7,14},{8,1},{9,0},... | collective-permute-start | bytes 147464 | tf_op jit(solution)/shard_map/ppermute | solution.py:449
  31.3 3.8 %collective-permute-start.8 = (f32[96,128]{1,0:T(8,128)S(1)}, f32[96,128]{1,0:T(8,128)S(1)}, u32[]{:S(2)}, u32[]{:S(2)}) collective-permute-start(f32[96,128]{1,0:T(8,128)S(1)} %add.16), channel_id=1, source_target_pairs={{0,17},{1,16},{2,19},{3,18},{4,21},{5,20},{6,23},{7,22},{8,25},{9,... | collective-permute-start | bytes 147464 | tf_op jit(solution)/shard_map/ppermute | solution.py:449
  35.1 4.1 %collective-permute-start.9 = (f32[96,128]{1,0:T(8,128)S(1)}, f32[96,128]{1,0:T(8,128)S(1)}, u32[]{:S(2)}, u32[]{:S(2)}) collective-permute-start(f32[96,128]{1,0:T(8,128)S(1)} %add.17), channel_id=1, source_target_pairs={{0,3},{1,2},{2,1},{3,0},{4,7},{5,6},{6,5},{7,4},{8,11},{9,10},{10,... | collective-permute-start | bytes 147464 | tf_op jit(solution)/shard_map/ppermute | solution.py:449
  39.3 4.8 %collective-permute-start.10 = (f32[96,128]{1,0:T(8,128)S(1)}, f32[96,128]{1,0:T(8,128)S(1)}, u32[]{:S(2)}, u32[]{:S(2)}) collective-permute-start(f32[96,128]{1,0:T(8,128)S(1)} %add.18), channel_id=1, source_target_pairs={{0,5},{1,4},{2,7},{3,6},{4,1},{5,0},{6,3},{7,2},{8,13},{9,12},{10,... | collective-permute-start | bytes 147464 | tf_op jit(solution)/shard_map/ppermute | solution.py:449
  44.1 1.3 %collective-permute-start.11 = (f32[96,128]{1,0:T(8,128)S(1)}, f32[96,128]{1,0:T(8,128)S(1)}, u32[]{:S(2)}, u32[]{:S(2)}) collective-permute-start(f32[96,128]{1,0:T(8,128)S(1)} %add.19.own_ref), channel_id=1, source_target_pairs={{0,1},{1,0},{2,3},{3,2},{4,5},{5,4},{6,7},{7,6},{8,9},{9,8},{10,11... | collective-permute-start | bytes 147464 | tf_op jit(solution)/shard_map/ppermute | solution.py:449

commit v9 on v8

--- a/solution.py
+++ b/solution.py
@@ -17,6 +17,7 @@
 HEIGHT_EVOLVE = 24
 SIDE = 64
 VMEM_BYTES = 24 * 1024 * 1024
+EARLY_ROWS = 3
 LOCAL_COST = pl.CostEstimate(flops=10**9, bytes_accessed=10**6, transcendentals=0)
 EDGE_VMEM_BYTES = 52 * 1024 * 1024
 LANES = 128
@@ -210,7 +211,7 @@
     return jnp.concatenate([x] * (height // SUB), axis=0)
 
 
-def edge_kernel(fields, height, tangents_hbm, coeffs_hbm, last_out, first_out, near, far, near_fast, far_fast, tangents, coeffs, sems):
+def edge_kernel(fields, height, tangents_hbm, coeffs_hbm, last_out, first_out, near, far, far_late, tangents, coeffs, sems):
     chunks = fields // height
     span = height * SUB
     loads = [
@@ -244,8 +245,12 @@
             count = STEPS - f
             for j in range(count):
                 top, bottom = rows[f][j], rows[f][SUB - count + j]
-                (near if f else near_fast)[j + f, at, :] = pick(odd, top, bottom)
-                (far if f else far_fast)[j + f, at, :] = pick(odd, bottom, top)
+                row = f * STEPS + j
+                near[1 + row, at, :] = pick(odd, top, bottom)
+                if row < EARLY_ROWS:
+                    far[1 + row, at, :] = pick(odd, bottom, top)
+                else:
+                    far_late[row - EARLY_ROWS, at, :] = pick(odd, bottom, top)
 
     for g, load in enumerate(loads):
         load.wait()
@@ -378,7 +383,7 @@
         ]
 
 
-def extended_rows(own, near, far, near_fast, far_fast, at):
+def extended_rows(own, near, far, far_late, at):
     tile, tiles = lax.axis_index("tile"), lax.axis_size("tile")
     odd, at_top, at_bottom = tile % 2 == 1, tile == 0, tile == tiles - 1
     out = []
@@ -386,22 +391,24 @@
         count = STEPS - f
         rows = dict(enumerate(own[f]))
         for j in range(count):
-            one, two = ((near if f else near_fast)[j + f, at, :], (far if f else far_fast)[j + f, at, :])
+            row = f * STEPS + j
+            one = near[1 + row, at, :]
+            two = far[1 + row, at, :] if row < EARLY_ROWS else far_late[row - EARLY_ROWS, at, :]
             rows[j - count] = pick(at_top, own[f][count - 1 - j], pick(odd, one, two))
             rows[SUB + j] = pick(at_bottom, own[f][SUB - 1 - j], pick(odd, two, one))
         out.append(rows)
     return out
 
 
-def evolve_kernel(fields, height, tangents, coeffs, near, far, near_fast, far_fast, middle_gram, row_coeffs, cells):
-    coeff_rows = extended_rows(own_coeffs(coeffs), near, far, near_fast, far_fast, pl.ds(fields, SUB))
+def evolve_kernel(fields, height, tangents, coeffs, near, far, far_late, middle_gram, row_coeffs, cells):
+    coeff_rows = extended_rows(own_coeffs(coeffs), near, far, far_late, pl.ds(fields, SUB))
     for f in range(2):
         for r in range(1 - STEPS, SUB + STEPS - 1):
             row_coeffs[f, r + STEPS - 1, :, :] = coeff_rows[f][r] + (1.0 - 4.0 * diffusion) * (1 - f)
 
     for g in range(fields // height):
         at = chunk(g, height)
-        fast, slow = extended_rows(own_rows(tangents, g, height), near, far, near_fast, far_fast, at)
+        fast, slow = extended_rows(own_rows(tangents, g, height), near, far, far_late, at)
         for step in range(1, STEPS + 1):
             margin = STEPS - step
             new_fast = {}
@@ -477,15 +484,15 @@
     fields = tangents.shape[1]
     padded = fields + SUB
     rows = tangents.reshape(2, fields * tangents.shape[2], tangents.shape[3])
-    message, strip = (STEPS, padded, LANES), (padded, LANES)
+    strip = (padded, LANES)
+    early, late = (1 + EARLY_ROWS,) + strip, (2 * STEPS - 1 - EARLY_ROWS,) + strip
     inputs = (rows, jnp.stack([reaction_self, reaction_cross]))
-    last, first, near, far, near_fast, far_fast = local_call(
-        functools.partial(edge_kernel, fields, HEIGHT_EDGE), "edges", [strip] * 2 + [message] * 4,
+    last, first, near, far, far_late = local_call(
+        functools.partial(edge_kernel, fields, HEIGHT_EDGE), "edges", [strip] * 2 + [(2 * STEPS, padded, LANES), early, late],
         [a.shape for a in inputs] + [pltpu.SemaphoreType.DMA((fields // HEIGHT_EDGE + 1,))], *inputs,
         hbm=True, vmem=EDGE_VMEM_BYTES,
     )
-    near, far = swap(near, "tile", 0), swap(far, "tile", 1)
-    near_fast, far_fast = swap(near_fast, "tile", 0), swap(far_fast, "tile", 1)
+    near, far, far_late = swap(near, "tile", 0), swap(far, "tile", 1), swap(far_late, "tile", 1)
     (row_mirror,) = local_call(row_mirror_kernel, "row_mirror", [(2,) + strip], [], last, first)
     strips, near_cols, far_cols = local_call(
         column_kernel, "columns", [(4,) + strip, strip, strip], [], last, first, row_mirror, near, far
@@ -495,7 +502,7 @@
     near_cols = swap(near_cols, "grp", 0)
     (middle_gram,) = local_call(
         functools.partial(evolve_kernel, fields, HEIGHT_EVOLVE), "evolve", [(fields, fields)],
-        [(2, SUB + 2 * STEPS - 2, SUB, LANES), (fields, 2 * SUB * LANES)], *inputs, near, far, near_fast, far_fast,
+        [(2, SUB + 2 * STEPS - 2, SUB, LANES), (fields, 2 * SUB * LANES)], *inputs, near, far, far_late,
     )
     side_blocks = fields // SIDE
     blocks = side_blocks * (side_blocks + 1) // 2

time: 51.8 us -> 51.5 us (level)
    ppermute x6, starting transfers between devices: 12.9 us -> 15.9 us  [exchange(): return lax.ppermute(cells, ('grp', 'tile'), moves)]
    ppermute x6 -> x5, starting transfers between devices: 9.6 us -> 6.74 us  [swap(): return lax.ppermute(cells, axis, pairs + [(b, a) for a, b in pairs])]
  transfers between devices with their start and end apart: 12 -> 11, of which waited for: 6 -> 5; matrix products, arithmetic and copies ran while one was open for 0% -> 0% of each run, Pallas kernels for 23% -> 23%
where the time goes in v9:
time: 51.5 us; the launch traced here: 51.3 us
  Pallas kernels  22.7 us (44%)
  starting transfers between devices  22.6 us (44%)
  waiting for transfers between devices  4.39 us (9%)
  between operations  0.76 us (1%)
  other arithmetic  0.75 us (1%)
    pallas_call x10, Pallas kernels, local_call(): pl.pallas_call(body, out_shape=[jax.ShapeDtypeStruct(s, jnp.float32) for...  22.7 us
    ppermute x6, starting transfers between devices, exchange(): return lax.ppermute(cells, ('grp', 'tile'), moves)  15.9 us
    ppermute x5, starting transfers between devices, swap(): return lax.ppermute(cells, axis, pairs + [(b, a) for a, b in pairs])  6.74 us
    ppermute x6, waiting for transfers between devices, exchange(): return lax.ppermute(cells, ('grp', 'tile'), moves)  4.38 us
  transfers between devices with their start and end apart: 11, of which 5 were waited for; matrix products, arithmetic and copies ran while one was open for 0% of the time, Pallas kernels for 23%

profile of v9, /device:TPU:0, one launch (start us, length us, event | category | flops | bytes accessed | tf_op | source)
XLA Modules:
  0.0 51.3 jit_solution(7137043558156071796)
XLA Ops:
  0.6 0.7 %pad_maximum_fusion.coeffs_hbm.coeffs = f32[2,8,128]{2,1,0:T(8,128)S(1)} fusion(f32[1,8,128]{2,1,0:T(8,128)} %bitcast.6, f32[1,8,128]{2,1,0:T(8,128)} %bitcast.7), kind=kLoop, calls=%fused_computation.2 | loop fusion | flops 2048 | bytes 16384 | tf_op jit(solution)/shard_map/stack | solution.py:489
  1.3 2.8 %edges.1 = (f32[200,128]{1,0:T(8,128)S(1)}, f32[200,128]{1,0:T(8,128)S(1)}, f32[8,200,128]{2,1,0:T(8,128)S(1)}, f32[4,200,128]{2,1,0:T(8,128)S(1)}, f32[4,200,128]{2,1,0:T(8,128)}) custom-call(f32[2,1536,128]{2,1,0:T(8,128)} %bitcast.4, f32[2,8,128]{2,1,0:T(8,128)S(1)} %pad_maximum_fusion.coeffs_hbm.coeffs), custom_call_target="tpu_custom_call" | custom-call | tf_op jit(solution)/shard_map/edges/pallas_call | solution.py:433
  4.1 0.0 copy-start
  4.1 0.5 %collective-permute-start = (f32[8,200,128]{2,1,0:T(8,128)S(1)}, f32[8,200,128]{2,1,0:T(8,128)S(1)}, u32[]{:S(2)}, u32[]{:S(2)}) collective-permute-start(f32[8,200,128]{2,1,0:T(8,128)S(1)} %get-tuple-element.20), channel_id=1, source_target_pairs={{0,1},{2,3},{4,5},{6,7},{1,0},{3,2},{5,4},{7,6},{8,9},{10,11},{12,... | collective-permute-start | bytes 2457608 | tf_op jit(solution)/shard_map/ppermute | solution.py:450
  4.7 0.7 %collective-permute-start.1 = (f32[4,200,128]{2,1,0:T(8,128)S(1)}, f32[4,200,128]{2,1,0:T(8,128)S(1)}, u32[]{:S(2)}, u32[]{:S(2)}) collective-permute-start(f32[4,200,128]{2,1,0:T(8,128)S(1)} %get-tuple-element.21), channel_id=1, source_target_pairs={{1,2},{3,4},{5,6},{2,1},{4,3},{6,5},{9,10},{11,12},{13,14},{10,9},... | collective-permute-start | bytes 1228808 | tf_op jit(solution)/shard_map/ppermute | solution.py:450
  5.3 1.4 %collective-permute-start.2 = (f32[4,200,128]{2,1,0:T(8,128)}, f32[4,200,128]{2,1,0:T(8,128)}, u32[]{:S(2)}, u32[]{:S(2)}) collective-permute-start(f32[4,200,128]{2,1,0:T(8,128)} %get-tuple-element.22), channel_id=1, source_target_pairs={{1,2},{3,4},{5,6},{2,1},{4,3},{6,5},{9,10},{11,12},{13,14},{10,9},... | collective-permute-start | bytes 1228808 | tf_op jit(solution)/shard_map/ppermute | solution.py:450
  6.8 0.5 row_mirror.1.mirrored
  7.3 0.0 collective-permute-done.1.far
  7.3 0.0 collective-permute-done.near
  7.3 1.0 %columns.1 = (f32[4,200,128]{2,1,0:T(8,128)S(1)}, f32[200,128]{1,0:T(8,128)}, f32[200,128]{1,0:T(8,128)S(1)}) custom-call(f32[200,128]{1,0:T(8,128)S(1)} %get-tuple-element.23.last, f32[200,128]{1,0:T(8,128)S(1)} %get-tuple-element.24.first, f32[2,200,128]{2,1,0:T(8,128)S(1)} %row_mirror.1.mirrored, f32[8,200,128]{2,1,0:T(8,128)S(1)} %collective-permute-done.near, ...), custom_call_target="tpu_custom_call" | custom-call | tf_op jit(solution)/shard_map/columns/pallas_call | solution.py:433
  8.3 2.6 %collective-permute-start.3 = (f32[200,128]{1,0:T(8,128)}, f32[200,128]{1,0:T(8,128)S(1)}, u32[]{:S(2)}, u32[]{:S(2)}) collective-permute-start(f32[200,128]{1,0:T(8,128)} %get-tuple-element.26), channel_id=1, source_target_pairs={{0,8},{16,24},{8,0},{24,16},{1,9},{17,25},{9,1},{25,17},{2,10},{18... | collective-permute-start | bytes 307208 | tf_op jit(solution)/shard_map/ppermute | solution.py:450
  10.9 1.5 %collective-permute-start.4 = (f32[200,128]{1,0:T(8,128)S(1)}, f32[200,128]{1,0:T(8,128)S(1)}, u32[]{:S(2)}, u32[]{:S(2)}) collective-permute-start(f32[200,128]{1,0:T(8,128)S(1)} %get-tuple-element.27), channel_id=1, source_target_pairs={{8,16},{0,24},{16,8},{24,0},{9,17},{1,25},{17,9},{25,1},{10,18},{2... | collective-permute-start | bytes 307208 | tf_op jit(solution)/shard_map/ppermute | solution.py:450
  12.4 0.5 column_mirror.1.mirrored
  12.9 0.0 collective-permute-done.2.far_late
  12.9 0.0 copy-done
  12.9 4.6 %evolve.1.middle_gram = f32[192,192]{1,0:T(8,128)S(1)} custom-call(f32[2,1536,128]{2,1,0:T(8,128)S(1)} %bitcast.5, f32[2,8,128]{2,1,0:T(8,128)S(1)} %pad_maximum_fusion.coeffs_hbm.coeffs, f32[8,200,128]{2,1,0:T(8,128)S(1)} %collective-permute-done.near, f32[4,200,128]{2,1,0:T(8,128)S(1)} %collective-permute-done.1.far, ...), custom_call_target="tpu_custom_call" | custom-call | tf_op jit(solution)/shard_map/evolve/pallas_call | solution.py:433
  17.5 0.0 collective-permute-done.3.near
  17.5 0.0 collective-permute-done.4.far
  17.5 2.0 %gram.1 = f32[192,128]{1,0:T(8,128)S(1)} custom-call(f32[192,192]{1,0:T(8,128)S(1)} %evolve.1.middle_gram, f32[4,200,128]{2,1,0:T(8,128)S(1)} %get-tuple-element.25.strips, f32[2,200,128]{2,1,0:T(8,128)S(1)} %column_mirror.1.mirrored, f32[200,128]{1,0:T(8,128)S(1)} %collective-permute-done.3.near, f32[200,128]{1,0:T(8,128)S(1)} %collective-permute-done.4.far), custom_call_target="tpu_custom_call" | custom-call | tf_op jit(solution)/shard_map/gram/pallas_call | solution.py:433
  19.6 6.8 %collective-permute-start.5 = (f32[96,128]{1,0:T(8,128)S(1)}, f32[96,128]{1,0:T(8,128)S(1)}, u32[]{:S(2)}, u32[]{:S(2)}) collective-permute-start(f32[96,128]{1,0:T(8,128)S(1)} %slice_select_fusion), channel_id=1, source_target_pairs={{0,1},{1,0},{2,3},{3,2},{4,5},{5,4},{6,7},{7,6},{8,9},{9,8},{10,11... | collective-permute-start | bytes 147464 | tf_op jit(solution)/shard_map/ppermute | solution.py:456
  26.3 0.9 %collective-permute-done.5 = f32[96,128]{1,0:T(8,128)S(1)} collective-permute-done((f32[96,128]{1,0:T(8,128)S(1)}, f32[96,128]{1,0:T(8,128)S(1)}, u32[]{:S(2)}, u32[]{:S(2)}) %collective-permute-start.5) | collective-permute-done | bytes 49184 | tf_op jit(solution)/shard_map/ppermute | solution.py:456
  27.2 1.8 %collective-permute-start.6 = (f32[96,128]{1,0:T(8,128)S(1)}, f32[96,128]{1,0:T(8,128)S(1)}, u32[]{:S(2)}, u32[]{:S(2)}) collective-permute-start(f32[96,128]{1,0:T(8,128)S(1)} %select_add_fusion), channel_id=1, source_target_pairs={{0,9},{1,8},{2,11},{3,10},{4,13},{5,12},{6,15},{7,14},{8,1},{9,0},... | collective-permute-start | bytes 147464 | tf_op jit(solution)/shard_map/ppermute | solution.py:456
  29.0 2.0 %local_factor.3 = (f32[64,192]{1,0:T(8,128)S(1)}, f32[128,128]{1,0:T(8,128)S(1)}) custom-call(f32[192,128]{1,0:T(8,128)S(1)} %gram.1), custom_call_target="tpu_custom_call" | custom-call | flops 1000000000 | bytes 1000000 | tf_op jit(solution)/shard_map/local_factor/pallas_call | solution.py:433
  31.0 0.0 collective-permute-done.6
  31.0 1.6 %collective-permute-start.7 = (f32[96,128]{1,0:T(8,128)S(1)}, f32[96,128]{1,0:T(8,128)S(1)}, u32[]{:S(2)}, u32[]{:S(2)}) collective-permute-start(f32[96,128]{1,0:T(8,128)S(1)} %add.16), channel_id=1, source_target_pairs={{0,17},{1,16},{2,19},{3,18},{4,21},{5,20},{6,23},{7,22},{8,25},{9,... | collective-permute-start | bytes 147464 | tf_op jit(solution)/shard_map/ppermute | solution.py:456
  32.6 1.9 %local_factor.4 = (f32[64,128]{1,0:T(8,128)S(1)}, f32[64,64]{1,0:T(8,128)S(1)}) custom-call(f32[128,128]{1,0:T(8,128)S(1)} %get-tuple-element.29.gram), custom_call_target="tpu_custom_call" | custom-call | flops 1000000000 | bytes 1000000 | tf_op jit(solution)/shard_map/local_factor/pallas_call | solution.py:433
  34.6 0.2 collective-permute-done.7
  34.8 2.4 %collective-permute-start.8 = (f32[96,128]{1,0:T(8,128)S(1)}, f32[96,128]{1,0:T(8,128)S(1)}, u32[]{:S(2)}, u32[]{:S(2)}) collective-permute-start(f32[96,128]{1,0:T(8,128)S(1)} %add.17), channel_id=1, source_target_pairs={{0,3},{1,2},{2,1},{3,0},{4,7},{5,6},{6,5},{7,4},{8,11},{9,10},{10,... | collective-permute-start | bytes 147464 | tf_op jit(solution)/shard_map/ppermute | solution.py:456
  37.2 1.3 %local_factor.5.refs_2_ = f32[64,64]{1,0:T(8,128)S(1)} custom-call(f32[64,64]{1,0:T(8,128)S(1)} %get-tuple-element.31.gram), custom_call_target="tpu_custom_call" | custom-call | flops 1000000000 | bytes 1000000 | tf_op jit(solution)/shard_map/local_factor/pallas_call | solution.py:433
  38.5 0.5 collective-permute-done.8
  39.0 3.0 %collective-permute-start.9 = (f32[96,128]{1,0:T(8,128)S(1)}, f32[96,128]{1,0:T(8,128)S(1)}, u32[]{:S(2)}, u32[]{:S(2)}) collective-permute-start(f32[96,128]{1,0:T(8,128)S(1)} %add.18), channel_id=1, source_target_pairs={{0,5},{1,4},{2,7},{3,6},{4,1},{5,0},{6,3},{7,2},{8,13},{9,12},{10,... | collective-permute-start | bytes 147464 | tf_op jit(solution)/shard_map/ppermute | solution.py:456
  42.0 1.8 %collective-permute-done.9 = f32[96,128]{1,0:T(8,128)S(1)} collective-permute-done((f32[96,128]{1,0:T(8,128)S(1)}, f32[96,128]{1,0:T(8,128)S(1)}, u32[]{:S(2)}, u32[]{:S(2)}) %collective-permute-start.9) | collective-permute-done | bytes 49184 | tf_op jit(solution)/shard_map/ppermute | solution.py:456
  43.8 0.3 collective-permute-start.10
  44.2 0.9 %collective-permute-done.10.other_ref = f32[96,128]{1,0:T(8,128)S(1)} collective-permute-done((f32[96,128]{1,0:T(8,128)S(1)}, f32[96,128]{1,0:T(8,128)S(1)}, u32[]{:S(2)}, u32[]{:S(2)}) %collective-permute-start.10) | collective-permute-done | bytes 49184 | tf_op jit(solution)/shard_map/ppermute | solution.py:456
  45.1 6.2 %factor.1 = (f32[192,192]{1,0:T(8,128)}, f32[1,192]{1,0:T(1,128)}) custom-call(f32[96,128]{1,0:T(8,128)S(1)} %add.19.own_ref, f32[96,128]{1,0:T(8,128)S(1)} %collective-permute-done.10.other_ref, f32[64,192]{1,0:T(8,128)S(1)} %get-tuple-element.33.refs_0_, f32[64,128]{1,0:T(8,128)S(1)} %get-tuple-element.34.refs_1_, f32[64,64]{1,0:T(8,128)S(1)} %local_factor.5.refs_2_), custom_call_target="tpu_custom_call" | custom-call | tf_op jit(solution)/shard_map/factor/pallas_call | solution.py:433
  (6 shorter events, 0.0 us)
Async XLA Ops:
  4.1 8.8 %copy-start = (f32[2,192,8,128]{3,2,1,0:T(8,128)S(1)}, f32[2,192,8,128]{3,2,1,0:T(8,128)}, u32[]{:S(2)}) copy-start(f32[2,192,8,128]{3,2,1,0:T(8,128)} %param.3) | copy-start | bytes 4718596
  4.1 3.1 %collective-permute-start = (f32[8,200,128]{2,1,0:T(8,128)S(1)}, f32[8,200,128]{2,1,0:T(8,128)S(1)}, u32[]{:S(2)}, u32[]{:S(2)}) collective-permute-start(f32[8,200,128]{2,1,0:T(8,128)S(1)} %get-tuple-element.20), channel_id=1, source_target_pairs={{0,1},{2,3},{4,5},{6,7},{1,0},{3,2},{5,4},{7,6},{8,9},{10,11},{12,... | collective-permute-start | bytes 2457608 | tf_op jit(solution)/shard_map/ppermute | solution.py:450
  4.7 2.6 %collective-permute-start.1 = (f32[4,200,128]{2,1,0:T(8,128)S(1)}, f32[4,200,128]{2,1,0:T(8,128)S(1)}, u32[]{:S(2)}, u32[]{:S(2)}) collective-permute-start(f32[4,200,128]{2,1,0:T(8,128)S(1)} %get-tuple-element.21), channel_id=1, source_target_pairs={{1,2},{3,4},{5,6},{2,1},{4,3},{6,5},{9,10},{11,12},{13,14},{10,9},... | collective-permute-start | bytes 1228808 | tf_op jit(solution)/shard_map/ppermute | solution.py:450
  5.3 7.6 %collective-permute-start.2 = (f32[4,200,128]{2,1,0:T(8,128)}, f32[4,200,128]{2,1,0:T(8,128)}, u32[]{:S(2)}, u32[]{:S(2)}) collective-permute-start(f32[4,200,128]{2,1,0:T(8,128)} %get-tuple-element.22), channel_id=1, source_target_pairs={{1,2},{3,4},{5,6},{2,1},{4,3},{6,5},{9,10},{11,12},{13,14},{10,9},... | collective-permute-start | bytes 1228808 | tf_op jit(solution)/shard_map/ppermute | solution.py:450
  8.3 9.3 %collective-permute-start.3 = (f32[200,128]{1,0:T(8,128)}, f32[200,128]{1,0:T(8,128)S(1)}, u32[]{:S(2)}, u32[]{:S(2)}) collective-permute-start(f32[200,128]{1,0:T(8,128)} %get-tuple-element.26), channel_id=1, source_target_pairs={{0,8},{16,24},{8,0},{24,16},{1,9},{17,25},{9,1},{25,17},{2,10},{18... | collective-permute-start | bytes 307208 | tf_op jit(solution)/shard_map/ppermute | solution.py:450
  10.9 6.6 %collective-permute-start.4 = (f32[200,128]{1,0:T(8,128)S(1)}, f32[200,128]{1,0:T(8,128)S(1)}, u32[]{:S(2)}, u32[]{:S(2)}) collective-permute-start(f32[200,128]{1,0:T(8,128)S(1)} %get-tuple-element.27), channel_id=1, source_target_pairs={{8,16},{0,24},{16,8},{24,0},{9,17},{1,25},{17,9},{25,1},{10,18},{2... | collective-permute-start | bytes 307208 | tf_op jit(solution)/shard_map/ppermute | solution.py:450
  19.6 7.7 %collective-permute-start.5 = (f32[96,128]{1,0:T(8,128)S(1)}, f32[96,128]{1,0:T(8,128)S(1)}, u32[]{:S(2)}, u32[]{:S(2)}) collective-permute-start(f32[96,128]{1,0:T(8,128)S(1)} %slice_select_fusion), channel_id=1, source_target_pairs={{0,1},{1,0},{2,3},{3,2},{4,5},{5,4},{6,7},{7,6},{8,9},{9,8},{10,11... | collective-permute-start | bytes 147464 | tf_op jit(solution)/shard_map/ppermute | solution.py:456
  27.2 3.8 %collective-permute-start.6 = (f32[96,128]{1,0:T(8,128)S(1)}, f32[96,128]{1,0:T(8,128)S(1)}, u32[]{:S(2)}, u32[]{:S(2)}) collective-permute-start(f32[96,128]{1,0:T(8,128)S(1)} %select_add_fusion), channel_id=1, source_target_pairs={{0,9},{1,8},{2,11},{3,10},{4,13},{5,12},{6,15},{7,14},{8,1},{9,0},... | collective-permute-start | bytes 147464 | tf_op jit(solution)/shard_map/ppermute | solution.py:456
  31.0 3.8 %collective-permute-start.7 = (f32[96,128]{1,0:T(8,128)S(1)}, f32[96,128]{1,0:T(8,128)S(1)}, u32[]{:S(2)}, u32[]{:S(2)}) collective-permute-start(f32[96,128]{1,0:T(8,128)S(1)} %add.16), channel_id=1, source_target_pairs={{0,17},{1,16},{2,19},{3,18},{4,21},{5,20},{6,23},{7,22},{8,25},{9,... | collective-permute-start | bytes 147464 | tf_op jit(solution)/shard_map/ppermute | solution.py:456
  34.8 4.2 %collective-permute-start.8 = (f32[96,128]{1,0:T(8,128)S(1)}, f32[96,128]{1,0:T(8,128)S(1)}, u32[]{:S(2)}, u32[]{:S(2)}) collective-permute-start(f32[96,128]{1,0:T(8,128)S(1)} %add.17), channel_id=1, source_target_pairs={{0,3},{1,2},{2,1},{3,0},{4,7},{5,6},{6,5},{7,4},{8,11},{9,10},{10,... | collective-permute-start | bytes 147464 | tf_op jit(solution)/shard_map/ppermute | solution.py:456
  39.0 4.8 %collective-permute-start.9 = (f32[96,128]{1,0:T(8,128)S(1)}, f32[96,128]{1,0:T(8,128)S(1)}, u32[]{:S(2)}, u32[]{:S(2)}) collective-permute-start(f32[96,128]{1,0:T(8,128)S(1)} %add.18), channel_id=1, source_target_pairs={{0,5},{1,4},{2,7},{3,6},{4,1},{5,0},{6,3},{7,2},{8,13},{9,12},{10,... | collective-permute-start | bytes 147464 | tf_op jit(solution)/shard_map/ppermute | solution.py:456
  43.8 1.3 %collective-permute-start.10 = (f32[96,128]{1,0:T(8,128)S(1)}, f32[96,128]{1,0:T(8,128)S(1)}, u32[]{:S(2)}, u32[]{:S(2)}) collective-permute-start(f32[96,128]{1,0:T(8,128)S(1)} %add.19.own_ref), channel_id=1, source_target_pairs={{0,1},{1,0},{2,3},{3,2},{4,5},{5,4},{6,7},{7,6},{8,9},{9,8},{10,11... | collective-permute-start | bytes 147464 | tf_op jit(solution)/shard_map/ppermute | solution.py:456

commit v10 on v9

--- a/solution.py
+++ b/solution.py
@@ -47,12 +47,62 @@
 def block_pairs(n):
     return [(i, j) for i in range(n) for j in range(i, n)]
 
+def square_masks():
+    row = lax.broadcasted_iota(jnp.int32, (SIDE, SIDE), 0)
+    col = lax.broadcasted_iota(jnp.int32, (SIDE, SIDE), 1)
+    return row, col
+
+
+def packed_rows(n):
+    count = n // 2 + n * (n - 1) // 2 + 1
+    return count * SIDE // 2
+
+
+def pack_blocks(whole, n):
+    row, col = square_masks()
+
+    def block(i, j):
+        return whole[i*SIDE:(i+1)*SIDE, j*SIDE:(j+1)*SIDE]
+
+    squares, below = [], jnp.zeros((SIDE, SIDE), jnp.float32)
+    for m in range(n // 2):
+        second = block(2*m + 1, 2*m + 1)
+        line = jnp.sum(jnp.where(row == col, second, 0.0), axis=0, keepdims=True)
+        at = SIDE - 1 - 2*m
+        turned = jnp.concatenate([line[:, at:], line[:, :at]], axis=1)
+        below = jnp.where(row == at, line, jnp.where(row == at - 1, turned, below))
+        squares.append(jnp.where(row <= col, block(2*m, 2*m), second))
+    squares += [block(i, j) for i, j in block_pairs(n) if i < j]
+    squares.append(jnp.where(row <= col, block(n - 1, n - 1), below) if n % 2 else below)
+    lines = [jnp.concatenate(squares[i:i+2], axis=1) for i in range(0, len(squares) - 1, 2)]
+    if len(squares) % 2:
+        lines.append(jnp.concatenate([squares[-1][:SIDE // 2], squares[-1][SIDE // 2:]], axis=1))
+    return jnp.concatenate(lines, axis=0)
+
+
 def unpack_blocks(packed, n):
-    out = {}
-    for index, key in enumerate(block_pairs(n)):
-        row, half = divmod(index, 2)
-        out[key] = packed[row*SIDE:(row+1)*SIDE, half*SIDE:(half+1)*SIDE]
-    return out
+    row, col = square_masks()
+    count = packed.shape[0] * 2 // SIDE
+    squares = []
+    for i in range(count // 2):
+        squares += [packed[i*SIDE:(i+1)*SIDE, :SIDE], packed[i*SIDE:(i+1)*SIDE, SIDE:]]
+    if count % 2:
+        rest = packed[count // 2 * SIDE:]
+        squares.append(jnp.concatenate([rest[:, :SIDE], rest[:, SIDE:]], axis=0))
+    last = squares[-1]
+    blocks = dict(zip([(i, j) for i, j in block_pairs(n) if i < j], squares[n // 2:-1]))
+    for m in range(n // 2):
+        both, other = squares[m], squares[m].T
+        at = SIDE - 1 - 2*m
+        line, turned = last[at:at + 1], last[at - 1:at]
+        turned = jnp.concatenate([turned[:, SIDE - at:], turned[:, :SIDE - at]], axis=1)
+        line = jnp.where(col[:1] < at, line, turned)
+        blocks[2*m, 2*m] = jnp.where(row <= col, both, other)
+        blocks[2*m + 1, 2*m + 1] = jnp.where(row > col, both, jnp.where(row < col, other, line))
+    if n % 2:
+        blocks[n - 1, n - 1] = jnp.where(row <= col, last, last.T)
+    return blocks
+
 
 def spread_lane(x, lane):
     return jnp.broadcast_to(x[:, lane:lane+1], (x.shape[0], LANES))
@@ -116,18 +166,11 @@
         out.append((whole[:, :SIDE], whole[:, SIDE:]))
     return out
 
-def square_masks():
-    row = lax.broadcasted_iota(jnp.int32, (SIDE, SIDE), 0)
-    col = lax.broadcasted_iota(jnp.int32, (SIDE, SIDE), 1)
-    return row <= col, row == col
-
-
-def local_kernel(n, packed, gram, panel, *after):
-    blocks = unpack_blocks(gram[...], n) if packed else {
-        (i, j): gram[i*SIDE:(i+1)*SIDE, j*SIDE:(j+1)*SIDE] for i, j in block_pairs(n)
-    }
+def local_kernel(n, gram, panel, *after):
+    blocks = {(i, j): gram[i*SIDE:(i+1)*SIDE, j*SIDE:(j+1)*SIDE] for i, j in block_pairs(n)}
+    row, col = square_masks()
     ((factor, inverse),) = factor_blocks([blocks[0, 0]])
-    panel[:, :SIDE] = jnp.where(square_masks()[0], factor, 0.0)
+    panel[:, :SIDE] = jnp.where(row <= col, factor, 0.0)
     if n > 1:
         row = dot_nn(inverse, jnp.concatenate([blocks[0, j] for j in range(1, n)], axis=1))
         panel[:, SIDE:] = row
@@ -137,12 +180,12 @@
             after[0][at] = blocks[i + 1, j + 1] - less[at]
 
 
-def local_factor(packed, n):
-    panels, left = [], packed
+def local_factor(gram, n):
+    panels, left = [], gram
     for k in range(n):
         m = n - k
         shapes = [(SIDE, m*SIDE)] + ([((m-1)*SIDE, (m-1)*SIDE)] if m > 1 else [])
-        panel, *left = local_call(functools.partial(local_kernel, m, k == 0), "local_factor", shapes, [], left, cost=LOCAL_COST)
+        panel, *left = local_call(functools.partial(local_kernel, m), "local_factor", shapes, [], left, cost=LOCAL_COST)
         left = left[0] if left else None
         panels.append(panel)
     return panels
@@ -153,7 +196,8 @@
     high_half = parity()
     own, other = own_ref[...], other_ref[...]
     total = unpack_blocks(jnp.concatenate([jnp.where(high_half, other, own), jnp.where(high_half, own, other)], axis=0), n)
-    diag = square_masks()[1]
+    row, col = square_masks()
+    diag = row == col
     rest = {j: [local[i][:, (j-i)*SIDE:(j-i+1)*SIDE] for i in range(j + 1)] for j in range(n)}
     for k in range(n):
         ((factor, inverse),) = factor_blocks([total[k, k]])
@@ -345,7 +389,7 @@
         mirrored[...] = jnp.zeros(mirrored.shape, jnp.float32)
 
 
-def gram_kernel(fields, height, middle_gram, strips, mirrored, near, far, gram, halo, ends):
+def gram_kernel(fields, height, middle_gram, strips, mirrored, near, far, packed, gram, halo, ends):
     grp, grps = lax.axis_index("grp"), lax.axis_size("grp")
     grp_odd = grp % 2 == 1
     one, two = near[...], far[...]
@@ -376,11 +420,8 @@
         ends[at, :] = jnp.where(l < LANES // 2, joined[0], roll(joined[1], LANES // 2))
 
     whole = middle_gram[...] + gram_of(ends[...])
-    for index, (i, j) in enumerate(block_pairs(fields // SIDE)):
-        row, half = divmod(index, 2)
-        gram[row * SIDE:(row + 1) * SIDE, half * SIDE:(half + 1) * SIDE] = whole[
-            i * SIDE:(i + 1) * SIDE, j * SIDE:(j + 1) * SIDE
-        ]
+    gram[...] = whole
+    packed[...] = pack_blocks(whole, fields // SIDE)
 
 
 def extended_rows(own, near, far, far_late, at):
@@ -505,13 +546,12 @@
         [(2, SUB + 2 * STEPS - 2, SUB, LANES), (fields, 2 * SUB * LANES)], *inputs, near, far, far_late,
     )
     side_blocks = fields // SIDE
-    blocks = side_blocks * (side_blocks + 1) // 2
-    (packed,) = local_call(
-        functools.partial(gram_kernel, fields, HEIGHT_STRIP), "gram", [((blocks + 1) // 2 * SIDE, 2 * SIDE)],
+    packed, gram = local_call(
+        functools.partial(gram_kernel, fields, HEIGHT_STRIP), "gram", [(packed_rows(side_blocks), 2 * SIDE), (fields, fields)],
         [(2,) + strip, (fields, LANES)], middle_gram, strips, column_mirror, near_cols, far_cols,
     )
     block_total = lax.axis_size("grp") * lax.axis_size("tile")
-    corrections, growth = factor_call(*sum_blocks(packed, local_factor(packed, side_blocks)), fields, math.sqrt(block_total))
+    corrections, growth = factor_call(*sum_blocks(packed, local_factor(gram, side_blocks)), fields, math.sqrt(block_total))
     return (corrections, growth)
 
 

time: 51.5 us -> 50.6 us (0.983)
  no operation moved by 1% of the time
where the time goes in v10:
time: 50.6 us; the launch traced here: 50.3 us
  Pallas kernels  22.6 us (45%)
  starting transfers between devices  22.2 us (44%)
  waiting for transfers between devices  4.01 us (8%)
  between operations  0.76 us (2%)
  other arithmetic  0.75 us (1%)
    pallas_call x10, Pallas kernels, local_call(): pl.pallas_call(body, out_shape=[jax.ShapeDtypeStruct(s, jnp.float32) for...  22.6 us
    ppermute x6, starting transfers between devices, exchange(): return lax.ppermute(cells, ('grp', 'tile'), moves)  15.4 us
    ppermute x5, starting transfers between devices, swap(): return lax.ppermute(cells, axis, pairs + [(b, a) for a, b in pairs])  6.74 us
    ppermute x6, waiting for transfers between devices, exchange(): return lax.ppermute(cells, ('grp', 'tile'), moves)  4 us
  transfers between devices with their start and end apart: 11, of which 5 were waited for; matrix products, arithmetic and copies ran while one was open for 0% of the time, Pallas kernels for 23%

profile of v10, /device:TPU:0, one launch (start us, length us, event | category | flops | bytes accessed | tf_op | source)
XLA Modules:
  0.0 50.3 jit_solution(18368521603522649883)
XLA Ops:
  0.6 0.7 %pad_maximum_fusion.coeffs_hbm.coeffs = f32[2,8,128]{2,1,0:T(8,128)S(1)} fusion(f32[1,8,128]{2,1,0:T(8,128)} %bitcast.6, f32[1,8,128]{2,1,0:T(8,128)} %bitcast.7), kind=kLoop, calls=%fused_computation.2 | loop fusion | flops 2048 | bytes 16384 | tf_op jit(solution)/shard_map/stack | solution.py:530
  1.3 2.8 %edges.1 = (f32[200,128]{1,0:T(8,128)S(1)}, f32[200,128]{1,0:T(8,128)S(1)}, f32[8,200,128]{2,1,0:T(8,128)S(1)}, f32[4,200,128]{2,1,0:T(8,128)S(1)}, f32[4,200,128]{2,1,0:T(8,128)}) custom-call(f32[2,1536,128]{2,1,0:T(8,128)} %bitcast.4, f32[2,8,128]{2,1,0:T(8,128)S(1)} %pad_maximum_fusion.coeffs_hbm.coeffs), custom_call_target="tpu_custom_call" | custom-call | tf_op jit(solution)/shard_map/edges/pallas_call | solution.py:474
  4.1 0.0 copy-start
  4.1 0.5 %collective-permute-start = (f32[8,200,128]{2,1,0:T(8,128)S(1)}, f32[8,200,128]{2,1,0:T(8,128)S(1)}, u32[]{:S(2)}, u32[]{:S(2)}) collective-permute-start(f32[8,200,128]{2,1,0:T(8,128)S(1)} %get-tuple-element.22), channel_id=1, source_target_pairs={{0,1},{2,3},{4,5},{6,7},{1,0},{3,2},{5,4},{7,6},{8,9},{10,11},{12,... | collective-permute-start | bytes 2457608 | tf_op jit(solution)/shard_map/ppermute | solution.py:491
  4.6 0.7 %collective-permute-start.1 = (f32[4,200,128]{2,1,0:T(8,128)S(1)}, f32[4,200,128]{2,1,0:T(8,128)S(1)}, u32[]{:S(2)}, u32[]{:S(2)}) collective-permute-start(f32[4,200,128]{2,1,0:T(8,128)S(1)} %get-tuple-element.23), channel_id=1, source_target_pairs={{1,2},{3,4},{5,6},{2,1},{4,3},{6,5},{9,10},{11,12},{13,14},{10,9},... | collective-permute-start | bytes 1228808 | tf_op jit(solution)/shard_map/ppermute | solution.py:491
  5.3 1.4 %collective-permute-start.2 = (f32[4,200,128]{2,1,0:T(8,128)}, f32[4,200,128]{2,1,0:T(8,128)}, u32[]{:S(2)}, u32[]{:S(2)}) collective-permute-start(f32[4,200,128]{2,1,0:T(8,128)} %get-tuple-element.24), channel_id=1, source_target_pairs={{1,2},{3,4},{5,6},{2,1},{4,3},{6,5},{9,10},{11,12},{13,14},{10,9},... | collective-permute-start | bytes 1228808 | tf_op jit(solution)/shard_map/ppermute | solution.py:491
  6.7 0.5 row_mirror.1.mirrored
  7.2 0.0 collective-permute-done.1.far
  7.3 0.0 collective-permute-done.near
  7.3 1.0 %columns.1 = (f32[4,200,128]{2,1,0:T(8,128)S(1)}, f32[200,128]{1,0:T(8,128)}, f32[200,128]{1,0:T(8,128)S(1)}) custom-call(f32[200,128]{1,0:T(8,128)S(1)} %get-tuple-element.25.last, f32[200,128]{1,0:T(8,128)S(1)} %get-tuple-element.26.first, f32[2,200,128]{2,1,0:T(8,128)S(1)} %row_mirror.1.mirrored, f32[8,200,128]{2,1,0:T(8,128)S(1)} %collective-permute-done.near, ...), custom_call_target="tpu_custom_call" | custom-call | tf_op jit(solution)/shard_map/columns/pallas_call | solution.py:474
  8.3 2.6 %collective-permute-start.3 = (f32[200,128]{1,0:T(8,128)}, f32[200,128]{1,0:T(8,128)S(1)}, u32[]{:S(2)}, u32[]{:S(2)}) collective-permute-start(f32[200,128]{1,0:T(8,128)} %get-tuple-element.28), channel_id=1, source_target_pairs={{0,8},{16,24},{8,0},{24,16},{1,9},{17,25},{9,1},{25,17},{2,10},{18... | collective-permute-start | bytes 307208 | tf_op jit(solution)/shard_map/ppermute | solution.py:491
  10.9 1.5 %collective-permute-start.4 = (f32[200,128]{1,0:T(8,128)S(1)}, f32[200,128]{1,0:T(8,128)S(1)}, u32[]{:S(2)}, u32[]{:S(2)}) collective-permute-start(f32[200,128]{1,0:T(8,128)S(1)} %get-tuple-element.29), channel_id=1, source_target_pairs={{8,16},{0,24},{16,8},{24,0},{9,17},{1,25},{17,9},{25,1},{10,18},{2... | collective-permute-start | bytes 307208 | tf_op jit(solution)/shard_map/ppermute | solution.py:491
  12.4 0.5 column_mirror.1.mirrored
  12.9 0.0 collective-permute-done.2.far_late
  12.9 0.0 copy-done
  12.9 4.6 %evolve.1.middle_gram = f32[192,192]{1,0:T(8,128)S(1)} custom-call(f32[2,1536,128]{2,1,0:T(8,128)S(1)} %bitcast.5, f32[2,8,128]{2,1,0:T(8,128)S(1)} %pad_maximum_fusion.coeffs_hbm.coeffs, f32[8,200,128]{2,1,0:T(8,128)S(1)} %collective-permute-done.near, f32[4,200,128]{2,1,0:T(8,128)S(1)} %collective-permute-done.1.far, ...), custom_call_target="tpu_custom_call" | custom-call | tf_op jit(solution)/shard_map/evolve/pallas_call | solution.py:474
  17.5 0.0 collective-permute-done.3.near
  17.5 0.0 collective-permute-done.4.far
  17.5 2.2 %gram.1 = (f32[160,128]{1,0:T(8,128)S(1)}, f32[192,192]{1,0:T(8,128)S(1)}) custom-call(f32[192,192]{1,0:T(8,128)S(1)} %evolve.1.middle_gram, f32[4,200,128]{2,1,0:T(8,128)S(1)} %get-tuple-element.27.strips, f32[2,200,128]{2,1,0:T(8,128)S(1)} %column_mirror.1.mirrored, f32[200,128]{1,0:T(8,128)S(1)} %collective-permute-done.3.near, ...), custom_call_target="tpu_custom_call" | custom-call | tf_op jit(solution)/shard_map/gram/pallas_call | solution.py:474
  19.8 6.8 %collective-permute-start.5 = (f32[80,128]{1,0:T(8,128)S(1)}, f32[80,128]{1,0:T(8,128)S(1)}, u32[]{:S(2)}, u32[]{:S(2)}) collective-permute-start(f32[80,128]{1,0:T(8,128)S(1)} %slice_select_fusion), channel_id=1, source_target_pairs={{0,1},{1,0},{2,3},{3,2},{4,5},{5,4},{6,7},{7,6},{8,9},{9,8},{10,11... | collective-permute-start | bytes 122888 | tf_op jit(solution)/shard_map/ppermute | solution.py:497
  26.6 0.9 %collective-permute-done.5 = f32[80,128]{1,0:T(8,128)S(1)} collective-permute-done((f32[80,128]{1,0:T(8,128)S(1)}, f32[80,128]{1,0:T(8,128)S(1)}, u32[]{:S(2)}, u32[]{:S(2)}) %collective-permute-start.5) | collective-permute-done | bytes 40992 | tf_op jit(solution)/shard_map/ppermute | solution.py:497
  27.4 1.8 %collective-permute-start.6 = (f32[80,128]{1,0:T(8,128)S(1)}, f32[80,128]{1,0:T(8,128)S(1)}, u32[]{:S(2)}, u32[]{:S(2)}) collective-permute-start(f32[80,128]{1,0:T(8,128)S(1)} %select_add_fusion), channel_id=1, source_target_pairs={{0,9},{1,8},{2,11},{3,10},{4,13},{5,12},{6,15},{7,14},{8,1},{9,0},... | collective-permute-start | bytes 122888 | tf_op jit(solution)/shard_map/ppermute | solution.py:497
  29.2 2.0 %local_factor.3 = (f32[64,192]{1,0:T(8,128)S(1)}, f32[128,128]{1,0:T(8,128)S(1)}) custom-call(f32[192,192]{1,0:T(8,128)S(1)} %get-tuple-element.31.gram), custom_call_target="tpu_custom_call" | custom-call | flops 1000000000 | bytes 1000000 | tf_op jit(solution)/shard_map/local_factor/pallas_call | solution.py:474
  31.2 0.0 collective-permute-done.6
  31.2 1.5 %collective-permute-start.7 = (f32[80,128]{1,0:T(8,128)S(1)}, f32[80,128]{1,0:T(8,128)S(1)}, u32[]{:S(2)}, u32[]{:S(2)}) collective-permute-start(f32[80,128]{1,0:T(8,128)S(1)} %add.16), channel_id=1, source_target_pairs={{0,17},{1,16},{2,19},{3,18},{4,21},{5,20},{6,23},{7,22},{8,25},{9,... | collective-permute-start | bytes 122888 | tf_op jit(solution)/shard_map/ppermute | solution.py:497
  32.7 1.9 %local_factor.4 = (f32[64,128]{1,0:T(8,128)S(1)}, f32[64,64]{1,0:T(8,128)S(1)}) custom-call(f32[128,128]{1,0:T(8,128)S(1)} %get-tuple-element.33.gram), custom_call_target="tpu_custom_call" | custom-call | flops 1000000000 | bytes 1000000 | tf_op jit(solution)/shard_map/local_factor/pallas_call | solution.py:474
  34.6 0.2 collective-permute-done.7
  34.8 2.1 %collective-permute-start.8 = (f32[80,128]{1,0:T(8,128)S(1)}, f32[80,128]{1,0:T(8,128)S(1)}, u32[]{:S(2)}, u32[]{:S(2)}) collective-permute-start(f32[80,128]{1,0:T(8,128)S(1)} %add.17), channel_id=1, source_target_pairs={{0,3},{1,2},{2,1},{3,0},{4,7},{5,6},{6,5},{7,4},{8,11},{9,10},{10,... | collective-permute-start | bytes 122888 | tf_op jit(solution)/shard_map/ppermute | solution.py:497
  36.9 1.3 %local_factor.5.refs_2_ = f32[64,64]{1,0:T(8,128)S(1)} custom-call(f32[64,64]{1,0:T(8,128)S(1)} %get-tuple-element.35.gram), custom_call_target="tpu_custom_call" | custom-call | flops 1000000000 | bytes 1000000 | tf_op jit(solution)/shard_map/local_factor/pallas_call | solution.py:474
  38.2 0.4 collective-permute-done.8
  38.6 2.9 %collective-permute-start.9 = (f32[80,128]{1,0:T(8,128)S(1)}, f32[80,128]{1,0:T(8,128)S(1)}, u32[]{:S(2)}, u32[]{:S(2)}) collective-permute-start(f32[80,128]{1,0:T(8,128)S(1)} %add.18), channel_id=1, source_target_pairs={{0,5},{1,4},{2,7},{3,6},{4,1},{5,0},{6,3},{7,2},{8,13},{9,12},{10,... | collective-permute-start | bytes 122888 | tf_op jit(solution)/shard_map/ppermute | solution.py:497
  41.5 1.7 %collective-permute-done.9 = f32[80,128]{1,0:T(8,128)S(1)} collective-permute-done((f32[80,128]{1,0:T(8,128)S(1)}, f32[80,128]{1,0:T(8,128)S(1)}, u32[]{:S(2)}, u32[]{:S(2)}) %collective-permute-start.9) | collective-permute-done | bytes 40992 | tf_op jit(solution)/shard_map/ppermute | solution.py:497
  43.2 0.4 collective-permute-start.10
  43.6 0.9 %collective-permute-done.10.other_ref = f32[80,128]{1,0:T(8,128)S(1)} collective-permute-done((f32[80,128]{1,0:T(8,128)S(1)}, f32[80,128]{1,0:T(8,128)S(1)}, u32[]{:S(2)}, u32[]{:S(2)}) %collective-permute-start.10) | collective-permute-done | bytes 40992 | tf_op jit(solution)/shard_map/ppermute | solution.py:497
  44.5 5.9 %factor.1 = (f32[192,192]{1,0:T(8,128)}, f32[1,192]{1,0:T(1,128)}) custom-call(f32[80,128]{1,0:T(8,128)S(1)} %add.19.own_ref, f32[80,128]{1,0:T(8,128)S(1)} %collective-permute-done.10.other_ref, f32[64,192]{1,0:T(8,128)S(1)} %get-tuple-element.37.refs_0_, f32[64,128]{1,0:T(8,128)S(1)} %get-tuple-element.38.refs_1_, f32[64,64]{1,0:T(8,128)S(1)} %local_factor.5.refs_2_), custom_call_target="tpu_custom_call" | custom-call | tf_op jit(solution)/shard_map/factor/pallas_call | solution.py:474
  (6 shorter events, 0.0 us)
Async XLA Ops:
  4.1 8.8 %copy-start = (f32[2,192,8,128]{3,2,1,0:T(8,128)S(1)}, f32[2,192,8,128]{3,2,1,0:T(8,128)}, u32[]{:S(2)}) copy-start(f32[2,192,8,128]{3,2,1,0:T(8,128)} %param.3) | copy-start | bytes 4718596
  4.1 3.1 %collective-permute-start = (f32[8,200,128]{2,1,0:T(8,128)S(1)}, f32[8,200,128]{2,1,0:T(8,128)S(1)}, u32[]{:S(2)}, u32[]{:S(2)}) collective-permute-start(f32[8,200,128]{2,1,0:T(8,128)S(1)} %get-tuple-element.22), channel_id=1, source_target_pairs={{0,1},{2,3},{4,5},{6,7},{1,0},{3,2},{5,4},{7,6},{8,9},{10,11},{12,... | collective-permute-start | bytes 2457608 | tf_op jit(solution)/shard_map/ppermute | solution.py:491
  4.6 2.6 %collective-permute-start.1 = (f32[4,200,128]{2,1,0:T(8,128)S(1)}, f32[4,200,128]{2,1,0:T(8,128)S(1)}, u32[]{:S(2)}, u32[]{:S(2)}) collective-permute-start(f32[4,200,128]{2,1,0:T(8,128)S(1)} %get-tuple-element.23), channel_id=1, source_target_pairs={{1,2},{3,4},{5,6},{2,1},{4,3},{6,5},{9,10},{11,12},{13,14},{10,9},... | collective-permute-start | bytes 1228808 | tf_op jit(solution)/shard_map/ppermute | solution.py:491
  5.3 7.6 %collective-permute-start.2 = (f32[4,200,128]{2,1,0:T(8,128)}, f32[4,200,128]{2,1,0:T(8,128)}, u32[]{:S(2)}, u32[]{:S(2)}) collective-permute-start(f32[4,200,128]{2,1,0:T(8,128)} %get-tuple-element.24), channel_id=1, source_target_pairs={{1,2},{3,4},{5,6},{2,1},{4,3},{6,5},{9,10},{11,12},{13,14},{10,9},... | collective-permute-start | bytes 1228808 | tf_op jit(solution)/shard_map/ppermute | solution.py:491
  8.3 9.3 %collective-permute-start.3 = (f32[200,128]{1,0:T(8,128)}, f32[200,128]{1,0:T(8,128)S(1)}, u32[]{:S(2)}, u32[]{:S(2)}) collective-permute-start(f32[200,128]{1,0:T(8,128)} %get-tuple-element.28), channel_id=1, source_target_pairs={{0,8},{16,24},{8,0},{24,16},{1,9},{17,25},{9,1},{25,17},{2,10},{18... | collective-permute-start | bytes 307208 | tf_op jit(solution)/shard_map/ppermute | solution.py:491
  10.9 6.6 %collective-permute-start.4 = (f32[200,128]{1,0:T(8,128)S(1)}, f32[200,128]{1,0:T(8,128)S(1)}, u32[]{:S(2)}, u32[]{:S(2)}) collective-permute-start(f32[200,128]{1,0:T(8,128)S(1)} %get-tuple-element.29), channel_id=1, source_target_pairs={{8,16},{0,24},{16,8},{24,0},{9,17},{1,25},{17,9},{25,1},{10,18},{2... | collective-permute-start | bytes 307208 | tf_op jit(solution)/shard_map/ppermute | solution.py:491
  19.8 7.7 %collective-permute-start.5 = (f32[80,128]{1,0:T(8,128)S(1)}, f32[80,128]{1,0:T(8,128)S(1)}, u32[]{:S(2)}, u32[]{:S(2)}) collective-permute-start(f32[80,128]{1,0:T(8,128)S(1)} %slice_select_fusion), channel_id=1, source_target_pairs={{0,1},{1,0},{2,3},{3,2},{4,5},{5,4},{6,7},{7,6},{8,9},{9,8},{10,11... | collective-permute-start | bytes 122888 | tf_op jit(solution)/shard_map/ppermute | solution.py:497
  27.4 3.8 %collective-permute-start.6 = (f32[80,128]{1,0:T(8,128)S(1)}, f32[80,128]{1,0:T(8,128)S(1)}, u32[]{:S(2)}, u32[]{:S(2)}) collective-permute-start(f32[80,128]{1,0:T(8,128)S(1)} %select_add_fusion), channel_id=1, source_target_pairs={{0,9},{1,8},{2,11},{3,10},{4,13},{5,12},{6,15},{7,14},{8,1},{9,0},... | collective-permute-start | bytes 122888 | tf_op jit(solution)/shard_map/ppermute | solution.py:497
  31.2 3.6 %collective-permute-start.7 = (f32[80,128]{1,0:T(8,128)S(1)}, f32[80,128]{1,0:T(8,128)S(1)}, u32[]{:S(2)}, u32[]{:S(2)}) collective-permute-start(f32[80,128]{1,0:T(8,128)S(1)} %add.16), channel_id=1, source_target_pairs={{0,17},{1,16},{2,19},{3,18},{4,21},{5,20},{6,23},{7,22},{8,25},{9,... | collective-permute-start | bytes 122888 | tf_op jit(solution)/shard_map/ppermute | solution.py:497
  34.8 3.8 %collective-permute-start.8 = (f32[80,128]{1,0:T(8,128)S(1)}, f32[80,128]{1,0:T(8,128)S(1)}, u32[]{:S(2)}, u32[]{:S(2)}) collective-permute-start(f32[80,128]{1,0:T(8,128)S(1)} %add.17), channel_id=1, source_target_pairs={{0,3},{1,2},{2,1},{3,0},{4,7},{5,6},{6,5},{7,4},{8,11},{9,10},{10,... | collective-permute-start | bytes 122888 | tf_op jit(solution)/shard_map/ppermute | solution.py:497
  38.6 4.6 %collective-permute-start.9 = (f32[80,128]{1,0:T(8,128)S(1)}, f32[80,128]{1,0:T(8,128)S(1)}, u32[]{:S(2)}, u32[]{:S(2)}) collective-permute-start(f32[80,128]{1,0:T(8,128)S(1)} %add.18), channel_id=1, source_target_pairs={{0,5},{1,4},{2,7},{3,6},{4,1},{5,0},{6,3},{7,2},{8,13},{9,12},{10,... | collective-permute-start | bytes 122888 | tf_op jit(solution)/shard_map/ppermute | solution.py:497
  43.2 1.3 %collective-permute-start.10 = (f32[80,128]{1,0:T(8,128)S(1)}, f32[80,128]{1,0:T(8,128)S(1)}, u32[]{:S(2)}, u32[]{:S(2)}) collective-permute-start(f32[80,128]{1,0:T(8,128)S(1)} %add.19.own_ref), channel_id=1, source_target_pairs={{0,1},{1,0},{2,3},{3,2},{4,5},{5,4},{6,7},{7,6},{8,9},{9,8},{10,11... | collective-permute-start | bytes 122888 | tf_op jit(solution)/shard_map/ppermute | solution.py:497

commit v11 on v10

--- a/solution.py
+++ b/solution.py
@@ -419,7 +419,7 @@
         joined = [jnp.where(l % SUB < STEPS, side[1], side[0]) for side in pair]
         ends[at, :] = jnp.where(l < LANES // 2, joined[0], roll(joined[1], LANES // 2))
 
-    whole = middle_gram[...] + gram_of(ends[...])
+    whole = middle_gram[...] + dot_nt(ends[...], ends[...])
     gram[...] = whole
     packed[...] = pack_blocks(whole, fields // SIDE)
 

time: 50.6 us -> 50.4 us (level)
  no operation moved by 1% of the time
where the time goes in v11:
time: 50.4 us; the launch traced here: 50.2 us
  Pallas kernels  22.5 us (45%)
  starting transfers between devices  22.1 us (44%)
  waiting for transfers between devices  4.01 us (8%)
  other arithmetic  0.75 us (1%)
  between operations  0.75 us (1%)
    pallas_call x10, Pallas kernels, local_call(): pl.pallas_call(body, out_shape=[jax.ShapeDtypeStruct(s, jnp.float32) for...  22.5 us
    ppermute x6, starting transfers between devices, exchange(): return lax.ppermute(cells, ('grp', 'tile'), moves)  15.4 us
    ppermute x5, starting transfers between devices, swap(): return lax.ppermute(cells, axis, pairs + [(b, a) for a, b in pairs])  6.74 us
    ppermute x6, waiting for transfers between devices, exchange(): return lax.ppermute(cells, ('grp', 'tile'), moves)  4 us
  transfers between devices with their start and end apart: 11, of which 5 were waited for; matrix products, arithmetic and copies ran while one was open for 0% of the time, Pallas kernels for 23%

profile of v11, /device:TPU:0, one launch (start us, length us, event | category | flops | bytes accessed | tf_op | source)
XLA Modules:
  0.0 50.2 jit_solution(4718223955757925684)
XLA Ops:
  0.6 0.7 %pad_maximum_fusion.coeffs_hbm.coeffs = f32[2,8,128]{2,1,0:T(8,128)S(1)} fusion(f32[1,8,128]{2,1,0:T(8,128)} %bitcast.6, f32[1,8,128]{2,1,0:T(8,128)} %bitcast.7), kind=kLoop, calls=%fused_computation.2 | loop fusion | flops 2048 | bytes 16384 | tf_op jit(solution)/shard_map/stack | solution.py:530
  1.3 2.8 %edges.1 = (f32[200,128]{1,0:T(8,128)S(1)}, f32[200,128]{1,0:T(8,128)S(1)}, f32[8,200,128]{2,1,0:T(8,128)S(1)}, f32[4,200,128]{2,1,0:T(8,128)S(1)}, f32[4,200,128]{2,1,0:T(8,128)}) custom-call(f32[2,1536,128]{2,1,0:T(8,128)} %bitcast.4, f32[2,8,128]{2,1,0:T(8,128)S(1)} %pad_maximum_fusion.coeffs_hbm.coeffs), custom_call_target="tpu_custom_call" | custom-call | tf_op jit(solution)/shard_map/edges/pallas_call | solution.py:474
  4.1 0.0 copy-start
  4.1 0.5 %collective-permute-start = (f32[8,200,128]{2,1,0:T(8,128)S(1)}, f32[8,200,128]{2,1,0:T(8,128)S(1)}, u32[]{:S(2)}, u32[]{:S(2)}) collective-permute-start(f32[8,200,128]{2,1,0:T(8,128)S(1)} %get-tuple-element.22), channel_id=1, source_target_pairs={{0,1},{2,3},{4,5},{6,7},{1,0},{3,2},{5,4},{7,6},{8,9},{10,11},{12,... | collective-permute-start | bytes 2457608 | tf_op jit(solution)/shard_map/ppermute | solution.py:491
  4.6 0.7 %collective-permute-start.1 = (f32[4,200,128]{2,1,0:T(8,128)S(1)}, f32[4,200,128]{2,1,0:T(8,128)S(1)}, u32[]{:S(2)}, u32[]{:S(2)}) collective-permute-start(f32[4,200,128]{2,1,0:T(8,128)S(1)} %get-tuple-element.23), channel_id=1, source_target_pairs={{1,2},{3,4},{5,6},{2,1},{4,3},{6,5},{9,10},{11,12},{13,14},{10,9},... | collective-permute-start | bytes 1228808 | tf_op jit(solution)/shard_map/ppermute | solution.py:491
  5.3 1.4 %collective-permute-start.2 = (f32[4,200,128]{2,1,0:T(8,128)}, f32[4,200,128]{2,1,0:T(8,128)}, u32[]{:S(2)}, u32[]{:S(2)}) collective-permute-start(f32[4,200,128]{2,1,0:T(8,128)} %get-tuple-element.24), channel_id=1, source_target_pairs={{1,2},{3,4},{5,6},{2,1},{4,3},{6,5},{9,10},{11,12},{13,14},{10,9},... | collective-permute-start | bytes 1228808 | tf_op jit(solution)/shard_map/ppermute | solution.py:491
  6.7 0.5 row_mirror.1.mirrored
  7.2 0.0 collective-permute-done.1.far
  7.3 0.0 collective-permute-done.near
  7.3 1.0 %columns.1 = (f32[4,200,128]{2,1,0:T(8,128)S(1)}, f32[200,128]{1,0:T(8,128)}, f32[200,128]{1,0:T(8,128)S(1)}) custom-call(f32[200,128]{1,0:T(8,128)S(1)} %get-tuple-element.25.last, f32[200,128]{1,0:T(8,128)S(1)} %get-tuple-element.26.first, f32[2,200,128]{2,1,0:T(8,128)S(1)} %row_mirror.1.mirrored, f32[8,200,128]{2,1,0:T(8,128)S(1)} %collective-permute-done.near, ...), custom_call_target="tpu_custom_call" | custom-call | tf_op jit(solution)/shard_map/columns/pallas_call | solution.py:474
  8.3 2.6 %collective-permute-start.3 = (f32[200,128]{1,0:T(8,128)}, f32[200,128]{1,0:T(8,128)S(1)}, u32[]{:S(2)}, u32[]{:S(2)}) collective-permute-start(f32[200,128]{1,0:T(8,128)} %get-tuple-element.28), channel_id=1, source_target_pairs={{0,8},{16,24},{8,0},{24,16},{1,9},{17,25},{9,1},{25,17},{2,10},{18... | collective-permute-start | bytes 307208 | tf_op jit(solution)/shard_map/ppermute | solution.py:491
  10.9 1.5 %collective-permute-start.4 = (f32[200,128]{1,0:T(8,128)S(1)}, f32[200,128]{1,0:T(8,128)S(1)}, u32[]{:S(2)}, u32[]{:S(2)}) collective-permute-start(f32[200,128]{1,0:T(8,128)S(1)} %get-tuple-element.29), channel_id=1, source_target_pairs={{8,16},{0,24},{16,8},{24,0},{9,17},{1,25},{17,9},{25,1},{10,18},{2... | collective-permute-start | bytes 307208 | tf_op jit(solution)/shard_map/ppermute | solution.py:491
  12.4 0.5 column_mirror.1.mirrored
  12.9 0.0 collective-permute-done.2.far_late
  12.9 0.0 copy-done
  12.9 4.6 %evolve.1.middle_gram = f32[192,192]{1,0:T(8,128)S(1)} custom-call(f32[2,1536,128]{2,1,0:T(8,128)S(1)} %bitcast.5, f32[2,8,128]{2,1,0:T(8,128)S(1)} %pad_maximum_fusion.coeffs_hbm.coeffs, f32[8,200,128]{2,1,0:T(8,128)S(1)} %collective-permute-done.near, f32[4,200,128]{2,1,0:T(8,128)S(1)} %collective-permute-done.1.far, ...), custom_call_target="tpu_custom_call" | custom-call | tf_op jit(solution)/shard_map/evolve/pallas_call | solution.py:474
  17.5 0.0 collective-permute-done.3.near
  17.5 0.0 collective-permute-done.4.far
  17.5 2.1 %gram.1 = (f32[160,128]{1,0:T(8,128)S(1)}, f32[192,192]{1,0:T(8,128)S(1)}) custom-call(f32[192,192]{1,0:T(8,128)S(1)} %evolve.1.middle_gram, f32[4,200,128]{2,1,0:T(8,128)S(1)} %get-tuple-element.27.strips, f32[2,200,128]{2,1,0:T(8,128)S(1)} %column_mirror.1.mirrored, f32[200,128]{1,0:T(8,128)S(1)} %collective-permute-done.3.near, ...), custom_call_target="tpu_custom_call" | custom-call | tf_op jit(solution)/shard_map/gram/pallas_call | solution.py:474
  19.7 6.8 %collective-permute-start.5 = (f32[80,128]{1,0:T(8,128)S(1)}, f32[80,128]{1,0:T(8,128)S(1)}, u32[]{:S(2)}, u32[]{:S(2)}) collective-permute-start(f32[80,128]{1,0:T(8,128)S(1)} %slice_select_fusion), channel_id=1, source_target_pairs={{0,1},{1,0},{2,3},{3,2},{4,5},{5,4},{6,7},{7,6},{8,9},{9,8},{10,11... | collective-permute-start | bytes 122888 | tf_op jit(solution)/shard_map/ppermute | solution.py:497
  26.4 0.9 %collective-permute-done.5 = f32[80,128]{1,0:T(8,128)S(1)} collective-permute-done((f32[80,128]{1,0:T(8,128)S(1)}, f32[80,128]{1,0:T(8,128)S(1)}, u32[]{:S(2)}, u32[]{:S(2)}) %collective-permute-start.5) | collective-permute-done | bytes 40992 | tf_op jit(solution)/shard_map/ppermute | solution.py:497
  27.3 1.8 %collective-permute-start.6 = (f32[80,128]{1,0:T(8,128)S(1)}, f32[80,128]{1,0:T(8,128)S(1)}, u32[]{:S(2)}, u32[]{:S(2)}) collective-permute-start(f32[80,128]{1,0:T(8,128)S(1)} %select_add_fusion), channel_id=1, source_target_pairs={{0,9},{1,8},{2,11},{3,10},{4,13},{5,12},{6,15},{7,14},{8,1},{9,0},... | collective-permute-start | bytes 122888 | tf_op jit(solution)/shard_map/ppermute | solution.py:497
  29.1 2.0 %local_factor.3 = (f32[64,192]{1,0:T(8,128)S(1)}, f32[128,128]{1,0:T(8,128)S(1)}) custom-call(f32[192,192]{1,0:T(8,128)S(1)} %get-tuple-element.31.gram), custom_call_target="tpu_custom_call" | custom-call | flops 1000000000 | bytes 1000000 | tf_op jit(solution)/shard_map/local_factor/pallas_call | solution.py:474
  31.1 0.0 collective-permute-done.6
  31.1 1.5 %collective-permute-start.7 = (f32[80,128]{1,0:T(8,128)S(1)}, f32[80,128]{1,0:T(8,128)S(1)}, u32[]{:S(2)}, u32[]{:S(2)}) collective-permute-start(f32[80,128]{1,0:T(8,128)S(1)} %add.16), channel_id=1, source_target_pairs={{0,17},{1,16},{2,19},{3,18},{4,21},{5,20},{6,23},{7,22},{8,25},{9,... | collective-permute-start | bytes 122888 | tf_op jit(solution)/shard_map/ppermute | solution.py:497
  32.6 1.9 %local_factor.4 = (f32[64,128]{1,0:T(8,128)S(1)}, f32[64,64]{1,0:T(8,128)S(1)}) custom-call(f32[128,128]{1,0:T(8,128)S(1)} %get-tuple-element.33.gram), custom_call_target="tpu_custom_call" | custom-call | flops 1000000000 | bytes 1000000 | tf_op jit(solution)/shard_map/local_factor/pallas_call | solution.py:474
  34.5 0.2 collective-permute-done.7
  34.7 2.1 %collective-permute-start.8 = (f32[80,128]{1,0:T(8,128)S(1)}, f32[80,128]{1,0:T(8,128)S(1)}, u32[]{:S(2)}, u32[]{:S(2)}) collective-permute-start(f32[80,128]{1,0:T(8,128)S(1)} %add.17), channel_id=1, source_target_pairs={{0,3},{1,2},{2,1},{3,0},{4,7},{5,6},{6,5},{7,4},{8,11},{9,10},{10,... | collective-permute-start | bytes 122888 | tf_op jit(solution)/shard_map/ppermute | solution.py:497
  36.8 1.3 %local_factor.5.refs_2_ = f32[64,64]{1,0:T(8,128)S(1)} custom-call(f32[64,64]{1,0:T(8,128)S(1)} %get-tuple-element.35.gram), custom_call_target="tpu_custom_call" | custom-call | flops 1000000000 | bytes 1000000 | tf_op jit(solution)/shard_map/local_factor/pallas_call | solution.py:474
  38.1 0.4 collective-permute-done.8
  38.5 2.9 %collective-permute-start.9 = (f32[80,128]{1,0:T(8,128)S(1)}, f32[80,128]{1,0:T(8,128)S(1)}, u32[]{:S(2)}, u32[]{:S(2)}) collective-permute-start(f32[80,128]{1,0:T(8,128)S(1)} %add.18), channel_id=1, source_target_pairs={{0,5},{1,4},{2,7},{3,6},{4,1},{5,0},{6,3},{7,2},{8,13},{9,12},{10,... | collective-permute-start | bytes 122888 | tf_op jit(solution)/shard_map/ppermute | solution.py:497
  41.4 1.7 %collective-permute-done.9 = f32[80,128]{1,0:T(8,128)S(1)} collective-permute-done((f32[80,128]{1,0:T(8,128)S(1)}, f32[80,128]{1,0:T(8,128)S(1)}, u32[]{:S(2)}, u32[]{:S(2)}) %collective-permute-start.9) | collective-permute-done | bytes 40992 | tf_op jit(solution)/shard_map/ppermute | solution.py:497
  43.1 0.4 collective-permute-start.10
  43.5 0.9 %collective-permute-done.10.other_ref = f32[80,128]{1,0:T(8,128)S(1)} collective-permute-done((f32[80,128]{1,0:T(8,128)S(1)}, f32[80,128]{1,0:T(8,128)S(1)}, u32[]{:S(2)}, u32[]{:S(2)}) %collective-permute-start.10) | collective-permute-done | bytes 40992 | tf_op jit(solution)/shard_map/ppermute | solution.py:497
  44.3 5.9 %factor.1 = (f32[192,192]{1,0:T(8,128)}, f32[1,192]{1,0:T(1,128)}) custom-call(f32[80,128]{1,0:T(8,128)S(1)} %add.19.own_ref, f32[80,128]{1,0:T(8,128)S(1)} %collective-permute-done.10.other_ref, f32[64,192]{1,0:T(8,128)S(1)} %get-tuple-element.37.refs_0_, f32[64,128]{1,0:T(8,128)S(1)} %get-tuple-element.38.refs_1_, f32[64,64]{1,0:T(8,128)S(1)} %local_factor.5.refs_2_), custom_call_target="tpu_custom_call" | custom-call | tf_op jit(solution)/shard_map/factor/pallas_call | solution.py:474
  (6 shorter events, 0.0 us)
Async XLA Ops:
  4.1 8.8 %copy-start = (f32[2,192,8,128]{3,2,1,0:T(8,128)S(1)}, f32[2,192,8,128]{3,2,1,0:T(8,128)}, u32[]{:S(2)}) copy-start(f32[2,192,8,128]{3,2,1,0:T(8,128)} %param.3) | copy-start | bytes 4718596
  4.1 3.1 %collective-permute-start = (f32[8,200,128]{2,1,0:T(8,128)S(1)}, f32[8,200,128]{2,1,0:T(8,128)S(1)}, u32[]{:S(2)}, u32[]{:S(2)}) collective-permute-start(f32[8,200,128]{2,1,0:T(8,128)S(1)} %get-tuple-element.22), channel_id=1, source_target_pairs={{0,1},{2,3},{4,5},{6,7},{1,0},{3,2},{5,4},{7,6},{8,9},{10,11},{12,... | collective-permute-start | bytes 2457608 | tf_op jit(solution)/shard_map/ppermute | solution.py:491
  4.6 2.6 %collective-permute-start.1 = (f32[4,200,128]{2,1,0:T(8,128)S(1)}, f32[4,200,128]{2,1,0:T(8,128)S(1)}, u32[]{:S(2)}, u32[]{:S(2)}) collective-permute-start(f32[4,200,128]{2,1,0:T(8,128)S(1)} %get-tuple-element.23), channel_id=1, source_target_pairs={{1,2},{3,4},{5,6},{2,1},{4,3},{6,5},{9,10},{11,12},{13,14},{10,9},... | collective-permute-start | bytes 1228808 | tf_op jit(solution)/shard_map/ppermute | solution.py:491
  5.3 7.6 %collective-permute-start.2 = (f32[4,200,128]{2,1,0:T(8,128)}, f32[4,200,128]{2,1,0:T(8,128)}, u32[]{:S(2)}, u32[]{:S(2)}) collective-permute-start(f32[4,200,128]{2,1,0:T(8,128)} %get-tuple-element.24), channel_id=1, source_target_pairs={{1,2},{3,4},{5,6},{2,1},{4,3},{6,5},{9,10},{11,12},{13,14},{10,9},... | collective-permute-start | bytes 1228808 | tf_op jit(solution)/shard_map/ppermute | solution.py:491
  8.3 9.3 %collective-permute-start.3 = (f32[200,128]{1,0:T(8,128)}, f32[200,128]{1,0:T(8,128)S(1)}, u32[]{:S(2)}, u32[]{:S(2)}) collective-permute-start(f32[200,128]{1,0:T(8,128)} %get-tuple-element.28), channel_id=1, source_target_pairs={{0,8},{16,24},{8,0},{24,16},{1,9},{17,25},{9,1},{25,17},{2,10},{18... | collective-permute-start | bytes 307208 | tf_op jit(solution)/shard_map/ppermute | solution.py:491
  10.9 6.6 %collective-permute-start.4 = (f32[200,128]{1,0:T(8,128)S(1)}, f32[200,128]{1,0:T(8,128)S(1)}, u32[]{:S(2)}, u32[]{:S(2)}) collective-permute-start(f32[200,128]{1,0:T(8,128)S(1)} %get-tuple-element.29), channel_id=1, source_target_pairs={{8,16},{0,24},{16,8},{24,0},{9,17},{1,25},{17,9},{25,1},{10,18},{2... | collective-permute-start | bytes 307208 | tf_op jit(solution)/shard_map/ppermute | solution.py:491
  19.7 7.6 %collective-permute-start.5 = (f32[80,128]{1,0:T(8,128)S(1)}, f32[80,128]{1,0:T(8,128)S(1)}, u32[]{:S(2)}, u32[]{:S(2)}) collective-permute-start(f32[80,128]{1,0:T(8,128)S(1)} %slice_select_fusion), channel_id=1, source_target_pairs={{0,1},{1,0},{2,3},{3,2},{4,5},{5,4},{6,7},{7,6},{8,9},{9,8},{10,11... | collective-permute-start | bytes 122888 | tf_op jit(solution)/shard_map/ppermute | solution.py:497
  27.3 3.8 %collective-permute-start.6 = (f32[80,128]{1,0:T(8,128)S(1)}, f32[80,128]{1,0:T(8,128)S(1)}, u32[]{:S(2)}, u32[]{:S(2)}) collective-permute-start(f32[80,128]{1,0:T(8,128)S(1)} %select_add_fusion), channel_id=1, source_target_pairs={{0,9},{1,8},{2,11},{3,10},{4,13},{5,12},{6,15},{7,14},{8,1},{9,0},... | collective-permute-start | bytes 122888 | tf_op jit(solution)/shard_map/ppermute | solution.py:497
  31.1 3.6 %collective-permute-start.7 = (f32[80,128]{1,0:T(8,128)S(1)}, f32[80,128]{1,0:T(8,128)S(1)}, u32[]{:S(2)}, u32[]{:S(2)}) collective-permute-start(f32[80,128]{1,0:T(8,128)S(1)} %add.16), channel_id=1, source_target_pairs={{0,17},{1,16},{2,19},{3,18},{4,21},{5,20},{6,23},{7,22},{8,25},{9,... | collective-permute-start | bytes 122888 | tf_op jit(solution)/shard_map/ppermute | solution.py:497
  34.7 3.8 %collective-permute-start.8 = (f32[80,128]{1,0:T(8,128)S(1)}, f32[80,128]{1,0:T(8,128)S(1)}, u32[]{:S(2)}, u32[]{:S(2)}) collective-permute-start(f32[80,128]{1,0:T(8,128)S(1)} %add.17), channel_id=1, source_target_pairs={{0,3},{1,2},{2,1},{3,0},{4,7},{5,6},{6,5},{7,4},{8,11},{9,10},{10,... | collective-permute-start | bytes 122888 | tf_op jit(solution)/shard_map/ppermute | solution.py:497
  38.5 4.6 %collective-permute-start.9 = (f32[80,128]{1,0:T(8,128)S(1)}, f32[80,128]{1,0:T(8,128)S(1)}, u32[]{:S(2)}, u32[]{:S(2)}) collective-permute-start(f32[80,128]{1,0:T(8,128)S(1)} %add.18), channel_id=1, source_target_pairs={{0,5},{1,4},{2,7},{3,6},{4,1},{5,0},{6,3},{7,2},{8,13},{9,12},{10,... | collective-permute-start | bytes 122888 | tf_op jit(solution)/shard_map/ppermute | solution.py:497
  43.1 1.3 %collective-permute-start.10 = (f32[80,128]{1,0:T(8,128)S(1)}, f32[80,128]{1,0:T(8,128)S(1)}, u32[]{:S(2)}, u32[]{:S(2)}) collective-permute-start(f32[80,128]{1,0:T(8,128)S(1)} %add.19.own_ref), channel_id=1, source_target_pairs={{0,1},{1,0},{2,3},{3,2},{4,5},{5,4},{6,7},{7,6},{8,9},{9,8},{10,11... | collective-permute-start | bytes 122888 | tf_op jit(solution)/shard_map/ppermute | solution.py:497

commit v12 on v11

--- a/solution.py
+++ b/solution.py
@@ -511,10 +511,10 @@
     high_half = parity()
     low, high = packed[:half], packed[half:]
     part = jnp.where(high_half, high, low) + exchange(jnp.where(high_half, low, high), 0, 1)
-    for axis in ("grp", "tile"):
+    for axis in ("tile", "grp"):
         bit = 1 if axis == "grp" else 2
         while bit < lax.axis_size(axis):
-            if axis == "tile" and 2 * bit >= lax.axis_size(axis):
+            if axis == "grp" and 2 * bit >= lax.axis_size(axis):
                 part, beside = lax.optimization_barrier((part, beside))
             part = part + (exchange(part, bit, 1) if axis == "grp" else exchange(part, 0, bit + 1))
             bit *= 2

time: 50.4 us -> 50.5 us (level)
  waiting for transfers between devices: 4.01 us -> 4.85 us
  starting transfers between devices: 22.1 us -> 21.3 us
    ppermute x6, waiting for transfers between devices: 4 us -> 4.84 us  [exchange(): return lax.ppermute(cells, ('grp', 'tile'), moves)]
    ppermute x6, starting transfers between devices: 15.4 us -> 14.6 us  [exchange(): return lax.ppermute(cells, ('grp', 'tile'), moves)]
  transfers between devices with their start and end apart: 11 -> 11, of which waited for: 5 -> 4; matrix products, arithmetic and copies ran while one was open for 0% -> 0% of each run, Pallas kernels for 23% -> 23%
where the time goes in v12:
time: 50.5 us; the launch traced here: 50.2 us
  Pallas kernels  22.5 us (45%)
  starting transfers between devices  21.3 us (42%)
  waiting for transfers between devices  4.85 us (10%)
  between operations  0.76 us (2%)
  other arithmetic  0.75 us (1%)
    pallas_call x10, Pallas kernels, local_call(): pl.pallas_call(body, out_shape=[jax.ShapeDtypeStruct(s, jnp.float32) for...  22.5 us
    ppermute x6, starting transfers between devices, exchange(): return lax.ppermute(cells, ('grp', 'tile'), moves)  14.6 us
    ppermute x5, starting transfers between devices, swap(): return lax.ppermute(cells, axis, pairs + [(b, a) for a, b in pairs])  6.74 us
    ppermute x6, waiting for transfers between devices, exchange(): return lax.ppermute(cells, ('grp', 'tile'), moves)  4.84 us
  transfers between devices with their start and end apart: 11, of which 4 were waited for; matrix products, arithmetic and copies ran while one was open for 0% of the time, Pallas kernels for 23%

profile of v12, /device:TPU:0, one launch (start us, length us, event | category | flops | bytes accessed | tf_op | source)
XLA Modules:
  0.0 50.2 jit_solution(7736049696692301182)
XLA Ops:
  0.6 0.7 %pad_maximum_fusion.coeffs_hbm.coeffs = f32[2,8,128]{2,1,0:T(8,128)S(1)} fusion(f32[1,8,128]{2,1,0:T(8,128)} %bitcast.6, f32[1,8,128]{2,1,0:T(8,128)} %bitcast.7), kind=kLoop, calls=%fused_computation.2 | loop fusion | flops 2048 | bytes 16384 | tf_op jit(solution)/shard_map/stack | solution.py:530
  1.3 2.8 %edges.1 = (f32[200,128]{1,0:T(8,128)S(1)}, f32[200,128]{1,0:T(8,128)S(1)}, f32[8,200,128]{2,1,0:T(8,128)S(1)}, f32[4,200,128]{2,1,0:T(8,128)S(1)}, f32[4,200,128]{2,1,0:T(8,128)}) custom-call(f32[2,1536,128]{2,1,0:T(8,128)} %bitcast.4, f32[2,8,128]{2,1,0:T(8,128)S(1)} %pad_maximum_fusion.coeffs_hbm.coeffs), custom_call_target="tpu_custom_call" | custom-call | tf_op jit(solution)/shard_map/edges/pallas_call | solution.py:474
  4.1 0.0 copy-start
  4.1 0.5 %collective-permute-start = (f32[8,200,128]{2,1,0:T(8,128)S(1)}, f32[8,200,128]{2,1,0:T(8,128)S(1)}, u32[]{:S(2)}, u32[]{:S(2)}) collective-permute-start(f32[8,200,128]{2,1,0:T(8,128)S(1)} %get-tuple-element.22), channel_id=1, source_target_pairs={{0,1},{2,3},{4,5},{6,7},{1,0},{3,2},{5,4},{7,6},{8,9},{10,11},{12,... | collective-permute-start | bytes 2457608 | tf_op jit(solution)/shard_map/ppermute | solution.py:491
  4.6 0.7 %collective-permute-start.1 = (f32[4,200,128]{2,1,0:T(8,128)S(1)}, f32[4,200,128]{2,1,0:T(8,128)S(1)}, u32[]{:S(2)}, u32[]{:S(2)}) collective-permute-start(f32[4,200,128]{2,1,0:T(8,128)S(1)} %get-tuple-element.23), channel_id=1, source_target_pairs={{1,2},{3,4},{5,6},{2,1},{4,3},{6,5},{9,10},{11,12},{13,14},{10,9},... | collective-permute-start | bytes 1228808 | tf_op jit(solution)/shard_map/ppermute | solution.py:491
  5.3 1.4 %collective-permute-start.2 = (f32[4,200,128]{2,1,0:T(8,128)}, f32[4,200,128]{2,1,0:T(8,128)}, u32[]{:S(2)}, u32[]{:S(2)}) collective-permute-start(f32[4,200,128]{2,1,0:T(8,128)} %get-tuple-element.24), channel_id=1, source_target_pairs={{1,2},{3,4},{5,6},{2,1},{4,3},{6,5},{9,10},{11,12},{13,14},{10,9},... | collective-permute-start | bytes 1228808 | tf_op jit(solution)/shard_map/ppermute | solution.py:491
  6.7 0.5 row_mirror.1.mirrored
  7.2 0.0 collective-permute-done.1.far
  7.3 0.0 collective-permute-done.near
  7.3 1.0 %columns.1 = (f32[4,200,128]{2,1,0:T(8,128)S(1)}, f32[200,128]{1,0:T(8,128)}, f32[200,128]{1,0:T(8,128)S(1)}) custom-call(f32[200,128]{1,0:T(8,128)S(1)} %get-tuple-element.25.last, f32[200,128]{1,0:T(8,128)S(1)} %get-tuple-element.26.first, f32[2,200,128]{2,1,0:T(8,128)S(1)} %row_mirror.1.mirrored, f32[8,200,128]{2,1,0:T(8,128)S(1)} %collective-permute-done.near, ...), custom_call_target="tpu_custom_call" | custom-call | tf_op jit(solution)/shard_map/columns/pallas_call | solution.py:474
  8.3 2.6 %collective-permute-start.3 = (f32[200,128]{1,0:T(8,128)}, f32[200,128]{1,0:T(8,128)S(1)}, u32[]{:S(2)}, u32[]{:S(2)}) collective-permute-start(f32[200,128]{1,0:T(8,128)} %get-tuple-element.28), channel_id=1, source_target_pairs={{0,8},{16,24},{8,0},{24,16},{1,9},{17,25},{9,1},{25,17},{2,10},{18... | collective-permute-start | bytes 307208 | tf_op jit(solution)/shard_map/ppermute | solution.py:491
  10.9 1.5 %collective-permute-start.4 = (f32[200,128]{1,0:T(8,128)S(1)}, f32[200,128]{1,0:T(8,128)S(1)}, u32[]{:S(2)}, u32[]{:S(2)}) collective-permute-start(f32[200,128]{1,0:T(8,128)S(1)} %get-tuple-element.29), channel_id=1, source_target_pairs={{8,16},{0,24},{16,8},{24,0},{9,17},{1,25},{17,9},{25,1},{10,18},{2... | collective-permute-start | bytes 307208 | tf_op jit(solution)/shard_map/ppermute | solution.py:491
  12.4 0.5 column_mirror.1.mirrored
  12.9 0.0 collective-permute-done.2.far_late
  12.9 0.0 copy-done
  12.9 4.6 %evolve.1.middle_gram = f32[192,192]{1,0:T(8,128)S(1)} custom-call(f32[2,1536,128]{2,1,0:T(8,128)S(1)} %bitcast.5, f32[2,8,128]{2,1,0:T(8,128)S(1)} %pad_maximum_fusion.coeffs_hbm.coeffs, f32[8,200,128]{2,1,0:T(8,128)S(1)} %collective-permute-done.near, f32[4,200,128]{2,1,0:T(8,128)S(1)} %collective-permute-done.1.far, ...), custom_call_target="tpu_custom_call" | custom-call | tf_op jit(solution)/shard_map/evolve/pallas_call | solution.py:474
  17.5 0.0 collective-permute-done.3.near
  17.5 0.0 collective-permute-done.4.far
  17.5 2.1 %gram.1 = (f32[160,128]{1,0:T(8,128)S(1)}, f32[192,192]{1,0:T(8,128)S(1)}) custom-call(f32[192,192]{1,0:T(8,128)S(1)} %evolve.1.middle_gram, f32[4,200,128]{2,1,0:T(8,128)S(1)} %get-tuple-element.27.strips, f32[2,200,128]{2,1,0:T(8,128)S(1)} %column_mirror.1.mirrored, f32[200,128]{1,0:T(8,128)S(1)} %collective-permute-done.3.near, ...), custom_call_target="tpu_custom_call" | custom-call | tf_op jit(solution)/shard_map/gram/pallas_call | solution.py:474
  19.7 6.8 %collective-permute-start.5 = (f32[80,128]{1,0:T(8,128)S(1)}, f32[80,128]{1,0:T(8,128)S(1)}, u32[]{:S(2)}, u32[]{:S(2)}) collective-permute-start(f32[80,128]{1,0:T(8,128)S(1)} %slice_select_fusion), channel_id=1, source_target_pairs={{0,1},{1,0},{2,3},{3,2},{4,5},{5,4},{6,7},{7,6},{8,9},{9,8},{10,11... | collective-permute-start | bytes 122888 | tf_op jit(solution)/shard_map/ppermute | solution.py:497
  26.4 0.9 %collective-permute-done.5 = f32[80,128]{1,0:T(8,128)S(1)} collective-permute-done((f32[80,128]{1,0:T(8,128)S(1)}, f32[80,128]{1,0:T(8,128)S(1)}, u32[]{:S(2)}, u32[]{:S(2)}) %collective-permute-start.5) | collective-permute-done | bytes 40992 | tf_op jit(solution)/shard_map/ppermute | solution.py:497
  27.3 2.4 %collective-permute-start.6 = (f32[80,128]{1,0:T(8,128)S(1)}, f32[80,128]{1,0:T(8,128)S(1)}, u32[]{:S(2)}, u32[]{:S(2)}) collective-permute-start(f32[80,128]{1,0:T(8,128)S(1)} %select_add_fusion), channel_id=1, source_target_pairs={{0,3},{1,2},{2,1},{3,0},{4,7},{5,6},{6,5},{7,4},{8,11},{9,10},{10,... | collective-permute-start | bytes 122888 | tf_op jit(solution)/shard_map/ppermute | solution.py:497
  29.7 2.0 %local_factor.3 = (f32[64,192]{1,0:T(8,128)S(1)}, f32[128,128]{1,0:T(8,128)S(1)}) custom-call(f32[192,192]{1,0:T(8,128)S(1)} %get-tuple-element.31.gram), custom_call_target="tpu_custom_call" | custom-call | flops 1000000000 | bytes 1000000 | tf_op jit(solution)/shard_map/local_factor/pallas_call | solution.py:474
  31.7 0.0 collective-permute-done.6
  31.8 2.5 %collective-permute-start.7 = (f32[80,128]{1,0:T(8,128)S(1)}, f32[80,128]{1,0:T(8,128)S(1)}, u32[]{:S(2)}, u32[]{:S(2)}) collective-permute-start(f32[80,128]{1,0:T(8,128)S(1)} %add.16), channel_id=1, source_target_pairs={{0,5},{1,4},{2,7},{3,6},{4,1},{5,0},{6,3},{7,2},{8,13},{9,12},{10,... | collective-permute-start | bytes 122888 | tf_op jit(solution)/shard_map/ppermute | solution.py:497
  34.3 1.9 %local_factor.4 = (f32[64,128]{1,0:T(8,128)S(1)}, f32[64,64]{1,0:T(8,128)S(1)}) custom-call(f32[128,128]{1,0:T(8,128)S(1)} %get-tuple-element.33.gram), custom_call_target="tpu_custom_call" | custom-call | flops 1000000000 | bytes 1000000 | tf_op jit(solution)/shard_map/local_factor/pallas_call | solution.py:474
  36.2 0.0 collective-permute-done.7
  36.2 1.5 %collective-permute-start.8 = (f32[80,128]{1,0:T(8,128)S(1)}, f32[80,128]{1,0:T(8,128)S(1)}, u32[]{:S(2)}, u32[]{:S(2)}) collective-permute-start(f32[80,128]{1,0:T(8,128)S(1)} %add.17), channel_id=1, source_target_pairs={{0,9},{1,8},{2,11},{3,10},{4,13},{5,12},{6,15},{7,14},{8,1},{9,0},... | collective-permute-start | bytes 122888 | tf_op jit(solution)/shard_map/ppermute | solution.py:497
  37.7 1.3 %local_factor.5.refs_2_ = f32[64,64]{1,0:T(8,128)S(1)} custom-call(f32[64,64]{1,0:T(8,128)S(1)} %get-tuple-element.35.gram), custom_call_target="tpu_custom_call" | custom-call | flops 1000000000 | bytes 1000000 | tf_op jit(solution)/shard_map/local_factor/pallas_call | solution.py:474
  39.0 0.7 %collective-permute-done.8 = f32[80,128]{1,0:T(8,128)S(1)} collective-permute-done((f32[80,128]{1,0:T(8,128)S(1)}, f32[80,128]{1,0:T(8,128)S(1)}, u32[]{:S(2)}, u32[]{:S(2)}) %collective-permute-start.8) | collective-permute-done | bytes 40992 | tf_op jit(solution)/shard_map/ppermute | solution.py:497
  39.7 1.0 %collective-permute-start.9 = (f32[80,128]{1,0:T(8,128)S(1)}, f32[80,128]{1,0:T(8,128)S(1)}, u32[]{:S(2)}, u32[]{:S(2)}) collective-permute-start(f32[80,128]{1,0:T(8,128)S(1)} %add.18), channel_id=1, source_target_pairs={{0,17},{1,16},{2,19},{3,18},{4,21},{5,20},{6,23},{7,22},{8,25},{9,... | collective-permute-start | bytes 122888 | tf_op jit(solution)/shard_map/ppermute | solution.py:497
  40.8 2.4 %collective-permute-done.9 = f32[80,128]{1,0:T(8,128)S(1)} collective-permute-done((f32[80,128]{1,0:T(8,128)S(1)}, f32[80,128]{1,0:T(8,128)S(1)}, u32[]{:S(2)}, u32[]{:S(2)}) %collective-permute-start.9) | collective-permute-done | bytes 40992 | tf_op jit(solution)/shard_map/ppermute | solution.py:497
  43.2 0.3 collective-permute-start.10
  43.5 0.9 %collective-permute-done.10.other_ref = f32[80,128]{1,0:T(8,128)S(1)} collective-permute-done((f32[80,128]{1,0:T(8,128)S(1)}, f32[80,128]{1,0:T(8,128)S(1)}, u32[]{:S(2)}, u32[]{:S(2)}) %collective-permute-start.10) | collective-permute-done | bytes 40992 | tf_op jit(solution)/shard_map/ppermute | solution.py:497
  44.4 5.8 %factor.1 = (f32[192,192]{1,0:T(8,128)}, f32[1,192]{1,0:T(1,128)}) custom-call(f32[80,128]{1,0:T(8,128)S(1)} %add.19.own_ref, f32[80,128]{1,0:T(8,128)S(1)} %collective-permute-done.10.other_ref, f32[64,192]{1,0:T(8,128)S(1)} %get-tuple-element.37.refs_0_, f32[64,128]{1,0:T(8,128)S(1)} %get-tuple-element.38.refs_1_, f32[64,64]{1,0:T(8,128)S(1)} %local_factor.5.refs_2_), custom_call_target="tpu_custom_call" | custom-call | tf_op jit(solution)/shard_map/factor/pallas_call | solution.py:474
  (6 shorter events, 0.0 us)
Async XLA Ops:
  4.1 8.8 %copy-start = (f32[2,192,8,128]{3,2,1,0:T(8,128)S(1)}, f32[2,192,8,128]{3,2,1,0:T(8,128)}, u32[]{:S(2)}) copy-start(f32[2,192,8,128]{3,2,1,0:T(8,128)} %param.3) | copy-start | bytes 4718596
  4.1 3.1 %collective-permute-start = (f32[8,200,128]{2,1,0:T(8,128)S(1)}, f32[8,200,128]{2,1,0:T(8,128)S(1)}, u32[]{:S(2)}, u32[]{:S(2)}) collective-permute-start(f32[8,200,128]{2,1,0:T(8,128)S(1)} %get-tuple-element.22), channel_id=1, source_target_pairs={{0,1},{2,3},{4,5},{6,7},{1,0},{3,2},{5,4},{7,6},{8,9},{10,11},{12,... | collective-permute-start | bytes 2457608 | tf_op jit(solution)/shard_map/ppermute | solution.py:491
  4.6 2.6 %collective-permute-start.1 = (f32[4,200,128]{2,1,0:T(8,128)S(1)}, f32[4,200,128]{2,1,0:T(8,128)S(1)}, u32[]{:S(2)}, u32[]{:S(2)}) collective-permute-start(f32[4,200,128]{2,1,0:T(8,128)S(1)} %get-tuple-element.23), channel_id=1, source_target_pairs={{1,2},{3,4},{5,6},{2,1},{4,3},{6,5},{9,10},{11,12},{13,14},{10,9},... | collective-permute-start | bytes 1228808 | tf_op jit(solution)/shard_map/ppermute | solution.py:491
  5.3 7.6 %collective-permute-start.2 = (f32[4,200,128]{2,1,0:T(8,128)}, f32[4,200,128]{2,1,0:T(8,128)}, u32[]{:S(2)}, u32[]{:S(2)}) collective-permute-start(f32[4,200,128]{2,1,0:T(8,128)} %get-tuple-element.24), channel_id=1, source_target_pairs={{1,2},{3,4},{5,6},{2,1},{4,3},{6,5},{9,10},{11,12},{13,14},{10,9},... | collective-permute-start | bytes 1228808 | tf_op jit(solution)/shard_map/ppermute | solution.py:491
  8.3 9.3 %collective-permute-start.3 = (f32[200,128]{1,0:T(8,128)}, f32[200,128]{1,0:T(8,128)S(1)}, u32[]{:S(2)}, u32[]{:S(2)}) collective-permute-start(f32[200,128]{1,0:T(8,128)} %get-tuple-element.28), channel_id=1, source_target_pairs={{0,8},{16,24},{8,0},{24,16},{1,9},{17,25},{9,1},{25,17},{2,10},{18... | collective-permute-start | bytes 307208 | tf_op jit(solution)/shard_map/ppermute | solution.py:491
  10.9 6.6 %collective-permute-start.4 = (f32[200,128]{1,0:T(8,128)S(1)}, f32[200,128]{1,0:T(8,128)S(1)}, u32[]{:S(2)}, u32[]{:S(2)}) collective-permute-start(f32[200,128]{1,0:T(8,128)S(1)} %get-tuple-element.29), channel_id=1, source_target_pairs={{8,16},{0,24},{16,8},{24,0},{9,17},{1,25},{17,9},{25,1},{10,18},{2... | collective-permute-start | bytes 307208 | tf_op jit(solution)/shard_map/ppermute | solution.py:491
  19.7 7.6 %collective-permute-start.5 = (f32[80,128]{1,0:T(8,128)S(1)}, f32[80,128]{1,0:T(8,128)S(1)}, u32[]{:S(2)}, u32[]{:S(2)}) collective-permute-start(f32[80,128]{1,0:T(8,128)S(1)} %slice_select_fusion), channel_id=1, source_target_pairs={{0,1},{1,0},{2,3},{3,2},{4,5},{5,4},{6,7},{7,6},{8,9},{9,8},{10,11... | collective-permute-start | bytes 122888 | tf_op jit(solution)/shard_map/ppermute | solution.py:497
  27.3 4.4 %collective-permute-start.6 = (f32[80,128]{1,0:T(8,128)S(1)}, f32[80,128]{1,0:T(8,128)S(1)}, u32[]{:S(2)}, u32[]{:S(2)}) collective-permute-start(f32[80,128]{1,0:T(8,128)S(1)} %select_add_fusion), channel_id=1, source_target_pairs={{0,3},{1,2},{2,1},{3,0},{4,7},{5,6},{6,5},{7,4},{8,11},{9,10},{10,... | collective-permute-start | bytes 122888 | tf_op jit(solution)/shard_map/ppermute | solution.py:497
  31.8 4.5 %collective-permute-start.7 = (f32[80,128]{1,0:T(8,128)S(1)}, f32[80,128]{1,0:T(8,128)S(1)}, u32[]{:S(2)}, u32[]{:S(2)}) collective-permute-start(f32[80,128]{1,0:T(8,128)S(1)} %add.16), channel_id=1, source_target_pairs={{0,5},{1,4},{2,7},{3,6},{4,1},{5,0},{6,3},{7,2},{8,13},{9,12},{10,... | collective-permute-start | bytes 122888 | tf_op jit(solution)/shard_map/ppermute | solution.py:497
  36.2 3.5 %collective-permute-start.8 = (f32[80,128]{1,0:T(8,128)S(1)}, f32[80,128]{1,0:T(8,128)S(1)}, u32[]{:S(2)}, u32[]{:S(2)}) collective-permute-start(f32[80,128]{1,0:T(8,128)S(1)} %add.17), channel_id=1, source_target_pairs={{0,9},{1,8},{2,11},{3,10},{4,13},{5,12},{6,15},{7,14},{8,1},{9,0},... | collective-permute-start | bytes 122888 | tf_op jit(solution)/shard_map/ppermute | solution.py:497
  39.7 3.4 %collective-permute-start.9 = (f32[80,128]{1,0:T(8,128)S(1)}, f32[80,128]{1,0:T(8,128)S(1)}, u32[]{:S(2)}, u32[]{:S(2)}) collective-permute-start(f32[80,128]{1,0:T(8,128)S(1)} %add.18), channel_id=1, source_target_pairs={{0,17},{1,16},{2,19},{3,18},{4,21},{5,20},{6,23},{7,22},{8,25},{9,... | collective-permute-start | bytes 122888 | tf_op jit(solution)/shard_map/ppermute | solution.py:497
  43.2 1.2 %collective-permute-start.10 = (f32[80,128]{1,0:T(8,128)S(1)}, f32[80,128]{1,0:T(8,128)S(1)}, u32[]{:S(2)}, u32[]{:S(2)}) collective-permute-start(f32[80,128]{1,0:T(8,128)S(1)} %add.19.own_ref), channel_id=1, source_target_pairs={{0,1},{1,0},{2,3},{3,2},{4,5},{5,4},{6,7},{7,6},{8,9},{9,8},{10,11... | collective-permute-start | bytes 122888 | tf_op jit(solution)/shard_map/ppermute | solution.py:497
